TPU v7x, 512 devices: a whole 4x4x16 slice. The times are simulated.
512 devices in a mesh: row: 16 (over z_hi, x, core), col: 32 (over y, z_lo).
Axes of the slice: x: 4, y: 4, z: 16 (z_hi: 2, z_lo: 8; z = z_hi * 8 + z_lo), core: 2. Of those that a mesh axis runs over, the one named last changes fastest.
Arguments:
- volt_init: float32 [128, 512, 400], P('row', 'col'), may hold values from -6 to 6
- curr_init: float32 [128, 512, 400], P('row', 'col'), may hold values from -6 to 6
- local_inverse: bfloat16 [128, 400, 400], P('row'), may hold values from -1 to 2, as said below
- schur_inverse: bfloat16 [4096, 4096], P('row', 'col'), may hold values from -1 to 2, as said below
- ind_gain: float32 [128, 400], P('row'), may hold values from 0.05 to 0.5
- tie: float32 [128, 64], P('row'), may hold values from 0.3 to 3
- port_map: int32 [128, 64], P('row'), may hold values from 0 to 4095
- breaker: int32 [128, 512, 400], P('row', 'col'), may hold values 0 or 1
- fault_time: int32 [512], P('col'), may hold values from 0 to 2
- fault_node: int32 [512], P('col'), may hold values from 0 to 51199
Outputs:
- volt_final: float32 [128, 512, 400], P('row', 'col')
- curr_final: float32 [128, 512, 400], P('row', 'col')
- iface_volt: float32 [512, 4096], P('col', 'row')
Inputs may be any that keep to these rules, and one draw needn't show every extreme that they name: `local_inverse`: diagonal entries between 0.5 and 1.5; off-diagonal entries independent. `schur_inverse`: diagonal entries between 0.5 and 1.5; off-diagonal entries independent.
All inputs are finite; a program needn't handle non-finite values. No bound on the sum of `breaker` on one device may be relied on, other than what follows from the above.
Results may differ from a plain program's by a relative error of at most 0.0068.
Values may be sent and summed in bfloat16 or wider, within the bound.
No kernel may reach another device: no remote copies, remote signals or barrier semaphores. Data moves between devices by JAX's collectives and lax.ppermute only.
A program may use at most 64 MiB of HBM per device.

v0:
```python
import jax
import jax.numpy as jnp
from jax import lax
from jax.sharding import PartitionSpec as P

STEPS = 2


def local(
    volt_init,
    curr_init,
    local_inverse,
    schur_inverse,
    ind_gain,
    tie,
    port_map,
    breaker,
    fault_time,
    fault_node,
):
    sub_count, scen_count, node_count = volt_init.shape
    port_count = tie.shape[1]
    iface_width = lax.axis_size("row") * schur_inverse.shape[0]
    volt = volt_init
    curr = curr_init
    closed = breaker.astype(jnp.float32)
    first_sub = lax.axis_index("row") * sub_count
    node_ids = (first_sub + jnp.arange(sub_count, dtype=jnp.int32))[
        :, None
    ] * node_count + jnp.arange(node_count, dtype=jnp.int32)[None, :]
    hits = node_ids[:, None, :] == fault_node[None, :, None]
    flat_map = port_map.reshape(-1)
    port_inverse = local_inverse[:, :port_count, :]
    iface_block = jnp.zeros((scen_count, schur_inverse.shape[0]), jnp.float32)
    for step in range(STEPS):
        hist = closed * (curr + ind_gain[:, None, :] * volt)
        active = (step >= fault_time)[None, :, None]
        fault_on = jnp.where(hits & active, 1.0, 0.0).astype(jnp.float32)
        inject = (-hist - 2.0 * fault_on * volt).astype(jnp.bfloat16)
        open_volt = jnp.einsum(
            "ksn,knm->ksm", inject, local_inverse, preferred_element_type=jnp.float32
        )
        values = tie[:, None, :] * open_volt[:, :, :port_count]
        flat_values = jnp.transpose(values, (0, 2, 1)).reshape(sub_count * port_count, scen_count)
        partial_rhs = jax.ops.segment_sum(flat_values, flat_map, iface_width).T
        owned = lax.psum_scatter(partial_rhs, "row", scatter_dimension=1, tiled=True)
        rhs_half = lax.all_gather(owned.astype(jnp.bfloat16), "row", axis=1, tiled=True)
        iface_block = lax.dot_general(
            rhs_half,
            lax.all_gather(schur_inverse, "col", axis=1, tiled=True),
            (((1,), (1,)), ((), ())),
            preferred_element_type=jnp.float32,
        )
        iface_full = lax.all_gather(iface_block, "row", axis=1, tiled=True)
        picked = jnp.take(iface_full, flat_map, axis=1).reshape(scen_count, sub_count, port_count)
        drive = (tie[:, None, :] * jnp.transpose(picked, (1, 0, 2))).astype(jnp.bfloat16)
        volt_next = open_volt + jnp.einsum(
            "ksp,kpn->ksn", drive, port_inverse, preferred_element_type=jnp.float32
        )
        curr = closed * (curr + ind_gain[:, None, :] * (volt_next + volt))
        volt = volt_next
    return (volt, curr, iface_block)


def solution(mesh):
    placed = (
        P("row", "col", None),
        P("row", "col", None),
        P("row", None, None),
        P("row", "col"),
        P("row", None),
        P("row", None),
        P("row", None),
        P("row", "col", None),
        P("col"),
        P("col"),
    )
    return jax.shard_map(
        local,
        mesh=mesh,
        in_specs=placed,
        out_specs=(P("row", "col", None), P("row", "col", None), P("col", "row")),
        check_vma=False,
    )
```

profile of v0, /device:TPU:1, one launch (start us, length us, event | category | flops | bytes accessed | tf_op | source)
XLA Modules:
  0.0 528.2 jit_solution(18253948877012956297)
XLA Ops:
  8.1 1.2 broadcast_compare_fusion
  9.3 0.8 reshape.77
  10.1 2.8 fusion.6
  13.0 0.7 copy-done.3
  13.8 3.7 scatter_custom_fusion
  19.3 122.5 %reduce-scatter.3.cloned.1.call-done = f32[16,256]{0,1:T(8,128)} async-done(((f32[16,4096]{0,1:T(8,128)}), f32[16,256]{0,1:T(8,128)}) %reduce-scatter.3.cloned.1.call-update) | async-done | bytes 16400 | tf_op jit(solution)/shard_map/reduce_scatter | solution.py:46
  141.7 0.9 convert_element_type.29
  142.6 48.3 %all_gather.16 = bf16[16,4096]{0,1:T(8,128)(2,1)S(1)} all-gather(bf16[16,256]{0,1:T(8,128)(2,1)S(1)} %convert_element_type.29), channel_id=1, replica_groups=mesh['row'=16,'col'=32] {'row'}, dimensions={1}, use_global_device_ids=true | all-gather | bytes 139264 | tf_op jit(solution)/shard_map/all_gather | solution.py:47
  190.9 30.9 %all-gather.2.cloned.1.call-done = bf16[256,4096]{1,0:T(8,128)(2,1)} async-done(((bf16[256,128]{1,0:T(8,128)(2,1)}), bf16[256,4096]{1,0:T(8,128)(2,1)}) %all-gather.2.cloned.1.call-update) | async-done | bytes 2097168 | tf_op jit(solution)/shard_map/all_gather | solution.py:50
  221.8 2.2 fusion.36
  224.1 65.0 %all_gather.18 = f32[16,4096]{1,0:T(8,128)} all-gather(f32[16,256]{1,0:T(8,128)S(1)} %fusion.36), channel_id=1, replica_groups=mesh['row'=16,'col'=32] {'row'}, dimensions={1}, use_global_device_ids=true | all-gather | bytes 278528 | tf_op jit(solution)/shard_map/all_gather | solution.py:54
  289.0 2.9 copy.25
  292.0 3.4 gather_fusion
  295.3 1.8 broadcast_select_fusion.1
  297.1 1.7 copy.26
  298.8 1.2 convolution_add_fusion.1
  300.1 1.7 fusion.7
  301.8 0.7 copy-done.4
  302.5 0.6 fusion.22
  303.2 1.7 copy.32
  304.8 4.0 scatter_custom_fusion.1
  308.9 114.5 %reduce-scatter.5.cloned.1.call-done = f32[16,256]{0,1:T(8,128)} async-done(((f32[16,4096]{0,1:T(8,128)}), f32[16,256]{0,1:T(8,128)}) %reduce-scatter.5.cloned.1.call-update) | async-done | bytes 16400 | tf_op jit(solution)/shard_map/reduce_scatter | solution.py:46
  423.4 0.9 convert_element_type.33
  424.3 45.2 %all_gather.19 = bf16[16,4096]{0,1:T(8,128)(2,1)S(1)} all-gather(bf16[16,256]{0,1:T(8,128)(2,1)S(1)} %convert_element_type.33), channel_id=1, replica_groups=mesh['row'=16,'col'=32] {'row'}, dimensions={1}, use_global_device_ids=true | all-gather | bytes 139264 | tf_op jit(solution)/shard_map/all_gather | solution.py:47
  469.6 2.2 fusion.37
  471.8 0.6 copy-done.7
  472.5 36.4 %all_gather.20 = f32[16,4096]{1,0:T(8,128)} all-gather(f32[16,256]{1,0:T(8,128)S(1)} %fusion.37), channel_id=1, replica_groups=mesh['row'=16,'col'=32] {'row'}, dimensions={1}, use_global_device_ids=true | all-gather | bytes 278528 | tf_op jit(solution)/shard_map/all_gather | solution.py:54
  508.8 2.9 copy.29
  511.7 3.4 gather_fusion.1
  515.1 1.8 broadcast_select_fusion
  516.9 1.7 copy.30
  518.6 2.2 add_multiply_fusion
  (32 shorter events, 2.1 us)
Async XLA Ops:
  8.0 133.7 %reduce-scatter.3.cloned.1.call-start = ((), (), s32[]{:S(2)}) async-start(), calls=%async_computation.2 | async-start | bytes 2228224 | tf_op jit(solution)/shard_map/reduce_scatter | solution.py:46
  10.1 8.7 %copy-start.10 = (s32[512]{0:T(512)}, s32[512]{0:T(512)S(1)}, u32[]{:S(2)}) copy-start(s32[512]{0:T(512)S(1)} %reshape.77) | copy-start | bytes 6148
  10.1 2.8 copy-start.6
  10.1 3.5 copy-start.8
  13.0 0.7 copy-start.3
  17.5 204.3 %all-gather.2.cloned.1.call-start = ((), (), s32[]{:S(2)}) async-start(), calls=%async_computation.3 | async-start | bytes 2162688 | tf_op jit(solution)/shard_map/all_gather | solution.py:50
  18.1 405.4 %reduce-scatter.5.cloned.1.call-start = ((), (), s32[]{:S(2)}) async-start(), calls=%async_computation.4 | async-start | bytes 2228224 | tf_op jit(solution)/shard_map/reduce_scatter | solution.py:46
  224.1 74.8 %copy-start = (bf16[8,400,400]{2,1,0:T(8,128)(2,1)S(1)}, bf16[8,400,400]{2,1,0:T(8,128)(2,1)}, u32[]{:S(2)}) copy-start(bf16[8,400,400]{2,1,0:T(8,128)(2,1)} %param.14) | copy-start | bytes 7680004
  289.0 11.0 %copy-start.1 = (f32[8,16,400]{2,1,0:T(8,128)S(1)}, f32[8,16,400]{2,1,0:T(8,128)}, u32[]{:S(2)}) copy-start(f32[8,16,400]{2,1,0:T(8,128)} %param.12) | copy-start | bytes 614404
  289.0 11.0 %copy-start.5 = (f32[8,400]{1,0:T(8,128)S(1)}, f32[8,400]{1,0:T(8,128)}, u32[]{:S(2)}) copy-start(f32[8,400]{1,0:T(8,128)} %param.16) | copy-start | bytes 38404
  300.0 1.8 copy-start.2
  300.1 2.5 copy-start.9
  301.8 0.7 copy-start.4
  471.8 0.6 copy-start.7
Sparse Core Ops, SparseCore 0:
  17.6 124.0 reduce-scatter.2
  309.0 114.3 reduce-scatter.4
Sparse Core Ops, SparseCore 1:
  20.0 201.8 all-gather.1
where the time goes:
time: 529 us; the launch traced here: 528 us
  waiting for transfers between devices  268 us (51%)
  blocking collectives  195 us (37%)
  local copies, waits for them, and re-layouts  20.6 us (4%)
  other arithmetic  16.2 us (3%)
  between operations  15.6 us (3%)
  matrix products  12.4 us (2%)
    reduce_scatter x2, waiting for transfers between devices, local(): lax.psum_scatter(partial_rhs, 'row', scatter_dimension=1, tiled=True)  237 us
    all_gather x2, blocking collectives, local(): iface_full = lax.all_gather(iface_block, 'row', axis=1, tiled=True)  101 us
    all_gather x2, blocking collectives, local(): lax.all_gather(owned.astype(jnp.bfloat16), 'row', axis=1, tiled=True)  93.5 us
    all_gather x1, waiting for transfers between devices, local(): lax.all_gather(schur_inverse, 'col', axis=1, tiled=True)  30.9 us
  transfers between devices with their start and end apart: 3, of which 3 were waited for; matrix products, arithmetic and copies ran while one was open for 0% of the time, Pallas kernels for 0%

commit v1 on v0

v1 whole, which is shorter than its diff:
```python
import functools

import jax
import jax.numpy as jnp
from jax import lax
from jax.experimental import pallas as pl
from jax.experimental.pallas import tpu as pltpu
from jax.sharding import PartitionSpec as P

ROWS = 16
COLS = 32
SUBS = 8
SCEN = 16
NODES = 400
PORTS = 64
OWN = SUBS * PORTS
BLOCK = 256
LANES = 128
TILES = OWN // LANES
VALUE_ROWS = TILES * SCEN
Z_GROUPS = [[8 * y + z for z in range(8)] for y in range(4)]
Y_GROUPS = [[8 * y + z for y in range(4)] for z in range(8)]
VMEM_BYTES = 40 << 20

NN = (((1,), (0,)), ((), ()))
NT = (((1,), (1,)), ((), ()))


def dot(a, b, dims=NN):
    return lax.dot_general(a, b, dims, preferred_element_type=jnp.float32)


def flat_row(ref):
    return jnp.concatenate([ref[k : k + 1, :] for k in range(SUBS)], axis=1)


def column(ref):
    place = lax.broadcasted_iota(jnp.int32, (SCEN, 1), 0)
    out = jnp.zeros((SCEN, 1), jnp.int32)
    for s in range(SCEN):
        out = jnp.where(place == s, ref[s], out)
    return out


def open_circuit(step, volts, currs, closed, gain_ref, inv_wait, inv_ref, time_ref, node_ref, tie_ref, open_ref, send_ref):
    fault_node = column(node_ref)
    active = step >= column(time_ref)
    fault_node = jnp.where(active, fault_node, -1)
    first = lax.axis_index("row") * SUBS
    lane = lax.broadcasted_iota(jnp.int32, (SCEN, NODES), 1)
    parts = []
    for k in range(SUBS):
        volt = volts(k)
        hist = closed(k) * (currs(k) + gain_ref[k : k + 1, :] * volt)
        hit = lane + (first + k) * NODES == fault_node
        inject = (-hist - jnp.where(hit, 2.0 * volt, 0.0)).astype(jnp.bfloat16)
        inv_wait(k)
        open_k = dot(inject, inv_ref[k])
        open_ref[k] = open_k
        parts.append(tie_ref[k : k + 1, :] * open_k[:, :PORTS])
    values = jnp.concatenate(parts, axis=1).astype(jnp.bfloat16)
    for r in range(ROWS):
        for t in range(TILES):
            send_ref[r, t * SCEN : (t + 1) * SCEN, :] = values[:, t * LANES : (t + 1) * LANES]


def inverse_copies(inv_hbm, inv_ref, sems):
    copies = [pltpu.make_async_copy(inv_hbm.at[k], inv_ref.at[k], sems.at[k]) for k in range(SUBS)]
    for copy in copies:
        copy.start()
    return copies


def first_kernel(time_ref, node_ref, volt_ref, curr_ref, breaker_ref, gain_ref, tie_ref, map_ref, inv_hbm, open_ref, send_ref, inv_ref, sems):
    copies = inverse_copies(inv_hbm, inv_ref, sems)
    mapped = flat_row(map_ref)
    rows = [(mapped // BLOCK).astype(jnp.float32), (mapped % BLOCK).astype(jnp.float32)]
    rows = [row[:, t * LANES : (t + 1) * LANES] for row in rows for t in range(TILES)]
    tail = jnp.concatenate(rows + [jnp.zeros((16 - len(rows), LANES), jnp.float32)], axis=0).astype(jnp.bfloat16)
    for r in range(ROWS):
        send_ref[r, VALUE_ROWS : VALUE_ROWS + 16, :] = tail
    open_circuit(
        0,
        lambda k: volt_ref[k],
        lambda k: curr_ref[k],
        lambda k: breaker_ref[k].astype(jnp.float32),
        gain_ref,
        lambda k: copies[k].wait(),
        inv_ref,
        time_ref,
        node_ref,
        tie_ref,
        open_ref,
        send_ref,
    )


def interface_kernel(recv_ref, map_ref, schur_hbm, iface_ref, send_ref, schur_ref, sems):
    copies = [pltpu.make_async_copy(schur_hbm.at[y], schur_ref.at[y], sems.at[y]) for y in range(4)]
    for copy in copies:
        copy.start()
    low = lax.broadcasted_iota(jnp.int32, (BLOCK, OWN), 0)
    rhs = jnp.zeros((ROWS * SCEN, BLOCK), jnp.float32)
    for r in range(ROWS):
        tail = map_ref[r, VALUE_ROWS : VALUE_ROWS + 16, :].astype(jnp.float32)
        hi = jnp.concatenate([tail[t : t + 1] for t in range(TILES)], axis=1).astype(jnp.int32)
        lo = jnp.concatenate([tail[TILES + t : TILES + t + 1] for t in range(TILES)], axis=1).astype(jnp.int32)
        values = jnp.concatenate([recv_ref[r, t * SCEN : (t + 1) * SCEN, :] for t in range(TILES)], axis=1)
        values = values.astype(jnp.float32)
        left = jnp.concatenate([jnp.where(hi == h, values, 0.0) for h in range(ROWS)], axis=0).astype(jnp.bfloat16)
        right = jnp.where(low == lo, 1.0, 0.0).astype(jnp.bfloat16)
        rhs += dot(left, right, NT)
    rhs = rhs.astype(jnp.bfloat16)
    total = jnp.zeros((SCEN, BLOCK), jnp.float32)
    for h in range(ROWS):
        if h % 4 == 0:
            copies[h // 4].wait()
        pair = schur_ref[h // 4, 2 * (h % 4)], schur_ref[h // 4, 2 * (h % 4) + 1]
        total += dot(rhs[h * SCEN : (h + 1) * SCEN, :], jnp.concatenate(pair, axis=1), NT)
    iface_ref[...] = total
    half = total.astype(jnp.bfloat16)
    for r in range(ROWS):
        send_ref[r] = half


def driven(recv_ref, map_ref, tie_ref):
    mapped = flat_row(map_ref)
    hi = mapped // BLOCK
    low = lax.broadcasted_iota(jnp.int32, (BLOCK, OWN), 0)
    right = jnp.where(low == mapped % BLOCK, 1.0, 0.0).astype(jnp.bfloat16)
    found = dot(recv_ref[...].reshape(ROWS * SCEN, BLOCK), right)
    picked = jnp.zeros((SCEN, OWN), jnp.float32)
    for r in range(ROWS):
        picked += jnp.where(hi == r, found[r * SCEN : (r + 1) * SCEN, :], 0.0)
    return (flat_row(tie_ref) * picked).astype(jnp.bfloat16)


def update(k, drive, open_ref, inv, volt, curr_ref, breaker_ref, gain_ref):
    volt_next = open_ref[k] + dot(drive[:, k * PORTS : (k + 1) * PORTS], inv)
    closed = breaker_ref[k].astype(jnp.float32)
    curr = closed * (curr_ref[k] + gain_ref[k : k + 1, :] * (volt_next + volt))
    return volt_next, curr


def middle_kernel(time_ref, node_ref, recv_ref, open_prev_ref, volt_ref, curr_ref, breaker_ref, gain_ref, tie_ref, map_ref, inv_hbm, volt_out, curr_out, open_ref, send_ref, inv_ref, sems):
    copies = inverse_copies(inv_hbm, inv_ref, sems)
    drive = driven(recv_ref, map_ref, tie_ref)
    for k in range(SUBS):
        copies[k].wait()
        volt_out[k], curr_out[k] = update(k, drive, open_prev_ref, inv_ref[k, :PORTS, :], volt_ref[k], curr_ref, breaker_ref, gain_ref)
    open_circuit(
        1,
        lambda k: volt_out[k],
        lambda k: curr_out[k],
        lambda k: breaker_ref[k].astype(jnp.float32),
        gain_ref,
        lambda k: None,
        inv_ref,
        time_ref,
        node_ref,
        tie_ref,
        open_ref,
        send_ref,
    )


def last_kernel(recv_ref, open_prev_ref, volt_ref, curr_ref, breaker_ref, gain_ref, tie_ref, map_ref, inv_hbm, volt_out, curr_out, inv_ref, sems):
    copies = [pltpu.make_async_copy(inv_hbm.at[k, :PORTS], inv_ref.at[k], sems.at[k]) for k in range(SUBS)]
    for copy in copies:
        copy.start()
    drive = driven(recv_ref, map_ref, tie_ref)
    for k in range(SUBS):
        copies[k].wait()
        volt_out[k], curr_out[k] = update(k, drive, open_prev_ref, inv_ref[k], volt_ref[k], curr_ref, breaker_ref, gain_ref)


SMEM = pl.BlockSpec(memory_space=pltpu.SMEM)
VMEM = pl.BlockSpec(memory_space=pltpu.VMEM)
ANY = pl.BlockSpec(memory_space=pl.ANY)


def call(body, ins, outs, scratch, flops, moved):
    return pl.pallas_call(
        body,
        out_shape=[jax.ShapeDtypeStruct(shape, kind) for shape, kind in outs],
        in_specs=ins,
        out_specs=[VMEM] * len(outs),
        scratch_shapes=scratch,
        compiler_params=pltpu.CompilerParams(vmem_limit_bytes=VMEM_BYTES),
        cost_estimate=pl.CostEstimate(flops=flops, bytes_accessed=moved, transcendentals=0),
    )


STATE = ((SUBS, SCEN, NODES), jnp.float32)
INVERSE = [pltpu.VMEM((SUBS, NODES, NODES), jnp.bfloat16), pltpu.SemaphoreType.DMA((SUBS,))]
OPEN_FLOPS = 2 * SUBS * SCEN * NODES * NODES


def local(volt, curr, local_inverse, schur_inverse, ind_gain, tie, port_map, breaker, fault_time, fault_node):
    with jax.named_scope("schur_rows"):
        blocks = jnp.broadcast_to(schur_inverse[None], (8, BLOCK, LANES))
        blocks = lax.all_to_all(blocks, "col", 0, 0, axis_index_groups=Z_GROUPS)
        blocks = jnp.broadcast_to(blocks[None], (4, 8, BLOCK, LANES))
        schur_rows = lax.all_to_all(blocks, "col", 0, 0, axis_index_groups=Y_GROUPS)

    first = call(
        first_kernel,
        [SMEM] * 2 + [VMEM] * 6 + [ANY],
        [STATE, ((ROWS, VALUE_ROWS + 16, LANES), jnp.bfloat16)],
        INVERSE,
        OPEN_FLOPS,
        4 << 20,
    )
    interface = call(
        interface_kernel,
        [VMEM] * 2 + [ANY],
        [((SCEN, BLOCK), jnp.float32), ((ROWS, SCEN, BLOCK), jnp.bfloat16)],
        [pltpu.VMEM((4, 8, BLOCK, LANES), jnp.bfloat16), pltpu.SemaphoreType.DMA((4,))],
        2 * 256 * 256 * 8192,
        3 << 20,
    )
    middle = call(
        middle_kernel,
        [SMEM] * 2 + [VMEM] * 8 + [ANY],
        [STATE, STATE, STATE, ((ROWS, VALUE_ROWS, LANES), jnp.bfloat16)],
        INVERSE,
        OPEN_FLOPS,
        4 << 20,
    )
    last = call(
        last_kernel,
        [VMEM] * 8 + [ANY],
        [STATE, STATE],
        [pltpu.VMEM((SUBS, PORTS, NODES), jnp.bfloat16), pltpu.SemaphoreType.DMA((SUBS,))],
        OPEN_FLOPS // 8,
        2 << 20,
    )

    exchange = functools.partial(lax.all_to_all, axis_name="row", split_axis=0, concat_axis=0)
    opened, send = first(fault_time, fault_node, volt, curr, breaker, ind_gain, tie, port_map, local_inverse)
    maps = exchange(send)
    _, send = interface(maps, maps, schur_rows)
    volt, curr, opened, send = middle(fault_time, fault_node, exchange(send), opened, volt, curr, breaker, ind_gain, tie, port_map, local_inverse)
    iface_block, send = interface(exchange(send), maps, schur_rows)
    volt, curr = last(exchange(send), opened, volt, curr, breaker, ind_gain, tie, port_map, local_inverse)
    return volt, curr, iface_block


def solution(mesh):
    placed = (
        P("row", "col", None),
        P("row", "col", None),
        P("row", None, None),
        P("row", "col"),
        P("row", None),
        P("row", None),
        P("row", None),
        P("row", "col", None),
        P("col"),
        P("col"),
    )
    return jax.shard_map(
        local,
        mesh=mesh,
        in_specs=placed,
        out_specs=(P("row", "col", None), P("row", "col", None), P("col", "row")),
        check_vma=False,
    )
```

time: 529 us -> 199 us (0.38)
  the two profiles are of different devices: /device:TPU:1 before, /device:TPU:33 now
where the time goes in v1:
time: 199 us; the launch traced here: 198 us
  blocking collectives  170 us (85%)
  Pallas kernels  18.6 us (9%)
  local copies, waits for them, and re-layouts  8.72 us (4%)
    all_to_all x1, blocking collectives, local(): maps = exchange(send)  44.1 us
    all_to_all x2, blocking collectives, local(): exchange(send)  41.8 us
    all_to_all x1, blocking collectives, local(): blocks = lax.all_to_all(blocks, 'col', 0, 0, axis_index_groups=Z_GROUPS)  30.6 us
    all_to_all x1, blocking collectives, local(): schur_rows = lax.all_to_all(blocks, 'col', 0, 0, axis_index_groups=Y_GROUPS)  27.9 us
    all_to_all x1, blocking collectives, local(): iface_block, send = interface(exchange(send), maps, schur_rows)  26.1 us
    unnamed x28, local copies, waits for them, and re-layouts  8.19 us
    pallas_call x1, Pallas kernels, local(): middle(fault_time, fault_node, exchange(send), opened, volt, curr, breake...  4.16 us

profile of v1, /device:TPU:33, one launch (start us, length us, event | category | flops | bytes accessed | tf_op | source)
XLA Modules:
  0.0 198.5 jit_solution(6610552326212474172)
XLA Ops:
  0.6 0.0 copy-start
  0.6 1.9 copy-done
  2.6 0.0 copy-start.2
  2.6 0.9 copy-done.2
  3.5 0.0 copy-start.4
  3.5 0.9 copy-done.4
  4.5 0.0 copy-start.6
  4.5 0.9 copy-done.6
  5.4 0.0 copy-start.8
  5.4 0.7 copy-done.8
  6.1 0.7 copy-done.9
  6.8 0.7 copy-done.10
  7.5 0.7 copy-done.11
  8.2 0.7 copy-done.12
  8.8 3.9 %shard_map.121 = (f32[8,16,400]{2,1,0:T(8,128)S(1)}, bf16[16,80,128]{2,1,0:T(8,128)(2,1)S(1)}) custom-call(s32[16]{0:T(128)S(1)} %copy-done.11, s32[16]{0:T(128)S(1)} %copy-done.12, f32[8,16,400]{2,1,0:T(8,128)S(1)} %copy-done.4, f32[8,16,400]{2,1,0:T(8,128)S(1)} %copy-done.6, s32[8,16,400]{2,1,0:T(8,128)S(1)} %copy-done.2, f32[8,400]{1,0:T(8,128)S(1)} %copy-done.8, ...), custom_call_target="tpu_custom_call" | custom-call | flops 40960000 | bytes 4194304 | tf_op jit(solution)/shard_map/pallas_call | solution.py:240
  12.7 44.1 %all_to_all.30.recv_ref.map_ref = bf16[16,80,128]{2,1,0:T(8,128)(2,1)S(1)} all-to-all(bf16[16,80,128]{2,1,0:T(8,128)(2,1)S(1)} %get-tuple-element.14), channel_id=1, replica_groups=mesh['row'=16,'col'=32] {'row'}, dimensions={0} | all-to-all | bytes 655360 | tf_op jit(solution)/shard_map/all_to_all | solution.py:241
  56.8 0.0 copy-done.13
  56.8 0.1 broadcast_in_dim.4
  56.8 30.6 %all_to_all.31 = bf16[8,256,128]{2,1,0:T(8,128)(2,1)S(1)} all-to-all(bf16[8,256,128]{2,1,0:T(8,128)(2,1)S(1)} %broadcast_in_dim.4), channel_id=1, replica_groups={{0,1,2,3,4,5,6,7},{8,9,10,11,12,13,14,15},{16,17,18,19,20,21,22,23},{24..., dimensions={0} | all-to-all | bytes 1048576 | tf_op jit(solution)/shard_map/schur_rows/all_to_all | solution.py:202
  87.4 0.5 broadcast_in_dim.5
  87.9 27.9 %all_to_all.32.schur_hbm = bf16[4,8,256,128]{3,2,1,0:T(8,128)(2,1)S(1)} all-to-all(bf16[4,8,256,128]{3,2,1,0:T(8,128)(2,1)S(1)} %broadcast_in_dim.5), channel_id=1, replica_groups={{0,8,16,24},{1,9,17,25},{2,10,18,26},{3,11,19,27},{4,12,20,28},{5,13,21..., dimensions={0} | all-to-all | bytes 4194304 | tf_op jit(solution)/shard_map/schur_rows/all_to_all | solution.py:204
  115.8 3.8 %shard_map.122 = (f32[16,256]{1,0:T(8,128)}, bf16[16,16,256]{2,1,0:T(8,128)(2,1)S(1)}) custom-call(bf16[16,80,128]{2,1,0:T(8,128)(2,1)S(1)} %all_to_all.30.recv_ref.map_ref, bf16[16,80,128]{2,1,0:T(8,128)(2,1)S(1)} %all_to_all.30.recv_ref.map_ref, bf16[4,8,256,128]{3,2,1,0:T(8,128)(2,1)S(1)} %all_to_all.32.schur_hbm), custom_call_target="tpu_custom_call" | custom-call | flops 1073741824 | bytes 3145728 | tf_op jit(solution)/shard_map/pallas_call | solution.py:242
  119.6 23.9 %all_to_all.33.recv_ref = bf16[16,16,256]{2,1,0:T(8,128)(2,1)S(1)} all-to-all(bf16[16,16,256]{2,1,0:T(8,128)(2,1)S(1)} %get-tuple-element.15), channel_id=1, replica_groups=mesh['row'=16,'col'=32] {'row'}, dimensions={0} | all-to-all | bytes 262144 | tf_op jit(solution)/shard_map/all_to_all | solution.py:243
  143.6 0.0 copy-done.1
  143.6 0.0 copy-done.3
  143.6 0.0 copy-done.5
  143.6 0.0 copy-done.7
  143.6 4.2 %shard_map.123 = (f32[8,16,400]{2,1,0:T(8,128)S(1)}, f32[8,16,400]{2,1,0:T(8,128)S(1)}, f32[8,16,400]{2,1,0:T(8,128)S(1)}, bf16[16,64,128]{2,1,0:T(8,128)(2,1)S(1)}) custom-call(s32[16]{0:T(128)S(1)} %copy-done.11, s32[16]{0:T(128)S(1)} %copy-done.12, bf16[16,16,256]{2,1,0:T(8,128)(2,1)S(1)} %all_to_all.33.recv_ref, ...), custom_call_target="tpu_custom_call" | custom-call | flops 40960000 | bytes 4194304 | tf_op jit(solution)/shard_map/pallas_call | solution.py:243
  147.8 26.1 %all_to_all.34.recv_ref = bf16[16,64,128]{2,1,0:T(8,128)(2,1)S(1)} all-to-all(bf16[16,64,128]{2,1,0:T(8,128)(2,1)S(1)} %get-tuple-element.17), channel_id=1, replica_groups=mesh['row'=16,'col'=32] {'row'}, dimensions={0} | all-to-all | bytes 524288 | tf_op jit(solution)/shard_map/all_to_all | solution.py:244
  173.9 3.8 %shard_map.124 = (f32[16,256]{1,0:T(8,128)}, bf16[16,16,256]{2,1,0:T(8,128)(2,1)S(1)}) custom-call(bf16[16,64,128]{2,1,0:T(8,128)(2,1)S(1)} %all_to_all.34.recv_ref, bf16[16,80,128]{2,1,0:T(8,128)(2,1)S(1)} %all_to_all.30.recv_ref.map_ref, bf16[4,8,256,128]{3,2,1,0:T(8,128)(2,1)S(1)} %all_to_all.32.schur_hbm), custom_call_target="tpu_custom_call" | custom-call | flops 1073741824 | bytes 3145728 | tf_op jit(solution)/shard_map/pallas_call | solution.py:244
  177.7 17.9 %all_to_all.35.recv_ref = bf16[16,16,256]{2,1,0:T(8,128)(2,1)S(1)} all-to-all(bf16[16,16,256]{2,1,0:T(8,128)(2,1)S(1)} %get-tuple-element.18), channel_id=1, replica_groups=mesh['row'=16,'col'=32] {'row'}, dimensions={0} | all-to-all | bytes 262144 | tf_op jit(solution)/shard_map/all_to_all | solution.py:245
  195.6 2.9 %shard_map.125 = (f32[8,16,400]{2,1,0:T(8,128)}, f32[8,16,400]{2,1,0:T(8,128)}) custom-call(bf16[16,16,256]{2,1,0:T(8,128)(2,1)S(1)} %all_to_all.35.recv_ref, f32[8,16,400]{2,1,0:T(8,128)S(1)} %get-tuple-element.19.open_prev_ref, f32[8,16,400]{2,1,0:T(8,128)S(1)} %get-tuple-element.20.volt_ref, f32[8,16,400]{2,1,0:T(8,128)S(1)} %get-tuple-element.21.curr_ref, ...), custom_call_target="tpu_custom_call" | custom-call | flops 5120000 | bytes 2097152 | tf_op jit(solution)/shard_map/pallas_call | solution.py:245
  (9 shorter events, 0.0 us)
Async XLA Ops:
  0.6 1.9 copy-start
  2.6 0.9 copy-start.2
  3.5 0.9 copy-start.4
  4.5 0.9 copy-start.6
  5.4 0.7 copy-start.8
  6.1 0.7 copy-start.9
  6.8 0.7 copy-start.10
  7.5 0.7 copy-start.11
  8.2 0.7 copy-start.12
  8.8 47.9 %copy-start.13 = (bf16[256,128]{1,0:T(8,128)(2,1)S(1)}, bf16[256,128]{1,0:T(8,128)(2,1)}, u32[]{:S(2)}) copy-start(bf16[256,128]{1,0:T(8,128)(2,1)} %param.13) | copy-start | bytes 196612
  115.8 27.8 %copy-start.1 = (bf16[8,400,400]{2,1,0:T(8,128)(2,1)S(1)}, bf16[8,400,400]{2,1,0:T(8,128)(2,1)}, u32[]{:S(2)}) copy-start(bf16[8,400,400]{2,1,0:T(8,128)(2,1)} %inv_hbm.5) | copy-start | bytes 7680004
  115.8 27.8 %copy-start.3 = (s32[8,16,400]{2,1,0:T(8,128)S(1)}, s32[8,16,400]{2,1,0:T(8,128)}, u32[]{:S(2)}) copy-start(s32[8,16,400]{2,1,0:T(8,128)} %breaker_ref.5) | copy-start | bytes 614404
  115.8 27.8 %copy-start.5 = (f32[8,16,400]{2,1,0:T(8,128)S(1)}, f32[8,16,400]{2,1,0:T(8,128)}, u32[]{:S(2)}) copy-start(f32[8,16,400]{2,1,0:T(8,128)} %volt_ref.3) | copy-start | bytes 614404
  115.8 27.8 %copy-start.7 = (f32[8,16,400]{2,1,0:T(8,128)S(1)}, f32[8,16,400]{2,1,0:T(8,128)}, u32[]{:S(2)}) copy-start(f32[8,16,400]{2,1,0:T(8,128)} %curr_ref.3) | copy-start | bytes 614404

commit v2 on v1

--- a/solution.py
+++ b/solution.py
@@ -18,9 +18,9 @@
 LANES = 128
 TILES = OWN // LANES
 VALUE_ROWS = TILES * SCEN
-Z_GROUPS = [[8 * y + z for z in range(8)] for y in range(4)]
-Y_GROUPS = [[8 * y + z for y in range(4)] for z in range(8)]
+QUADS = [[4 * q + z for z in range(4)] for q in range(8)]
 VMEM_BYTES = 40 << 20
+ALL_VMEM = 60 << 20
 
 NN = (((1,), (0,)), ((), ()))
 NT = (((1,), (1,)), ((), ()))
@@ -95,8 +95,9 @@
     )
 
 
-def interface_kernel(recv_ref, map_ref, schur_hbm, iface_ref, send_ref, schur_ref, sems):
-    copies = [pltpu.make_async_copy(schur_hbm.at[y], schur_ref.at[y], sems.at[y]) for y in range(4)]
+def interface_kernel(recv_ref, map_ref, *refs):
+    parts, (iface_ref, send_ref, schur_ref, rhs_ref, sems) = refs[:4], refs[4:]
+    copies = [pltpu.make_async_copy(parts[n], schur_ref.at[n], sems.at[n]) for n in range(4)]
     for copy in copies:
         copy.start()
     low = lax.broadcasted_iota(jnp.int32, (BLOCK, OWN), 0)
@@ -110,13 +111,17 @@
         left = jnp.concatenate([jnp.where(hi == h, values, 0.0) for h in range(ROWS)], axis=0).astype(jnp.bfloat16)
         right = jnp.where(low == lo, 1.0, 0.0).astype(jnp.bfloat16)
         rhs += dot(left, right, NT)
-    rhs = rhs.astype(jnp.bfloat16)
+    rhs_ref[...] = rhs.astype(jnp.bfloat16).reshape(ROWS, SCEN, BLOCK)
+    col = lax.axis_index("col")
+    own_y, own_half = col // 8, (col // 4) % 2
     total = jnp.zeros((SCEN, BLOCK), jnp.float32)
-    for h in range(ROWS):
-        if h % 4 == 0:
-            copies[h // 4].wait()
-        pair = schur_ref[h // 4, 2 * (h % 4)], schur_ref[h // 4, 2 * (h % 4) + 1]
-        total += dot(rhs[h * SCEN : (h + 1) * SCEN, :], jnp.concatenate(pair, axis=1), NT)
+    for n in range(4):
+        copies[n].wait()
+        for other in range(2):
+            first = 4 * ((own_y + 4 - n) % 4) + 2 * ((own_half + other) % 2)
+            for p in range(2):
+                pair = schur_ref[n, 2 * p, other], schur_ref[n, 2 * p + 1, other]
+                total += dot(rhs_ref[first + p], jnp.concatenate(pair, axis=1), NT)
     iface_ref[...] = total
     half = total.astype(jnp.bfloat16)
     for r in range(ROWS):
@@ -179,14 +184,14 @@
 ANY = pl.BlockSpec(memory_space=pl.ANY)
 
 
-def call(body, ins, outs, scratch, flops, moved):
+def call(body, ins, outs, scratch, flops, moved, vmem=VMEM_BYTES):
     return pl.pallas_call(
         body,
         out_shape=[jax.ShapeDtypeStruct(shape, kind) for shape, kind in outs],
         in_specs=ins,
         out_specs=[VMEM] * len(outs),
         scratch_shapes=scratch,
-        compiler_params=pltpu.CompilerParams(vmem_limit_bytes=VMEM_BYTES),
+        compiler_params=pltpu.CompilerParams(vmem_limit_bytes=vmem),
         cost_estimate=pl.CostEstimate(flops=flops, bytes_accessed=moved, transcendentals=0),
     )
 
@@ -197,12 +202,6 @@
 
 
 def local(volt, curr, local_inverse, schur_inverse, ind_gain, tie, port_map, breaker, fault_time, fault_node):
-    with jax.named_scope("schur_rows"):
-        blocks = jnp.broadcast_to(schur_inverse[None], (8, BLOCK, LANES))
-        blocks = lax.all_to_all(blocks, "col", 0, 0, axis_index_groups=Z_GROUPS)
-        blocks = jnp.broadcast_to(blocks[None], (4, 8, BLOCK, LANES))
-        schur_rows = lax.all_to_all(blocks, "col", 0, 0, axis_index_groups=Y_GROUPS)
-
     first = call(
         first_kernel,
         [SMEM] * 2 + [VMEM] * 6 + [ANY],
@@ -210,12 +209,13 @@
         INVERSE,
         OPEN_FLOPS,
         4 << 20,
+        ALL_VMEM,
     )
     interface = call(
         interface_kernel,
-        [VMEM] * 2 + [ANY],
+        [VMEM] * 2 + [ANY] * 4,
         [((SCEN, BLOCK), jnp.float32), ((ROWS, SCEN, BLOCK), jnp.bfloat16)],
-        [pltpu.VMEM((4, 8, BLOCK, LANES), jnp.bfloat16), pltpu.SemaphoreType.DMA((4,))],
+        [pltpu.VMEM((4, 4, 2, BLOCK, LANES), jnp.bfloat16), pltpu.VMEM((ROWS, SCEN, BLOCK), jnp.bfloat16), pltpu.SemaphoreType.DMA((4,))],
         2 * 256 * 256 * 8192,
         3 << 20,
     )
@@ -237,11 +237,20 @@
     )
 
     exchange = functools.partial(lax.all_to_all, axis_name="row", split_axis=0, concat_axis=0)
+    with jax.named_scope("schur_z"):
+        across = lax.ppermute(schur_inverse, "col", [(c, c ^ 4) for c in range(COLS)])
     opened, send = first(fault_time, fault_node, volt, curr, breaker, ind_gain, tie, port_map, local_inverse)
+    across, send = lax.optimization_barrier((across, send))
+    with jax.named_scope("schur_z"):
+        blocks = jnp.broadcast_to(jnp.stack([schur_inverse, across])[None], (4, 2, BLOCK, LANES))
+        blocks = lax.all_to_all(blocks, "col", 0, 0, axis_index_groups=QUADS)
+    blocks, send = lax.optimization_barrier((blocks, send))
+    with jax.named_scope("schur_y"):
+        schur_rows = [blocks] + [lax.ppermute(blocks, "col", [(c, (c + 8 * n) % COLS) for c in range(COLS)]) for n in (1, 2, 3)]
     maps = exchange(send)
-    _, send = interface(maps, maps, schur_rows)
+    _, send = interface(maps, maps, *schur_rows)
     volt, curr, opened, send = middle(fault_time, fault_node, exchange(send), opened, volt, curr, breaker, ind_gain, tie, port_map, local_inverse)
-    iface_block, send = interface(exchange(send), maps, schur_rows)
+    iface_block, send = interface(exchange(send), maps, *schur_rows)
     volt, curr = last(exchange(send), opened, volt, curr, breaker, ind_gain, tie, port_map, local_inverse)
     return volt, curr, iface_block
 

time: 199 us -> 183 us (0.920)
  blocking collectives: 170 us -> 95.9 us
  starting transfers between devices: 0 us -> 35.7 us
  waiting for transfers between devices: 0 us -> 22.2 us
  Pallas kernels: 18.6 us -> 21.3 us
  local copies, waits for them, and re-layouts: 8.72 us -> 6.73 us
    all_to_all x4 -> x2, blocking collectives: 129 us -> 48.6 us  [the longest x1 30.7 us: local(): iface_block, send = interface(exchange(send), maps, *schur_rows)]
    ppermute x0 -> x4, waiting for transfers between devices: none -> 22.2 us  [the longest x3 22.2 us: local(): lax.ppermute(blocks, 'col', [(c, (c + 8 * n) % COLS) for c in range(COLS)])]
    ppermute x0 -> x4, starting transfers between devices: none -> 18.4 us  [the longest x3 9.49 us: local(): lax.ppermute(blocks, 'col', [(c, (c + 8 * n) % COLS) for c in range(COLS)])]
    all_to_all x0 -> x1, starting transfers between devices: none -> 17.2 us  [local(): maps = exchange(send)]
    all_to_all x2, blocking collectives: 41.8 us -> 47.3 us  [local(): exchange(send)]
    pallas_call x2, Pallas kernels: 7.66 us -> 9.78 us  [the longest x1 4.97 us: local(): _, send = interface(maps, maps, *schur_rows)]
    unnamed x28 -> x44, local copies, waits for them, and re-layouts: 8.19 us -> 6.66 us
  transfers between devices with their start and end apart: 0 -> 5, of which waited for: 0 -> 2; matrix products, arithmetic and copies ran while one was open for 0% -> 0% of each run, Pallas kernels for 0% -> 2%
where the time goes in v2:
time: 183 us
  blocking collectives  95.9 us (52%)
  starting transfers between devices  35.7 us (20%)
  waiting for transfers between devices  22.2 us (12%)
  Pallas kernels  21.3 us (12%)
  local copies, waits for them, and re-layouts  6.73 us (4%)
    all_to_all x2, blocking collectives, local(): exchange(send)  47.3 us
    all_to_all x1, blocking collectives, local(): iface_block, send = interface(exchange(send), maps, *schur_rows)  30.7 us
    ppermute x3, waiting for transfers between devices, local(): lax.ppermute(blocks, 'col', [(c, (c + 8 * n) % COLS) for c in range(COLS)])  22.2 us
    all_to_all x1, blocking collectives, local(): blocks = lax.all_to_all(blocks, 'col', 0, 0, axis_index_groups=QUADS)  17.9 us
    all_to_all x1, starting transfers between devices, local(): maps = exchange(send)  17.2 us
    ppermute x3, starting transfers between devices, local(): lax.ppermute(blocks, 'col', [(c, (c + 8 * n) % COLS) for c in range(COLS)])  9.49 us
    ppermute x1, starting transfers between devices, local(): lax.ppermute(schur_inverse, 'col', [(c, c ^ 4) for c in range(COLS)])  8.95 us
    unnamed x44, local copies, waits for them, and re-layouts  6.66 us
  transfers between devices with their start and end apart: 5, of which 2 were waited for; matrix products, arithmetic and copies ran while one was open for 0% of the time, Pallas kernels for 2%

profile of v2, /device:TPU:33, one launch (start us, length us, event | category | flops | bytes accessed | tf_op | source)
XLA Modules:
  0.0 182.7 jit_solution(16159776863241327090)
XLA Ops:
  0.6 8.9 %collective-permute-start = (bf16[256,128]{1,0:T(8,128)(2,1)}, bf16[256,128]{1,0:T(8,128)(2,1)S(1)}, u32[]{:S(2)}, u32[]{:S(2)}) collective-permute-start(bf16[256,128]{1,0:T(8,128)(2,1)} %param.13), channel_id=1, source_target_pairs={{0,4},{1,5},{2,6},{3,7},{4,0},{5,1},{6,2},{7,3},{8,12},{9,13},{10,... | collective-permute-start | bytes 196616 | tf_op jit(solution)/shard_map/schur_z/ppermute | solution.py:241
  9.6 4.4 %shard_map.121 = (f32[8,16,400]{2,1,0:T(8,128)}, bf16[16,80,128]{2,1,0:T(8,128)(2,1)}) custom-call(s32[16]{0:T(128)} %time_ref.3, s32[16]{0:T(128)} %node_ref.3, f32[8,16,400]{2,1,0:T(8,128)} %volt_ref.3, f32[8,16,400]{2,1,0:T(8,128)} %curr_ref.3, s32[8,16,400]{2,1,0:T(8,128)} %breaker_ref.5, f32[8,400]{1,0:T(8,128)} %gain_ref.5, f32[8,64]{1,0:T(8,128)} %tie_ref.5, ...), custom_call_target="tpu_custom_call" | custom-call | flops 40960000 | bytes 4194304 | tf_op jit(solution)/shard_map/pallas_call | solution.py:242
  14.1 0.0 collective-permute-done
  14.1 0.0 copy-start.7
  14.1 0.0 copy-start
  14.1 0.0 copy-start.1
  14.1 0.1 broadcast_in_dim.2
  14.2 17.9 %all_to_all.25.refs_0_ = bf16[4,2,256,128]{3,2,1,0:T(8,128)(2,1)} all-to-all(bf16[4,2,256,128]{3,2,1,0:T(8,128)(2,1)S(1)} %broadcast_in_dim.2), channel_id=1, replica_groups={{0,1,2,3},{4,5,6,7},{8,9,10,11},{12,13,14,15},{16,17,18,19},{20,21,22,2..., dimensions={0} | all-to-all | bytes 1048576 | tf_op jit(solution)/shard_map/schur_z/all_to_all | solution.py:246
  32.1 17.2 %all-to-all-start.1 = ((bf16[16,80,128]{2,1,0:T(8,128)(2,1)}), bf16[16,80,128]{2,1,0:T(8,128)(2,1)}, u32[]{:S(2)}, u32[]{:S(2)}) async-start(bf16[16,80,128]{2,1,0:T(8,128)(2,1)} %get-tuple-element.21), calls=%async_computation.1 | async-start | bytes 655360 | tf_op jit(solution)/shard_map/all_to_all | solution.py:250
  49.3 4.6 %collective-permute-start.3 = (bf16[4,2,256,128]{3,2,1,0:T(8,128)(2,1)}, bf16[4,2,256,128]{3,2,1,0:T(8,128)(2,1)S(1)}, u32[]{:S(2)}, u32[]{:S(2)}) collective-permute-start(bf16[4,2,256,128]{3,2,1,0:T(8,128)(2,1)} %all_to_all.25.refs_0_), channel_id=1, source_target_pairs={{0,24},{1,25},{2,26},{3,27},{4,28},{5,29},{6,30},{7,31},{8,0},{9,1... | collective-permute-start | bytes 1572872 | tf_op jit(solution)/shard_map/schur_y/ppermute | solution.py:249
  54.0 2.3 %collective-permute-start.2 = (bf16[4,2,256,128]{3,2,1,0:T(8,128)(2,1)}, bf16[4,2,256,128]{3,2,1,0:T(8,128)(2,1)S(1)}, u32[]{:S(2)}, u32[]{:S(2)}) collective-permute-start(bf16[4,2,256,128]{3,2,1,0:T(8,128)(2,1)} %all_to_all.25.refs_0_), channel_id=1, source_target_pairs={{0,16},{1,17},{2,18},{3,19},{4,20},{5,21},{6,22},{7,23},{8,24},{9,... | collective-permute-start | bytes 1572872 | tf_op jit(solution)/shard_map/schur_y/ppermute | solution.py:249
  56.2 2.6 %collective-permute-start.1 = (bf16[4,2,256,128]{3,2,1,0:T(8,128)(2,1)}, bf16[4,2,256,128]{3,2,1,0:T(8,128)(2,1)S(1)}, u32[]{:S(2)}, u32[]{:S(2)}) collective-permute-start(bf16[4,2,256,128]{3,2,1,0:T(8,128)(2,1)} %all_to_all.25.refs_0_), channel_id=1, source_target_pairs={{0,8},{1,9},{2,10},{3,11},{4,12},{5,13},{6,14},{7,15},{8,16},{9,17... | collective-permute-start | bytes 1572872 | tf_op jit(solution)/shard_map/schur_y/ppermute | solution.py:249
  58.8 17.7 %collective-permute-done.3.refs_3_ = bf16[4,2,256,128]{3,2,1,0:T(8,128)(2,1)S(1)} collective-permute-done((bf16[4,2,256,128]{3,2,1,0:T(8,128)(2,1)}, bf16[4,2,256,128]{3,2,1,0:T(8,128)(2,1)S(1)}, u32[]{:S(2)}, u32[]{:S(2)}) %collective-permute-start.3) | collective-permute-done | bytes 524320 | tf_op jit(solution)/shard_map/schur_y/ppermute | solution.py:249
  76.5 0.8 copy-done.12
  77.3 0.8 copy-done.15
  78.1 4.5 %collective-permute-done.1.refs_1_ = bf16[4,2,256,128]{3,2,1,0:T(8,128)(2,1)S(1)} collective-permute-done((bf16[4,2,256,128]{3,2,1,0:T(8,128)(2,1)}, bf16[4,2,256,128]{3,2,1,0:T(8,128)(2,1)S(1)}, u32[]{:S(2)}, u32[]{:S(2)}) %collective-permute-start.1) | collective-permute-done | bytes 524320 | tf_op jit(solution)/shard_map/schur_y/ppermute | solution.py:249
  82.7 0.8 copy-done.18
  83.5 0.0 all-to-all-done.1.recv_ref.map_ref
  83.5 1.0 copy-done.4
  84.5 1.0 copy-done.13
  85.6 1.0 copy-done.16
  86.6 1.0 copy-done.19
  87.6 0.0 copy-start.9
  87.7 0.0 copy-start.10
  87.7 0.0 copy-start.11
  87.7 5.0 %shard_map.122 = (f32[16,256]{1,0:T(8,128)}, bf16[16,16,256]{2,1,0:T(8,128)(2,1)S(1)}) custom-call(bf16[16,80,128]{2,1,0:T(8,128)(2,1)} %all-to-all-done.1.recv_ref.map_ref, bf16[16,80,128]{2,1,0:T(8,128)(2,1)} %all-to-all-done.1.recv_ref.map_ref, bf16[4,2,256,128]{3,2,1,0:T(8,128)(2,1)S(1)} %copy-done.4, bf16[4,2,256,128]{3,2,1,0:T(8,128)(2,1)S(1)} %copy-done.19, ...), custom_call_target="tpu_custom_call" | custom-call | flops 1073741824 | bytes 3145728 | tf_op jit(solution)/shard_map/pallas_call | solution.py:251
  92.7 29.3 %all_to_all.26.recv_ref = bf16[16,16,256]{2,1,0:T(8,128)(2,1)S(1)} all-to-all(bf16[16,16,256]{2,1,0:T(8,128)(2,1)S(1)} %get-tuple-element.23), channel_id=1, replica_groups=mesh['row'=16,'col'=32] {'row'}, dimensions={0} | all-to-all | bytes 262144 | tf_op jit(solution)/shard_map/all_to_all | solution.py:252
  122.1 4.2 %shard_map.123 = (f32[8,16,400]{2,1,0:T(8,128)S(1)}, f32[8,16,400]{2,1,0:T(8,128)S(1)}, f32[8,16,400]{2,1,0:T(8,128)S(1)}, bf16[16,64,128]{2,1,0:T(8,128)(2,1)S(1)}) custom-call(s32[16]{0:T(128)S(1)} %copy-done.10, s32[16]{0:T(128)S(1)} %copy-done.11, bf16[16,16,256]{2,1,0:T(8,128)(2,1)S(1)} %all_to_all.26.recv_ref, f32[8,16,400]{2,1,0:T(8,128)S(1)} %copy-done.6, ...), custom_call_target="tpu_custom_call" | custom-call | flops 40960000 | bytes 4194304 | tf_op jit(solution)/shard_map/pallas_call | solution.py:252
  126.3 30.7 %all_to_all.27.recv_ref = bf16[16,64,128]{2,1,0:T(8,128)(2,1)S(1)} all-to-all(bf16[16,64,128]{2,1,0:T(8,128)(2,1)S(1)} %get-tuple-element.25), channel_id=1, replica_groups=mesh['row'=16,'col'=32] {'row'}, dimensions={0} | all-to-all | bytes 524288 | tf_op jit(solution)/shard_map/all_to_all | solution.py:253
  157.0 4.8 %shard_map.124 = (f32[16,256]{1,0:T(8,128)}, bf16[16,16,256]{2,1,0:T(8,128)(2,1)S(1)}) custom-call(bf16[16,64,128]{2,1,0:T(8,128)(2,1)S(1)} %all_to_all.27.recv_ref, bf16[16,80,128]{2,1,0:T(8,128)(2,1)} %all-to-all-done.1.recv_ref.map_ref, bf16[4,2,256,128]{3,2,1,0:T(8,128)(2,1)S(1)} %copy-done.5, bf16[4,2,256,128]{3,2,1,0:T(8,128)(2,1)S(1)} %copy-done.20, ...), custom_call_target="tpu_custom_call" | custom-call | flops 1073741824 | bytes 3145728 | tf_op jit(solution)/shard_map/pallas_call | solution.py:253
  161.8 17.9 %all_to_all.28.recv_ref = bf16[16,16,256]{2,1,0:T(8,128)(2,1)S(1)} all-to-all(bf16[16,16,256]{2,1,0:T(8,128)(2,1)S(1)} %get-tuple-element.26), channel_id=1, replica_groups=mesh['row'=16,'col'=32] {'row'}, dimensions={0} | all-to-all | bytes 262144 | tf_op jit(solution)/shard_map/all_to_all | solution.py:254
  179.8 2.9 %shard_map.125 = (f32[8,16,400]{2,1,0:T(8,128)}, f32[8,16,400]{2,1,0:T(8,128)}) custom-call(bf16[16,16,256]{2,1,0:T(8,128)(2,1)S(1)} %all_to_all.28.recv_ref, f32[8,16,400]{2,1,0:T(8,128)S(1)} %get-tuple-element.27.open_prev_ref, f32[8,16,400]{2,1,0:T(8,128)S(1)} %get-tuple-element.28.volt_ref, f32[8,16,400]{2,1,0:T(8,128)S(1)} %get-tuple-element.29.curr_ref, ...), custom_call_target="tpu_custom_call" | custom-call | flops 5120000 | bytes 2097152 | tf_op jit(solution)/shard_map/pallas_call | solution.py:254
  (33 shorter events, 0.1 us)
Async XLA Ops:
  0.6 13.4 %copy-start.21 = (bf16[256,128]{1,0:T(8,128)(2,1)S(1)}, bf16[256,128]{1,0:T(8,128)(2,1)}, u32[]{:S(2)}) copy-start(bf16[256,128]{1,0:T(8,128)(2,1)} %param.13) | copy-start | bytes 196612
  0.6 13.4 %collective-permute-start = (bf16[256,128]{1,0:T(8,128)(2,1)}, bf16[256,128]{1,0:T(8,128)(2,1)S(1)}, u32[]{:S(2)}, u32[]{:S(2)}) collective-permute-start(bf16[256,128]{1,0:T(8,128)(2,1)} %param.13), channel_id=1, source_target_pairs={{0,4},{1,5},{2,6},{3,7},{4,0},{5,1},{6,2},{7,3},{8,12},{9,13},{10,... | collective-permute-start | bytes 196616 | tf_op jit(solution)/shard_map/schur_z/ppermute | solution.py:241
  14.1 107.9 %copy-start.7 = (f32[8,400]{1,0:T(8,128)S(1)}, f32[8,400]{1,0:T(8,128)}, u32[]{:S(2)}) copy-start(f32[8,400]{1,0:T(8,128)} %gain_ref.5) | copy-start | bytes 38404
  14.1 107.9 %copy-start = (bf16[8,400,400]{2,1,0:T(8,128)(2,1)S(1)}, bf16[8,400,400]{2,1,0:T(8,128)(2,1)}, u32[]{:S(2)}) copy-start(bf16[8,400,400]{2,1,0:T(8,128)(2,1)} %inv_hbm.5) | copy-start | bytes 7680004
  14.1 107.9 %copy-start.1 = (s32[8,16,400]{2,1,0:T(8,128)S(1)}, s32[8,16,400]{2,1,0:T(8,128)}, u32[]{:S(2)}) copy-start(s32[8,16,400]{2,1,0:T(8,128)} %breaker_ref.5) | copy-start | bytes 614404
  32.1 51.4 %all-to-all-start.1 = ((bf16[16,80,128]{2,1,0:T(8,128)(2,1)}), bf16[16,80,128]{2,1,0:T(8,128)(2,1)}, u32[]{:S(2)}, u32[]{:S(2)}) async-start(bf16[16,80,128]{2,1,0:T(8,128)(2,1)} %get-tuple-element.21), calls=%async_computation.1 | async-start | bytes 655360 | tf_op jit(solution)/shard_map/all_to_all | solution.py:250
  49.3 27.2 %collective-permute-start.3 = (bf16[4,2,256,128]{3,2,1,0:T(8,128)(2,1)}, bf16[4,2,256,128]{3,2,1,0:T(8,128)(2,1)S(1)}, u32[]{:S(2)}, u32[]{:S(2)}) collective-permute-start(bf16[4,2,256,128]{3,2,1,0:T(8,128)(2,1)} %all_to_all.25.refs_0_), channel_id=1, source_target_pairs={{0,24},{1,25},{2,26},{3,27},{4,28},{5,29},{6,30},{7,31},{8,0},{9,1... | collective-permute-start | bytes 1572872 | tf_op jit(solution)/shard_map/schur_y/ppermute | solution.py:249
  54.0 23.4 %collective-permute-start.2 = (bf16[4,2,256,128]{3,2,1,0:T(8,128)(2,1)}, bf16[4,2,256,128]{3,2,1,0:T(8,128)(2,1)S(1)}, u32[]{:S(2)}, u32[]{:S(2)}) collective-permute-start(bf16[4,2,256,128]{3,2,1,0:T(8,128)(2,1)} %all_to_all.25.refs_0_), channel_id=1, source_target_pairs={{0,16},{1,17},{2,18},{3,19},{4,20},{5,21},{6,22},{7,23},{8,24},{9,... | collective-permute-start | bytes 1572872 | tf_op jit(solution)/shard_map/schur_y/ppermute | solution.py:249
  56.2 26.4 %collective-permute-start.1 = (bf16[4,2,256,128]{3,2,1,0:T(8,128)(2,1)}, bf16[4,2,256,128]{3,2,1,0:T(8,128)(2,1)S(1)}, u32[]{:S(2)}, u32[]{:S(2)}) collective-permute-start(bf16[4,2,256,128]{3,2,1,0:T(8,128)(2,1)} %all_to_all.25.refs_0_), channel_id=1, source_target_pairs={{0,8},{1,9},{2,10},{3,11},{4,12},{5,13},{6,14},{7,15},{8,16},{9,17... | collective-permute-start | bytes 1572872 | tf_op jit(solution)/shard_map/schur_y/ppermute | solution.py:249
  76.5 0.8 copy-start.12
  77.3 0.8 copy-start.15
  82.6 0.8 copy-start.18
  83.5 1.0 copy-start.4
  84.5 1.0 copy-start.13
  85.6 1.0 copy-start.16
  86.6 1.0 copy-start.19
  87.6 34.4 %copy-start.2 = (f32[8,16,400]{2,1,0:T(8,128)S(1)}, f32[8,16,400]{2,1,0:T(8,128)}, u32[]{:S(2)}) copy-start(f32[8,16,400]{2,1,0:T(8,128)} %volt_ref.3) | copy-start | bytes 614404
  87.6 34.4 %copy-start.3 = (f32[8,16,400]{2,1,0:T(8,128)S(1)}, f32[8,16,400]{2,1,0:T(8,128)}, u32[]{:S(2)}) copy-start(f32[8,16,400]{2,1,0:T(8,128)} %curr_ref.3) | copy-start | bytes 614404
  87.6 34.4 %copy-start.6 = (f32[8,16,400]{2,1,0:T(8,128)S(1)}, f32[8,16,400]{2,1,0:T(8,128)}, u32[]{:S(2)}) copy-start(f32[8,16,400]{2,1,0:T(8,128)} %get-tuple-element.24.open_prev_ref) | copy-start | bytes 614404
  87.6 34.4 %copy-start.8 = (f32[8,64]{1,0:T(8,128)S(1)}, f32[8,64]{1,0:T(8,128)}, u32[]{:S(2)}) copy-start(f32[8,64]{1,0:T(8,128)} %tie_ref.5) | copy-start | bytes 6148
  87.6 34.4 %copy-start.9 = (s32[8,64]{1,0:T(8,128)S(1)}, s32[8,64]{1,0:T(8,128)}, u32[]{:S(2)}) copy-start(s32[8,64]{1,0:T(8,128)} %map_ref.5) | copy-start | bytes 6148
  87.7 34.4 %copy-start.10 = (s32[16]{0:T(128)S(1)}, s32[16]{0:T(128)}, u32[]{:S(2)}) copy-start(s32[16]{0:T(128)} %time_ref.3) | copy-start | bytes 196
  87.7 34.4 %copy-start.11 = (s32[16]{0:T(128)S(1)}, s32[16]{0:T(128)}, u32[]{:S(2)}) copy-start(s32[16]{0:T(128)} %node_ref.3) | copy-start | bytes 196
  92.7 64.3 %copy-start.5 = (bf16[4,2,256,128]{3,2,1,0:T(8,128)(2,1)S(1)}, bf16[4,2,256,128]{3,2,1,0:T(8,128)(2,1)}, u32[]{:S(2)}) copy-start(bf16[4,2,256,128]{3,2,1,0:T(8,128)(2,1)} %all_to_all.25.refs_0_) | copy-start | bytes 1572868
  92.7 64.3 %copy-start.14 = (bf16[4,2,256,128]{3,2,1,0:T(8,128)(2,1)S(1)}, bf16[4,2,256,128]{3,2,1,0:T(8,128)(2,1)}, u32[]{:S(2)}) copy-start(bf16[4,2,256,128]{3,2,1,0:T(8,128)(2,1)} %copy-done.12) | copy-start | bytes 1572868
  92.7 64.3 %copy-start.17 = (bf16[4,2,256,128]{3,2,1,0:T(8,128)(2,1)S(1)}, bf16[4,2,256,128]{3,2,1,0:T(8,128)(2,1)}, u32[]{:S(2)}) copy-start(bf16[4,2,256,128]{3,2,1,0:T(8,128)(2,1)} %copy-done.15) | copy-start | bytes 1572868
  92.7 64.3 %copy-start.20 = (bf16[4,2,256,128]{3,2,1,0:T(8,128)(2,1)S(1)}, bf16[4,2,256,128]{3,2,1,0:T(8,128)(2,1)}, u32[]{:S(2)}) copy-start(bf16[4,2,256,128]{3,2,1,0:T(8,128)(2,1)} %copy-done.18) | copy-start | bytes 1572868

commit v3 on v1

--- a/solution.py
+++ b/solution.py
@@ -18,9 +18,9 @@
 LANES = 128
 TILES = OWN // LANES
 VALUE_ROWS = TILES * SCEN
-Z_GROUPS = [[8 * y + z for z in range(8)] for y in range(4)]
 Y_GROUPS = [[8 * y + z for y in range(4)] for z in range(8)]
 VMEM_BYTES = 40 << 20
+ALL_VMEM = 60 << 20
 
 NN = (((1,), (0,)), ((), ()))
 NT = (((1,), (1,)), ((), ()))
@@ -95,10 +95,7 @@
     )
 
 
-def interface_kernel(recv_ref, map_ref, schur_hbm, iface_ref, send_ref, schur_ref, sems):
-    copies = [pltpu.make_async_copy(schur_hbm.at[y], schur_ref.at[y], sems.at[y]) for y in range(4)]
-    for copy in copies:
-        copy.start()
+def right_hand_side(recv_ref, map_ref, rhs_ref):
     low = lax.broadcasted_iota(jnp.int32, (BLOCK, OWN), 0)
     rhs = jnp.zeros((ROWS * SCEN, BLOCK), jnp.float32)
     for r in range(ROWS):
@@ -111,16 +108,48 @@
         right = jnp.where(low == lo, 1.0, 0.0).astype(jnp.bfloat16)
         rhs += dot(left, right, NT)
     rhs = rhs.astype(jnp.bfloat16)
+    for h in range(ROWS):
+        for side in range(2):
+            rhs_ref[2 * h + side] = rhs[h * SCEN : (h + 1) * SCEN, side * LANES : (side + 1) * LANES]
+
+
+def schur_copies(schur_hbm, schur_ref, sems):
+    copies = [pltpu.make_async_copy(schur_hbm.at[y], schur_ref.at[y], sems.at[y]) for y in range(4)]
+    for copy in copies:
+        copy.start()
+    return copies
+
+
+def schur_product(rhs_ref, schur_ref, copies, iface_ref, send_ref):
+    own_z = lax.axis_index("col") % 8
     total = jnp.zeros((SCEN, BLOCK), jnp.float32)
-    for h in range(ROWS):
-        if h % 4 == 0:
-            copies[h // 4].wait()
-        pair = schur_ref[h // 4, 2 * (h % 4)], schur_ref[h // 4, 2 * (h % 4) + 1]
-        total += dot(rhs[h * SCEN : (h + 1) * SCEN, :], jnp.concatenate(pair, axis=1), NT)
+    for y in range(4):
+        copies[y].wait()
+        for x in (0, 2):
+            for o in range(2):
+                col = 8 * y + jnp.bitwise_xor(own_z, x + 4 * o)
+                left = jnp.concatenate([rhs_ref[col], rhs_ref[jnp.bitwise_xor(col, 1)]], axis=1)
+                right = jnp.concatenate([schur_ref[y, x, o], schur_ref[y, x + 1, o]], axis=1)
+                total += dot(left, right, NT)
     iface_ref[...] = total
     half = total.astype(jnp.bfloat16)
     for r in range(ROWS):
         send_ref[r] = half
+
+
+def rhs_kernel(recv_ref, rhs_ref):
+    right_hand_side(recv_ref, recv_ref, rhs_ref)
+
+
+def product_kernel(rhs_ref, schur_hbm, iface_ref, send_ref, schur_ref, sems):
+    copies = schur_copies(schur_hbm, schur_ref, sems)
+    schur_product(rhs_ref, schur_ref, copies, iface_ref, send_ref)
+
+
+def interface_kernel(recv_ref, map_ref, schur_hbm, iface_ref, send_ref, schur_ref, rhs_ref, sems):
+    copies = schur_copies(schur_hbm, schur_ref, sems)
+    right_hand_side(recv_ref, map_ref, rhs_ref)
+    schur_product(rhs_ref, schur_ref, copies, iface_ref, send_ref)
 
 
 def driven(recv_ref, map_ref, tie_ref):
@@ -179,14 +208,14 @@
 ANY = pl.BlockSpec(memory_space=pl.ANY)
 
 
-def call(body, ins, outs, scratch, flops, moved):
+def call(body, ins, outs, scratch, flops, moved, vmem=VMEM_BYTES):
     return pl.pallas_call(
         body,
         out_shape=[jax.ShapeDtypeStruct(shape, kind) for shape, kind in outs],
         in_specs=ins,
         out_specs=[VMEM] * len(outs),
         scratch_shapes=scratch,
-        compiler_params=pltpu.CompilerParams(vmem_limit_bytes=VMEM_BYTES),
+        compiler_params=pltpu.CompilerParams(vmem_limit_bytes=vmem),
         cost_estimate=pl.CostEstimate(flops=flops, bytes_accessed=moved, transcendentals=0),
     )
 
@@ -197,12 +226,6 @@
 
 
 def local(volt, curr, local_inverse, schur_inverse, ind_gain, tie, port_map, breaker, fault_time, fault_node):
-    with jax.named_scope("schur_rows"):
-        blocks = jnp.broadcast_to(schur_inverse[None], (8, BLOCK, LANES))
-        blocks = lax.all_to_all(blocks, "col", 0, 0, axis_index_groups=Z_GROUPS)
-        blocks = jnp.broadcast_to(blocks[None], (4, 8, BLOCK, LANES))
-        schur_rows = lax.all_to_all(blocks, "col", 0, 0, axis_index_groups=Y_GROUPS)
-
     first = call(
         first_kernel,
         [SMEM] * 2 + [VMEM] * 6 + [ANY],
@@ -210,12 +233,25 @@
         INVERSE,
         OPEN_FLOPS,
         4 << 20,
+        ALL_VMEM,
+    )
+    faces = [((SCEN, BLOCK), jnp.float32), ((ROWS, SCEN, BLOCK), jnp.bfloat16)]
+    schur_scratch = pltpu.VMEM((4, 4, 2, BLOCK, LANES), jnp.bfloat16)
+    rhs_shape = ((COLS, SCEN, LANES), jnp.bfloat16)
+    summed = call(rhs_kernel, [VMEM], [rhs_shape], [], 2 * 256 * 256 * 8192, 1 << 20)
+    product = call(
+        product_kernel,
+        [VMEM, ANY],
+        faces,
+        [schur_scratch, pltpu.SemaphoreType.DMA((4,))],
+        2 * 16 * 256 * 4096,
+        3 << 20,
     )
     interface = call(
         interface_kernel,
         [VMEM] * 2 + [ANY],
-        [((SCEN, BLOCK), jnp.float32), ((ROWS, SCEN, BLOCK), jnp.bfloat16)],
-        [pltpu.VMEM((4, 8, BLOCK, LANES), jnp.bfloat16), pltpu.SemaphoreType.DMA((4,))],
+        faces,
+        [schur_scratch, pltpu.VMEM(*rhs_shape), pltpu.SemaphoreType.DMA((4,))],
         2 * 256 * 256 * 8192,
         3 << 20,
     )
@@ -237,9 +273,20 @@
     )
 
     exchange = functools.partial(lax.all_to_all, axis_name="row", split_axis=0, concat_axis=0)
+    with jax.named_scope("schur_z"):
+        across = lax.ppermute(schur_inverse, "col", [(c, c ^ 4) for c in range(COLS)])
     opened, send = first(fault_time, fault_node, volt, curr, breaker, ind_gain, tie, port_map, local_inverse)
+    across, send = lax.optimization_barrier((across, send))
     maps = exchange(send)
-    _, send = interface(maps, maps, schur_rows)
+    with jax.named_scope("schur_z"):
+        pair = jnp.stack([schur_inverse, across])
+        quad = [pair] + [lax.ppermute(pair, "col", [(c, c ^ n) for c in range(COLS)]) for n in (1, 2, 3)]
+    quad, maps = lax.optimization_barrier((quad, maps))
+    with jax.named_scope("schur_y"):
+        blocks = jnp.broadcast_to(jnp.stack(quad)[None], (4, 4, 2, BLOCK, LANES))
+        schur_rows = lax.all_to_all(blocks, "col", 0, 0, axis_index_groups=Y_GROUPS)
+    (rhs,) = summed(maps)
+    _, send = product(rhs, schur_rows)
     volt, curr, opened, send = middle(fault_time, fault_node, exchange(send), opened, volt, curr, breaker, ind_gain, tie, port_map, local_inverse)
     iface_block, send = interface(exchange(send), maps, schur_rows)
     volt, curr = last(exchange(send), opened, volt, curr, breaker, ind_gain, tie, port_map, local_inverse)

time: 199 us -> 178 us (0.89)
  blocking collectives: 170 us -> 70.8 us
  waiting for transfers between devices: 0 us -> 42.7 us
  starting transfers between devices: 0 us -> 39.2 us
  local copies, waits for them, and re-layouts: 8.72 us -> 4.36 us
    all_to_all x3 -> x0, blocking collectives: 103 us -> none  [the longest x1 44.1 us: local(): maps = exchange(send)]
    all_to_all x0 -> x2, waiting for transfers between devices: none -> 23.8 us  [the longest x1 22.8 us: local(): schur_rows = lax.all_to_all(blocks, 'col', 0, 0, axis_index_groups=Y_GROUPS)]
    all_to_all x0 -> x2, starting transfers between devices: none -> 21.3 us  [the longest x1 16.8 us: local(): maps = exchange(send)]
    ppermute x0 -> x4, waiting for transfers between devices: none -> 18.9 us  [the longest x3 18.9 us: local(): lax.ppermute(pair, 'col', [(c, c ^ n) for c in range(COLS)])]
    ppermute x0 -> x4, starting transfers between devices: none -> 17.9 us  [the longest x3 8.98 us: local(): lax.ppermute(pair, 'col', [(c, c ^ n) for c in range(COLS)])]
    all_to_all x2, blocking collectives: 41.8 us -> 47.6 us  [local(): exchange(send)]
    unnamed x28 -> x32, local copies, waits for them, and re-layouts: 8.19 us -> 2.58 us
    all_to_all x1, blocking collectives: 26.1 us -> 23.2 us  [local(): iface_block, send = interface(exchange(send), maps, schur_rows)]
  transfers between devices with their start and end apart: 0 -> 6, of which waited for: 0 -> 4; matrix products, arithmetic and copies ran while one was open for 0% -> 0% of each run, Pallas kernels for 0% -> 3%
where the time goes in v3:
time: 178 us
  blocking collectives  70.8 us (40%)
  waiting for transfers between devices  42.7 us (24%)
  starting transfers between devices  39.2 us (22%)
  Pallas kernels  19.7 us (11%)
  local copies, waits for them, and re-layouts  4.36 us (2%)
    all_to_all x2, blocking collectives, local(): exchange(send)  47.6 us
    all_to_all x1, blocking collectives, local(): iface_block, send = interface(exchange(send), maps, schur_rows)  23.2 us
    all_to_all x1, waiting for transfers between devices, local(): schur_rows = lax.all_to_all(blocks, 'col', 0, 0, axis_index_groups=Y_GROUPS)  22.8 us
    ppermute x3, waiting for transfers between devices, local(): lax.ppermute(pair, 'col', [(c, c ^ n) for c in range(COLS)])  18.9 us
    all_to_all x1, starting transfers between devices, local(): maps = exchange(send)  16.8 us
    ppermute x3, starting transfers between devices, local(): lax.ppermute(pair, 'col', [(c, c ^ n) for c in range(COLS)])  8.98 us
    ppermute x1, starting transfers between devices, local(): lax.ppermute(schur_inverse, 'col', [(c, c ^ 4) for c in range(COLS)])  8.95 us
    all_to_all x1, starting transfers between devices, local(): schur_rows = lax.all_to_all(blocks, 'col', 0, 0, axis_index_groups=Y_GROUPS)  4.46 us
  transfers between devices with their start and end apart: 6, of which 4 were waited for; matrix products, arithmetic and copies ran while one was open for 0% of the time, Pallas kernels for 3%

profile of v3, /device:TPU:33, one launch (start us, length us, event | category | flops | bytes accessed | tf_op | source)
XLA Modules:
  0.0 177.7 jit_solution(17821112016602085501)
XLA Ops:
  0.6 8.9 %collective-permute-start = (bf16[256,128]{1,0:T(8,128)(2,1)}, bf16[256,128]{1,0:T(8,128)(2,1)S(1)}, u32[]{:S(2)}, u32[]{:S(2)}) collective-permute-start(bf16[256,128]{1,0:T(8,128)(2,1)} %param.13), channel_id=1, source_target_pairs={{0,4},{1,5},{2,6},{3,7},{4,0},{5,1},{6,2},{7,3},{8,12},{9,13},{10,... | collective-permute-start | bytes 196616 | tf_op jit(solution)/shard_map/schur_z/ppermute | solution.py:277
  9.6 4.4 %shard_map.121 = (f32[8,16,400]{2,1,0:T(8,128)}, bf16[16,80,128]{2,1,0:T(8,128)(2,1)}) custom-call(s32[16]{0:T(128)} %time_ref.3, s32[16]{0:T(128)} %node_ref.3, f32[8,16,400]{2,1,0:T(8,128)} %volt_ref.3, f32[8,16,400]{2,1,0:T(8,128)} %curr_ref.3, s32[8,16,400]{2,1,0:T(8,128)} %breaker_ref.5, f32[8,400]{1,0:T(8,128)} %gain_ref.5, f32[8,64]{1,0:T(8,128)} %tie_ref.5, ...), custom_call_target="tpu_custom_call" | custom-call | flops 40960000 | bytes 4194304 | tf_op jit(solution)/shard_map/pallas_call | solution.py:278
  14.1 0.0 collective-permute-done
  14.1 16.8 %all-to-all-start = ((bf16[16,80,128]{2,1,0:T(8,128)(2,1)}), bf16[16,80,128]{2,1,0:T(8,128)(2,1)S(1)}, u32[]{:S(2)}, u32[]{:S(2)}) async-start(bf16[16,80,128]{2,1,0:T(8,128)(2,1)} %get-tuple-element.23), calls=%async_computation | async-start | bytes 655360 | tf_op jit(solution)/shard_map/all_to_all | solution.py:280
  30.9 0.0 copy-done.15
  30.9 4.0 %collective-permute-start.1 = (bf16[2,256,128]{2,1,0:T(8,128)(2,1)S(1)}, bf16[2,256,128]{2,1,0:T(8,128)(2,1)S(1)}, u32[]{:S(2)}, u32[]{:S(2)}) collective-permute-start(bf16[2,256,128]{2,1,0:T(8,128)(2,1)S(1)} %pad_maximum_fusion.1), channel_id=1, source_target_pairs={{0,1},{1,0},{2,3},{3,2},{4,5},{5,4},{6,7},{7,6},{8,9},{9,8},{10,11... | collective-permute-start | bytes 393224 | tf_op jit(solution)/shard_map/schur_z/ppermute | solution.py:283
  34.9 1.9 %collective-permute-start.2 = (bf16[2,256,128]{2,1,0:T(8,128)(2,1)S(1)}, bf16[2,256,128]{2,1,0:T(8,128)(2,1)S(1)}, u32[]{:S(2)}, u32[]{:S(2)}) collective-permute-start(bf16[2,256,128]{2,1,0:T(8,128)(2,1)S(1)} %pad_maximum_fusion.1), channel_id=1, source_target_pairs={{0,2},{1,3},{2,0},{3,1},{4,6},{5,7},{6,4},{7,5},{8,10},{9,11},{10,... | collective-permute-start | bytes 393224 | tf_op jit(solution)/shard_map/schur_z/ppermute | solution.py:283
  36.8 3.1 %collective-permute-start.3 = (bf16[2,256,128]{2,1,0:T(8,128)(2,1)S(1)}, bf16[2,256,128]{2,1,0:T(8,128)(2,1)S(1)}, u32[]{:S(2)}, u32[]{:S(2)}) collective-permute-start(bf16[2,256,128]{2,1,0:T(8,128)(2,1)S(1)} %pad_maximum_fusion.1), channel_id=1, source_target_pairs={{0,3},{1,2},{2,1},{3,0},{4,7},{5,6},{6,5},{7,4},{8,11},{9,10},{10,... | collective-permute-start | bytes 393224 | tf_op jit(solution)/shard_map/schur_z/ppermute | solution.py:283
  39.9 12.7 %collective-permute-done.1 = bf16[2,256,128]{2,1,0:T(8,128)(2,1)S(1)} collective-permute-done((bf16[2,256,128]{2,1,0:T(8,128)(2,1)S(1)}, bf16[2,256,128]{2,1,0:T(8,128)(2,1)S(1)}, u32[]{:S(2)}, u32[]{:S(2)}) %collective-permute-start.1) | collective-permute-done | bytes 131104 | tf_op jit(solution)/shard_map/schur_z/ppermute | solution.py:283
  52.6 0.0 collective-permute-done.2
  52.6 6.2 %collective-permute-done.3 = bf16[2,256,128]{2,1,0:T(8,128)(2,1)S(1)} collective-permute-done((bf16[2,256,128]{2,1,0:T(8,128)(2,1)S(1)}, bf16[2,256,128]{2,1,0:T(8,128)(2,1)S(1)}, u32[]{:S(2)}, u32[]{:S(2)}) %collective-permute-start.3) | collective-permute-done | bytes 131104 | tf_op jit(solution)/shard_map/schur_z/ppermute | solution.py:283
  58.8 1.1 all-to-all-done.recv_ref.map_ref
  59.8 0.1 pad_maximum_fusion
  59.9 1.8 %broadcast_in_dim.2 = bf16[4,4,2,256,128]{4,3,2,1,0:T(8,128)(2,1)} broadcast(bf16[4,2,256,128]{3,2,1,0:T(8,128)(2,1)S(1)} %pad_maximum_fusion), dimensions={1,2,3,4} | broadcast | bytes 2621440 | tf_op jit(solution)/shard_map/schur_y/broadcast_in_dim | solution.py:286
  61.7 4.5 %all-to-all-start.1 = ((bf16[4,4,2,256,128]{4,3,2,1,0:T(8,128)(2,1)}), bf16[4,4,2,256,128]{4,3,2,1,0:T(8,128)(2,1)}, u32[]{:S(2)}, u32[]{:S(2)}) async-start(bf16[4,4,2,256,128]{4,3,2,1,0:T(8,128)(2,1)} %broadcast_in_dim.2), calls=%async_computation.1 | async-start | bytes 4194304 | tf_op jit(solution)/shard_map/schur_y/all_to_all | solution.py:287
  66.2 1.0 copy-done.5
  67.1 1.4 shard_map.122.rhs_ref
  68.6 0.0 copy-start.9
  68.6 0.6 copy-done.9
  69.2 22.8 %all-to-all-done.1.schur_hbm = bf16[4,4,2,256,128]{4,3,2,1,0:T(8,128)(2,1)} async-done(((bf16[4,4,2,256,128]{4,3,2,1,0:T(8,128)(2,1)}), bf16[4,4,2,256,128]{4,3,2,1,0:T(8,128)(2,1)}, u32[]{:S(2)}, u32[]{:S(2)}) %all-to-all-start.1) | async-done | bytes 2097184 | tf_op jit(solution)/shard_map/schur_y/all_to_all | solution.py:287
  92.0 0.9 copy-done.10
  92.9 0.0 copy-start.12
  92.9 0.0 copy-start.13
  93.0 0.0 copy-start.14
  93.0 3.1 %shard_map.123 = (f32[16,256]{1,0:T(8,128)}, bf16[16,16,256]{2,1,0:T(8,128)(2,1)S(1)}) custom-call(bf16[32,16,128]{2,1,0:T(8,128)(2,1)S(1)} %copy-done.10, bf16[4,4,2,256,128]{4,3,2,1,0:T(8,128)(2,1)} %all-to-all-done.1.schur_hbm), custom_call_target="tpu_custom_call" | custom-call | flops 33554432 | bytes 3145728 | tf_op jit(solution)/shard_map/pallas_call | solution.py:289
  96.0 29.5 %all_to_all.25.recv_ref = bf16[16,16,256]{2,1,0:T(8,128)(2,1)S(1)} all-to-all(bf16[16,16,256]{2,1,0:T(8,128)(2,1)S(1)} %get-tuple-element.29), channel_id=1, replica_groups=mesh['row'=16,'col'=32] {'row'}, dimensions={0} | all-to-all | bytes 262144 | tf_op jit(solution)/shard_map/all_to_all | solution.py:290
  125.6 0.0 copy-done.1
  125.7 4.2 %shard_map.124 = (f32[8,16,400]{2,1,0:T(8,128)S(1)}, f32[8,16,400]{2,1,0:T(8,128)S(1)}, f32[8,16,400]{2,1,0:T(8,128)S(1)}, bf16[16,64,128]{2,1,0:T(8,128)(2,1)S(1)}) custom-call(s32[16]{0:T(128)S(1)} %copy-done.13, s32[16]{0:T(128)S(1)} %copy-done.14, bf16[16,16,256]{2,1,0:T(8,128)(2,1)S(1)} %all_to_all.25.recv_ref, f32[8,16,400]{2,1,0:T(8,128)S(1)} %copy-done.7, ...), custom_call_target="tpu_custom_call" | custom-call | flops 40960000 | bytes 4194304 | tf_op jit(solution)/shard_map/pallas_call | solution.py:290
  129.9 23.2 %all_to_all.26.recv_ref = bf16[16,64,128]{2,1,0:T(8,128)(2,1)S(1)} all-to-all(bf16[16,64,128]{2,1,0:T(8,128)(2,1)S(1)} %get-tuple-element.31), channel_id=1, replica_groups=mesh['row'=16,'col'=32] {'row'}, dimensions={0} | all-to-all | bytes 524288 | tf_op jit(solution)/shard_map/all_to_all | solution.py:291
  153.1 3.7 %shard_map.125 = (f32[16,256]{1,0:T(8,128)}, bf16[16,16,256]{2,1,0:T(8,128)(2,1)S(1)}) custom-call(bf16[16,64,128]{2,1,0:T(8,128)(2,1)S(1)} %all_to_all.26.recv_ref, bf16[16,80,128]{2,1,0:T(8,128)(2,1)S(1)} %copy-done.6, bf16[4,4,2,256,128]{4,3,2,1,0:T(8,128)(2,1)} %all-to-all-done.1.schur_hbm), custom_call_target="tpu_custom_call" | custom-call | flops 1073741824 | bytes 3145728 | tf_op jit(solution)/shard_map/pallas_call | solution.py:291
  156.8 18.1 %all_to_all.27.recv_ref = bf16[16,16,256]{2,1,0:T(8,128)(2,1)S(1)} all-to-all(bf16[16,16,256]{2,1,0:T(8,128)(2,1)S(1)} %get-tuple-element.32), channel_id=1, replica_groups=mesh['row'=16,'col'=32] {'row'}, dimensions={0} | all-to-all | bytes 262144 | tf_op jit(solution)/shard_map/all_to_all | solution.py:292
  174.9 2.9 %shard_map.126 = (f32[8,16,400]{2,1,0:T(8,128)}, f32[8,16,400]{2,1,0:T(8,128)}) custom-call(bf16[16,16,256]{2,1,0:T(8,128)(2,1)S(1)} %all_to_all.27.recv_ref, f32[8,16,400]{2,1,0:T(8,128)S(1)} %get-tuple-element.33.open_prev_ref, f32[8,16,400]{2,1,0:T(8,128)S(1)} %get-tuple-element.34.volt_ref, f32[8,16,400]{2,1,0:T(8,128)S(1)} %get-tuple-element.35.curr_ref, ...), custom_call_target="tpu_custom_call" | custom-call | flops 5120000 | bytes 2097152 | tf_op jit(solution)/shard_map/pallas_call | solution.py:292
  (24 shorter events, 0.1 us)
Async XLA Ops:
  0.6 30.2 %copy-start.15 = (bf16[256,128]{1,0:T(8,128)(2,1)S(1)}, bf16[256,128]{1,0:T(8,128)(2,1)}, u32[]{:S(2)}) copy-start(bf16[256,128]{1,0:T(8,128)(2,1)} %param.13) | copy-start | bytes 196612
  0.6 13.4 %collective-permute-start = (bf16[256,128]{1,0:T(8,128)(2,1)}, bf16[256,128]{1,0:T(8,128)(2,1)S(1)}, u32[]{:S(2)}, u32[]{:S(2)}) collective-permute-start(bf16[256,128]{1,0:T(8,128)(2,1)} %param.13), channel_id=1, source_target_pairs={{0,4},{1,5},{2,6},{3,7},{4,0},{5,1},{6,2},{7,3},{8,12},{9,13},{10,... | collective-permute-start | bytes 196616 | tf_op jit(solution)/shard_map/schur_z/ppermute | solution.py:277
  14.1 45.8 %all-to-all-start = ((bf16[16,80,128]{2,1,0:T(8,128)(2,1)}), bf16[16,80,128]{2,1,0:T(8,128)(2,1)S(1)}, u32[]{:S(2)}, u32[]{:S(2)}) async-start(bf16[16,80,128]{2,1,0:T(8,128)(2,1)} %get-tuple-element.23), calls=%async_computation | async-start | bytes 655360 | tf_op jit(solution)/shard_map/all_to_all | solution.py:280
  30.9 21.7 %collective-permute-start.1 = (bf16[2,256,128]{2,1,0:T(8,128)(2,1)S(1)}, bf16[2,256,128]{2,1,0:T(8,128)(2,1)S(1)}, u32[]{:S(2)}, u32[]{:S(2)}) collective-permute-start(bf16[2,256,128]{2,1,0:T(8,128)(2,1)S(1)} %pad_maximum_fusion.1), channel_id=1, source_target_pairs={{0,1},{1,0},{2,3},{3,2},{4,5},{5,4},{6,7},{7,6},{8,9},{9,8},{10,11... | collective-permute-start | bytes 393224 | tf_op jit(solution)/shard_map/schur_z/ppermute | solution.py:283
  34.9 17.7 %collective-permute-start.2 = (bf16[2,256,128]{2,1,0:T(8,128)(2,1)S(1)}, bf16[2,256,128]{2,1,0:T(8,128)(2,1)S(1)}, u32[]{:S(2)}, u32[]{:S(2)}) collective-permute-start(bf16[2,256,128]{2,1,0:T(8,128)(2,1)S(1)} %pad_maximum_fusion.1), channel_id=1, source_target_pairs={{0,2},{1,3},{2,0},{3,1},{4,6},{5,7},{6,4},{7,5},{8,10},{9,11},{10,... | collective-permute-start | bytes 393224 | tf_op jit(solution)/shard_map/schur_z/ppermute | solution.py:283
  36.8 22.0 %collective-permute-start.3 = (bf16[2,256,128]{2,1,0:T(8,128)(2,1)S(1)}, bf16[2,256,128]{2,1,0:T(8,128)(2,1)S(1)}, u32[]{:S(2)}, u32[]{:S(2)}) collective-permute-start(bf16[2,256,128]{2,1,0:T(8,128)(2,1)S(1)} %pad_maximum_fusion.1), channel_id=1, source_target_pairs={{0,3},{1,2},{2,1},{3,0},{4,7},{5,6},{6,5},{7,4},{8,11},{9,10},{10,... | collective-permute-start | bytes 393224 | tf_op jit(solution)/shard_map/schur_z/ppermute | solution.py:283
  59.8 1.9 %copy-start.4 = (bf16[16,80,128]{2,1,0:T(8,128)(2,1)}, bf16[16,80,128]{2,1,0:T(8,128)(2,1)S(1)}, u32[]{:S(2)}) copy-start(bf16[16,80,128]{2,1,0:T(8,128)(2,1)S(1)} %all-to-all-done.recv_ref.map_ref) | copy-start | bytes 983044
  61.7 30.3 %all-to-all-start.1 = ((bf16[4,4,2,256,128]{4,3,2,1,0:T(8,128)(2,1)}), bf16[4,4,2,256,128]{4,3,2,1,0:T(8,128)(2,1)}, u32[]{:S(2)}, u32[]{:S(2)}) async-start(bf16[4,4,2,256,128]{4,3,2,1,0:T(8,128)(2,1)} %broadcast_in_dim.2), calls=%async_computation.1 | async-start | bytes 4194304 | tf_op jit(solution)/shard_map/schur_y/all_to_all | solution.py:287
  66.2 1.0 copy-start.5
  67.1 58.5 %copy-start = (bf16[8,400,400]{2,1,0:T(8,128)(2,1)S(1)}, bf16[8,400,400]{2,1,0:T(8,128)(2,1)}, u32[]{:S(2)}) copy-start(bf16[8,400,400]{2,1,0:T(8,128)(2,1)} %inv_hbm.5) | copy-start | bytes 7680004
  68.6 0.7 copy-start.9
  69.2 56.4 %copy-start.1 = (s32[8,16,400]{2,1,0:T(8,128)S(1)}, s32[8,16,400]{2,1,0:T(8,128)}, u32[]{:S(2)}) copy-start(s32[8,16,400]{2,1,0:T(8,128)} %breaker_ref.5) | copy-start | bytes 614404
  69.2 56.4 %copy-start.8 = (f32[8,400]{1,0:T(8,128)S(1)}, f32[8,400]{1,0:T(8,128)}, u32[]{:S(2)}) copy-start(f32[8,400]{1,0:T(8,128)} %gain_ref.5) | copy-start | bytes 38404
  92.0 0.9 copy-start.10
  92.9 32.7 %copy-start.2 = (f32[8,16,400]{2,1,0:T(8,128)S(1)}, f32[8,16,400]{2,1,0:T(8,128)}, u32[]{:S(2)}) copy-start(f32[8,16,400]{2,1,0:T(8,128)} %volt_ref.3) | copy-start | bytes 614404
  92.9 32.7 %copy-start.3 = (f32[8,16,400]{2,1,0:T(8,128)S(1)}, f32[8,16,400]{2,1,0:T(8,128)}, u32[]{:S(2)}) copy-start(f32[8,16,400]{2,1,0:T(8,128)} %curr_ref.3) | copy-start | bytes 614404
  92.9 32.7 %copy-start.7 = (f32[8,16,400]{2,1,0:T(8,128)S(1)}, f32[8,16,400]{2,1,0:T(8,128)}, u32[]{:S(2)}) copy-start(f32[8,16,400]{2,1,0:T(8,128)} %get-tuple-element.30.open_prev_ref) | copy-start | bytes 614404
  92.9 32.7 %copy-start.11 = (f32[8,64]{1,0:T(8,128)S(1)}, f32[8,64]{1,0:T(8,128)}, u32[]{:S(2)}) copy-start(f32[8,64]{1,0:T(8,128)} %tie_ref.5) | copy-start | bytes 6148
  92.9 32.7 %copy-start.12 = (s32[8,64]{1,0:T(8,128)S(1)}, s32[8,64]{1,0:T(8,128)}, u32[]{:S(2)}) copy-start(s32[8,64]{1,0:T(8,128)} %map_ref.5) | copy-start | bytes 6148
  92.9 32.7 %copy-start.13 = (s32[16]{0:T(128)S(1)}, s32[16]{0:T(128)}, u32[]{:S(2)}) copy-start(s32[16]{0:T(128)} %time_ref.3) | copy-start | bytes 196
  93.0 32.7 %copy-start.14 = (s32[16]{0:T(128)S(1)}, s32[16]{0:T(128)}, u32[]{:S(2)}) copy-start(s32[16]{0:T(128)} %node_ref.3) | copy-start | bytes 196
  125.7 27.4 %copy-start.6 = (bf16[16,80,128]{2,1,0:T(8,128)(2,1)S(1)}, bf16[16,80,128]{2,1,0:T(8,128)(2,1)}, u32[]{:S(2)}) copy-start(bf16[16,80,128]{2,1,0:T(8,128)(2,1)} %copy-done.4) | copy-start | bytes 983044

commit v4 on v2

v4 whole, which is shorter than its diff:
```python
import functools

import jax
import jax.numpy as jnp
from jax import lax
from jax.experimental import pallas as pl
from jax.experimental.pallas import tpu as pltpu
from jax.sharding import PartitionSpec as P

ROWS = 16
COLS = 32
SUBS = 8
SCEN = 16
NODES = 400
PORTS = 64
OWN = SUBS * PORTS
BLOCK = 256
LANES = 128
TILES = OWN // LANES
VALUE_ROWS = TILES * SCEN
QUADS = [[4 * q + z for z in range(4)] for q in range(8)]
VMEM_BYTES = 60 << 20

NN = (((1,), (0,)), ((), ()))
NT = (((1,), (1,)), ((), ()))


def dot(a, b, dims=NN):
    return lax.dot_general(a, b, dims, preferred_element_type=jnp.float32)


def flat_row(ref):
    return jnp.concatenate([ref[k : k + 1, :] for k in range(SUBS)], axis=1)


def column(ref):
    place = lax.broadcasted_iota(jnp.int32, (SCEN, 1), 0)
    out = jnp.zeros((SCEN, 1), jnp.int32)
    for s in range(SCEN):
        out = jnp.where(place == s, ref[s], out)
    return out


def open_circuit(step, volts, currs, breaker_ref, gain_ref, inv_copies, inv_ref, time_ref, node_ref, tie_ref, open_ref, send_ref):
    fault_node = jnp.where(step >= column(time_ref), column(node_ref), -1)
    first = lax.axis_index("row") * SUBS
    lane = lax.broadcasted_iota(jnp.int32, (SCEN, NODES), 1)
    parts = []
    for k in range(SUBS):
        volt = volts[k]
        hist = breaker_ref[k].astype(jnp.float32) * (currs[k] + gain_ref[k : k + 1, :] * volt)
        hit = lane + (first + k) * NODES == fault_node
        inject = (-hist - jnp.where(hit, 2.0 * volt, 0.0)).astype(jnp.bfloat16)
        if inv_copies:
            inv_copies[k].wait()
        open_k = dot(inject, inv_ref[k])
        open_ref[k] = open_k
        parts.append(tie_ref[k : k + 1, :] * open_k[:, :PORTS])
    values = jnp.concatenate(parts, axis=1).astype(jnp.bfloat16)
    for r in range(ROWS):
        for t in range(TILES):
            send_ref[r, t * SCEN : (t + 1) * SCEN, :] = values[:, t * LANES : (t + 1) * LANES]


def fetch(sources, targets, sems):
    copies = [pltpu.make_async_copy(a, b, sems.at[n]) for n, (a, b) in enumerate(zip(sources, targets))]
    for copy in copies:
        copy.start()
    return copies


def by_subnetwork(ref, rows=None):
    return [ref.at[k] if rows is None else ref.at[k, pl.ds(0, rows)] for k in range(SUBS)]


def first_kernel(time_ref, node_ref, volt_hbm, curr_hbm, breaker_hbm, gain_hbm, tie_hbm, map_hbm, inv_hbm, open_ref, send_ref, map_ref, gain_ref, tie_ref, volt_ref, curr_ref, breaker_ref, inv_ref, sems):
    copies = fetch(
        [map_hbm, gain_hbm, tie_hbm, volt_hbm, curr_hbm, breaker_hbm] + by_subnetwork(inv_hbm),
        [map_ref, gain_ref, tie_ref, volt_ref, curr_ref, breaker_ref] + by_subnetwork(inv_ref),
        sems,
    )
    copies[0].wait()
    mapped = flat_row(map_ref)
    rows = [(mapped // BLOCK).astype(jnp.float32), (mapped % BLOCK).astype(jnp.float32)]
    rows = [row[:, t * LANES : (t + 1) * LANES] for row in rows for t in range(TILES)]
    tail = jnp.concatenate(rows + [jnp.zeros((16 - len(rows), LANES), jnp.float32)], axis=0).astype(jnp.bfloat16)
    for r in range(ROWS):
        send_ref[r, VALUE_ROWS : VALUE_ROWS + 16, :] = tail
    for copy in copies[1:6]:
        copy.wait()
    open_circuit(0, volt_ref, curr_ref, breaker_ref, gain_ref, copies[6:], inv_ref, time_ref, node_ref, tie_ref, open_ref, send_ref)


def right_hand_side(recv_ref, map_ref, rhs_ref):
    low = lax.broadcasted_iota(jnp.int32, (BLOCK, OWN), 0)
    rhs = jnp.zeros((ROWS * SCEN, BLOCK), jnp.float32)
    for r in range(ROWS):
        tail = map_ref[r, VALUE_ROWS : VALUE_ROWS + 16, :].astype(jnp.float32)
        hi = jnp.concatenate([tail[t : t + 1] for t in range(TILES)], axis=1).astype(jnp.int32)
        lo = jnp.concatenate([tail[TILES + t : TILES + t + 1] for t in range(TILES)], axis=1).astype(jnp.int32)
        values = jnp.concatenate([recv_ref[r, t * SCEN : (t + 1) * SCEN, :] for t in range(TILES)], axis=1)
        values = values.astype(jnp.float32)
        left = jnp.concatenate([jnp.where(hi == h, values, 0.0) for h in range(ROWS)], axis=0).astype(jnp.bfloat16)
        right = jnp.where(low == lo, 1.0, 0.0).astype(jnp.bfloat16)
        rhs += dot(left, right, NT)
    rhs_ref[...] = rhs.astype(jnp.bfloat16).reshape(ROWS, SCEN, BLOCK)


def schur_copies(parts, schur_ref, sems):
    own, back, ahead, far_low, far_high = parts
    low, high = schur_ref.at[2, pl.ds(0, 2)], schur_ref.at[2, pl.ds(2, 2)]
    return fetch([own, back, ahead, far_low, far_high], [schur_ref.at[0], schur_ref.at[1], schur_ref.at[3], low, high], sems)


def schur_product(rhs_ref, schur_ref, copies, iface_ref, send_ref):
    col = lax.axis_index("col")
    own_y, own_half = col // 8, (col // 4) % 2
    total = jnp.zeros((SCEN, BLOCK), jnp.float32)
    for n, waits in ((0, copies[:1]), (1, copies[1:2]), (3, copies[2:3]), (2, copies[3:])):
        for copy in waits:
            copy.wait()
        for other in range(2):
            first = 4 * ((own_y + 4 - n) % 4) + 2 * ((own_half + other) % 2)
            for p in range(2):
                pair = schur_ref[n, 2 * p, other], schur_ref[n, 2 * p + 1, other]
                total += dot(rhs_ref[first + p], jnp.concatenate(pair, axis=1), NT)
    iface_ref[...] = total
    for r in range(ROWS):
        send_ref[r] = total


def rhs_kernel(recv_ref, rhs_ref):
    right_hand_side(recv_ref, recv_ref, rhs_ref)


def product_kernel(rhs_ref, *refs):
    parts, (iface_ref, send_ref, schur_ref, sems) = refs[:5], refs[5:]
    copies = schur_copies(parts, schur_ref, sems)
    schur_product(rhs_ref, schur_ref, copies, iface_ref, send_ref)


def interface_kernel(recv_ref, map_ref, *refs):
    parts, (iface_ref, send_ref, schur_ref, rhs_ref, sems) = refs[:5], refs[5:]
    copies = schur_copies(parts, schur_ref, sems)
    right_hand_side(recv_ref, map_ref, rhs_ref)
    schur_product(rhs_ref, schur_ref, copies, iface_ref, send_ref)


def port_kernel(map_ref, tie_ref, out_ref):
    mapped = flat_row(map_ref)
    rows = [(mapped // BLOCK).astype(jnp.float32), (mapped % BLOCK).astype(jnp.float32), flat_row(tie_ref)]
    out_ref[...] = jnp.concatenate(rows + [jnp.zeros((8 - len(rows), OWN), jnp.float32)], axis=0)


def driven(recv_ref, ports):
    hi, lo = ports[0:1].astype(jnp.int32), ports[1:2].astype(jnp.int32)
    low = lax.broadcasted_iota(jnp.int32, (BLOCK, OWN), 0)
    right = jnp.where(low == lo, 1.0, 0.0).astype(jnp.bfloat16)
    volts = recv_ref[...].reshape(ROWS * SCEN, BLOCK)
    coarse = volts.astype(jnp.bfloat16)
    found = dot(coarse, right) + dot((volts - coarse.astype(jnp.float32)).astype(jnp.bfloat16), right)
    picked = jnp.zeros((SCEN, OWN), jnp.float32)
    for r in range(ROWS):
        picked += jnp.where(hi == r, found[r * SCEN : (r + 1) * SCEN, :], 0.0)
    return (ports[2:3] * picked).astype(jnp.bfloat16)


def update(k, drive, open_ref, inv, volt, curr, breaker_ref, gain_ref):
    volt_next = open_ref[k] + dot(drive[:, k * PORTS : (k + 1) * PORTS], inv)
    closed = breaker_ref[k].astype(jnp.float32)
    return volt_next, closed * (curr + gain_ref[k : k + 1, :] * (volt_next + volt))


def middle_kernel(time_ref, node_ref, recv_ref, open_prev_ref, volt_hbm, curr_hbm, breaker_hbm, gain_hbm, tie_hbm, ports_hbm, inv_hbm, volt_out, curr_out, open_ref, send_ref, ports_ref, gain_ref, tie_ref, volt_ref, curr_ref, breaker_ref, inv_ref, sems):
    copies = fetch(
        [ports_hbm, tie_hbm, gain_hbm, volt_hbm, curr_hbm, breaker_hbm] + by_subnetwork(inv_hbm),
        [ports_ref, tie_ref, gain_ref, volt_ref, curr_ref, breaker_ref] + by_subnetwork(inv_ref),
        sems,
    )
    copies[0].wait()
    drive = driven(recv_ref, ports_ref[...])
    for copy in copies[1:6]:
        copy.wait()
    for k in range(SUBS):
        copies[6 + k].wait()
        volt_out[k], curr_out[k] = update(k, drive, open_prev_ref, inv_ref[k, :PORTS, :], volt_ref[k], curr_ref[k], breaker_ref, gain_ref)
    open_circuit(1, volt_out, curr_out, breaker_ref, gain_ref, None, inv_ref, time_ref, node_ref, tie_ref, open_ref, send_ref)


def last_kernel(recv_ref, open_prev_ref, volt_ref, curr_ref, breaker_hbm, gain_hbm, ports_hbm, inv_hbm, volt_out, curr_out, ports_ref, gain_ref, breaker_ref, inv_ref, sems):
    copies = fetch(
        [ports_hbm, gain_hbm, breaker_hbm] + by_subnetwork(inv_hbm, PORTS),
        [ports_ref, gain_ref, breaker_ref] + by_subnetwork(inv_ref),
        sems,
    )
    copies[0].wait()
    drive = driven(recv_ref, ports_ref[...])
    for copy in copies[1:3]:
        copy.wait()
    for k in range(SUBS):
        copies[3 + k].wait()
        volt_out[k], curr_out[k] = update(k, drive, open_prev_ref, inv_ref[k], volt_ref[k], curr_ref[k], breaker_ref, gain_ref)


SMEM = pl.BlockSpec(memory_space=pltpu.SMEM)
VMEM = pl.BlockSpec(memory_space=pltpu.VMEM)
HBM = pl.BlockSpec(memory_space=pltpu.HBM)


def call(body, ins, outs, scratch, flops, moved):
    return pl.pallas_call(
        body,
        out_shape=[jax.ShapeDtypeStruct(shape, kind) for shape, kind in outs],
        in_specs=ins,
        out_specs=[VMEM] * len(outs),
        scratch_shapes=scratch,
        compiler_params=pltpu.CompilerParams(vmem_limit_bytes=VMEM_BYTES),
        cost_estimate=pl.CostEstimate(flops=flops, bytes_accessed=moved, transcendentals=0),
    )


STATE = ((SUBS, SCEN, NODES), jnp.float32)
PREP_FLOPS = 100_000_000_000_000
OPEN_FLOPS = 2 * SUBS * SCEN * NODES * NODES
SMALL = [
    pltpu.VMEM((SUBS, PORTS), jnp.int32),
    pltpu.VMEM((SUBS, NODES), jnp.float32),
    pltpu.VMEM((SUBS, PORTS), jnp.float32),
]
PORT_ROWS = pltpu.VMEM((8, OWN), jnp.float32)
BREAKER = pltpu.VMEM((SUBS, SCEN, NODES), jnp.int32)
INVERSE = pltpu.VMEM((SUBS, NODES, NODES), jnp.bfloat16)


def local(volt, curr, local_inverse, schur_inverse, ind_gain, tie, port_map, breaker, fault_time, fault_node):
    first = call(
        first_kernel,
        [SMEM] * 2 + [HBM] * 7,
        [STATE, ((ROWS, VALUE_ROWS + 16, LANES), jnp.bfloat16)],
        SMALL + [pltpu.VMEM(*STATE)] * 2 + [BREAKER, INVERSE, pltpu.SemaphoreType.DMA((6 + SUBS,))],
        OPEN_FLOPS,
        4 << 20,
    )
    faces = [((SCEN, BLOCK), jnp.float32), ((ROWS, SCEN, BLOCK), jnp.float32)]
    schur_scratch = pltpu.VMEM((4, 4, 2, BLOCK, LANES), jnp.bfloat16)
    rhs_shape = ((ROWS, SCEN, BLOCK), jnp.bfloat16)
    summed = call(rhs_kernel, [VMEM], [rhs_shape], [], 2 * 256 * 256 * 8192, 1 << 20)
    product = call(
        product_kernel,
        [VMEM] + [HBM] * 5,
        faces,
        [schur_scratch, pltpu.SemaphoreType.DMA((5,))],
        2 * 16 * 256 * 4096,
        3 << 20,
    )
    interface = call(
        interface_kernel,
        [VMEM] * 2 + [HBM] * 5,
        faces,
        [schur_scratch, pltpu.VMEM(*rhs_shape), pltpu.SemaphoreType.DMA((5,))],
        2 * 256 * 256 * 8192,
        3 << 20,
    )
    middle = call(
        middle_kernel,
        [SMEM] * 2 + [VMEM] * 2 + [HBM] * 7,
        [STATE, STATE, STATE, ((ROWS, VALUE_ROWS, LANES), jnp.bfloat16)],
        [PORT_ROWS] + SMALL[1:] + [pltpu.VMEM(*STATE)] * 2 + [BREAKER, INVERSE, pltpu.SemaphoreType.DMA((6 + SUBS,))],
        OPEN_FLOPS,
        4 << 20,
    )
    last = call(
        last_kernel,
        [VMEM] * 4 + [HBM] * 4,
        [STATE, STATE],
        [PORT_ROWS, SMALL[1], BREAKER, pltpu.VMEM((SUBS, PORTS, NODES), jnp.bfloat16), pltpu.SemaphoreType.DMA((3 + SUBS,))],
        OPEN_FLOPS // 8,
        2 << 20,
    )

    described = call(port_kernel, [VMEM] * 2, [((8, OWN), jnp.float32)], [], PREP_FLOPS, 1 << 20)

    exchange = functools.partial(lax.all_to_all, axis_name="row", split_axis=0, concat_axis=0)
    def along_y(block, steps):
        return lax.ppermute(block, "col", [(c, (c + 8 * steps) % COLS) for c in range(COLS)])

    with jax.named_scope("schur_z"):
        across = lax.ppermute(schur_inverse, "col", [(c, c ^ 4) for c in range(COLS)])
    opened, send = first(fault_time, fault_node, volt, curr, breaker, ind_gain, tie, port_map, local_inverse)
    across, send = lax.optimization_barrier((across, send))
    with jax.named_scope("schur_z"):
        own = jnp.broadcast_to(jnp.stack([schur_inverse, across])[None], (4, 2, BLOCK, LANES))
        own = lax.all_to_all(own, "col", 0, 0, axis_index_groups=QUADS)
    own, send, own_ports = lax.optimization_barrier((own, send, port_map))
    with jax.named_scope("schur_y"):
        back, ahead = along_y(own, 1), along_y(own, -1)
        schur_rows = own, back, ahead, along_y(back[:2], 1), along_y(ahead[2:], -1)
    maps = exchange(send)
    (ports,) = described(own_ports, tie)
    (rhs,) = summed(maps)
    rhs, ports = lax.optimization_barrier((rhs, ports))
    _, send = product(rhs, *schur_rows)
    volt, curr, opened, send = middle(fault_time, fault_node, exchange(send), opened, volt, curr, breaker, ind_gain, tie, ports, local_inverse)
    iface_block, send = interface(exchange(send), maps, *schur_rows)
    volt, curr = last(exchange(send), opened, volt, curr, breaker, ind_gain, ports, local_inverse)
    return volt, curr, iface_block


def solution(mesh):
    placed = (
        P("row", "col", None),
        P("row", "col", None),
        P("row", None, None),
        P("row", "col"),
        P("row", None),
        P("row", None),
        P("row", None),
        P("row", "col", None),
        P("col"),
        P("col"),
    )
    return jax.shard_map(
        local,
        mesh=mesh,
        in_specs=placed,
        out_specs=(P("row", "col", None), P("row", "col", None), P("col", "row")),
        check_vma=False,
    )
```

time: 183 us -> 180 us (0.984)
  Pallas kernels: 21.3 us -> 26.7 us
  local copies, waits for them, and re-layouts: 6.73 us -> 1.67 us
  waiting for transfers between devices: 22.2 us -> 17.3 us
  starting transfers between devices: 35.7 us -> 39.2 us
  blocking collectives: 95.9 us -> 93.8 us
    ppermute x3 -> x4, waiting for transfers between devices: 22.2 us -> 0.01 us  [along_y(): lax.ppermute(block, 'col', [(c, (c + 8 * steps) % COLS) for c in range(CO...]
    all_to_all x1, waiting for transfers between devices: 0.01 us -> 17.2 us  [local(): maps = exchange(send)]
    all_to_all x1, blocking collectives: 30.7 us -> 23 us  [local(): iface_block, send = interface(exchange(send), maps, *schur_rows)]
    unnamed x44 -> x8, local copies, waits for them, and re-layouts: 6.66 us -> 0.02 us
    all_to_all x2, blocking collectives: 47.3 us -> 53.1 us  [local(): exchange(send)]
    pallas_call x2 -> x4, Pallas kernels: 7.85 us -> 12.7 us  [the longest x1 4.23 us: local(): last(exchange(send), opened, volt, curr, breaker, ind_gain, ports, local_...]
    ppermute x3 -> x4, starting transfers between devices: 9.49 us -> 13.3 us  [along_y(): lax.ppermute(block, 'col', [(c, (c + 8 * steps) % COLS) for c in range(CO...]
  transfers between devices with their start and end apart: 5 -> 6, of which waited for: 2 -> 1; matrix products, arithmetic and copies ran while one was open for 0% -> 1% of each run, Pallas kernels for 2% -> 5%
where the time goes in v4:
time: 180 us; the launch traced here: 179 us
  blocking collectives  93.8 us (52%)
  starting transfers between devices  39.2 us (22%)
  Pallas kernels  26.7 us (15%)
  waiting for transfers between devices  17.3 us (10%)
    all_to_all x2, blocking collectives, local(): exchange(send)  53.1 us
    all_to_all x1, blocking collectives, local(): iface_block, send = interface(exchange(send), maps, *schur_rows)  23 us
    all_to_all x1, blocking collectives, local(): own = lax.all_to_all(own, 'col', 0, 0, axis_index_groups=QUADS)  17.7 us
    all_to_all x1, waiting for transfers between devices, local(): maps = exchange(send)  17.2 us
    all_to_all x1, starting transfers between devices, local(): maps = exchange(send)  16.9 us
    ppermute x4, starting transfers between devices, along_y(): lax.ppermute(block, 'col', [(c, (c + 8 * steps) % COLS) for c in range(CO...  13.3 us
    ppermute x1, starting transfers between devices, local(): lax.ppermute(schur_inverse, 'col', [(c, c ^ 4) for c in range(COLS)])  8.95 us
    pallas_call x1, Pallas kernels, local(): iface_block, send = interface(exchange(send), maps, *schur_rows)  4.88 us
  transfers between devices with their start and end apart: 6, of which 1 were waited for; matrix products, arithmetic and copies ran while one was open for 1% of the time, Pallas kernels for 5%

profile of v4, /device:TPU:33, one launch (start us, length us, event | category | flops | bytes accessed | tf_op | source)
XLA Modules:
  0.0 179.3 jit_solution(15165192113709118284)
XLA Ops:
  0.6 0.0 copy-start.3
  0.6 8.9 %collective-permute-start = (bf16[256,128]{1,0:T(8,128)(2,1)}, bf16[256,128]{1,0:T(8,128)(2,1)S(1)}, u32[]{:S(2)}, u32[]{:S(2)}) collective-permute-start(bf16[256,128]{1,0:T(8,128)(2,1)} %param.13), channel_id=1, source_target_pairs={{0,4},{1,5},{2,6},{3,7},{4,0},{5,1},{6,2},{7,3},{8,12},{9,13},{10,... | collective-permute-start | bytes 196616 | tf_op jit(solution)/shard_map/schur_z/ppermute | solution.py:288
  9.6 4.3 %shard_map.121 = (f32[8,16,400]{2,1,0:T(8,128)}, bf16[16,80,128]{2,1,0:T(8,128)(2,1)}) custom-call(s32[16]{0:T(128)} %time_ref.3, s32[16]{0:T(128)} %node_ref.3, f32[8,16,400]{2,1,0:T(8,128)} %volt_hbm.3, f32[8,16,400]{2,1,0:T(8,128)} %curr_hbm.3, s32[8,16,400]{2,1,0:T(8,128)} %breaker_hbm.5, f32[8,400]{1,0:T(8,128)} %gain_hbm.5, f32[8,64]{1,0:T(8,128)} %tie_hbm.3, ...), custom_call_target="tpu_custom_call" | custom-call | flops 40960000 | bytes 4194304 | tf_op jit(solution)/shard_map/pallas_call | solution.py:289
  13.9 0.0 collective-permute-done
  13.9 0.0 copy-done.3
  14.0 0.1 broadcast_in_dim.2
  14.0 17.7 %all_to_all.25.refs_0_ = bf16[4,2,256,128]{3,2,1,0:T(8,128)(2,1)S(1)} all-to-all(bf16[4,2,256,128]{3,2,1,0:T(8,128)(2,1)S(1)} %broadcast_in_dim.2), channel_id=1, replica_groups={{0,1,2,3},{4,5,6,7},{8,9,10,11},{12,13,14,15},{16,17,18,19},{20,21,22,2..., dimensions={0} | all-to-all | bytes 1048576 | tf_op jit(solution)/shard_map/schur_z/all_to_all | solution.py:293
  31.7 4.6 %collective-permute-start.2 = (bf16[4,2,256,128]{3,2,1,0:T(8,128)(2,1)S(1)}, bf16[4,2,256,128]{3,2,1,0:T(8,128)(2,1)S(1)}, u32[]{:S(2)}, u32[]{:S(2)}) collective-permute-start(bf16[4,2,256,128]{3,2,1,0:T(8,128)(2,1)S(1)} %all_to_all.25.refs_0_), channel_id=1, source_target_pairs={{0,24},{1,25},{2,26},{3,27},{4,28},{5,29},{6,30},{7,31},{8,0},{9,1... | collective-permute-start | bytes 1572872 | tf_op jit(solution)/shard_map/schur_y/ppermute | solution.py:285
  36.4 1.9 %collective-permute-start.1 = (bf16[4,2,256,128]{3,2,1,0:T(8,128)(2,1)S(1)}, bf16[4,2,256,128]{3,2,1,0:T(8,128)(2,1)S(1)}, u32[]{:S(2)}, u32[]{:S(2)}) collective-permute-start(bf16[4,2,256,128]{3,2,1,0:T(8,128)(2,1)S(1)} %all_to_all.25.refs_0_), channel_id=1, source_target_pairs={{0,8},{1,9},{2,10},{3,11},{4,12},{5,13},{6,14},{7,15},{8,16},{9,17... | collective-permute-start | bytes 1572872 | tf_op jit(solution)/shard_map/schur_y/ppermute | solution.py:285
  38.3 16.9 %all-to-all-start.1 = ((bf16[16,80,128]{2,1,0:T(8,128)(2,1)}), bf16[16,80,128]{2,1,0:T(8,128)(2,1)}, u32[]{:S(2)}, u32[]{:S(2)}) async-start(bf16[16,80,128]{2,1,0:T(8,128)(2,1)} %get-tuple-element.24), calls=%async_computation.1 | async-start | bytes 655360 | tf_op jit(solution)/shard_map/all_to_all | solution.py:298
  55.2 0.0 collective-permute-done.2.refs_2_
  55.2 0.0 copy-start.1
  55.2 0.8 slice.9
  56.0 4.8 %collective-permute-start.4 = (bf16[2,2,256,128]{3,2,1,0:T(8,128)(2,1)}, bf16[2,2,256,128]{3,2,1,0:T(8,128)(2,1)}, u32[]{:S(2)}, u32[]{:S(2)}) collective-permute-start(bf16[2,2,256,128]{3,2,1,0:T(8,128)(2,1)} %slice.9), channel_id=1, source_target_pairs={{0,24},{1,25},{2,26},{3,27},{4,28},{5,29},{6,30},{7,31},{8,0},{9,1... | collective-permute-start | bytes 786440 | tf_op jit(solution)/shard_map/schur_y/ppermute | solution.py:285
  60.9 0.0 collective-permute-done.1.refs_1_
  60.9 0.0 copy-start.2
  60.9 0.8 slice.8
  61.7 1.9 %collective-permute-start.3 = (bf16[2,2,256,128]{3,2,1,0:T(8,128)(2,1)}, bf16[2,2,256,128]{3,2,1,0:T(8,128)(2,1)}, u32[]{:S(2)}, u32[]{:S(2)}) collective-permute-start(bf16[2,2,256,128]{3,2,1,0:T(8,128)(2,1)} %slice.8), channel_id=1, source_target_pairs={{0,8},{1,9},{2,10},{3,11},{4,12},{5,13},{6,14},{7,15},{8,16},{9,17... | collective-permute-start | bytes 786440 | tf_op jit(solution)/shard_map/schur_y/ppermute | solution.py:285
  63.6 1.4 shard_map.123.ports_hbm
  65.0 0.0 copy-done
  65.0 0.0 copy-done.1
  65.0 17.2 %all-to-all-done.1.recv_ref.map_ref = bf16[16,80,128]{2,1,0:T(8,128)(2,1)} async-done(((bf16[16,80,128]{2,1,0:T(8,128)(2,1)}), bf16[16,80,128]{2,1,0:T(8,128)(2,1)}, u32[]{:S(2)}, u32[]{:S(2)}) %all-to-all-start.1) | async-done | bytes 327712 | tf_op jit(solution)/shard_map/all_to_all | solution.py:298
  82.2 3.1 %shard_map.122.rhs_ref = bf16[16,16,256]{2,1,0:T(8,128)(2,1)} custom-call(bf16[16,80,128]{2,1,0:T(8,128)(2,1)} %all-to-all-done.1.recv_ref.map_ref), custom_call_target="tpu_custom_call" | custom-call | flops 1073741824 | bytes 1048576 | tf_op jit(solution)/shard_map/pallas_call | solution.py:300
  85.3 0.0 collective-permute-done.4.refs_4_
  85.3 0.0 collective-permute-done.3.refs_3_
  85.3 4.0 %shard_map.124 = (f32[16,256]{1,0:T(8,128)}, f32[16,16,256]{2,1,0:T(8,128)}) custom-call(bf16[16,16,256]{2,1,0:T(8,128)(2,1)} %shard_map.122.rhs_ref, bf16[4,2,256,128]{3,2,1,0:T(8,128)(2,1)} %copy-done, bf16[4,2,256,128]{3,2,1,0:T(8,128)(2,1)} %copy-done.2, bf16[4,2,256,128]{3,2,1,0:T(8,128)(2,1)} %copy-done.1, ...), custom_call_target="tpu_custom_call" | custom-call | flops 33554432 | bytes 3145728 | tf_op jit(solution)/shard_map/pallas_call | solution.py:302
  89.4 29.2 %all_to_all.26.recv_ref = f32[16,16,256]{2,1,0:T(8,128)} all-to-all(f32[16,16,256]{2,1,0:T(8,128)} %get-tuple-element.28), channel_id=1, replica_groups=mesh['row'=16,'col'=32] {'row'}, dimensions={0} | all-to-all | bytes 524288 | tf_op jit(solution)/shard_map/all_to_all | solution.py:303
  118.5 4.8 %shard_map.125 = (f32[8,16,400]{2,1,0:T(8,128)}, f32[8,16,400]{2,1,0:T(8,128)}, f32[8,16,400]{2,1,0:T(8,128)}, bf16[16,64,128]{2,1,0:T(8,128)(2,1)}) custom-call(s32[16]{0:T(128)} %time_ref.3, s32[16]{0:T(128)} %node_ref.3, f32[16,16,256]{2,1,0:T(8,128)} %all_to_all.26.recv_ref, f32[8,16,400]{2,1,0:T(8,128)} %get-tuple-element.29.open_prev_ref, ...), custom_call_target="tpu_custom_call" | custom-call | flops 40960000 | bytes 4194304 | tf_op jit(solution)/shard_map/pallas_call | solution.py:303
  123.3 23.0 %all_to_all.27.recv_ref = bf16[16,64,128]{2,1,0:T(8,128)(2,1)} all-to-all(bf16[16,64,128]{2,1,0:T(8,128)(2,1)} %get-tuple-element.31), channel_id=1, replica_groups=mesh['row'=16,'col'=32] {'row'}, dimensions={0} | all-to-all | bytes 524288 | tf_op jit(solution)/shard_map/all_to_all | solution.py:304
  146.3 4.9 %shard_map.126 = (f32[16,256]{1,0:T(8,128)}, f32[16,16,256]{2,1,0:T(8,128)}) custom-call(bf16[16,64,128]{2,1,0:T(8,128)(2,1)} %all_to_all.27.recv_ref, bf16[16,80,128]{2,1,0:T(8,128)(2,1)} %all-to-all-done.1.recv_ref.map_ref, bf16[4,2,256,128]{3,2,1,0:T(8,128)(2,1)} %copy-done, bf16[4,2,256,128]{3,2,1,0:T(8,128)(2,1)} %copy-done.2, ...), custom_call_target="tpu_custom_call" | custom-call | flops 1073741824 | bytes 3145728 | tf_op jit(solution)/shard_map/pallas_call | solution.py:304
  151.2 23.9 %all_to_all.28.recv_ref = f32[16,16,256]{2,1,0:T(8,128)} all-to-all(f32[16,16,256]{2,1,0:T(8,128)} %get-tuple-element.32), channel_id=1, replica_groups=mesh['row'=16,'col'=32] {'row'}, dimensions={0} | all-to-all | bytes 524288 | tf_op jit(solution)/shard_map/all_to_all | solution.py:305
  175.1 4.2 %shard_map.127 = (f32[8,16,400]{2,1,0:T(8,128)}, f32[8,16,400]{2,1,0:T(8,128)}) custom-call(f32[16,16,256]{2,1,0:T(8,128)} %all_to_all.28.recv_ref, f32[8,16,400]{2,1,0:T(8,128)} %get-tuple-element.33.open_prev_ref, f32[8,16,400]{2,1,0:T(8,128)} %get-tuple-element.34.volt_ref, f32[8,16,400]{2,1,0:T(8,128)} %get-tuple-element.35.curr_ref, ...), custom_call_target="tpu_custom_call" | custom-call | flops 5120000 | bytes 2097152 | tf_op jit(solution)/shard_map/pallas_call | solution.py:305
  (3 shorter events, 0.0 us)
Async XLA Ops:
  0.6 13.3 %copy-start.3 = (bf16[256,128]{1,0:T(8,128)(2,1)S(1)}, bf16[256,128]{1,0:T(8,128)(2,1)}, u32[]{:S(2)}) copy-start(bf16[256,128]{1,0:T(8,128)(2,1)} %param.13) | copy-start | bytes 196612
  0.6 13.3 %collective-permute-start = (bf16[256,128]{1,0:T(8,128)(2,1)}, bf16[256,128]{1,0:T(8,128)(2,1)S(1)}, u32[]{:S(2)}, u32[]{:S(2)}) collective-permute-start(bf16[256,128]{1,0:T(8,128)(2,1)} %param.13), channel_id=1, source_target_pairs={{0,4},{1,5},{2,6},{3,7},{4,0},{5,1},{6,2},{7,3},{8,12},{9,13},{10,... | collective-permute-start | bytes 196616 | tf_op jit(solution)/shard_map/schur_z/ppermute | solution.py:288
  31.7 33.3 %copy-start = (bf16[4,2,256,128]{3,2,1,0:T(8,128)(2,1)}, bf16[4,2,256,128]{3,2,1,0:T(8,128)(2,1)S(1)}, u32[]{:S(2)}) copy-start(bf16[4,2,256,128]{3,2,1,0:T(8,128)(2,1)S(1)} %all_to_all.25.refs_0_) | copy-start | bytes 1572868
  31.7 23.5 %collective-permute-start.2 = (bf16[4,2,256,128]{3,2,1,0:T(8,128)(2,1)S(1)}, bf16[4,2,256,128]{3,2,1,0:T(8,128)(2,1)S(1)}, u32[]{:S(2)}, u32[]{:S(2)}) collective-permute-start(bf16[4,2,256,128]{3,2,1,0:T(8,128)(2,1)S(1)} %all_to_all.25.refs_0_), channel_id=1, source_target_pairs={{0,24},{1,25},{2,26},{3,27},{4,28},{5,29},{6,30},{7,31},{8,0},{9,1... | collective-permute-start | bytes 1572872 | tf_op jit(solution)/shard_map/schur_y/ppermute | solution.py:285
  36.4 24.5 %collective-permute-start.1 = (bf16[4,2,256,128]{3,2,1,0:T(8,128)(2,1)S(1)}, bf16[4,2,256,128]{3,2,1,0:T(8,128)(2,1)S(1)}, u32[]{:S(2)}, u32[]{:S(2)}) collective-permute-start(bf16[4,2,256,128]{3,2,1,0:T(8,128)(2,1)S(1)} %all_to_all.25.refs_0_), channel_id=1, source_target_pairs={{0,8},{1,9},{2,10},{3,11},{4,12},{5,13},{6,14},{7,15},{8,16},{9,17... | collective-permute-start | bytes 1572872 | tf_op jit(solution)/shard_map/schur_y/ppermute | solution.py:285
  38.3 44.0 %all-to-all-start.1 = ((bf16[16,80,128]{2,1,0:T(8,128)(2,1)}), bf16[16,80,128]{2,1,0:T(8,128)(2,1)}, u32[]{:S(2)}, u32[]{:S(2)}) async-start(bf16[16,80,128]{2,1,0:T(8,128)(2,1)} %get-tuple-element.24), calls=%async_computation.1 | async-start | bytes 655360 | tf_op jit(solution)/shard_map/all_to_all | solution.py:298
  55.2 9.8 %copy-start.1 = (bf16[4,2,256,128]{3,2,1,0:T(8,128)(2,1)}, bf16[4,2,256,128]{3,2,1,0:T(8,128)(2,1)S(1)}, u32[]{:S(2)}) copy-start(bf16[4,2,256,128]{3,2,1,0:T(8,128)(2,1)S(1)} %collective-permute-done.2.refs_2_) | copy-start | bytes 1572868
  56.0 29.3 %collective-permute-start.4 = (bf16[2,2,256,128]{3,2,1,0:T(8,128)(2,1)}, bf16[2,2,256,128]{3,2,1,0:T(8,128)(2,1)}, u32[]{:S(2)}, u32[]{:S(2)}) collective-permute-start(bf16[2,2,256,128]{3,2,1,0:T(8,128)(2,1)} %slice.9), channel_id=1, source_target_pairs={{0,24},{1,25},{2,26},{3,27},{4,28},{5,29},{6,30},{7,31},{8,0},{9,1... | collective-permute-start | bytes 786440 | tf_op jit(solution)/shard_map/schur_y/ppermute | solution.py:285
  60.9 4.1 %copy-start.2 = (bf16[4,2,256,128]{3,2,1,0:T(8,128)(2,1)}, bf16[4,2,256,128]{3,2,1,0:T(8,128)(2,1)S(1)}, u32[]{:S(2)}) copy-start(bf16[4,2,256,128]{3,2,1,0:T(8,128)(2,1)S(1)} %collective-permute-done.1.refs_1_) | copy-start | bytes 1572868
  61.7 23.6 %collective-permute-start.3 = (bf16[2,2,256,128]{3,2,1,0:T(8,128)(2,1)}, bf16[2,2,256,128]{3,2,1,0:T(8,128)(2,1)}, u32[]{:S(2)}, u32[]{:S(2)}) collective-permute-start(bf16[2,2,256,128]{3,2,1,0:T(8,128)(2,1)} %slice.8), channel_id=1, source_target_pairs={{0,8},{1,9},{2,10},{3,11},{4,12},{5,13},{6,14},{7,15},{8,16},{9,17... | collective-permute-start | bytes 786440 | tf_op jit(solution)/shard_map/schur_y/ppermute | solution.py:285

commit v5 on v0

v5 whole, which is shorter than its diff:
```python
import functools

import jax
import jax.numpy as jnp
from jax import lax
from jax.experimental import pallas as pl
from jax.experimental.pallas import tpu as pltpu
from jax.sharding import PartitionSpec as P

ROWS = 16
COLS = 32
SUBS = 8
SCEN = 16
NODES = 400
PORTS = 64
OWN = SUBS * PORTS
BLOCK = 256
LANES = 128
TILES = OWN // LANES
VALUE_ROWS = TILES * SCEN
MAP_ROWS = 2 * TILES
VMEM_BYTES = 60 << 20
BF16, F32 = jnp.bfloat16, jnp.float32

NN = (((1,), (0,)), ((), ()))
NT = (((1,), (1,)), ((), ()))


def dot(a, b, dims=NN):
    return lax.dot_general(a, b, dims, preferred_element_type=F32)


def halves(x):
    coarse = x.astype(BF16)
    return coarse, (x - coarse.astype(F32)).astype(BF16)


def fetch(sources, targets, sems):
    copies = [pltpu.make_async_copy(a, b, sems.at[n]) for n, (a, b) in enumerate(zip(sources, targets))]
    for copy in copies:
        copy.start()
    return copies


def wait_for(copies):
    for copy in copies:
        copy.wait()


def each(ref, count):
    return [ref.at[k] for k in range(count)]


def flat_row(ref):
    return jnp.concatenate([ref[k : k + 1, :] for k in range(SUBS)], axis=1)


def tiles_of(row):
    return [row[:, t * LANES : (t + 1) * LANES] for t in range(TILES)]


def column(ref):
    place = lax.broadcasted_iota(jnp.int32, (SCEN, 1), 0)
    out = jnp.zeros((SCEN, 1), jnp.int32)
    for s in range(SCEN):
        out = jnp.where(place == s, ref[s], out)
    return out


def open_circuit(step, volts, currs, breaker_ref, gain_ref, inv_copies, inv_ref, time_ref, node_ref, tie_ref, open_ref, send_ref):
    fault_node = jnp.where(step >= column(time_ref), column(node_ref), -1)
    first = lax.axis_index("row") * SUBS
    lane = lax.broadcasted_iota(jnp.int32, (SCEN, NODES), 1)
    parts = []
    for k in range(SUBS):
        volt = volts[k]
        hist = breaker_ref[k].astype(F32) * (currs[k] + gain_ref[k : k + 1, :] * volt)
        hit = lane + (first + k) * NODES == fault_node
        inject = (-hist - jnp.where(hit, 2.0 * volt, 0.0)).astype(BF16)
        if inv_copies:
            inv_copies[k].wait()
        open_k = dot(inject, inv_ref[k])
        open_ref[k] = open_k
        parts.append(tie_ref[k : k + 1, :] * open_k[:, :PORTS])
    values = jnp.concatenate(parts, axis=1).astype(send_ref.dtype)
    for t, tile in enumerate(tiles_of(values)):
        for r in range(ROWS):
            send_ref[r, t * SCEN : (t + 1) * SCEN, :] = tile


def first_kernel(time_ref, node_ref, volt_hbm, curr_hbm, breaker_hbm, gain_hbm, tie_hbm, map_hbm, inv_hbm, open_ref, send_ref, map_ref, gain_ref, tie_ref, volt_ref, curr_ref, breaker_ref, inv_ref, sems):
    copies = fetch(
        [map_hbm, gain_hbm, tie_hbm, volt_hbm, curr_hbm, breaker_hbm] + each(inv_hbm, SUBS),
        [map_ref, gain_ref, tie_ref, volt_ref, curr_ref, breaker_ref] + each(inv_ref, SUBS),
        sems,
    )
    copies[0].wait()
    mapped = flat_row(map_ref)
    rows = tiles_of((mapped // BLOCK).astype(F32)) + tiles_of((mapped % BLOCK).astype(F32))
    tail = jnp.concatenate(rows, axis=0)
    for r in range(ROWS):
        send_ref[r, VALUE_ROWS:, :] = tail
    wait_for(copies[1:6])
    open_circuit(0, volt_ref, curr_ref, breaker_ref, gain_ref, copies[6:], inv_ref, time_ref, node_ref, tie_ref, open_ref, send_ref)


def right_hand_side(recv_ref, map_ref, ready):
    low = lax.broadcasted_iota(jnp.int32, (BLOCK, OWN), 0)
    rhs = jnp.zeros((ROWS * SCEN, BLOCK), F32)
    for r in range(ROWS):
        wait_for(ready(r))
        tail = map_ref[r].astype(jnp.int32)
        hi = jnp.concatenate([tail[t : t + 1] for t in range(TILES)], axis=1)
        lo = jnp.concatenate([tail[TILES + t : TILES + t + 1] for t in range(TILES)], axis=1)
        right = jnp.where(low == lo, 1.0, 0.0).astype(BF16)
        values = jnp.concatenate([recv_ref[r, t * SCEN : (t + 1) * SCEN, :] for t in range(TILES)], axis=1)
        for part in halves(values) if values.dtype == F32 else (values,):
            part = part.astype(F32)
            left = jnp.concatenate([jnp.where(hi == h, part, 0.0) for h in range(ROWS)], axis=0).astype(BF16)
            rhs += dot(left, right, NT)
    return rhs.astype(BF16).reshape(ROWS, SCEN, BLOCK)


def join_kernel(own_hbm, across_hbm, *refs):
    quads, (out_hbm, sems) = refs[:3], refs[3:]
    wait_for(fetch([own_hbm, across_hbm, *quads], [out_hbm.at[0, 0], out_hbm.at[0, 1]] + [out_hbm.at[x] for x in (1, 2, 3)], sems))


def schur_copies(parts, schur_ref, sems):
    own, back, ahead, far_low, far_high = parts
    low, high = schur_ref.at[2, pl.ds(0, 2)], schur_ref.at[2, pl.ds(2, 2)]
    return fetch([own, back, ahead, far_low, far_high], [schur_ref.at[0], schur_ref.at[1], schur_ref.at[3], low, high], sems)


def schur_product(rhs_ref, schur_ref, copies):
    col = lax.axis_index("col")
    own_y, own_z = col // 8, col % 8
    total = jnp.zeros((SCEN, BLOCK), F32)
    for n, waits in ((0, copies[:1]), (1, copies[1:2]), (3, copies[2:3]), (2, copies[3:])):
        wait_for(waits)
        for x in (0, 2):
            for o in range(2):
                place = 8 * ((own_y + 4 - n) % 4) + jnp.bitwise_xor(own_z, x + 4 * o)
                left = jnp.concatenate([rhs_ref[place], rhs_ref[jnp.bitwise_xor(place, 1)]], axis=1)
                right = jnp.concatenate([schur_ref[n, x, o], schur_ref[n, x + 1, o]], axis=1)
                total += dot(left, right, NT)
    return total


def keep(rhs, rhs_ref):
    for h in range(ROWS):
        for side in range(2):
            rhs_ref[2 * h + side] = rhs[h, :, side * LANES : (side + 1) * LANES]


def rhs_kernel(recv_hbm, rhs_ref, map_out, recv_ref, map_ref, sems):
    copies = fetch(
        [recv_hbm.at[r, pl.ds(0, VALUE_ROWS)] for r in range(ROWS)] + [recv_hbm.at[r, pl.ds(VALUE_ROWS, MAP_ROWS)] for r in range(ROWS)],
        each(recv_ref, ROWS) + each(map_ref, ROWS),
        sems,
    )
    keep(right_hand_side(recv_ref, map_ref, lambda r: (copies[r], copies[ROWS + r])), rhs_ref)
    map_out[...] = map_ref[...]


def product_kernel(rhs_hbm, *refs):
    parts, (send_ref, schur_ref, rhs_ref, sems, rhs_sem) = refs[:5], refs[5:]
    copies = schur_copies(parts, schur_ref, sems)
    wait_for(fetch([rhs_hbm], [rhs_ref], rhs_sem))
    total = schur_product(rhs_ref, schur_ref, copies)
    for r in range(ROWS):
        send_ref[r] = total


def interface_kernel(recv_hbm, map_hbm, *refs):
    parts, (iface_ref, send_ref, schur_ref, rhs_ref, recv_ref, map_ref, sems, recv_sems) = refs[:5], refs[5:]
    arrived = fetch([map_hbm] + each(recv_hbm, ROWS), [map_ref] + each(recv_ref, ROWS), recv_sems)
    copies = schur_copies(parts, schur_ref, sems)
    arrived[0].wait()
    keep(right_hand_side(recv_ref, map_ref, lambda r: (arrived[1 + r],)), rhs_ref)
    total = schur_product(rhs_ref, schur_ref, copies)
    iface_ref[...] = total
    half = total.astype(BF16)
    for r in range(ROWS):
        send_ref[r] = half


def driven(recv_ref, map_ref, tie_ref):
    mapped = flat_row(map_ref)
    hi = mapped // BLOCK
    low = lax.broadcasted_iota(jnp.int32, (BLOCK, OWN), 0)
    right = jnp.where(low == mapped % BLOCK, 1.0, 0.0).astype(BF16)
    volts = recv_ref[...].reshape(ROWS * SCEN, BLOCK)
    found = sum(dot(part, right) for part in (halves(volts) if volts.dtype == F32 else (volts,)))
    picked = jnp.zeros((SCEN, OWN), F32)
    for r in range(ROWS):
        picked += jnp.where(hi == r, found[r * SCEN : (r + 1) * SCEN, :], 0.0)
    return (flat_row(tie_ref) * picked).astype(BF16)


def update(k, drive, open_ref, inv, volt, curr, breaker_ref, gain_ref):
    volt_next = open_ref[k] + dot(drive[:, k * PORTS : (k + 1) * PORTS], inv)
    closed = breaker_ref[k].astype(F32)
    return volt_next, closed * (curr + gain_ref[k : k + 1, :] * (volt_next + volt))


def middle_kernel(time_ref, node_ref, recv_hbm, prev_hbm, volt_hbm, curr_hbm, breaker_hbm, gain_hbm, tie_hbm, map_hbm, inv_hbm, volt_out, curr_out, open_ref, send_ref, recv_ref, prev_ref, map_ref, gain_ref, tie_ref, volt_ref, curr_ref, breaker_ref, inv_ref, sems):
    copies = fetch(
        [map_hbm, tie_hbm, recv_hbm, gain_hbm, prev_hbm, volt_hbm, curr_hbm, breaker_hbm] + each(inv_hbm, SUBS),
        [map_ref, tie_ref, recv_ref, gain_ref, prev_ref, volt_ref, curr_ref, breaker_ref] + each(inv_ref, SUBS),
        sems,
    )
    wait_for(copies[:3])
    drive = driven(recv_ref, map_ref, tie_ref)
    wait_for(copies[3:8])
    for k in range(SUBS):
        copies[8 + k].wait()
        volt_out[k], curr_out[k] = update(k, drive, prev_ref, inv_ref[k, :PORTS, :], volt_ref[k], curr_ref[k], breaker_ref, gain_ref)
    open_circuit(1, volt_out, curr_out, breaker_ref, gain_ref, None, inv_ref, time_ref, node_ref, tie_ref, open_ref, send_ref)


def last_kernel(recv_hbm, prev_hbm, volt_hbm, curr_hbm, breaker_hbm, gain_hbm, tie_hbm, map_hbm, inv_hbm, volt_out, curr_out, recv_ref, prev_ref, map_ref, gain_ref, tie_ref, volt_ref, curr_ref, breaker_ref, inv_ref, sems):
    copies = fetch(
        [map_hbm, tie_hbm, recv_hbm, gain_hbm, prev_hbm, volt_hbm, curr_hbm, breaker_hbm] + [inv_hbm.at[k, pl.ds(0, PORTS)] for k in range(SUBS)],
        [map_ref, tie_ref, recv_ref, gain_ref, prev_ref, volt_ref, curr_ref, breaker_ref] + each(inv_ref, SUBS),
        sems,
    )
    wait_for(copies[:3])
    drive = driven(recv_ref, map_ref, tie_ref)
    wait_for(copies[3:])
    for k in range(SUBS):
        volt_out[k], curr_out[k] = update(k, drive, prev_ref, inv_ref[k], volt_ref[k], curr_ref[k], breaker_ref, gain_ref)


SMEM = pl.BlockSpec(memory_space=pltpu.SMEM)
VMEM = pl.BlockSpec(memory_space=pltpu.VMEM)
HBM = pl.BlockSpec(memory_space=pltpu.HBM)

STATE = ((SUBS, SCEN, NODES), F32)
SCHUR = ((4, 4, 2, BLOCK, LANES), BF16)
RHS = ((COLS, SCEN, LANES), BF16)
MAPS = ((ROWS, MAP_ROWS, LANES), F32)
FACE = (ROWS, SCEN, BLOCK)
GIGA = 1_000_000_000


def held(*shapes):
    return [pltpu.VMEM(*shape) for shape in shapes]


def copies_of(count):
    return [pltpu.SemaphoreType.DMA((count,))]


SMALL = held(((SUBS, PORTS), jnp.int32), ((SUBS, NODES), F32), ((SUBS, PORTS), F32))
BREAKER = held(((SUBS, SCEN, NODES), jnp.int32))


def call(body, ins, outs, scratch, flops, moved, out_specs=None):
    return pl.pallas_call(
        body,
        out_shape=[jax.ShapeDtypeStruct(shape, kind) for shape, kind in outs],
        in_specs=ins,
        out_specs=out_specs or [VMEM] * len(outs),
        scratch_shapes=scratch,
        compiler_params=pltpu.CompilerParams(vmem_limit_bytes=VMEM_BYTES),
        cost_estimate=pl.CostEstimate(flops=flops, bytes_accessed=moved, transcendentals=0),
    )


first = call(
    first_kernel,
    [SMEM] * 2 + [HBM] * 7,
    [STATE, ((ROWS, VALUE_ROWS + MAP_ROWS, LANES), F32)],
    SMALL + held(STATE, STATE) + BREAKER + held(((SUBS, NODES, NODES), BF16)) + copies_of(6 + SUBS),
    GIGA,
    4 << 20,
)
join = call(join_kernel, [HBM] * 5, [((4, 2, BLOCK, LANES), BF16)], copies_of(5), 100_000 * GIGA, 1 << 20, [HBM])
summed = call(
    rhs_kernel,
    [HBM],
    [RHS, MAPS],
    held(((ROWS, VALUE_ROWS, LANES), F32), MAPS) + copies_of(2 * ROWS),
    GIGA,
    1 << 20,
)
product = call(product_kernel, [HBM] * 6, [(FACE, F32)], held(SCHUR, RHS) + copies_of(5) + copies_of(1), GIGA, 3 << 20)
interface = call(
    interface_kernel,
    [HBM] * 7,
    [(FACE[1:], F32), (FACE, BF16)],
    held(SCHUR, RHS, ((ROWS, VALUE_ROWS, LANES), BF16), MAPS) + copies_of(5) + copies_of(1 + ROWS),
    GIGA,
    3 << 20,
)
middle = call(
    middle_kernel,
    [SMEM] * 2 + [HBM] * 9,
    [STATE, STATE, STATE, ((ROWS, VALUE_ROWS, LANES), BF16)],
    held((FACE, F32), STATE) + SMALL + held(STATE, STATE) + BREAKER + held(((SUBS, NODES, NODES), BF16)) + copies_of(8 + SUBS),
    GIGA,
    4 << 20,
)
last = call(
    last_kernel,
    [HBM] * 9,
    [STATE, STATE],
    held((FACE, BF16), STATE) + SMALL + held(STATE, STATE) + BREAKER + held(((SUBS, PORTS, NODES), BF16)) + copies_of(8 + SUBS),
    GIGA,
    2 << 20,
)


def along_z(block, flip):
    return lax.ppermute(block, "col", [(c, c ^ flip) for c in range(COLS)])


def along_y(block, steps):
    return lax.ppermute(block, "col", [(c, (c + 8 * steps) % COLS) for c in range(COLS)])


def local(volt, curr, local_inverse, schur_inverse, ind_gain, tie, port_map, breaker, fault_time, fault_node):
    exchange = functools.partial(lax.all_to_all, axis_name="row", split_axis=0, concat_axis=0)
    fixed = breaker, ind_gain, tie, port_map, local_inverse
    with jax.named_scope("schur_z"):
        across = along_z(schur_inverse, 4)
    opened, send = first(fault_time, fault_node, volt, curr, *fixed)
    across, send = lax.optimization_barrier((across, send))
    with jax.named_scope("schur_z"):
        pair = jnp.stack([schur_inverse, across])
        (own,) = join(schur_inverse, across, *(along_z(pair, x) for x in (1, 2, 3)))
    with jax.named_scope("schur_y"):
        back, ahead = along_y(own, 1), along_y(own, -1)
        schur_rows = own, back, ahead, along_y(back[:2], 1), along_y(ahead[2:], -1)
    rhs, maps = summed(exchange(send))
    (send,) = product(rhs, *schur_rows)
    volt, curr, opened, send = middle(fault_time, fault_node, exchange(send), opened, volt, curr, *fixed)
    iface_block, send = interface(exchange(send), maps, *schur_rows)
    volt, curr = last(exchange(send), opened, volt, curr, *fixed)
    return volt, curr, iface_block


def solution(mesh):
    placed = (
        P("row", "col", None),
        P("row", "col", None),
        P("row", None, None),
        P("row", "col"),
        P("row", None),
        P("row", None),
        P("row", None),
        P("row", "col", None),
        P("col"),
        P("col"),
    )
    return jax.shard_map(
        local,
        mesh=mesh,
        in_specs=placed,
        out_specs=(P("row", "col", None), P("row", "col", None), P("col", "row")),
        check_vma=False,
    )
```

time: 529 us -> 197 us (0.37)
  the two profiles are of different devices: /device:TPU:1 before, /device:TPU:33 now
where the time goes in v5:
time: 197 us; the launch traced here: 196 us
  blocking collectives  86.6 us (44%)
  starting transfers between devices  50 us (25%)
  Pallas kernels  46.3 us (24%)
  waiting for transfers between devices  9.75 us (5%)
  local copies, waits for them, and re-layouts  2.06 us (1%)
    all_to_all x1, blocking collectives, local(): exchange(send)  40.7 us
    all_to_all x1, blocking collectives, local(): iface_block, send = interface(exchange(send), maps, *schur_rows)  25.2 us
    all_to_all x1, blocking collectives, local(): volt, curr = last(exchange(send), opened, volt, curr, *fixed)  20.7 us
    ppermute x4, starting transfers between devices, along_z(): return lax.ppermute(block, 'col', [(c, c ^ flip) for c in range(COLS)])  19.2 us
    pallas_call x1, Pallas kernels, local(): own, = join(schur_inverse, across, *(along_z(pair, x) for x in (1, 2, 3)))  17 us
    all_to_all x1, starting transfers between devices, local(): rhs, maps = summed(exchange(send))  17 us
    ppermute x4, starting transfers between devices, along_y(): lax.ppermute(block, 'col', [(c, (c + 8 * steps) % COLS) for c in range(CO...  13.8 us
    ppermute x4, waiting for transfers between devices, along_y(): lax.ppermute(block, 'col', [(c, (c + 8 * steps) % COLS) for c in range(CO...  9.73 us
  transfers between devices with their start and end apart: 9, of which 2 were waited for; matrix products, arithmetic and copies ran while one was open for 0% of the time, Pallas kernels for 15%

profile of v5, /device:TPU:33, one launch (start us, length us, event | category | flops | bytes accessed | tf_op | source)
XLA Modules:
  0.0 195.6 jit_solution(8102412561920952481)
XLA Ops:
  0.6 0.0 copy-start.2
  0.6 9.0 %collective-permute-start = (bf16[256,128]{1,0:T(8,128)(2,1)}, bf16[256,128]{1,0:T(8,128)(2,1)S(1)}, u32[]{:S(2)}, u32[]{:S(2)}) collective-permute-start(bf16[256,128]{1,0:T(8,128)(2,1)} %own_hbm.1), channel_id=1, source_target_pairs={{0,4},{1,5},{2,6},{3,7},{4,0},{5,1},{6,2},{7,3},{8,12},{9,13},{10,... | collective-permute-start | bytes 196616 | tf_op jit(solution)/shard_map/schur_z/ppermute | solution.py:316
  9.6 4.4 %shard_map.121 = (f32[8,16,400]{2,1,0:T(8,128)}, f32[16,72,128]{2,1,0:T(8,128)}) custom-call(s32[16]{0:T(128)} %time_ref.3, s32[16]{0:T(128)} %node_ref.3, f32[8,16,400]{2,1,0:T(8,128)} %volt_hbm.3, f32[8,16,400]{2,1,0:T(8,128)} %curr_hbm.3, s32[8,16,400]{2,1,0:T(8,128)} %breaker_hbm.5, f32[8,400]{1,0:T(8,128)} %gain_hbm.5, f32[8,64]{1,0:T(8,128)} %tie_hbm.5, ...), custom_call_target="tpu_custom_call" | custom-call | flops 1000000000 | bytes 4194304 | tf_op jit(solution)/shard_map/pallas_call | solution.py:328
  14.0 0.0 collective-permute-done.across_hbm
  14.1 3.5 %collective-permute-start.3 = (bf16[2,256,128]{2,1,0:T(8,128)(2,1)S(1)}, bf16[2,256,128]{2,1,0:T(8,128)(2,1)S(1)}, u32[]{:S(2)}, u32[]{:S(2)}) collective-permute-start(bf16[2,256,128]{2,1,0:T(8,128)(2,1)S(1)} %pad_maximum_fusion), channel_id=1, source_target_pairs={{0,3},{1,2},{2,1},{3,0},{4,7},{5,6},{6,5},{7,4},{8,11},{9,10},{10,... | collective-permute-start | bytes 393224 | tf_op jit(solution)/shard_map/schur_z/ppermute | solution.py:316
  17.6 3.6 %collective-permute-start.2 = (bf16[2,256,128]{2,1,0:T(8,128)(2,1)S(1)}, bf16[2,256,128]{2,1,0:T(8,128)(2,1)S(1)}, u32[]{:S(2)}, u32[]{:S(2)}) collective-permute-start(bf16[2,256,128]{2,1,0:T(8,128)(2,1)S(1)} %pad_maximum_fusion), channel_id=1, source_target_pairs={{0,2},{1,3},{2,0},{3,1},{4,6},{5,7},{6,4},{7,5},{8,10},{9,11},{10,... | collective-permute-start | bytes 393224 | tf_op jit(solution)/shard_map/schur_z/ppermute | solution.py:316
  21.3 3.1 %collective-permute-start.1 = (bf16[2,256,128]{2,1,0:T(8,128)(2,1)S(1)}, bf16[2,256,128]{2,1,0:T(8,128)(2,1)S(1)}, u32[]{:S(2)}, u32[]{:S(2)}) collective-permute-start(bf16[2,256,128]{2,1,0:T(8,128)(2,1)S(1)} %pad_maximum_fusion), channel_id=1, source_target_pairs={{0,1},{1,0},{2,3},{3,2},{4,5},{5,4},{6,7},{7,6},{8,9},{9,8},{10,11... | collective-permute-start | bytes 393224 | tf_op jit(solution)/shard_map/schur_z/ppermute | solution.py:316
  24.4 17.0 %all-to-all-start = ((f32[16,72,128]{2,1,0:T(8,128)}), f32[16,72,128]{2,1,0:T(8,128)}, u32[]{:S(2)}, u32[]{:S(2)}) async-start(f32[16,72,128]{2,1,0:T(8,128)} %get-tuple-element.18), calls=%async_computation | async-start | bytes 1179648 | tf_op jit(solution)/shard_map/all_to_all | solution.py:336
  41.4 0.0 collective-permute-done.2.refs_1_
  41.4 0.0 collective-permute-done.1.refs_0_
  41.4 0.6 copy-done.6
  42.0 0.1 copy-done.7
  42.0 0.7 copy-done.8
  42.7 17.0 %schur_z.1.refs_0_ = bf16[4,2,256,128]{3,2,1,0:T(8,128)(2,1)} custom-call(bf16[256,128]{1,0:T(8,128)(2,1)} %own_hbm.1, bf16[256,128]{1,0:T(8,128)(2,1)} %copy-done.3, bf16[2,256,128]{2,1,0:T(8,128)(2,1)} %copy-done.8, bf16[2,256,128]{2,1,0:T(8,128)(2,1)} %copy-done.7, bf16[2,256,128]{2,1,0:T(8,128)(2,1)} %copy-done.6), custom_call_target="tpu_custom_call" | custom-call | flops 100000000376832 | bytes 1048576 | tf_op jit(solution)/shard_map/schur_z/pallas_call | solution.py:332
  59.7 4.6 %collective-permute-start.5 = (bf16[4,2,256,128]{3,2,1,0:T(8,128)(2,1)}, bf16[4,2,256,128]{3,2,1,0:T(8,128)(2,1)S(1)}, u32[]{:S(2)}, u32[]{:S(2)}) collective-permute-start(bf16[4,2,256,128]{3,2,1,0:T(8,128)(2,1)} %schur_z.1.refs_0_), channel_id=1, source_target_pairs={{0,24},{1,25},{2,26},{3,27},{4,28},{5,29},{6,30},{7,31},{8,0},{9,1... | collective-permute-start | bytes 1572872 | tf_op jit(solution)/shard_map/schur_y/ppermute | solution.py:320
  64.4 1.9 collective-permute-start.4
  66.3 9.5 %collective-permute-done.5.refs_2_ = bf16[4,2,256,128]{3,2,1,0:T(8,128)(2,1)S(1)} collective-permute-done((bf16[4,2,256,128]{3,2,1,0:T(8,128)(2,1)}, bf16[4,2,256,128]{3,2,1,0:T(8,128)(2,1)S(1)}, u32[]{:S(2)}, u32[]{:S(2)}) %collective-permute-start.5) | collective-permute-done | bytes 524320 | tf_op jit(solution)/shard_map/schur_y/ppermute | solution.py:320
  75.9 5.3 %collective-permute-start.7 = (bf16[2,2,256,128]{3,2,1,0:T(8,128)(2,1)S(1)}, bf16[2,2,256,128]{3,2,1,0:T(8,128)(2,1)S(1)}, u32[]{:S(2)}, u32[]{:S(2)}) collective-permute-start(bf16[2,2,256,128]{3,2,1,0:T(8,128)(2,1)S(1)} %slice.9), channel_id=1, source_target_pairs={{0,24},{1,25},{2,26},{3,27},{4,28},{5,29},{6,30},{7,31},{8,0},{9,1... | collective-permute-start | bytes 786440 | tf_op jit(solution)/shard_map/schur_y/ppermute | solution.py:320
  81.2 1.9 collective-permute-start.6
  83.2 0.0 all-to-all-done.recv_hbm
  83.2 7.6 %shard_map.122 = (bf16[32,16,128]{2,1,0:T(8,128)(2,1)}, f32[16,8,128]{2,1,0:T(8,128)}) custom-call(f32[16,72,128]{2,1,0:T(8,128)} %all-to-all-done.recv_hbm), custom_call_target="tpu_custom_call" | custom-call | flops 1000000000 | bytes 1048576 | tf_op jit(solution)/shard_map/pallas_call | solution.py:336
  90.8 0.0 collective-permute-done.7.refs_4_
  90.8 0.2 collective-permute-done.6.refs_3_
  91.0 0.5 copy-done.4
  91.5 0.2 copy-done.5
  91.7 3.6 %shard_map.123 = f32[16,16,256]{2,1,0:T(8,128)} custom-call(bf16[32,16,128]{2,1,0:T(8,128)(2,1)} %get-tuple-element.19.rhs_hbm, bf16[4,2,256,128]{3,2,1,0:T(8,128)(2,1)} %schur_z.1.refs_0_, bf16[4,2,256,128]{3,2,1,0:T(8,128)(2,1)} %copy-done.1, bf16[4,2,256,128]{3,2,1,0:T(8,128)(2,1)} %copy-done, bf16[2,2,256,128]{3,2,1,0:T(8,128)(2,1)} %copy-done.5, ...), custom_call_target="tpu_custom_call" | custom-call | flops 1000000000 | bytes 3145728 | tf_op jit(solution)/shard_map/pallas_call | solution.py:337
  95.3 40.7 %all_to_all.20.recv_hbm = f32[16,16,256]{2,1,0:T(8,128)} all-to-all(f32[16,16,256]{2,1,0:T(8,128)} %shard_map.123), channel_id=1, replica_groups=mesh['row'=16,'col'=32] {'row'}, dimensions={0} | all-to-all | bytes 524288 | tf_op jit(solution)/shard_map/all_to_all | solution.py:338
  136.1 4.6 %shard_map.124 = (f32[8,16,400]{2,1,0:T(8,128)}, f32[8,16,400]{2,1,0:T(8,128)}, f32[8,16,400]{2,1,0:T(8,128)}, bf16[16,64,128]{2,1,0:T(8,128)(2,1)}) custom-call(s32[16]{0:T(128)} %time_ref.3, s32[16]{0:T(128)} %node_ref.3, f32[16,16,256]{2,1,0:T(8,128)} %all_to_all.20.recv_hbm, f32[8,16,400]{2,1,0:T(8,128)} %get-tuple-element.21.prev_hbm, ...), custom_call_target="tpu_custom_call" | custom-call | flops 1000000000 | bytes 4194304 | tf_op jit(solution)/shard_map/pallas_call | solution.py:338
  140.6 25.2 %all_to_all.21.recv_hbm = bf16[16,64,128]{2,1,0:T(8,128)(2,1)} all-to-all(bf16[16,64,128]{2,1,0:T(8,128)(2,1)} %get-tuple-element.22), channel_id=1, replica_groups=mesh['row'=16,'col'=32] {'row'}, dimensions={0} | all-to-all | bytes 524288 | tf_op jit(solution)/shard_map/all_to_all | solution.py:339
  165.8 6.5 %shard_map.125 = (f32[16,256]{1,0:T(8,128)}, bf16[16,16,256]{2,1,0:T(8,128)(2,1)}) custom-call(bf16[16,64,128]{2,1,0:T(8,128)(2,1)} %all_to_all.21.recv_hbm, f32[16,8,128]{2,1,0:T(8,128)} %get-tuple-element.23.map_hbm, bf16[4,2,256,128]{3,2,1,0:T(8,128)(2,1)} %schur_z.1.refs_0_, bf16[4,2,256,128]{3,2,1,0:T(8,128)(2,1)} %copy-done.1, ...), custom_call_target="tpu_custom_call" | custom-call | flops 1000000000 | bytes 3145728 | tf_op jit(solution)/shard_map/pallas_call | solution.py:339
  172.3 20.7 %all_to_all.22.recv_hbm = bf16[16,16,256]{2,1,0:T(8,128)(2,1)} all-to-all(bf16[16,16,256]{2,1,0:T(8,128)(2,1)} %get-tuple-element.24), channel_id=1, replica_groups=mesh['row'=16,'col'=32] {'row'}, dimensions={0} | all-to-all | bytes 262144 | tf_op jit(solution)/shard_map/all_to_all | solution.py:340
  193.0 2.6 %shard_map.126 = (f32[8,16,400]{2,1,0:T(8,128)}, f32[8,16,400]{2,1,0:T(8,128)}) custom-call(bf16[16,16,256]{2,1,0:T(8,128)(2,1)} %all_to_all.22.recv_hbm, f32[8,16,400]{2,1,0:T(8,128)} %get-tuple-element.25.prev_hbm, f32[8,16,400]{2,1,0:T(8,128)} %get-tuple-element.26.volt_hbm, f32[8,16,400]{2,1,0:T(8,128)} %get-tuple-element.27.curr_hbm, ...), custom_call_target="tpu_custom_call" | custom-call | flops 1000000000 | bytes 2097152 | tf_op jit(solution)/shard_map/pallas_call | solution.py:340
  (17 shorter events, 0.1 us)
Async XLA Ops:
  0.6 13.4 %copy-start.2 = (bf16[256,128]{1,0:T(8,128)(2,1)S(1)}, bf16[256,128]{1,0:T(8,128)(2,1)}, u32[]{:S(2)}) copy-start(bf16[256,128]{1,0:T(8,128)(2,1)} %own_hbm.1) | copy-start | bytes 196612
  0.6 13.4 %collective-permute-start = (bf16[256,128]{1,0:T(8,128)(2,1)}, bf16[256,128]{1,0:T(8,128)(2,1)S(1)}, u32[]{:S(2)}, u32[]{:S(2)}) collective-permute-start(bf16[256,128]{1,0:T(8,128)(2,1)} %own_hbm.1), channel_id=1, source_target_pairs={{0,4},{1,5},{2,6},{3,7},{4,0},{5,1},{6,2},{7,3},{8,12},{9,13},{10,... | collective-permute-start | bytes 196616 | tf_op jit(solution)/shard_map/schur_z/ppermute | solution.py:316
  14.0 27.4 %copy-start.3 = (bf16[256,128]{1,0:T(8,128)(2,1)}, bf16[256,128]{1,0:T(8,128)(2,1)S(1)}, u32[]{:S(2)}) copy-start(bf16[256,128]{1,0:T(8,128)(2,1)S(1)} %collective-permute-done.across_hbm) | copy-start | bytes 196612
  14.1 27.3 %collective-permute-start.3 = (bf16[2,256,128]{2,1,0:T(8,128)(2,1)S(1)}, bf16[2,256,128]{2,1,0:T(8,128)(2,1)S(1)}, u32[]{:S(2)}, u32[]{:S(2)}) collective-permute-start(bf16[2,256,128]{2,1,0:T(8,128)(2,1)S(1)} %pad_maximum_fusion), channel_id=1, source_target_pairs={{0,3},{1,2},{2,1},{3,0},{4,7},{5,6},{6,5},{7,4},{8,11},{9,10},{10,... | collective-permute-start | bytes 393224 | tf_op jit(solution)/shard_map/schur_z/ppermute | solution.py:316
  17.6 23.7 %collective-permute-start.2 = (bf16[2,256,128]{2,1,0:T(8,128)(2,1)S(1)}, bf16[2,256,128]{2,1,0:T(8,128)(2,1)S(1)}, u32[]{:S(2)}, u32[]{:S(2)}) collective-permute-start(bf16[2,256,128]{2,1,0:T(8,128)(2,1)S(1)} %pad_maximum_fusion), channel_id=1, source_target_pairs={{0,2},{1,3},{2,0},{3,1},{4,6},{5,7},{6,4},{7,5},{8,10},{9,11},{10,... | collective-permute-start | bytes 393224 | tf_op jit(solution)/shard_map/schur_z/ppermute | solution.py:316
  21.3 20.1 %collective-permute-start.1 = (bf16[2,256,128]{2,1,0:T(8,128)(2,1)S(1)}, bf16[2,256,128]{2,1,0:T(8,128)(2,1)S(1)}, u32[]{:S(2)}, u32[]{:S(2)}) collective-permute-start(bf16[2,256,128]{2,1,0:T(8,128)(2,1)S(1)} %pad_maximum_fusion), channel_id=1, source_target_pairs={{0,1},{1,0},{2,3},{3,2},{4,5},{5,4},{6,7},{7,6},{8,9},{9,8},{10,11... | collective-permute-start | bytes 393224 | tf_op jit(solution)/shard_map/schur_z/ppermute | solution.py:316
  24.4 58.8 %all-to-all-start = ((f32[16,72,128]{2,1,0:T(8,128)}), f32[16,72,128]{2,1,0:T(8,128)}, u32[]{:S(2)}, u32[]{:S(2)}) async-start(f32[16,72,128]{2,1,0:T(8,128)} %get-tuple-element.18), calls=%async_computation | async-start | bytes 1179648 | tf_op jit(solution)/shard_map/all_to_all | solution.py:336
  41.3 0.6 copy-start.6
  41.4 0.7 copy-start.7
  42.0 0.7 copy-start.8
  59.7 16.1 %collective-permute-start.5 = (bf16[4,2,256,128]{3,2,1,0:T(8,128)(2,1)}, bf16[4,2,256,128]{3,2,1,0:T(8,128)(2,1)S(1)}, u32[]{:S(2)}, u32[]{:S(2)}) collective-permute-start(bf16[4,2,256,128]{3,2,1,0:T(8,128)(2,1)} %schur_z.1.refs_0_), channel_id=1, source_target_pairs={{0,24},{1,25},{2,26},{3,27},{4,28},{5,29},{6,30},{7,31},{8,0},{9,1... | collective-permute-start | bytes 1572872 | tf_op jit(solution)/shard_map/schur_y/ppermute | solution.py:320
  64.4 16.8 %collective-permute-start.4 = (bf16[4,2,256,128]{3,2,1,0:T(8,128)(2,1)}, bf16[4,2,256,128]{3,2,1,0:T(8,128)(2,1)S(1)}, u32[]{:S(2)}, u32[]{:S(2)}) collective-permute-start(bf16[4,2,256,128]{3,2,1,0:T(8,128)(2,1)} %schur_z.1.refs_0_), channel_id=1, source_target_pairs={{0,8},{1,9},{2,10},{3,11},{4,12},{5,13},{6,14},{7,15},{8,16},{9,17... | collective-permute-start | bytes 1572872 | tf_op jit(solution)/shard_map/schur_y/ppermute | solution.py:320
  75.9 15.2 %copy-start = (bf16[4,2,256,128]{3,2,1,0:T(8,128)(2,1)}, bf16[4,2,256,128]{3,2,1,0:T(8,128)(2,1)S(1)}, u32[]{:S(2)}) copy-start(bf16[4,2,256,128]{3,2,1,0:T(8,128)(2,1)S(1)} %collective-permute-done.5.refs_2_) | copy-start | bytes 1572868
  75.9 14.9 %collective-permute-start.7 = (bf16[2,2,256,128]{3,2,1,0:T(8,128)(2,1)S(1)}, bf16[2,2,256,128]{3,2,1,0:T(8,128)(2,1)S(1)}, u32[]{:S(2)}, u32[]{:S(2)}) collective-permute-start(bf16[2,2,256,128]{3,2,1,0:T(8,128)(2,1)S(1)} %slice.9), channel_id=1, source_target_pairs={{0,24},{1,25},{2,26},{3,27},{4,28},{5,29},{6,30},{7,31},{8,0},{9,1... | collective-permute-start | bytes 786440 | tf_op jit(solution)/shard_map/schur_y/ppermute | solution.py:320
  81.2 9.8 %copy-start.1 = (bf16[4,2,256,128]{3,2,1,0:T(8,128)(2,1)}, bf16[4,2,256,128]{3,2,1,0:T(8,128)(2,1)S(1)}, u32[]{:S(2)}) copy-start(bf16[4,2,256,128]{3,2,1,0:T(8,128)(2,1)S(1)} %collective-permute-done.4.refs_1_) | copy-start | bytes 1572868
  81.2 9.8 %collective-permute-start.6 = (bf16[2,2,256,128]{3,2,1,0:T(8,128)(2,1)S(1)}, bf16[2,2,256,128]{3,2,1,0:T(8,128)(2,1)S(1)}, u32[]{:S(2)}, u32[]{:S(2)}) collective-permute-start(bf16[2,2,256,128]{3,2,1,0:T(8,128)(2,1)S(1)} %slice.8), channel_id=1, source_target_pairs={{0,8},{1,9},{2,10},{3,11},{4,12},{5,13},{6,14},{7,15},{8,16},{9,17... | collective-permute-start | bytes 786440 | tf_op jit(solution)/shard_map/schur_y/ppermute | solution.py:320
  90.8 0.7 copy-start.4
  91.0 0.7 copy-start.5

commit v6 on v5

--- a/solution.py
+++ b/solution.py
@@ -19,7 +19,9 @@
 TILES = OWN // LANES
 VALUE_ROWS = TILES * SCEN
 MAP_ROWS = 2 * TILES
-VMEM_BYTES = 60 << 20
+CORES = [[2 * n + core for n in range(ROWS // 2)] for core in range(2)]
+VMEM_BYTES = 16 << 20
+ALL_VMEM = 60 << 20
 BF16, F32 = jnp.bfloat16, jnp.float32
 
 NN = (((1,), (0,)), ((), ()))
@@ -84,7 +86,7 @@
         parts.append(tie_ref[k : k + 1, :] * open_k[:, :PORTS])
     values = jnp.concatenate(parts, axis=1).astype(send_ref.dtype)
     for t, tile in enumerate(tiles_of(values)):
-        for r in range(ROWS):
+        for r in range(send_ref.shape[0]):
             send_ref[r, t * SCEN : (t + 1) * SCEN, :] = tile
 
 
@@ -98,32 +100,35 @@
     mapped = flat_row(map_ref)
     rows = tiles_of((mapped // BLOCK).astype(F32)) + tiles_of((mapped % BLOCK).astype(F32))
     tail = jnp.concatenate(rows, axis=0)
-    for r in range(ROWS):
+    for r in range(send_ref.shape[0]):
         send_ref[r, VALUE_ROWS:, :] = tail
     wait_for(copies[1:6])
     open_circuit(0, volt_ref, curr_ref, breaker_ref, gain_ref, copies[6:], inv_ref, time_ref, node_ref, tie_ref, open_ref, send_ref)
 
 
-def right_hand_side(recv_ref, map_ref, ready):
-    low = lax.broadcasted_iota(jnp.int32, (BLOCK, OWN), 0)
+def right_hand_side(recv_ref, map_ref):
+    low = lax.broadcasted_iota(jnp.int32, (BLOCK, OWN), 0).astype(F32).astype(BF16)
+    one, zero = jnp.ones((), BF16), jnp.zeros((), BF16)
     rhs = jnp.zeros((ROWS * SCEN, BLOCK), F32)
     for r in range(ROWS):
-        wait_for(ready(r))
-        tail = map_ref[r].astype(jnp.int32)
+        tail = map_ref[r]
         hi = jnp.concatenate([tail[t : t + 1] for t in range(TILES)], axis=1)
         lo = jnp.concatenate([tail[TILES + t : TILES + t + 1] for t in range(TILES)], axis=1)
-        right = jnp.where(low == lo, 1.0, 0.0).astype(BF16)
+        hi = jnp.broadcast_to(hi, (SCEN, OWN)).astype(BF16)
+        right = jnp.where(low == lo.astype(BF16), one, zero)
         values = jnp.concatenate([recv_ref[r, t * SCEN : (t + 1) * SCEN, :] for t in range(TILES)], axis=1)
         for part in halves(values) if values.dtype == F32 else (values,):
-            part = part.astype(F32)
-            left = jnp.concatenate([jnp.where(hi == h, part, 0.0) for h in range(ROWS)], axis=0).astype(BF16)
+            left = jnp.concatenate([jnp.where(hi == h, part, zero) for h in range(ROWS)], axis=0)
             rhs += dot(left, right, NT)
     return rhs.astype(BF16).reshape(ROWS, SCEN, BLOCK)
 
 
-def join_kernel(own_hbm, across_hbm, *refs):
-    quads, (out_hbm, sems) = refs[:3], refs[3:]
-    wait_for(fetch([own_hbm, across_hbm, *quads], [out_hbm.at[0, 0], out_hbm.at[0, 1]] + [out_hbm.at[x] for x in (1, 2, 3)], sems))
+def join_kernel(own_ref, across_ref, *refs):
+    quads, (out_ref,) = refs[:3], refs[3:]
+    out_ref[0, 0] = own_ref[...]
+    out_ref[0, 1] = across_ref[...]
+    for x in (1, 2, 3):
+        out_ref[x] = quads[x - 1][...]
 
 
 def schur_copies(parts, schur_ref, sems):
@@ -135,16 +140,14 @@
 def schur_product(rhs_ref, schur_ref, copies):
     col = lax.axis_index("col")
     own_y, own_z = col // 8, col % 8
-    total = jnp.zeros((SCEN, BLOCK), F32)
-    for n, waits in ((0, copies[:1]), (1, copies[1:2]), (3, copies[2:3]), (2, copies[3:])):
-        wait_for(waits)
-        for x in (0, 2):
+    wait_for(copies)
+    left, right = [], []
+    for n in range(4):
+        for x in range(4):
             for o in range(2):
-                place = 8 * ((own_y + 4 - n) % 4) + jnp.bitwise_xor(own_z, x + 4 * o)
-                left = jnp.concatenate([rhs_ref[place], rhs_ref[jnp.bitwise_xor(place, 1)]], axis=1)
-                right = jnp.concatenate([schur_ref[n, x, o], schur_ref[n, x + 1, o]], axis=1)
-                total += dot(left, right, NT)
-    return total
+                left.append(rhs_ref[8 * ((own_y + 4 - n) % 4) + jnp.bitwise_xor(own_z, x + 4 * o)])
+                right.append(schur_ref[n, x, o])
+    return dot(jnp.concatenate(left, axis=1), jnp.concatenate(right, axis=1), NT)
 
 
 def keep(rhs, rhs_ref):
@@ -153,14 +156,15 @@
             rhs_ref[2 * h + side] = rhs[h, :, side * LANES : (side + 1) * LANES]
 
 
-def rhs_kernel(recv_hbm, rhs_ref, map_out, recv_ref, map_ref, sems):
-    copies = fetch(
-        [recv_hbm.at[r, pl.ds(0, VALUE_ROWS)] for r in range(ROWS)] + [recv_hbm.at[r, pl.ds(VALUE_ROWS, MAP_ROWS)] for r in range(ROWS)],
-        each(recv_ref, ROWS) + each(map_ref, ROWS),
-        sems,
-    )
-    keep(right_hand_side(recv_ref, map_ref, lambda r: (copies[r], copies[ROWS + r])), rhs_ref)
-    map_out[...] = map_ref[...]
+def two_parts(same, other, ref):
+    half = ROWS // 2
+    return [same, other], [ref.at[pl.ds(0, half)], ref.at[pl.ds(half, half)]]
+
+
+def rhs_kernel(same_hbm, other_hbm, rhs_ref, map_out, recv_ref, sems):
+    wait_for(fetch(*two_parts(same_hbm, other_hbm, recv_ref), sems))
+    map_out[...] = recv_ref[:, VALUE_ROWS:, :]
+    keep(right_hand_side(recv_ref, map_out), rhs_ref)
 
 
 def product_kernel(rhs_hbm, *refs):
@@ -168,16 +172,17 @@
     copies = schur_copies(parts, schur_ref, sems)
     wait_for(fetch([rhs_hbm], [rhs_ref], rhs_sem))
     total = schur_product(rhs_ref, schur_ref, copies)
-    for r in range(ROWS):
+    for r in range(send_ref.shape[0]):
         send_ref[r] = total
 
 
-def interface_kernel(recv_hbm, map_hbm, *refs):
+def interface_kernel(same_hbm, other_hbm, map_hbm, *refs):
     parts, (iface_ref, send_ref, schur_ref, rhs_ref, recv_ref, map_ref, sems, recv_sems) = refs[:5], refs[5:]
-    arrived = fetch([map_hbm] + each(recv_hbm, ROWS), [map_ref] + each(recv_ref, ROWS), recv_sems)
+    sources, targets = two_parts(same_hbm, other_hbm, recv_ref)
+    arrived = fetch([map_hbm] + sources, [map_ref] + targets, recv_sems)
     copies = schur_copies(parts, schur_ref, sems)
-    arrived[0].wait()
-    keep(right_hand_side(recv_ref, map_ref, lambda r: (arrived[1 + r],)), rhs_ref)
+    wait_for(arrived)
+    keep(right_hand_side(recv_ref, map_ref), rhs_ref)
     total = schur_product(rhs_ref, schur_ref, copies)
     iface_ref[...] = total
     half = total.astype(BF16)
@@ -185,7 +190,7 @@
         send_ref[r] = half
 
 
-def driven(recv_ref, map_ref, tie_ref):
+def driven(recv_ref, map_ref, tie_ref, sender):
     mapped = flat_row(map_ref)
     hi = mapped // BLOCK
     low = lax.broadcasted_iota(jnp.int32, (BLOCK, OWN), 0)
@@ -194,7 +199,7 @@
     found = sum(dot(part, right) for part in (halves(volts) if volts.dtype == F32 else (volts,)))
     picked = jnp.zeros((SCEN, OWN), F32)
     for r in range(ROWS):
-        picked += jnp.where(hi == r, found[r * SCEN : (r + 1) * SCEN, :], 0.0)
+        picked += jnp.where(hi == sender(r), found[r * SCEN : (r + 1) * SCEN, :], 0.0)
     return (flat_row(tie_ref) * picked).astype(BF16)
 
 
@@ -204,17 +209,24 @@
     return volt_next, closed * (curr + gain_ref[k : k + 1, :] * (volt_next + volt))
 
 
-def middle_kernel(time_ref, node_ref, recv_hbm, prev_hbm, volt_hbm, curr_hbm, breaker_hbm, gain_hbm, tie_hbm, map_hbm, inv_hbm, volt_out, curr_out, open_ref, send_ref, recv_ref, prev_ref, map_ref, gain_ref, tie_ref, volt_ref, curr_ref, breaker_ref, inv_ref, sems):
+def paired_sender(place):
+    core = lax.axis_index("row") % 2
+    half = ROWS // 2
+    return 2 * place + core if place < half else 2 * (place - half) + 1 - core
+
+
+def middle_kernel(time_ref, node_ref, same_hbm, other_hbm, prev_hbm, volt_hbm, curr_hbm, breaker_hbm, gain_hbm, tie_hbm, map_hbm, inv_hbm, volt_out, curr_out, open_ref, send_ref, recv_ref, prev_ref, map_ref, gain_ref, tie_ref, volt_ref, curr_ref, breaker_ref, inv_ref, sems):
+    sources, targets = two_parts(same_hbm, other_hbm, recv_ref)
     copies = fetch(
-        [map_hbm, tie_hbm, recv_hbm, gain_hbm, prev_hbm, volt_hbm, curr_hbm, breaker_hbm] + each(inv_hbm, SUBS),
-        [map_ref, tie_ref, recv_ref, gain_ref, prev_ref, volt_ref, curr_ref, breaker_ref] + each(inv_ref, SUBS),
+        [map_hbm, tie_hbm] + sources + [gain_hbm, prev_hbm, volt_hbm, curr_hbm, breaker_hbm] + each(inv_hbm, SUBS),
+        [map_ref, tie_ref] + targets + [gain_ref, prev_ref, volt_ref, curr_ref, breaker_ref] + each(inv_ref, SUBS),
         sems,
     )
-    wait_for(copies[:3])
-    drive = driven(recv_ref, map_ref, tie_ref)
-    wait_for(copies[3:8])
+    wait_for(copies[:4])
+    drive = driven(recv_ref, map_ref, tie_ref, paired_sender)
+    wait_for(copies[4:9])
     for k in range(SUBS):
-        copies[8 + k].wait()
+        copies[9 + k].wait()
         volt_out[k], curr_out[k] = update(k, drive, prev_ref, inv_ref[k, :PORTS, :], volt_ref[k], curr_ref[k], breaker_ref, gain_ref)
     open_circuit(1, volt_out, curr_out, breaker_ref, gain_ref, None, inv_ref, time_ref, node_ref, tie_ref, open_ref, send_ref)
 
@@ -226,7 +238,7 @@
         sems,
     )
     wait_for(copies[:3])
-    drive = driven(recv_ref, map_ref, tie_ref)
+    drive = driven(recv_ref, map_ref, tie_ref, lambda place: place)
     wait_for(copies[3:])
     for k in range(SUBS):
         volt_out[k], curr_out[k] = update(k, drive, prev_ref, inv_ref[k], volt_ref[k], curr_ref[k], breaker_ref, gain_ref)
@@ -256,14 +268,14 @@
 BREAKER = held(((SUBS, SCEN, NODES), jnp.int32))
 
 
-def call(body, ins, outs, scratch, flops, moved, out_specs=None):
+def call(body, ins, outs, scratch, flops, moved, vmem=VMEM_BYTES):
     return pl.pallas_call(
         body,
         out_shape=[jax.ShapeDtypeStruct(shape, kind) for shape, kind in outs],
         in_specs=ins,
-        out_specs=out_specs or [VMEM] * len(outs),
+        out_specs=[VMEM] * len(outs),
         scratch_shapes=scratch,
-        compiler_params=pltpu.CompilerParams(vmem_limit_bytes=VMEM_BYTES),
+        compiler_params=pltpu.CompilerParams(vmem_limit_bytes=vmem),
         cost_estimate=pl.CostEstimate(flops=flops, bytes_accessed=moved, transcendentals=0),
     )
 
@@ -271,34 +283,28 @@
 first = call(
     first_kernel,
     [SMEM] * 2 + [HBM] * 7,
-    [STATE, ((ROWS, VALUE_ROWS + MAP_ROWS, LANES), F32)],
+    [STATE, ((ROWS // 2, VALUE_ROWS + MAP_ROWS, LANES), F32)],
     SMALL + held(STATE, STATE) + BREAKER + held(((SUBS, NODES, NODES), BF16)) + copies_of(6 + SUBS),
     GIGA,
     4 << 20,
+    ALL_VMEM,
 )
-join = call(join_kernel, [HBM] * 5, [((4, 2, BLOCK, LANES), BF16)], copies_of(5), 100_000 * GIGA, 1 << 20, [HBM])
-summed = call(
-    rhs_kernel,
-    [HBM],
-    [RHS, MAPS],
-    held(((ROWS, VALUE_ROWS, LANES), F32), MAPS) + copies_of(2 * ROWS),
-    GIGA,
-    1 << 20,
-)
-product = call(product_kernel, [HBM] * 6, [(FACE, F32)], held(SCHUR, RHS) + copies_of(5) + copies_of(1), GIGA, 3 << 20)
+join = call(join_kernel, [VMEM] * 5, [((4, 2, BLOCK, LANES), BF16)], [], 100_000 * GIGA, 1 << 20, 8 << 20)
+summed = call(rhs_kernel, [HBM] * 2, [RHS, MAPS], held(((ROWS, VALUE_ROWS + MAP_ROWS, LANES), F32)) + copies_of(2), GIGA, 1 << 20)
+product = call(product_kernel, [HBM] * 6, [((ROWS // 2, SCEN, BLOCK), F32)], held(SCHUR, RHS) + copies_of(5) + copies_of(1), GIGA, 3 << 20)
 interface = call(
     interface_kernel,
-    [HBM] * 7,
+    [HBM] * 8,
     [(FACE[1:], F32), (FACE, BF16)],
-    held(SCHUR, RHS, ((ROWS, VALUE_ROWS, LANES), BF16), MAPS) + copies_of(5) + copies_of(1 + ROWS),
+    held(SCHUR, RHS, ((ROWS, VALUE_ROWS, LANES), BF16), MAPS) + copies_of(5) + copies_of(3),
     GIGA,
     3 << 20,
 )
 middle = call(
     middle_kernel,
-    [SMEM] * 2 + [HBM] * 9,
-    [STATE, STATE, STATE, ((ROWS, VALUE_ROWS, LANES), BF16)],
-    held((FACE, F32), STATE) + SMALL + held(STATE, STATE) + BREAKER + held(((SUBS, NODES, NODES), BF16)) + copies_of(8 + SUBS),
+    [SMEM] * 2 + [HBM] * 10,
+    [STATE, STATE, STATE, ((ROWS // 2, VALUE_ROWS, LANES), BF16)],
+    held((FACE, F32), STATE) + SMALL + held(STATE, STATE) + BREAKER + held(((SUBS, NODES, NODES), BF16)) + copies_of(9 + SUBS),
     GIGA,
     4 << 20,
 )
@@ -322,6 +328,11 @@
 
 def local(volt, curr, local_inverse, schur_inverse, ind_gain, tie, port_map, breaker, fault_time, fault_node):
     exchange = functools.partial(lax.all_to_all, axis_name="row", split_axis=0, concat_axis=0)
+
+    def paired_exchange(send):
+        same = exchange(send, axis_index_groups=CORES)
+        return same, lax.ppermute(same, "row", [(r, r ^ 1) for r in range(ROWS)])
+
     fixed = breaker, ind_gain, tie, port_map, local_inverse
     with jax.named_scope("schur_z"):
         across = along_z(schur_inverse, 4)
@@ -333,10 +344,10 @@
     with jax.named_scope("schur_y"):
         back, ahead = along_y(own, 1), along_y(own, -1)
         schur_rows = own, back, ahead, along_y(back[:2], 1), along_y(ahead[2:], -1)
-    rhs, maps = summed(exchange(send))
+    rhs, maps = summed(*paired_exchange(send))
     (send,) = product(rhs, *schur_rows)
-    volt, curr, opened, send = middle(fault_time, fault_node, exchange(send), opened, volt, curr, *fixed)
-    iface_block, send = interface(exchange(send), maps, *schur_rows)
+    volt, curr, opened, send = middle(fault_time, fault_node, *paired_exchange(send), opened, volt, curr, *fixed)
+    iface_block, send = interface(*paired_exchange(send), maps, *schur_rows)
     volt, curr = last(exchange(send), opened, volt, curr, *fixed)
     return volt, curr, iface_block
 

time: 197 us -> 161 us (0.82)
  blocking collectives: 86.6 us -> 55.6 us
  Pallas kernels: 46.3 us -> 20.2 us
  waiting for transfers between devices: 9.75 us -> 26.3 us
  starting transfers between devices: 50 us -> 57.4 us
    all_to_all x2, blocking collectives: 65.9 us -> 36.5 us  [paired_exchange(): same = exchange(send, axis_index_groups=CORES)]
    all_to_all x1, waiting for transfers between devices: 0.01 us -> 18.9 us  [paired_exchange(): same = exchange(send, axis_index_groups=CORES)]
    pallas_call x1, Pallas kernels: 17 us -> 0.04 us  [local(): own, = join(schur_inverse, across, *(along_z(pair, x) for x in (1, 2, 3)))]
    ppermute x0 -> x3, starting transfers between devices: none -> 9.55 us  [paired_exchange(): return (same, lax.ppermute(same, 'row', [(r, r ^ 1) for r in range(ROWS)]))]
    pallas_call x3, Pallas kernels: 18.7 us -> 12.4 us  [the longest x1 4.79 us: local(): middle(fault_time, fault_node, *paired_exchange(send), opened, volt, curr...]
    ppermute x4, waiting for transfers between devices: 9.73 us -> 5.41 us  [along_y(): lax.ppermute(block, 'col', [(c, (c + 8 * steps) % COLS) for c in range(CO...]
    pallas_call x1, Pallas kernels: 3.62 us -> 1.05 us  [local(): send, = product(rhs, *schur_rows)]
  transfers between devices with their start and end apart: 9 -> 12, of which waited for: 2 -> 4; matrix products, arithmetic and copies ran while one was open for 0% -> 0% of each run, Pallas kernels for 15% -> 5%
where the time goes in v6:
time: 161 us
  starting transfers between devices  57.4 us (36%)
  blocking collectives  55.6 us (35%)
  waiting for transfers between devices  26.3 us (16%)
  Pallas kernels  20.2 us (13%)
    all_to_all x2, blocking collectives, paired_exchange(): same = exchange(send, axis_index_groups=CORES)  36.5 us
    ppermute x4, starting transfers between devices, along_z(): return lax.ppermute(block, 'col', [(c, c ^ flip) for c in range(COLS)])  19.3 us
    all_to_all x1, blocking collectives, local(): volt, curr = last(exchange(send), opened, volt, curr, *fixed)  19.1 us
    all_to_all x1, waiting for transfers between devices, paired_exchange(): same = exchange(send, axis_index_groups=CORES)  18.9 us
    all_to_all x1, starting transfers between devices, paired_exchange(): same = exchange(send, axis_index_groups=CORES)  15.1 us
    ppermute x4, starting transfers between devices, along_y(): lax.ppermute(block, 'col', [(c, (c + 8 * steps) % COLS) for c in range(CO...  13.4 us
    ppermute x3, starting transfers between devices, paired_exchange(): return (same, lax.ppermute(same, 'row', [(r, r ^ 1) for r in range(ROWS)]))  9.55 us
    ppermute x4, waiting for transfers between devices, along_y(): lax.ppermute(block, 'col', [(c, (c + 8 * steps) % COLS) for c in range(CO...  5.41 us
  transfers between devices with their start and end apart: 12, of which 4 were waited for; matrix products, arithmetic and copies ran while one was open for 0% of the time, Pallas kernels for 5%

profile of v6, /device:TPU:33, one launch (start us, length us, event | category | flops | bytes accessed | tf_op | source)
XLA Modules:
  0.0 160.7 jit_solution(8911442067385633333)
XLA Ops:
  0.6 8.9 %collective-permute-start = (bf16[256,128]{1,0:T(8,128)(2,1)}, bf16[256,128]{1,0:T(8,128)(2,1)S(1)}, u32[]{:S(2)}, u32[]{:S(2)}) collective-permute-start(bf16[256,128]{1,0:T(8,128)(2,1)} %own_ref.1), channel_id=1, source_target_pairs={{0,4},{1,5},{2,6},{3,7},{4,0},{5,1},{6,2},{7,3},{8,12},{9,13},{10,... | collective-permute-start | bytes 196616 | tf_op jit(solution)/shard_map/schur_z/ppermute | solution.py:322
  9.6 4.3 %shard_map.121 = (f32[8,16,400]{2,1,0:T(8,128)}, f32[8,72,128]{2,1,0:T(8,128)}) custom-call(s32[16]{0:T(128)} %time_ref.3, s32[16]{0:T(128)} %node_ref.3, f32[8,16,400]{2,1,0:T(8,128)} %volt_hbm.3, f32[8,16,400]{2,1,0:T(8,128)} %curr_hbm.3, s32[8,16,400]{2,1,0:T(8,128)} %breaker_hbm.5, f32[8,400]{1,0:T(8,128)} %gain_hbm.5, f32[8,64]{1,0:T(8,128)} %tie_hbm.5, ...), custom_call_target="tpu_custom_call" | custom-call | flops 1000000000 | bytes 4194304 | tf_op jit(solution)/shard_map/pallas_call | solution.py:339
  13.9 3.5 %collective-permute-start.4 = (bf16[2,256,128]{2,1,0:T(8,128)(2,1)S(1)}, bf16[2,256,128]{2,1,0:T(8,128)(2,1)S(1)}, u32[]{:S(2)}, u32[]{:S(2)}) collective-permute-start(bf16[2,256,128]{2,1,0:T(8,128)(2,1)S(1)} %pad_maximum_fusion), channel_id=1, source_target_pairs={{0,3},{1,2},{2,1},{3,0},{4,7},{5,6},{6,5},{7,4},{8,11},{9,10},{10,... | collective-permute-start | bytes 393224 | tf_op jit(solution)/shard_map/schur_z/ppermute | solution.py:322
  17.5 3.8 %collective-permute-start.3 = (bf16[2,256,128]{2,1,0:T(8,128)(2,1)S(1)}, bf16[2,256,128]{2,1,0:T(8,128)(2,1)S(1)}, u32[]{:S(2)}, u32[]{:S(2)}) collective-permute-start(bf16[2,256,128]{2,1,0:T(8,128)(2,1)S(1)} %pad_maximum_fusion), channel_id=1, source_target_pairs={{0,2},{1,3},{2,0},{3,1},{4,6},{5,7},{6,4},{7,5},{8,10},{9,11},{10,... | collective-permute-start | bytes 393224 | tf_op jit(solution)/shard_map/schur_z/ppermute | solution.py:322
  21.3 3.1 %collective-permute-start.2 = (bf16[2,256,128]{2,1,0:T(8,128)(2,1)S(1)}, bf16[2,256,128]{2,1,0:T(8,128)(2,1)S(1)}, u32[]{:S(2)}, u32[]{:S(2)}) collective-permute-start(bf16[2,256,128]{2,1,0:T(8,128)(2,1)S(1)} %pad_maximum_fusion), channel_id=1, source_target_pairs={{0,1},{1,0},{2,3},{3,2},{4,5},{5,4},{6,7},{7,6},{8,9},{9,8},{10,11... | collective-permute-start | bytes 393224 | tf_op jit(solution)/shard_map/schur_z/ppermute | solution.py:322
  24.4 15.1 %all-to-all-start = ((f32[8,72,128]{2,1,0:T(8,128)}), f32[8,72,128]{2,1,0:T(8,128)}, u32[]{:S(2)}, u32[]{:S(2)}) async-start(f32[8,72,128]{2,1,0:T(8,128)} %get-tuple-element.18), calls=%async_computation | async-start | bytes 589824 | tf_op jit(solution)/shard_map/all_to_all | solution.py:333
  39.6 4.6 %collective-permute-start.6 = (bf16[4,2,256,128]{3,2,1,0:T(8,128)(2,1)S(1)}, bf16[4,2,256,128]{3,2,1,0:T(8,128)(2,1)S(1)}, u32[]{:S(2)}, u32[]{:S(2)}) collective-permute-start(bf16[4,2,256,128]{3,2,1,0:T(8,128)(2,1)S(1)} %schur_z.1.refs_0_), channel_id=1, source_target_pairs={{0,24},{1,25},{2,26},{3,27},{4,28},{5,29},{6,30},{7,31},{8,0},{9,1... | collective-permute-start | bytes 1572872 | tf_op jit(solution)/shard_map/schur_y/ppermute | solution.py:326
  44.2 1.9 %collective-permute-start.5 = (bf16[4,2,256,128]{3,2,1,0:T(8,128)(2,1)S(1)}, bf16[4,2,256,128]{3,2,1,0:T(8,128)(2,1)S(1)}, u32[]{:S(2)}, u32[]{:S(2)}) collective-permute-start(bf16[4,2,256,128]{3,2,1,0:T(8,128)(2,1)S(1)} %schur_z.1.refs_0_), channel_id=1, source_target_pairs={{0,8},{1,9},{2,10},{3,11},{4,12},{5,13},{6,14},{7,15},{8,16},{9,17... | collective-permute-start | bytes 1572872 | tf_op jit(solution)/shard_map/schur_y/ppermute | solution.py:326
  46.2 18.9 %all-to-all-done.same_hbm = f32[8,72,128]{2,1,0:T(8,128)} async-done(((f32[8,72,128]{2,1,0:T(8,128)}), f32[8,72,128]{2,1,0:T(8,128)}, u32[]{:S(2)}, u32[]{:S(2)}) %all-to-all-start) | async-done | bytes 294944 | tf_op jit(solution)/shard_map/all_to_all | solution.py:333
  65.1 2.7 %collective-permute-start.1 = (f32[8,72,128]{2,1,0:T(8,128)}, f32[8,72,128]{2,1,0:T(8,128)S(1)}, u32[]{:S(2)}, u32[]{:S(2)}) collective-permute-start(f32[8,72,128]{2,1,0:T(8,128)} %all-to-all-done.same_hbm), channel_id=1, source_target_pairs={{0,32},{32,0},{64,96},{96,64},{128,160},{160,128},{192,224},{224,1... | collective-permute-start | bytes 884744 | tf_op jit(solution)/shard_map/ppermute | solution.py:334
  67.8 4.6 %collective-permute-start.8 = (bf16[2,2,256,128]{3,2,1,0:T(8,128)(2,1)S(1)}, bf16[2,2,256,128]{3,2,1,0:T(8,128)(2,1)S(1)}, u32[]{:S(2)}, u32[]{:S(2)}) collective-permute-start(bf16[2,2,256,128]{3,2,1,0:T(8,128)(2,1)S(1)} %slice.9), channel_id=1, source_target_pairs={{0,24},{1,25},{2,26},{3,27},{4,28},{5,29},{6,30},{7,31},{8,0},{9,1... | collective-permute-start | bytes 786440 | tf_op jit(solution)/shard_map/schur_y/ppermute | solution.py:326
  72.5 0.0 copy-start
  72.5 0.0 copy-start.1
  72.5 0.0 copy-start.2
  72.6 0.0 copy-start.3
  72.6 0.0 copy-start.5
  72.6 0.0 copy-start.7
  72.6 0.0 copy-start.10
  72.6 2.2 %collective-permute-start.7 = (bf16[2,2,256,128]{3,2,1,0:T(8,128)(2,1)S(1)}, bf16[2,2,256,128]{3,2,1,0:T(8,128)(2,1)S(1)}, u32[]{:S(2)}, u32[]{:S(2)}) collective-permute-start(bf16[2,2,256,128]{3,2,1,0:T(8,128)(2,1)S(1)} %slice.8), channel_id=1, source_target_pairs={{0,8},{1,9},{2,10},{3,11},{4,12},{5,13},{6,14},{7,15},{8,16},{9,17... | collective-permute-start | bytes 786440 | tf_op jit(solution)/shard_map/schur_y/ppermute | solution.py:326
  74.8 3.4 %shard_map.122 = (bf16[32,16,128]{2,1,0:T(8,128)(2,1)S(1)}, f32[16,8,128]{2,1,0:T(8,128)S(1)}) custom-call(f32[8,72,128]{2,1,0:T(8,128)} %all-to-all-done.same_hbm, f32[8,72,128]{2,1,0:T(8,128)S(1)} %collective-permute-done.1.other_hbm), custom_call_target="tpu_custom_call" | custom-call | flops 1000000000 | bytes 1048576 | tf_op jit(solution)/shard_map/pallas_call | solution.py:347
  78.2 5.4 %collective-permute-done.7.refs_3_ = bf16[2,2,256,128]{3,2,1,0:T(8,128)(2,1)S(1)} collective-permute-done((bf16[2,2,256,128]{3,2,1,0:T(8,128)(2,1)S(1)}, bf16[2,2,256,128]{3,2,1,0:T(8,128)(2,1)S(1)}, u32[]{:S(2)}, u32[]{:S(2)}) %collective-permute-start.7) | collective-permute-done | bytes 262176 | tf_op jit(solution)/shard_map/schur_y/ppermute | solution.py:326
  83.6 1.0 shard_map.123
  84.7 17.1 %all_to_all.20.same_hbm = f32[8,16,256]{2,1,0:T(8,128)S(1)} all-to-all(f32[8,16,256]{2,1,0:T(8,128)S(1)} %shard_map.123), channel_id=1, replica_groups={{0,64,128,192,256,320,384,448},{32,96,160,224,288,352,416,480},{1,65,12..., dimensions={0} | all-to-all | bytes 262144 | tf_op jit(solution)/shard_map/all_to_all | solution.py:333
  101.7 4.4 %collective-permute-start.9 = (f32[8,16,256]{2,1,0:T(8,128)S(1)}, f32[8,16,256]{2,1,0:T(8,128)S(1)}, u32[]{:S(2)}, u32[]{:S(2)}) collective-permute-start(f32[8,16,256]{2,1,0:T(8,128)S(1)} %all_to_all.20.same_hbm), channel_id=1, source_target_pairs={{0,32},{32,0},{64,96},{96,64},{128,160},{160,128},{192,224},{224,1... | collective-permute-start | bytes 393224 | tf_op jit(solution)/shard_map/ppermute | solution.py:334
  106.2 1.0 collective-permute-done.9.other_hbm
  107.2 4.8 %shard_map.124 = (f32[8,16,400]{2,1,0:T(8,128)S(1)}, f32[8,16,400]{2,1,0:T(8,128)S(1)}, f32[8,16,400]{2,1,0:T(8,128)S(1)}, bf16[8,64,128]{2,1,0:T(8,128)(2,1)S(1)}) custom-call(s32[16]{0:T(128)S(1)} %copy-done.9, s32[16]{0:T(128)S(1)} %copy-done.10, f32[8,16,256]{2,1,0:T(8,128)S(1)} %all_to_all.20.same_hbm, ...), custom_call_target="tpu_custom_call" | custom-call | flops 1000000000 | bytes 4194304 | tf_op jit(solution)/shard_map/pallas_call | solution.py:349
  112.0 19.5 %all_to_all.21.same_hbm = bf16[8,64,128]{2,1,0:T(8,128)(2,1)S(1)} all-to-all(bf16[8,64,128]{2,1,0:T(8,128)(2,1)S(1)} %get-tuple-element.22), channel_id=1, replica_groups={{0,64,128,192,256,320,384,448},{32,96,160,224,288,352,416,480},{1,65,12..., dimensions={0} | all-to-all | bytes 262144 | tf_op jit(solution)/shard_map/all_to_all | solution.py:333
  131.5 2.5 %collective-permute-start.10 = (bf16[8,64,128]{2,1,0:T(8,128)(2,1)S(1)}, bf16[8,64,128]{2,1,0:T(8,128)(2,1)S(1)}, u32[]{:S(2)}, u32[]{:S(2)}) collective-permute-start(bf16[8,64,128]{2,1,0:T(8,128)(2,1)S(1)} %all_to_all.21.same_hbm), channel_id=1, source_target_pairs={{0,32},{32,0},{64,96},{96,64},{128,160},{160,128},{192,224},{224,1... | collective-permute-start | bytes 393224 | tf_op jit(solution)/shard_map/ppermute | solution.py:334
  133.9 1.0 collective-permute-done.10.other_hbm
  134.9 4.2 %shard_map.125 = (f32[16,256]{1,0:T(8,128)}, bf16[16,16,256]{2,1,0:T(8,128)(2,1)S(1)}) custom-call(bf16[8,64,128]{2,1,0:T(8,128)(2,1)S(1)} %all_to_all.21.same_hbm, bf16[8,64,128]{2,1,0:T(8,128)(2,1)S(1)} %collective-permute-done.10.other_hbm, f32[16,8,128]{2,1,0:T(8,128)S(1)} %get-tuple-element.23.map_hbm, bf16[4,2,256,128]{3,2,1,0:T(8,128)(2,1)S(1)} %schur_z.1.refs_0_, ...), custom_call_target="tpu_custom_call" | custom-call | flops 1000000000 | bytes 3145728 | tf_op jit(solution)/shard_map/pallas_call | solution.py:350
  139.1 19.1 %all_to_all.22.recv_hbm = bf16[16,16,256]{2,1,0:T(8,128)(2,1)S(1)} all-to-all(bf16[16,16,256]{2,1,0:T(8,128)(2,1)S(1)} %get-tuple-element.24), channel_id=1, replica_groups=mesh['row'=16,'col'=32] {'row'}, dimensions={0} | all-to-all | bytes 262144 | tf_op jit(solution)/shard_map/all_to_all | solution.py:351
  158.2 2.4 %shard_map.126 = (f32[8,16,400]{2,1,0:T(8,128)}, f32[8,16,400]{2,1,0:T(8,128)}) custom-call(bf16[16,16,256]{2,1,0:T(8,128)(2,1)S(1)} %all_to_all.22.recv_hbm, f32[8,16,400]{2,1,0:T(8,128)S(1)} %get-tuple-element.25.prev_hbm, f32[8,16,400]{2,1,0:T(8,128)S(1)} %get-tuple-element.26.volt_hbm, f32[8,16,400]{2,1,0:T(8,128)S(1)} %get-tuple-element.27.curr_hbm, ...), custom_call_target="tpu_custom_call" | custom-call | flops 1000000000 | bytes 2097152 | tf_op jit(solution)/shard_map/pallas_call | solution.py:351
  (27 shorter events, 0.1 us)
Async XLA Ops:
  0.6 13.3 %copy-start.6 = (bf16[256,128]{1,0:T(8,128)(2,1)S(1)}, bf16[256,128]{1,0:T(8,128)(2,1)}, u32[]{:S(2)}) copy-start(bf16[256,128]{1,0:T(8,128)(2,1)} %own_ref.1) | copy-start | bytes 196612
  0.6 13.3 %collective-permute-start = (bf16[256,128]{1,0:T(8,128)(2,1)}, bf16[256,128]{1,0:T(8,128)(2,1)S(1)}, u32[]{:S(2)}, u32[]{:S(2)}) collective-permute-start(bf16[256,128]{1,0:T(8,128)(2,1)} %own_ref.1), channel_id=1, source_target_pairs={{0,4},{1,5},{2,6},{3,7},{4,0},{5,1},{6,2},{7,3},{8,12},{9,13},{10,... | collective-permute-start | bytes 196616 | tf_op jit(solution)/shard_map/schur_z/ppermute | solution.py:322
  13.9 25.6 %collective-permute-start.4 = (bf16[2,256,128]{2,1,0:T(8,128)(2,1)S(1)}, bf16[2,256,128]{2,1,0:T(8,128)(2,1)S(1)}, u32[]{:S(2)}, u32[]{:S(2)}) collective-permute-start(bf16[2,256,128]{2,1,0:T(8,128)(2,1)S(1)} %pad_maximum_fusion), channel_id=1, source_target_pairs={{0,3},{1,2},{2,1},{3,0},{4,7},{5,6},{6,5},{7,4},{8,11},{9,10},{10,... | collective-permute-start | bytes 393224 | tf_op jit(solution)/shard_map/schur_z/ppermute | solution.py:322
  17.5 22.0 %collective-permute-start.3 = (bf16[2,256,128]{2,1,0:T(8,128)(2,1)S(1)}, bf16[2,256,128]{2,1,0:T(8,128)(2,1)S(1)}, u32[]{:S(2)}, u32[]{:S(2)}) collective-permute-start(bf16[2,256,128]{2,1,0:T(8,128)(2,1)S(1)} %pad_maximum_fusion), channel_id=1, source_target_pairs={{0,2},{1,3},{2,0},{3,1},{4,6},{5,7},{6,4},{7,5},{8,10},{9,11},{10,... | collective-permute-start | bytes 393224 | tf_op jit(solution)/shard_map/schur_z/ppermute | solution.py:322
  21.3 18.3 %collective-permute-start.2 = (bf16[2,256,128]{2,1,0:T(8,128)(2,1)S(1)}, bf16[2,256,128]{2,1,0:T(8,128)(2,1)S(1)}, u32[]{:S(2)}, u32[]{:S(2)}) collective-permute-start(bf16[2,256,128]{2,1,0:T(8,128)(2,1)S(1)} %pad_maximum_fusion), channel_id=1, source_target_pairs={{0,1},{1,0},{2,3},{3,2},{4,5},{5,4},{6,7},{7,6},{8,9},{9,8},{10,11... | collective-permute-start | bytes 393224 | tf_op jit(solution)/shard_map/schur_z/ppermute | solution.py:322
  24.4 40.7 %all-to-all-start = ((f32[8,72,128]{2,1,0:T(8,128)}), f32[8,72,128]{2,1,0:T(8,128)}, u32[]{:S(2)}, u32[]{:S(2)}) async-start(f32[8,72,128]{2,1,0:T(8,128)} %get-tuple-element.18), calls=%async_computation | async-start | bytes 589824 | tf_op jit(solution)/shard_map/all_to_all | solution.py:333
  39.6 28.2 %collective-permute-start.6 = (bf16[4,2,256,128]{3,2,1,0:T(8,128)(2,1)S(1)}, bf16[4,2,256,128]{3,2,1,0:T(8,128)(2,1)S(1)}, u32[]{:S(2)}, u32[]{:S(2)}) collective-permute-start(bf16[4,2,256,128]{3,2,1,0:T(8,128)(2,1)S(1)} %schur_z.1.refs_0_), channel_id=1, source_target_pairs={{0,24},{1,25},{2,26},{3,27},{4,28},{5,29},{6,30},{7,31},{8,0},{9,1... | collective-permute-start | bytes 1572872 | tf_op jit(solution)/shard_map/schur_y/ppermute | solution.py:326
  44.2 28.3 %collective-permute-start.5 = (bf16[4,2,256,128]{3,2,1,0:T(8,128)(2,1)S(1)}, bf16[4,2,256,128]{3,2,1,0:T(8,128)(2,1)S(1)}, u32[]{:S(2)}, u32[]{:S(2)}) collective-permute-start(bf16[4,2,256,128]{3,2,1,0:T(8,128)(2,1)S(1)} %schur_z.1.refs_0_), channel_id=1, source_target_pairs={{0,8},{1,9},{2,10},{3,11},{4,12},{5,13},{6,14},{7,15},{8,16},{9,17... | collective-permute-start | bytes 1572872 | tf_op jit(solution)/shard_map/schur_y/ppermute | solution.py:326
  65.1 9.7 %collective-permute-start.1 = (f32[8,72,128]{2,1,0:T(8,128)}, f32[8,72,128]{2,1,0:T(8,128)S(1)}, u32[]{:S(2)}, u32[]{:S(2)}) collective-permute-start(f32[8,72,128]{2,1,0:T(8,128)} %all-to-all-done.same_hbm), channel_id=1, source_target_pairs={{0,32},{32,0},{64,96},{96,64},{128,160},{160,128},{192,224},{224,1... | collective-permute-start | bytes 884744 | tf_op jit(solution)/shard_map/ppermute | solution.py:334
  67.8 10.4 %collective-permute-start.8 = (bf16[2,2,256,128]{3,2,1,0:T(8,128)(2,1)S(1)}, bf16[2,2,256,128]{3,2,1,0:T(8,128)(2,1)S(1)}, u32[]{:S(2)}, u32[]{:S(2)}) collective-permute-start(bf16[2,2,256,128]{3,2,1,0:T(8,128)(2,1)S(1)} %slice.9), channel_id=1, source_target_pairs={{0,24},{1,25},{2,26},{3,27},{4,28},{5,29},{6,30},{7,31},{8,0},{9,1... | collective-permute-start | bytes 786440 | tf_op jit(solution)/shard_map/schur_y/ppermute | solution.py:326
  72.5 34.6 %copy-start = (bf16[8,400,400]{2,1,0:T(8,128)(2,1)S(1)}, bf16[8,400,400]{2,1,0:T(8,128)(2,1)}, u32[]{:S(2)}) copy-start(bf16[8,400,400]{2,1,0:T(8,128)(2,1)} %inv_hbm.5) | copy-start | bytes 7680004
  72.5 34.6 %copy-start.1 = (s32[8,16,400]{2,1,0:T(8,128)S(1)}, s32[8,16,400]{2,1,0:T(8,128)}, u32[]{:S(2)}) copy-start(s32[8,16,400]{2,1,0:T(8,128)} %breaker_hbm.5) | copy-start | bytes 614404
  72.5 34.6 %copy-start.2 = (f32[8,16,400]{2,1,0:T(8,128)S(1)}, f32[8,16,400]{2,1,0:T(8,128)}, u32[]{:S(2)}) copy-start(f32[8,16,400]{2,1,0:T(8,128)} %volt_hbm.3) | copy-start | bytes 614404
  72.6 34.6 %copy-start.3 = (f32[8,16,400]{2,1,0:T(8,128)S(1)}, f32[8,16,400]{2,1,0:T(8,128)}, u32[]{:S(2)}) copy-start(f32[8,16,400]{2,1,0:T(8,128)} %curr_hbm.3) | copy-start | bytes 614404
  72.6 34.6 %copy-start.4 = (f32[8,16,400]{2,1,0:T(8,128)S(1)}, f32[8,16,400]{2,1,0:T(8,128)}, u32[]{:S(2)}) copy-start(f32[8,16,400]{2,1,0:T(8,128)} %get-tuple-element.21.prev_hbm) | copy-start | bytes 614404
  72.6 34.6 %copy-start.5 = (f32[8,400]{1,0:T(8,128)S(1)}, f32[8,400]{1,0:T(8,128)}, u32[]{:S(2)}) copy-start(f32[8,400]{1,0:T(8,128)} %gain_hbm.5) | copy-start | bytes 38404
  72.6 34.6 %copy-start.7 = (f32[8,64]{1,0:T(8,128)S(1)}, f32[8,64]{1,0:T(8,128)}, u32[]{:S(2)}) copy-start(f32[8,64]{1,0:T(8,128)} %tie_hbm.5) | copy-start | bytes 6148
  72.6 34.6 %copy-start.8 = (s32[8,64]{1,0:T(8,128)S(1)}, s32[8,64]{1,0:T(8,128)}, u32[]{:S(2)}) copy-start(s32[8,64]{1,0:T(8,128)} %map_hbm.5) | copy-start | bytes 6148
  72.6 34.6 %copy-start.9 = (s32[16]{0:T(128)S(1)}, s32[16]{0:T(128)}, u32[]{:S(2)}) copy-start(s32[16]{0:T(128)} %time_ref.3) | copy-start | bytes 196
  72.6 34.6 %copy-start.10 = (s32[16]{0:T(128)S(1)}, s32[16]{0:T(128)}, u32[]{:S(2)}) copy-start(s32[16]{0:T(128)} %node_ref.3) | copy-start | bytes 196
  72.6 11.0 %collective-permute-start.7 = (bf16[2,2,256,128]{3,2,1,0:T(8,128)(2,1)S(1)}, bf16[2,2,256,128]{3,2,1,0:T(8,128)(2,1)S(1)}, u32[]{:S(2)}, u32[]{:S(2)}) collective-permute-start(bf16[2,2,256,128]{3,2,1,0:T(8,128)(2,1)S(1)} %slice.8), channel_id=1, source_target_pairs={{0,8},{1,9},{2,10},{3,11},{4,12},{5,13},{6,14},{7,15},{8,16},{9,17... | collective-permute-start | bytes 786440 | tf_op jit(solution)/shard_map/schur_y/ppermute | solution.py:326
  101.7 5.4 %collective-permute-start.9 = (f32[8,16,256]{2,1,0:T(8,128)S(1)}, f32[8,16,256]{2,1,0:T(8,128)S(1)}, u32[]{:S(2)}, u32[]{:S(2)}) collective-permute-start(f32[8,16,256]{2,1,0:T(8,128)S(1)} %all_to_all.20.same_hbm), channel_id=1, source_target_pairs={{0,32},{32,0},{64,96},{96,64},{128,160},{160,128},{192,224},{224,1... | collective-permute-start | bytes 393224 | tf_op jit(solution)/shard_map/ppermute | solution.py:334
  131.5 3.4 %collective-permute-start.10 = (bf16[8,64,128]{2,1,0:T(8,128)(2,1)S(1)}, bf16[8,64,128]{2,1,0:T(8,128)(2,1)S(1)}, u32[]{:S(2)}, u32[]{:S(2)}) collective-permute-start(bf16[8,64,128]{2,1,0:T(8,128)(2,1)S(1)} %all_to_all.21.same_hbm), channel_id=1, source_target_pairs={{0,32},{32,0},{64,96},{96,64},{128,160},{160,128},{192,224},{224,1... | collective-permute-start | bytes 393224 | tf_op jit(solution)/shard_map/ppermute | solution.py:334

commit v7 on v6

--- a/solution.py
+++ b/solution.py
@@ -1,5 +1,3 @@
-import functools
-
 import jax
 import jax.numpy as jnp
 from jax import lax
@@ -20,6 +18,7 @@
 VALUE_ROWS = TILES * SCEN
 MAP_ROWS = 2 * TILES
 CORES = [[2 * n + core for n in range(ROWS // 2)] for core in range(2)]
+PAIRS = [[2 * n, 2 * n + 1] for n in range(ROWS // 2)]
 VMEM_BYTES = 16 << 20
 ALL_VMEM = 60 << 20
 BF16, F32 = jnp.bfloat16, jnp.float32
@@ -90,7 +89,7 @@
             send_ref[r, t * SCEN : (t + 1) * SCEN, :] = tile
 
 
-def first_kernel(time_ref, node_ref, volt_hbm, curr_hbm, breaker_hbm, gain_hbm, tie_hbm, map_hbm, inv_hbm, open_ref, send_ref, map_ref, gain_ref, tie_ref, volt_ref, curr_ref, breaker_ref, inv_ref, sems):
+def first_kernel(time_ref, node_ref, volt_hbm, curr_hbm, breaker_hbm, gain_hbm, tie_hbm, map_hbm, inv_hbm, open_ref, send_ref, right_ref, rows_ref, map_ref, gain_ref, tie_ref, volt_ref, curr_ref, breaker_ref, inv_ref, sems):
     copies = fetch(
         [map_hbm, gain_hbm, tie_hbm, volt_hbm, curr_hbm, breaker_hbm] + each(inv_hbm, SUBS),
         [map_ref, gain_ref, tie_ref, volt_ref, curr_ref, breaker_ref] + each(inv_ref, SUBS),
@@ -103,6 +102,9 @@
     for r in range(send_ref.shape[0]):
         send_ref[r, VALUE_ROWS:, :] = tail
     wait_for(copies[1:6])
+    low = lax.broadcasted_iota(jnp.int32, (BLOCK, OWN), 0)
+    right_ref[...] = jnp.where(low == mapped % BLOCK, 1.0, 0.0).astype(BF16)
+    rows_ref[...] = jnp.concatenate([(mapped // BLOCK).astype(F32), flat_row(tie_ref), jnp.zeros((6, OWN), F32)], axis=0)
     open_circuit(0, volt_ref, curr_ref, breaker_ref, gain_ref, copies[6:], inv_ref, time_ref, node_ref, tie_ref, open_ref, send_ref)
 
 
@@ -156,13 +158,8 @@
             rhs_ref[2 * h + side] = rhs[h, :, side * LANES : (side + 1) * LANES]
 
 
-def two_parts(same, other, ref):
-    half = ROWS // 2
-    return [same, other], [ref.at[pl.ds(0, half)], ref.at[pl.ds(half, half)]]
-
-
-def rhs_kernel(same_hbm, other_hbm, rhs_ref, map_out, recv_ref, sems):
-    wait_for(fetch(*two_parts(same_hbm, other_hbm, recv_ref), sems))
+def rhs_kernel(recv_hbm, rhs_ref, map_out, recv_ref, sems):
+    wait_for(fetch([recv_hbm], [recv_ref], sems))
     map_out[...] = recv_ref[:, VALUE_ROWS:, :]
     keep(right_hand_side(recv_ref, map_out), rhs_ref)
 
@@ -176,10 +173,9 @@
         send_ref[r] = total
 
 
-def interface_kernel(same_hbm, other_hbm, map_hbm, *refs):
+def interface_kernel(recv_hbm, map_hbm, *refs):
     parts, (iface_ref, send_ref, schur_ref, rhs_ref, recv_ref, map_ref, sems, recv_sems) = refs[:5], refs[5:]
-    sources, targets = two_parts(same_hbm, other_hbm, recv_ref)
-    arrived = fetch([map_hbm] + sources, [map_ref] + targets, recv_sems)
+    arrived = fetch([map_hbm, recv_hbm], [map_ref, recv_ref], recv_sems)
     copies = schur_copies(parts, schur_ref, sems)
     wait_for(arrived)
     keep(right_hand_side(recv_ref, map_ref), rhs_ref)
@@ -190,17 +186,14 @@
         send_ref[r] = half
 
 
-def driven(recv_ref, map_ref, tie_ref, sender):
-    mapped = flat_row(map_ref)
-    hi = mapped // BLOCK
-    low = lax.broadcasted_iota(jnp.int32, (BLOCK, OWN), 0)
-    right = jnp.where(low == mapped % BLOCK, 1.0, 0.0).astype(BF16)
+def driven(recv_ref, right_ref, rows_ref, sender):
+    hi = rows_ref[0:1, :].astype(jnp.int32)
     volts = recv_ref[...].reshape(ROWS * SCEN, BLOCK)
-    found = sum(dot(part, right) for part in (halves(volts) if volts.dtype == F32 else (volts,)))
+    found = sum(dot(part, right_ref[...]) for part in (halves(volts) if volts.dtype == F32 else (volts,)))
     picked = jnp.zeros((SCEN, OWN), F32)
-    for r in range(ROWS):
-        picked += jnp.where(hi == sender(r), found[r * SCEN : (r + 1) * SCEN, :], 0.0)
-    return (flat_row(tie_ref) * picked).astype(BF16)
+    for n in range(ROWS):
+        picked += jnp.where(hi == sender(n), found[n * SCEN : (n + 1) * SCEN, :], 0.0)
+    return (rows_ref[1:2, :] * picked).astype(BF16)
 
 
 def update(k, drive, open_ref, inv, volt, curr, breaker_ref, gain_ref):
@@ -210,35 +203,32 @@
 
 
 def paired_sender(place):
-    core = lax.axis_index("row") % 2
-    half = ROWS // 2
-    return 2 * place + core if place < half else 2 * (place - half) + 1 - core
-
-
-def middle_kernel(time_ref, node_ref, same_hbm, other_hbm, prev_hbm, volt_hbm, curr_hbm, breaker_hbm, gain_hbm, tie_hbm, map_hbm, inv_hbm, volt_out, curr_out, open_ref, send_ref, recv_ref, prev_ref, map_ref, gain_ref, tie_ref, volt_ref, curr_ref, breaker_ref, inv_ref, sems):
-    sources, targets = two_parts(same_hbm, other_hbm, recv_ref)
+    return 2 * (place % (ROWS // 2)) + place // (ROWS // 2)
+
+
+def middle_kernel(time_ref, node_ref, recv_hbm, prev_hbm, volt_hbm, curr_hbm, breaker_hbm, gain_hbm, tie_hbm, right_hbm, rows_hbm, inv_hbm, volt_out, curr_out, open_ref, send_ref, recv_ref, prev_ref, right_ref, rows_ref, gain_ref, tie_ref, volt_ref, curr_ref, breaker_ref, inv_ref, sems):
     copies = fetch(
-        [map_hbm, tie_hbm] + sources + [gain_hbm, prev_hbm, volt_hbm, curr_hbm, breaker_hbm] + each(inv_hbm, SUBS),
-        [map_ref, tie_ref] + targets + [gain_ref, prev_ref, volt_ref, curr_ref, breaker_ref] + each(inv_ref, SUBS),
+        [right_hbm, rows_hbm, recv_hbm, prev_hbm, volt_hbm, curr_hbm, breaker_hbm, gain_hbm, tie_hbm] + each(inv_hbm, SUBS),
+        [right_ref, rows_ref, recv_ref, prev_ref, volt_ref, curr_ref, breaker_ref, gain_ref, tie_ref] + each(inv_ref, SUBS),
         sems,
     )
-    wait_for(copies[:4])
-    drive = driven(recv_ref, map_ref, tie_ref, paired_sender)
-    wait_for(copies[4:9])
+    wait_for(copies[:3])
+    drive = driven(recv_ref, right_ref, rows_ref, paired_sender)
+    wait_for(copies[3:9])
     for k in range(SUBS):
         copies[9 + k].wait()
         volt_out[k], curr_out[k] = update(k, drive, prev_ref, inv_ref[k, :PORTS, :], volt_ref[k], curr_ref[k], breaker_ref, gain_ref)
     open_circuit(1, volt_out, curr_out, breaker_ref, gain_ref, None, inv_ref, time_ref, node_ref, tie_ref, open_ref, send_ref)
 
 
-def last_kernel(recv_hbm, prev_hbm, volt_hbm, curr_hbm, breaker_hbm, gain_hbm, tie_hbm, map_hbm, inv_hbm, volt_out, curr_out, recv_ref, prev_ref, map_ref, gain_ref, tie_ref, volt_ref, curr_ref, breaker_ref, inv_ref, sems):
+def last_kernel(recv_hbm, prev_hbm, volt_hbm, curr_hbm, breaker_hbm, gain_hbm, right_hbm, rows_hbm, inv_hbm, volt_out, curr_out, recv_ref, prev_ref, right_ref, rows_ref, gain_ref, volt_ref, curr_ref, breaker_ref, inv_ref, sems):
     copies = fetch(
-        [map_hbm, tie_hbm, recv_hbm, gain_hbm, prev_hbm, volt_hbm, curr_hbm, breaker_hbm] + [inv_hbm.at[k, pl.ds(0, PORTS)] for k in range(SUBS)],
-        [map_ref, tie_ref, recv_ref, gain_ref, prev_ref, volt_ref, curr_ref, breaker_ref] + each(inv_ref, SUBS),
+        [right_hbm, rows_hbm, recv_hbm, prev_hbm, volt_hbm, curr_hbm, breaker_hbm, gain_hbm] + [inv_hbm.at[k, pl.ds(0, PORTS)] for k in range(SUBS)],
+        [right_ref, rows_ref, recv_ref, prev_ref, volt_ref, curr_ref, breaker_ref, gain_ref] + each(inv_ref, SUBS),
         sems,
     )
     wait_for(copies[:3])
-    drive = driven(recv_ref, map_ref, tie_ref, lambda place: place)
+    drive = driven(recv_ref, right_ref, rows_ref, lambda place: place)
     wait_for(copies[3:])
     for k in range(SUBS):
         volt_out[k], curr_out[k] = update(k, drive, prev_ref, inv_ref[k], volt_ref[k], curr_ref[k], breaker_ref, gain_ref)
@@ -264,8 +254,10 @@
     return [pltpu.SemaphoreType.DMA((count,))]
 
 
-SMALL = held(((SUBS, PORTS), jnp.int32), ((SUBS, NODES), F32), ((SUBS, PORTS), F32))
+GAIN, TIE = held(((SUBS, NODES), F32), ((SUBS, PORTS), F32))
 BREAKER = held(((SUBS, SCEN, NODES), jnp.int32))
+INVERSE = held(((SUBS, NODES, NODES), BF16))
+PICK = [((BLOCK, OWN), BF16), ((8, OWN), F32)]
 
 
 def call(body, ins, outs, scratch, flops, moved, vmem=VMEM_BYTES):
@@ -283,20 +275,20 @@
 first = call(
     first_kernel,
     [SMEM] * 2 + [HBM] * 7,
-    [STATE, ((ROWS // 2, VALUE_ROWS + MAP_ROWS, LANES), F32)],
-    SMALL + held(STATE, STATE) + BREAKER + held(((SUBS, NODES, NODES), BF16)) + copies_of(6 + SUBS),
+    [STATE, ((ROWS // 2, VALUE_ROWS + MAP_ROWS, LANES), F32)] + PICK,
+    held(((SUBS, PORTS), jnp.int32)) + [GAIN, TIE] + held(STATE, STATE) + BREAKER + INVERSE + copies_of(6 + SUBS),
     GIGA,
     4 << 20,
     ALL_VMEM,
 )
 join = call(join_kernel, [VMEM] * 5, [((4, 2, BLOCK, LANES), BF16)], [], 100_000 * GIGA, 1 << 20, 8 << 20)
-summed = call(rhs_kernel, [HBM] * 2, [RHS, MAPS], held(((ROWS, VALUE_ROWS + MAP_ROWS, LANES), F32)) + copies_of(2), GIGA, 1 << 20)
+summed = call(rhs_kernel, [HBM], [RHS, MAPS], held(((ROWS, VALUE_ROWS + MAP_ROWS, LANES), F32)) + copies_of(1), GIGA, 1 << 20)
 product = call(product_kernel, [HBM] * 6, [((ROWS // 2, SCEN, BLOCK), F32)], held(SCHUR, RHS) + copies_of(5) + copies_of(1), GIGA, 3 << 20)
 interface = call(
     interface_kernel,
-    [HBM] * 8,
+    [HBM] * 7,
     [(FACE[1:], F32), (FACE, BF16)],
-    held(SCHUR, RHS, ((ROWS, VALUE_ROWS, LANES), BF16), MAPS) + copies_of(5) + copies_of(3),
+    held(SCHUR, RHS, ((ROWS, VALUE_ROWS, LANES), BF16), MAPS) + copies_of(5) + copies_of(2),
     GIGA,
     3 << 20,
 )
@@ -304,7 +296,7 @@
     middle_kernel,
     [SMEM] * 2 + [HBM] * 10,
     [STATE, STATE, STATE, ((ROWS // 2, VALUE_ROWS, LANES), BF16)],
-    held((FACE, F32), STATE) + SMALL + held(STATE, STATE) + BREAKER + held(((SUBS, NODES, NODES), BF16)) + copies_of(9 + SUBS),
+    held((FACE, F32), STATE, *PICK) + [GAIN, TIE] + held(STATE, STATE) + BREAKER + INVERSE + copies_of(9 + SUBS),
     GIGA,
     4 << 20,
 )
@@ -312,7 +304,7 @@
     last_kernel,
     [HBM] * 9,
     [STATE, STATE],
-    held((FACE, BF16), STATE) + SMALL + held(STATE, STATE) + BREAKER + held(((SUBS, PORTS, NODES), BF16)) + copies_of(8 + SUBS),
+    held((FACE, BF16), STATE, *PICK) + [GAIN] + held(STATE, STATE) + BREAKER + held(((SUBS, PORTS, NODES), BF16)) + copies_of(8 + SUBS),
     GIGA,
     2 << 20,
 )
@@ -326,17 +318,19 @@
     return lax.ppermute(block, "col", [(c, (c + 8 * steps) % COLS) for c in range(COLS)])
 
 
+def exchange(send, groups=None):
+    return lax.all_to_all(send, "row", 0, 0, axis_index_groups=groups)
+
+
+def paired_exchange(send):
+    both = lax.all_gather(exchange(send, CORES), "row", axis_index_groups=PAIRS)
+    return both.reshape(ROWS, *send.shape[1:])
+
+
 def local(volt, curr, local_inverse, schur_inverse, ind_gain, tie, port_map, breaker, fault_time, fault_node):
-    exchange = functools.partial(lax.all_to_all, axis_name="row", split_axis=0, concat_axis=0)
-
-    def paired_exchange(send):
-        same = exchange(send, axis_index_groups=CORES)
-        return same, lax.ppermute(same, "row", [(r, r ^ 1) for r in range(ROWS)])
-
-    fixed = breaker, ind_gain, tie, port_map, local_inverse
     with jax.named_scope("schur_z"):
         across = along_z(schur_inverse, 4)
-    opened, send = first(fault_time, fault_node, volt, curr, *fixed)
+    opened, send, *pick = first(fault_time, fault_node, volt, curr, breaker, ind_gain, tie, port_map, local_inverse)
     across, send = lax.optimization_barrier((across, send))
     with jax.named_scope("schur_z"):
         pair = jnp.stack([schur_inverse, across])
@@ -344,11 +338,11 @@
     with jax.named_scope("schur_y"):
         back, ahead = along_y(own, 1), along_y(own, -1)
         schur_rows = own, back, ahead, along_y(back[:2], 1), along_y(ahead[2:], -1)
-    rhs, maps = summed(*paired_exchange(send))
+    rhs, maps = summed(paired_exchange(send))
     (send,) = product(rhs, *schur_rows)
-    volt, curr, opened, send = middle(fault_time, fault_node, *paired_exchange(send), opened, volt, curr, *fixed)
-    iface_block, send = interface(*paired_exchange(send), maps, *schur_rows)
-    volt, curr = last(exchange(send), opened, volt, curr, *fixed)
+    volt, curr, opened, send = middle(fault_time, fault_node, paired_exchange(send), opened, volt, curr, breaker, ind_gain, tie, *pick, local_inverse)
+    iface_block, send = interface(paired_exchange(send), maps, *schur_rows)
+    volt, curr = last(exchange(send), opened, volt, curr, breaker, ind_gain, *pick, local_inverse)
     return volt, curr, iface_block
 
 

time: 161 us -> 159 us (0.988)
  blocking collectives: 55.6 us -> 78.6 us
  waiting for transfers between devices: 26.3 us -> 11.6 us
  starting transfers between devices: 57.4 us -> 48.2 us
    all_to_all x1, waiting for transfers between devices: 18.9 us -> 4.17 us  [exchange(): return lax.all_to_all(send, 'row', 0, 0, axis_index_groups=groups)]
    all_gather x0 -> x3, blocking collectives: none -> 12.4 us  [paired_exchange(): both = lax.all_gather(exchange(send, CORES), 'row', axis_index_groups=PAIRS)]
    all_to_all x3, blocking collectives: 55.6 us -> 66.2 us  [exchange(): return lax.all_to_all(send, 'row', 0, 0, axis_index_groups=groups)]
    ppermute x3 -> x0, starting transfers between devices: 9.55 us -> none  [paired_exchange(): return (same, lax.ppermute(same, 'row', [(r, r ^ 1) for r in range(ROWS)]))]
    ppermute x4, waiting for transfers between devices: 5.41 us -> 7.47 us  [along_y(): lax.ppermute(block, 'col', [(c, (c + 8 * steps) % COLS) for c in range(CO...]
    ppermute x3 -> x0, waiting for transfers between devices: 1.93 us -> none  [paired_exchange(): return (same, lax.ppermute(same, 'row', [(r, r ^ 1) for r in range(ROWS)]))]
  transfers between devices with their start and end apart: 12 -> 9, of which waited for: 4 -> 2; matrix products, arithmetic and copies ran while one was open for 0% -> 0% of each run, Pallas kernels for 5% -> 4%
where the time goes in v7:
time: 159 us; the launch traced here: 158 us
  blocking collectives  78.6 us (49%)
  starting transfers between devices  48.2 us (30%)
  Pallas kernels  18.7 us (12%)
  waiting for transfers between devices  11.6 us (7%)
    all_to_all x3, blocking collectives, exchange(): return lax.all_to_all(send, 'row', 0, 0, axis_index_groups=groups)  66.2 us
    ppermute x4, starting transfers between devices, along_z(): return lax.ppermute(block, 'col', [(c, c ^ flip) for c in range(COLS)])  19.3 us
    all_to_all x1, starting transfers between devices, exchange(): return lax.all_to_all(send, 'row', 0, 0, axis_index_groups=groups)  15.1 us
    ppermute x4, starting transfers between devices, along_y(): lax.ppermute(block, 'col', [(c, (c + 8 * steps) % COLS) for c in range(CO...  13.8 us
    all_gather x3, blocking collectives, paired_exchange(): both = lax.all_gather(exchange(send, CORES), 'row', axis_index_groups=PAIRS)  12.4 us
    ppermute x4, waiting for transfers between devices, along_y(): lax.ppermute(block, 'col', [(c, (c + 8 * steps) % COLS) for c in range(CO...  7.47 us
    pallas_call x1, Pallas kernels, local(): middle(fault_time, fault_node, paired_exchange(send), opened, volt, curr,...  4.44 us
    pallas_call x1, Pallas kernels, local(): first(fault_time, fault_node, volt, curr, breaker, ind_gain, tie, port_ma...  4.38 us
  transfers between devices with their start and end apart: 9, of which 2 were waited for; matrix products, arithmetic and copies ran while one was open for 0% of the time, Pallas kernels for 4%

profile of v7, /device:TPU:33, one launch (start us, length us, event | category | flops | bytes accessed | tf_op | source)
XLA Modules:
  0.0 158.2 jit_solution(10418293130128558484)
XLA Ops:
  0.6 8.9 %collective-permute-start = (bf16[256,128]{1,0:T(8,128)(2,1)}, bf16[256,128]{1,0:T(8,128)(2,1)S(1)}, u32[]{:S(2)}, u32[]{:S(2)}) collective-permute-start(bf16[256,128]{1,0:T(8,128)(2,1)} %own_ref.1), channel_id=1, source_target_pairs={{0,4},{1,5},{2,6},{3,7},{4,0},{5,1},{6,2},{7,3},{8,12},{9,13},{10,... | collective-permute-start | bytes 196616 | tf_op jit(solution)/shard_map/schur_z/ppermute | solution.py:314
  9.6 4.4 %shard_map.121 = (f32[8,16,400]{2,1,0:T(8,128)}, f32[8,72,128]{2,1,0:T(8,128)}, bf16[256,512]{1,0:T(8,128)(2,1)}, f32[8,512]{1,0:T(8,128)}) custom-call(s32[16]{0:T(128)} %time_ref.3, s32[16]{0:T(128)} %node_ref.3, f32[8,16,400]{2,1,0:T(8,128)} %volt_hbm.3, f32[8,16,400]{2,1,0:T(8,128)} %curr_hbm.3, s32[8,16,400]{2,1,0:T(8,128)} %breaker_hbm.5, ...), custom_call_target="tpu_custom_call" | custom-call | flops 1000000000 | bytes 4194304 | tf_op jit(solution)/shard_map/pallas_call | solution.py:333
  14.0 0.0 collective-permute-done.across_ref
  14.0 3.5 %collective-permute-start.3 = (bf16[2,256,128]{2,1,0:T(8,128)(2,1)S(1)}, bf16[2,256,128]{2,1,0:T(8,128)(2,1)S(1)}, u32[]{:S(2)}, u32[]{:S(2)}) collective-permute-start(bf16[2,256,128]{2,1,0:T(8,128)(2,1)S(1)} %pad_maximum_fusion), channel_id=1, source_target_pairs={{0,3},{1,2},{2,1},{3,0},{4,7},{5,6},{6,5},{7,4},{8,11},{9,10},{10,... | collective-permute-start | bytes 393224 | tf_op jit(solution)/shard_map/schur_z/ppermute | solution.py:314
  17.6 3.7 %collective-permute-start.2 = (bf16[2,256,128]{2,1,0:T(8,128)(2,1)S(1)}, bf16[2,256,128]{2,1,0:T(8,128)(2,1)S(1)}, u32[]{:S(2)}, u32[]{:S(2)}) collective-permute-start(bf16[2,256,128]{2,1,0:T(8,128)(2,1)S(1)} %pad_maximum_fusion), channel_id=1, source_target_pairs={{0,2},{1,3},{2,0},{3,1},{4,6},{5,7},{6,4},{7,5},{8,10},{9,11},{10,... | collective-permute-start | bytes 393224 | tf_op jit(solution)/shard_map/schur_z/ppermute | solution.py:314
  21.3 3.1 %collective-permute-start.1 = (bf16[2,256,128]{2,1,0:T(8,128)(2,1)S(1)}, bf16[2,256,128]{2,1,0:T(8,128)(2,1)S(1)}, u32[]{:S(2)}, u32[]{:S(2)}) collective-permute-start(bf16[2,256,128]{2,1,0:T(8,128)(2,1)S(1)} %pad_maximum_fusion), channel_id=1, source_target_pairs={{0,1},{1,0},{2,3},{3,2},{4,5},{5,4},{6,7},{7,6},{8,9},{9,8},{10,11... | collective-permute-start | bytes 393224 | tf_op jit(solution)/shard_map/schur_z/ppermute | solution.py:314
  24.4 15.1 %all-to-all-start = ((f32[8,72,128]{2,1,0:T(8,128)}), f32[8,72,128]{2,1,0:T(8,128)}, u32[]{:S(2)}, u32[]{:S(2)}) async-start(f32[8,72,128]{2,1,0:T(8,128)} %get-tuple-element.20), calls=%async_computation | async-start | bytes 589824 | tf_op jit(solution)/shard_map/all_to_all | solution.py:322
  39.5 0.0 collective-permute-done.3.refs_2_
  39.6 4.6 %collective-permute-start.5 = (bf16[4,2,256,128]{3,2,1,0:T(8,128)(2,1)S(1)}, bf16[4,2,256,128]{3,2,1,0:T(8,128)(2,1)S(1)}, u32[]{:S(2)}, u32[]{:S(2)}) collective-permute-start(bf16[4,2,256,128]{3,2,1,0:T(8,128)(2,1)S(1)} %schur_z.1.refs_0_), channel_id=1, source_target_pairs={{0,24},{1,25},{2,26},{3,27},{4,28},{5,29},{6,30},{7,31},{8,0},{9,1... | collective-permute-start | bytes 1572872 | tf_op jit(solution)/shard_map/schur_y/ppermute | solution.py:318
  44.2 1.9 %collective-permute-start.4 = (bf16[4,2,256,128]{3,2,1,0:T(8,128)(2,1)S(1)}, bf16[4,2,256,128]{3,2,1,0:T(8,128)(2,1)S(1)}, u32[]{:S(2)}, u32[]{:S(2)}) collective-permute-start(bf16[4,2,256,128]{3,2,1,0:T(8,128)(2,1)S(1)} %schur_z.1.refs_0_), channel_id=1, source_target_pairs={{0,8},{1,9},{2,10},{3,11},{4,12},{5,13},{6,14},{7,15},{8,16},{9,17... | collective-permute-start | bytes 1572872 | tf_op jit(solution)/shard_map/schur_y/ppermute | solution.py:318
  46.2 7.5 %collective-permute-done.5.refs_2_ = bf16[4,2,256,128]{3,2,1,0:T(8,128)(2,1)S(1)} collective-permute-done((bf16[4,2,256,128]{3,2,1,0:T(8,128)(2,1)S(1)}, bf16[4,2,256,128]{3,2,1,0:T(8,128)(2,1)S(1)}, u32[]{:S(2)}, u32[]{:S(2)}) %collective-permute-start.5) | collective-permute-done | bytes 524320 | tf_op jit(solution)/shard_map/schur_y/ppermute | solution.py:318
  53.6 5.3 %collective-permute-start.7 = (bf16[2,2,256,128]{3,2,1,0:T(8,128)(2,1)S(1)}, bf16[2,2,256,128]{3,2,1,0:T(8,128)(2,1)S(1)}, u32[]{:S(2)}, u32[]{:S(2)}) collective-permute-start(bf16[2,2,256,128]{3,2,1,0:T(8,128)(2,1)S(1)} %slice.9), channel_id=1, source_target_pairs={{0,24},{1,25},{2,26},{3,27},{4,28},{5,29},{6,30},{7,31},{8,0},{9,1... | collective-permute-start | bytes 786440 | tf_op jit(solution)/shard_map/schur_y/ppermute | solution.py:318
  59.0 1.9 %collective-permute-start.6 = (bf16[2,2,256,128]{3,2,1,0:T(8,128)(2,1)S(1)}, bf16[2,2,256,128]{3,2,1,0:T(8,128)(2,1)S(1)}, u32[]{:S(2)}, u32[]{:S(2)}) collective-permute-start(bf16[2,2,256,128]{3,2,1,0:T(8,128)(2,1)S(1)} %slice.8), channel_id=1, source_target_pairs={{0,8},{1,9},{2,10},{3,11},{4,12},{5,13},{6,14},{7,15},{8,16},{9,17... | collective-permute-start | bytes 786440 | tf_op jit(solution)/shard_map/schur_y/ppermute | solution.py:318
  60.9 4.2 %all-to-all-done = f32[8,72,128]{2,1,0:T(8,128)} async-done(((f32[8,72,128]{2,1,0:T(8,128)}), f32[8,72,128]{2,1,0:T(8,128)}, u32[]{:S(2)}, u32[]{:S(2)}) %all-to-all-start) | async-done | bytes 294944 | tf_op jit(solution)/shard_map/all_to_all | solution.py:322
  65.1 2.8 %all-gather.recv_hbm = f32[16,72,128]{2,1,0:T(8,128)S(1)} all-gather(f32[8,72,128]{2,1,0:T(8,128)} %all-to-all-done), channel_id=2, replica_groups={{0,32},{64,96},{128,160},{192,224},{256,288},{320,352},{384,416},{448,4..., dimensions={0}, use_global_device_ids=true | all-gather | bytes 884736 | tf_op jit(solution)/shard_map/all_gather | solution.py:326
  68.0 0.0 copy-start.4
  68.0 0.0 copy-start.5
  68.0 0.0 copy-start.6
  68.0 0.0 copy-start.7
  68.0 0.0 copy-start.9
  68.0 0.0 copy-start.10
  68.0 0.0 copy-start.11
  68.0 2.5 %shard_map.122 = (bf16[32,16,128]{2,1,0:T(8,128)(2,1)S(1)}, f32[16,8,128]{2,1,0:T(8,128)S(1)}) custom-call(f32[16,72,128]{2,1,0:T(8,128)S(1)} %all-gather.recv_hbm), custom_call_target="tpu_custom_call" | custom-call | flops 1000000000 | bytes 1048576 | tf_op jit(solution)/shard_map/pallas_call | solution.py:341
  70.6 1.1 shard_map.123
  71.6 26.6 %all_to_all.20 = f32[8,16,256]{2,1,0:T(8,128)S(1)} all-to-all(f32[8,16,256]{2,1,0:T(8,128)S(1)} %shard_map.123), channel_id=1, replica_groups={{0,64,128,192,256,320,384,448},{32,96,160,224,288,352,416,480},{1,65,12..., dimensions={0} | all-to-all | bytes 262144 | tf_op jit(solution)/shard_map/all_to_all | solution.py:322
  98.2 7.2 %all-gather.1.recv_hbm = f32[16,16,256]{2,1,0:T(8,128)S(1)} all-gather(f32[8,16,256]{2,1,0:T(8,128)S(1)} %all_to_all.20), channel_id=3, replica_groups={{0,32},{64,96},{128,160},{192,224},{256,288},{320,352},{384,416},{448,4..., dimensions={0}, use_global_device_ids=true | all-gather | bytes 393216 | tf_op jit(solution)/shard_map/all_gather | solution.py:326
  105.5 4.4 %shard_map.124 = (f32[8,16,400]{2,1,0:T(8,128)S(1)}, f32[8,16,400]{2,1,0:T(8,128)S(1)}, f32[8,16,400]{2,1,0:T(8,128)S(1)}, bf16[8,64,128]{2,1,0:T(8,128)(2,1)S(1)}) custom-call(s32[16]{0:T(128)S(1)} %copy-done.10, s32[16]{0:T(128)S(1)} %copy-done.11, f32[16,16,256]{2,1,0:T(8,128)S(1)} %all-gather.1.recv_hbm, f32[8,16,400]{2,1,0:T(8,128)S(1)} %copy-done.5, ...), custom_call_target="tpu_custom_call" | custom-call | flops 1000000000 | bytes 4194304 | tf_op jit(solution)/shard_map/pallas_call | solution.py:343
  109.9 20.0 %all_to_all.21 = bf16[8,64,128]{2,1,0:T(8,128)(2,1)S(1)} all-to-all(bf16[8,64,128]{2,1,0:T(8,128)(2,1)S(1)} %get-tuple-element.26), channel_id=1, replica_groups={{0,64,128,192,256,320,384,448},{32,96,160,224,288,352,416,480},{1,65,12..., dimensions={0} | all-to-all | bytes 262144 | tf_op jit(solution)/shard_map/all_to_all | solution.py:322
  129.9 2.3 %all-gather.2.recv_hbm = bf16[16,64,128]{2,1,0:T(8,128)(2,1)S(1)} all-gather(bf16[8,64,128]{2,1,0:T(8,128)(2,1)S(1)} %all_to_all.21), channel_id=4, replica_groups={{0,32},{64,96},{128,160},{192,224},{256,288},{320,352},{384,416},{448,4..., dimensions={0}, use_global_device_ids=true | all-gather | bytes 393216 | tf_op jit(solution)/shard_map/all_gather | solution.py:326
  132.3 3.9 %shard_map.125 = (f32[16,256]{1,0:T(8,128)}, bf16[16,16,256]{2,1,0:T(8,128)(2,1)S(1)}) custom-call(bf16[16,64,128]{2,1,0:T(8,128)(2,1)S(1)} %all-gather.2.recv_hbm, f32[16,8,128]{2,1,0:T(8,128)S(1)} %get-tuple-element.27.map_hbm, bf16[4,2,256,128]{3,2,1,0:T(8,128)(2,1)S(1)} %schur_z.1.refs_0_, bf16[4,2,256,128]{3,2,1,0:T(8,128)(2,1)S(1)} %collective-permute-done.4.refs_1_, ...), custom_call_target="tpu_custom_call" | custom-call | flops 1000000000 | bytes 3145728 | tf_op jit(solution)/shard_map/pallas_call | solution.py:344
  136.2 19.7 %all_to_all.22.recv_hbm = bf16[16,16,256]{2,1,0:T(8,128)(2,1)S(1)} all-to-all(bf16[16,16,256]{2,1,0:T(8,128)(2,1)S(1)} %get-tuple-element.28), channel_id=1, replica_groups=mesh['row'=16,'col'=32] {'row'}, dimensions={0} | all-to-all | bytes 262144 | tf_op jit(solution)/shard_map/all_to_all | solution.py:322
  155.8 2.4 %shard_map.126 = (f32[8,16,400]{2,1,0:T(8,128)}, f32[8,16,400]{2,1,0:T(8,128)}) custom-call(bf16[16,16,256]{2,1,0:T(8,128)(2,1)S(1)} %all_to_all.22.recv_hbm, f32[8,16,400]{2,1,0:T(8,128)S(1)} %get-tuple-element.29.prev_hbm, f32[8,16,400]{2,1,0:T(8,128)S(1)} %get-tuple-element.30.volt_hbm, f32[8,16,400]{2,1,0:T(8,128)S(1)} %get-tuple-element.31.curr_hbm, ...), custom_call_target="tpu_custom_call" | custom-call | flops 1000000000 | bytes 2097152 | tf_op jit(solution)/shard_map/pallas_call | solution.py:345
  (26 shorter events, 0.1 us)
Async XLA Ops:
  0.6 13.4 %copy-start.8 = (bf16[256,128]{1,0:T(8,128)(2,1)S(1)}, bf16[256,128]{1,0:T(8,128)(2,1)}, u32[]{:S(2)}) copy-start(bf16[256,128]{1,0:T(8,128)(2,1)} %own_ref.1) | copy-start | bytes 196612
  0.6 13.3 %collective-permute-start = (bf16[256,128]{1,0:T(8,128)(2,1)}, bf16[256,128]{1,0:T(8,128)(2,1)S(1)}, u32[]{:S(2)}, u32[]{:S(2)}) collective-permute-start(bf16[256,128]{1,0:T(8,128)(2,1)} %own_ref.1), channel_id=1, source_target_pairs={{0,4},{1,5},{2,6},{3,7},{4,0},{5,1},{6,2},{7,3},{8,12},{9,13},{10,... | collective-permute-start | bytes 196616 | tf_op jit(solution)/shard_map/schur_z/ppermute | solution.py:314
  14.0 25.5 %collective-permute-start.3 = (bf16[2,256,128]{2,1,0:T(8,128)(2,1)S(1)}, bf16[2,256,128]{2,1,0:T(8,128)(2,1)S(1)}, u32[]{:S(2)}, u32[]{:S(2)}) collective-permute-start(bf16[2,256,128]{2,1,0:T(8,128)(2,1)S(1)} %pad_maximum_fusion), channel_id=1, source_target_pairs={{0,3},{1,2},{2,1},{3,0},{4,7},{5,6},{6,5},{7,4},{8,11},{9,10},{10,... | collective-permute-start | bytes 393224 | tf_op jit(solution)/shard_map/schur_z/ppermute | solution.py:314
  17.6 21.9 %collective-permute-start.2 = (bf16[2,256,128]{2,1,0:T(8,128)(2,1)S(1)}, bf16[2,256,128]{2,1,0:T(8,128)(2,1)S(1)}, u32[]{:S(2)}, u32[]{:S(2)}) collective-permute-start(bf16[2,256,128]{2,1,0:T(8,128)(2,1)S(1)} %pad_maximum_fusion), channel_id=1, source_target_pairs={{0,2},{1,3},{2,0},{3,1},{4,6},{5,7},{6,4},{7,5},{8,10},{9,11},{10,... | collective-permute-start | bytes 393224 | tf_op jit(solution)/shard_map/schur_z/ppermute | solution.py:314
  21.3 18.3 %collective-permute-start.1 = (bf16[2,256,128]{2,1,0:T(8,128)(2,1)S(1)}, bf16[2,256,128]{2,1,0:T(8,128)(2,1)S(1)}, u32[]{:S(2)}, u32[]{:S(2)}) collective-permute-start(bf16[2,256,128]{2,1,0:T(8,128)(2,1)S(1)} %pad_maximum_fusion), channel_id=1, source_target_pairs={{0,1},{1,0},{2,3},{3,2},{4,5},{5,4},{6,7},{7,6},{8,9},{9,8},{10,11... | collective-permute-start | bytes 393224 | tf_op jit(solution)/shard_map/schur_z/ppermute | solution.py:314
  24.4 40.7 %all-to-all-start = ((f32[8,72,128]{2,1,0:T(8,128)}), f32[8,72,128]{2,1,0:T(8,128)}, u32[]{:S(2)}, u32[]{:S(2)}) async-start(f32[8,72,128]{2,1,0:T(8,128)} %get-tuple-element.20), calls=%async_computation | async-start | bytes 589824 | tf_op jit(solution)/shard_map/all_to_all | solution.py:322
  39.6 14.0 %collective-permute-start.5 = (bf16[4,2,256,128]{3,2,1,0:T(8,128)(2,1)S(1)}, bf16[4,2,256,128]{3,2,1,0:T(8,128)(2,1)S(1)}, u32[]{:S(2)}, u32[]{:S(2)}) collective-permute-start(bf16[4,2,256,128]{3,2,1,0:T(8,128)(2,1)S(1)} %schur_z.1.refs_0_), channel_id=1, source_target_pairs={{0,24},{1,25},{2,26},{3,27},{4,28},{5,29},{6,30},{7,31},{8,0},{9,1... | collective-permute-start | bytes 1572872 | tf_op jit(solution)/shard_map/schur_y/ppermute | solution.py:318
  44.2 14.7 %collective-permute-start.4 = (bf16[4,2,256,128]{3,2,1,0:T(8,128)(2,1)S(1)}, bf16[4,2,256,128]{3,2,1,0:T(8,128)(2,1)S(1)}, u32[]{:S(2)}, u32[]{:S(2)}) collective-permute-start(bf16[4,2,256,128]{3,2,1,0:T(8,128)(2,1)S(1)} %schur_z.1.refs_0_), channel_id=1, source_target_pairs={{0,8},{1,9},{2,10},{3,11},{4,12},{5,13},{6,14},{7,15},{8,16},{9,17... | collective-permute-start | bytes 1572872 | tf_op jit(solution)/shard_map/schur_y/ppermute | solution.py:318
  53.6 16.9 %collective-permute-start.7 = (bf16[2,2,256,128]{3,2,1,0:T(8,128)(2,1)S(1)}, bf16[2,2,256,128]{3,2,1,0:T(8,128)(2,1)S(1)}, u32[]{:S(2)}, u32[]{:S(2)}) collective-permute-start(bf16[2,2,256,128]{3,2,1,0:T(8,128)(2,1)S(1)} %slice.9), channel_id=1, source_target_pairs={{0,24},{1,25},{2,26},{3,27},{4,28},{5,29},{6,30},{7,31},{8,0},{9,1... | collective-permute-start | bytes 786440 | tf_op jit(solution)/shard_map/schur_y/ppermute | solution.py:318
  59.0 11.6 %collective-permute-start.6 = (bf16[2,2,256,128]{3,2,1,0:T(8,128)(2,1)S(1)}, bf16[2,2,256,128]{3,2,1,0:T(8,128)(2,1)S(1)}, u32[]{:S(2)}, u32[]{:S(2)}) collective-permute-start(bf16[2,2,256,128]{3,2,1,0:T(8,128)(2,1)S(1)} %slice.8), channel_id=1, source_target_pairs={{0,8},{1,9},{2,10},{3,11},{4,12},{5,13},{6,14},{7,15},{8,16},{9,17... | collective-permute-start | bytes 786440 | tf_op jit(solution)/shard_map/schur_y/ppermute | solution.py:318
  67.9 37.4 %copy-start = (bf16[8,400,400]{2,1,0:T(8,128)(2,1)S(1)}, bf16[8,400,400]{2,1,0:T(8,128)(2,1)}, u32[]{:S(2)}) copy-start(bf16[8,400,400]{2,1,0:T(8,128)(2,1)} %inv_hbm.5) | copy-start | bytes 7680004
  68.0 37.4 %copy-start.1 = (s32[8,16,400]{2,1,0:T(8,128)S(1)}, s32[8,16,400]{2,1,0:T(8,128)}, u32[]{:S(2)}) copy-start(s32[8,16,400]{2,1,0:T(8,128)} %breaker_hbm.5) | copy-start | bytes 614404
  68.0 37.4 %copy-start.2 = (f32[8,16,400]{2,1,0:T(8,128)S(1)}, f32[8,16,400]{2,1,0:T(8,128)}, u32[]{:S(2)}) copy-start(f32[8,16,400]{2,1,0:T(8,128)} %volt_hbm.3) | copy-start | bytes 614404
  68.0 37.4 %copy-start.3 = (f32[8,16,400]{2,1,0:T(8,128)S(1)}, f32[8,16,400]{2,1,0:T(8,128)}, u32[]{:S(2)}) copy-start(f32[8,16,400]{2,1,0:T(8,128)} %curr_hbm.3) | copy-start | bytes 614404
  68.0 37.4 %copy-start.4 = (bf16[256,512]{1,0:T(8,128)(2,1)S(1)}, bf16[256,512]{1,0:T(8,128)(2,1)}, u32[]{:S(2)}) copy-start(bf16[256,512]{1,0:T(8,128)(2,1)} %get-tuple-element.24.right_hbm) | copy-start | bytes 786436
  68.0 37.4 %copy-start.5 = (f32[8,16,400]{2,1,0:T(8,128)S(1)}, f32[8,16,400]{2,1,0:T(8,128)}, u32[]{:S(2)}) copy-start(f32[8,16,400]{2,1,0:T(8,128)} %get-tuple-element.23.prev_hbm) | copy-start | bytes 614404
  68.0 37.4 %copy-start.6 = (f32[8,400]{1,0:T(8,128)S(1)}, f32[8,400]{1,0:T(8,128)}, u32[]{:S(2)}) copy-start(f32[8,400]{1,0:T(8,128)} %gain_hbm.5) | copy-start | bytes 38404
  68.0 37.4 %copy-start.7 = (f32[8,512]{1,0:T(8,128)S(1)}, f32[8,512]{1,0:T(8,128)}, u32[]{:S(2)}) copy-start(f32[8,512]{1,0:T(8,128)} %get-tuple-element.25.rows_hbm) | copy-start | bytes 49156
  68.0 37.4 %copy-start.9 = (f32[8,64]{1,0:T(8,128)S(1)}, f32[8,64]{1,0:T(8,128)}, u32[]{:S(2)}) copy-start(f32[8,64]{1,0:T(8,128)} %tie_hbm.3) | copy-start | bytes 6148
  68.0 37.4 %copy-start.10 = (s32[16]{0:T(128)S(1)}, s32[16]{0:T(128)}, u32[]{:S(2)}) copy-start(s32[16]{0:T(128)} %time_ref.3) | copy-start | bytes 196
  68.0 37.4 %copy-start.11 = (s32[16]{0:T(128)S(1)}, s32[16]{0:T(128)}, u32[]{:S(2)}) copy-start(s32[16]{0:T(128)} %node_ref.3) | copy-start | bytes 196

commit v8 on v7

--- a/solution.py
+++ b/solution.py
@@ -17,7 +17,8 @@
 TILES = OWN // LANES
 VALUE_ROWS = TILES * SCEN
 MAP_ROWS = 2 * TILES
-CORES = [[2 * n + core for n in range(ROWS // 2)] for core in range(2)]
+TURNED = [(n + ROWS // 2) % ROWS for n in range(ROWS)]
+CORES = [[r for r in TURNED if r % 2 == core] for core in range(2)]
 PAIRS = [[2 * n, 2 * n + 1] for n in range(ROWS // 2)]
 VMEM_BYTES = 16 << 20
 ALL_VMEM = 60 << 20
@@ -203,7 +204,7 @@
 
 
 def paired_sender(place):
-    return 2 * (place % (ROWS // 2)) + place // (ROWS // 2)
+    return CORES[place // (ROWS // 2)][place % (ROWS // 2)]
 
 
 def middle_kernel(time_ref, node_ref, recv_hbm, prev_hbm, volt_hbm, curr_hbm, breaker_hbm, gain_hbm, tie_hbm, right_hbm, rows_hbm, inv_hbm, volt_out, curr_out, open_ref, send_ref, recv_ref, prev_ref, right_ref, rows_ref, gain_ref, tie_ref, volt_ref, curr_ref, breaker_ref, inv_ref, sems):
@@ -228,7 +229,7 @@
         sems,
     )
     wait_for(copies[:3])
-    drive = driven(recv_ref, right_ref, rows_ref, lambda place: place)
+    drive = driven(recv_ref, right_ref, rows_ref, TURNED.__getitem__)
     wait_for(copies[3:])
     for k in range(SUBS):
         volt_out[k], curr_out[k] = update(k, drive, prev_ref, inv_ref[k], volt_ref[k], curr_ref[k], breaker_ref, gain_ref)
@@ -318,7 +319,7 @@
     return lax.ppermute(block, "col", [(c, (c + 8 * steps) % COLS) for c in range(COLS)])
 
 
-def exchange(send, groups=None):
+def exchange(send, groups):
     return lax.all_to_all(send, "row", 0, 0, axis_index_groups=groups)
 
 
@@ -342,7 +343,7 @@
     (send,) = product(rhs, *schur_rows)
     volt, curr, opened, send = middle(fault_time, fault_node, paired_exchange(send), opened, volt, curr, breaker, ind_gain, tie, *pick, local_inverse)
     iface_block, send = interface(paired_exchange(send), maps, *schur_rows)
-    volt, curr = last(exchange(send), opened, volt, curr, breaker, ind_gain, *pick, local_inverse)
+    volt, curr = last(exchange(send, [TURNED]), opened, volt, curr, breaker, ind_gain, *pick, local_inverse)
     return volt, curr, iface_block
 
 

time: 159 us -> 149 us (0.937)
  the two profiles are of different devices: /device:TPU:33 before, /device:TPU:448 now
where the time goes in v8:
time: 149 us; the launch traced here: 148 us
  blocking collectives  77.6 us (52%)
  starting transfers between devices  37.2 us (25%)
  Pallas kernels  18.7 us (13%)
  waiting for transfers between devices  14 us (9%)
    all_to_all x3, blocking collectives, exchange(): return lax.all_to_all(send, 'row', 0, 0, axis_index_groups=groups)  71.2 us
    ppermute x4, starting transfers between devices, along_z(): return lax.ppermute(block, 'col', [(c, c ^ flip) for c in range(COLS)])  16 us
    ppermute x4, starting transfers between devices, along_y(): lax.ppermute(block, 'col', [(c, (c + 8 * steps) % COLS) for c in range(CO...  14.4 us
    ppermute x4, waiting for transfers between devices, along_y(): lax.ppermute(block, 'col', [(c, (c + 8 * steps) % COLS) for c in range(CO...  9.59 us
    all_to_all x1, starting transfers between devices, exchange(): return lax.all_to_all(send, 'row', 0, 0, axis_index_groups=groups)  6.81 us
    all_gather x3, blocking collectives, paired_exchange(): both = lax.all_gather(exchange(send, CORES), 'row', axis_index_groups=PAIRS)  6.39 us
    pallas_call x1, Pallas kernels, local(): middle(fault_time, fault_node, paired_exchange(send), opened, volt, curr,...  4.44 us
    pallas_call x1, Pallas kernels, local(): first(fault_time, fault_node, volt, curr, breaker, ind_gain, tie, port_ma...  4.38 us
  transfers between devices with their start and end apart: 9, of which 4 were waited for; matrix products, arithmetic and copies ran while one was open for 0% of the time, Pallas kernels for 5%

profile of v8, /device:TPU:448, one launch (start us, length us, event | category | flops | bytes accessed | tf_op | source)
XLA Modules:
  0.0 148.5 jit_solution(10810090983436868857)
XLA Ops:
  0.6 5.6 %collective-permute-start = (bf16[256,128]{1,0:T(8,128)(2,1)}, bf16[256,128]{1,0:T(8,128)(2,1)S(1)}, u32[]{:S(2)}, u32[]{:S(2)}) collective-permute-start(bf16[256,128]{1,0:T(8,128)(2,1)} %own_ref.1), channel_id=1, source_target_pairs={{0,4},{1,5},{2,6},{3,7},{4,0},{5,1},{6,2},{7,3},{8,12},{9,13},{10,... | collective-permute-start | bytes 196616 | tf_op jit(solution)/shard_map/schur_z/ppermute | solution.py:315
  6.2 4.4 %shard_map.121 = (f32[8,16,400]{2,1,0:T(8,128)}, f32[8,72,128]{2,1,0:T(8,128)}, bf16[256,512]{1,0:T(8,128)(2,1)}, f32[8,512]{1,0:T(8,128)}) custom-call(s32[16]{0:T(128)} %time_ref.3, s32[16]{0:T(128)} %node_ref.3, f32[8,16,400]{2,1,0:T(8,128)} %volt_hbm.3, f32[8,16,400]{2,1,0:T(8,128)} %curr_hbm.3, s32[8,16,400]{2,1,0:T(8,128)} %breaker_hbm.5, ...), custom_call_target="tpu_custom_call" | custom-call | flops 1000000000 | bytes 4194304 | tf_op jit(solution)/shard_map/pallas_call | solution.py:334
  10.6 2.9 %collective-permute-done.across_ref = bf16[256,128]{1,0:T(8,128)(2,1)S(1)} collective-permute-done((bf16[256,128]{1,0:T(8,128)(2,1)}, bf16[256,128]{1,0:T(8,128)(2,1)S(1)}, u32[]{:S(2)}, u32[]{:S(2)}) %collective-permute-start) | collective-permute-done | bytes 65568 | tf_op jit(solution)/shard_map/schur_z/ppermute | solution.py:315
  13.5 1.9 %collective-permute-start.3 = (bf16[2,256,128]{2,1,0:T(8,128)(2,1)S(1)}, bf16[2,256,128]{2,1,0:T(8,128)(2,1)S(1)}, u32[]{:S(2)}, u32[]{:S(2)}) collective-permute-start(bf16[2,256,128]{2,1,0:T(8,128)(2,1)S(1)} %pad_maximum_fusion), channel_id=1, source_target_pairs={{0,3},{1,2},{2,1},{3,0},{4,7},{5,6},{6,5},{7,4},{8,11},{9,10},{10,... | collective-permute-start | bytes 393224 | tf_op jit(solution)/shard_map/schur_z/ppermute | solution.py:315
  15.5 6.6 %collective-permute-start.2 = (bf16[2,256,128]{2,1,0:T(8,128)(2,1)S(1)}, bf16[2,256,128]{2,1,0:T(8,128)(2,1)S(1)}, u32[]{:S(2)}, u32[]{:S(2)}) collective-permute-start(bf16[2,256,128]{2,1,0:T(8,128)(2,1)S(1)} %pad_maximum_fusion), channel_id=1, source_target_pairs={{0,2},{1,3},{2,0},{3,1},{4,6},{5,7},{6,4},{7,5},{8,10},{9,11},{10,... | collective-permute-start | bytes 393224 | tf_op jit(solution)/shard_map/schur_z/ppermute | solution.py:315
  22.1 1.9 %collective-permute-start.1 = (bf16[2,256,128]{2,1,0:T(8,128)(2,1)S(1)}, bf16[2,256,128]{2,1,0:T(8,128)(2,1)S(1)}, u32[]{:S(2)}, u32[]{:S(2)}) collective-permute-start(bf16[2,256,128]{2,1,0:T(8,128)(2,1)S(1)} %pad_maximum_fusion), channel_id=1, source_target_pairs={{0,1},{1,0},{2,3},{3,2},{4,5},{5,4},{6,7},{7,6},{8,9},{9,8},{10,11... | collective-permute-start | bytes 393224 | tf_op jit(solution)/shard_map/schur_z/ppermute | solution.py:315
  24.0 6.8 %all-to-all-start = ((f32[8,72,128]{2,1,0:T(8,128)}), f32[8,72,128]{2,1,0:T(8,128)}, u32[]{:S(2)}, u32[]{:S(2)}) async-start(f32[8,72,128]{2,1,0:T(8,128)} %get-tuple-element.20), calls=%async_computation | async-start | bytes 589824 | tf_op jit(solution)/shard_map/all_to_all | solution.py:323
  30.9 4.9 %collective-permute-start.5 = (bf16[4,2,256,128]{3,2,1,0:T(8,128)(2,1)S(1)}, bf16[4,2,256,128]{3,2,1,0:T(8,128)(2,1)S(1)}, u32[]{:S(2)}, u32[]{:S(2)}) collective-permute-start(bf16[4,2,256,128]{3,2,1,0:T(8,128)(2,1)S(1)} %schur_z.1.refs_0_), channel_id=1, source_target_pairs={{0,24},{1,25},{2,26},{3,27},{4,28},{5,29},{6,30},{7,31},{8,0},{9,1... | collective-permute-start | bytes 1572872 | tf_op jit(solution)/shard_map/schur_y/ppermute | solution.py:319
  35.8 1.9 %collective-permute-start.4 = (bf16[4,2,256,128]{3,2,1,0:T(8,128)(2,1)S(1)}, bf16[4,2,256,128]{3,2,1,0:T(8,128)(2,1)S(1)}, u32[]{:S(2)}, u32[]{:S(2)}) collective-permute-start(bf16[4,2,256,128]{3,2,1,0:T(8,128)(2,1)S(1)} %schur_z.1.refs_0_), channel_id=1, source_target_pairs={{0,8},{1,9},{2,10},{3,11},{4,12},{5,13},{6,14},{7,15},{8,16},{9,17... | collective-permute-start | bytes 1572872 | tf_op jit(solution)/shard_map/schur_y/ppermute | solution.py:319
  37.7 8.6 %collective-permute-done.5.refs_2_ = bf16[4,2,256,128]{3,2,1,0:T(8,128)(2,1)S(1)} collective-permute-done((bf16[4,2,256,128]{3,2,1,0:T(8,128)(2,1)S(1)}, bf16[4,2,256,128]{3,2,1,0:T(8,128)(2,1)S(1)}, u32[]{:S(2)}, u32[]{:S(2)}) %collective-permute-start.5) | collective-permute-done | bytes 524320 | tf_op jit(solution)/shard_map/schur_y/ppermute | solution.py:319
  46.3 5.6 %collective-permute-start.7 = (bf16[2,2,256,128]{3,2,1,0:T(8,128)(2,1)S(1)}, bf16[2,2,256,128]{3,2,1,0:T(8,128)(2,1)S(1)}, u32[]{:S(2)}, u32[]{:S(2)}) collective-permute-start(bf16[2,2,256,128]{3,2,1,0:T(8,128)(2,1)S(1)} %slice.9), channel_id=1, source_target_pairs={{0,24},{1,25},{2,26},{3,27},{4,28},{5,29},{6,30},{7,31},{8,0},{9,1... | collective-permute-start | bytes 786440 | tf_op jit(solution)/shard_map/schur_y/ppermute | solution.py:319
  52.0 1.9 %collective-permute-start.6 = (bf16[2,2,256,128]{3,2,1,0:T(8,128)(2,1)S(1)}, bf16[2,2,256,128]{3,2,1,0:T(8,128)(2,1)S(1)}, u32[]{:S(2)}, u32[]{:S(2)}) collective-permute-start(bf16[2,2,256,128]{3,2,1,0:T(8,128)(2,1)S(1)} %slice.8), channel_id=1, source_target_pairs={{0,8},{1,9},{2,10},{3,11},{4,12},{5,13},{6,14},{7,15},{8,16},{9,17... | collective-permute-start | bytes 786440 | tf_op jit(solution)/shard_map/schur_y/ppermute | solution.py:319
  53.9 1.5 %all-to-all-done = f32[8,72,128]{2,1,0:T(8,128)} async-done(((f32[8,72,128]{2,1,0:T(8,128)}), f32[8,72,128]{2,1,0:T(8,128)}, u32[]{:S(2)}, u32[]{:S(2)}) %all-to-all-start) | async-done | bytes 294944 | tf_op jit(solution)/shard_map/all_to_all | solution.py:323
  55.4 2.4 %all-gather.recv_hbm = f32[16,72,128]{2,1,0:T(8,128)S(1)} all-gather(f32[8,72,128]{2,1,0:T(8,128)} %all-to-all-done), channel_id=2, replica_groups={{0,32},{64,96},{128,160},{192,224},{256,288},{320,352},{384,416},{448,4..., dimensions={0}, use_global_device_ids=true | all-gather | bytes 884736 | tf_op jit(solution)/shard_map/all_gather | solution.py:327
  57.8 0.0 copy-start.4
  57.9 0.0 copy-start.5
  57.9 0.0 copy-start.6
  57.9 0.0 copy-start.7
  57.9 0.0 copy-start.9
  57.9 0.0 copy-start.10
  57.9 0.0 copy-start.11
  57.9 2.5 %shard_map.122 = (bf16[32,16,128]{2,1,0:T(8,128)(2,1)S(1)}, f32[16,8,128]{2,1,0:T(8,128)S(1)}) custom-call(f32[16,72,128]{2,1,0:T(8,128)S(1)} %all-gather.recv_hbm), custom_call_target="tpu_custom_call" | custom-call | flops 1000000000 | bytes 1048576 | tf_op jit(solution)/shard_map/pallas_call | solution.py:342
  60.4 1.0 collective-permute-done.6.refs_3_
  61.5 1.0 shard_map.123
  62.5 30.2 %all_to_all.20 = f32[8,16,256]{2,1,0:T(8,128)S(1)} all-to-all(f32[8,16,256]{2,1,0:T(8,128)S(1)} %shard_map.123), channel_id=1, replica_groups={{256,320,384,448,0,64,128,192},{288,352,416,480,32,96,160,224},{257,321..., dimensions={0} | all-to-all | bytes 262144 | tf_op jit(solution)/shard_map/all_to_all | solution.py:323
  92.7 2.0 %all-gather.1.recv_hbm = f32[16,16,256]{2,1,0:T(8,128)S(1)} all-gather(f32[8,16,256]{2,1,0:T(8,128)S(1)} %all_to_all.20), channel_id=3, replica_groups={{0,32},{64,96},{128,160},{192,224},{256,288},{320,352},{384,416},{448,4..., dimensions={0}, use_global_device_ids=true | all-gather | bytes 393216 | tf_op jit(solution)/shard_map/all_gather | solution.py:327
  94.8 4.4 %shard_map.124 = (f32[8,16,400]{2,1,0:T(8,128)S(1)}, f32[8,16,400]{2,1,0:T(8,128)S(1)}, f32[8,16,400]{2,1,0:T(8,128)S(1)}, bf16[8,64,128]{2,1,0:T(8,128)(2,1)S(1)}) custom-call(s32[16]{0:T(128)S(1)} %copy-done.10, s32[16]{0:T(128)S(1)} %copy-done.11, f32[16,16,256]{2,1,0:T(8,128)S(1)} %all-gather.1.recv_hbm, f32[8,16,400]{2,1,0:T(8,128)S(1)} %copy-done.5, ...), custom_call_target="tpu_custom_call" | custom-call | flops 1000000000 | bytes 4194304 | tf_op jit(solution)/shard_map/pallas_call | solution.py:344
  99.2 20.7 %all_to_all.21 = bf16[8,64,128]{2,1,0:T(8,128)(2,1)S(1)} all-to-all(bf16[8,64,128]{2,1,0:T(8,128)(2,1)S(1)} %get-tuple-element.26), channel_id=1, replica_groups={{256,320,384,448,0,64,128,192},{288,352,416,480,32,96,160,224},{257,321..., dimensions={0} | all-to-all | bytes 262144 | tf_op jit(solution)/shard_map/all_to_all | solution.py:323
  119.9 2.0 %all-gather.2.recv_hbm = bf16[16,64,128]{2,1,0:T(8,128)(2,1)S(1)} all-gather(bf16[8,64,128]{2,1,0:T(8,128)(2,1)S(1)} %all_to_all.21), channel_id=4, replica_groups={{0,32},{64,96},{128,160},{192,224},{256,288},{320,352},{384,416},{448,4..., dimensions={0}, use_global_device_ids=true | all-gather | bytes 393216 | tf_op jit(solution)/shard_map/all_gather | solution.py:327
  121.9 3.9 %shard_map.125 = (f32[16,256]{1,0:T(8,128)}, bf16[16,16,256]{2,1,0:T(8,128)(2,1)S(1)}) custom-call(bf16[16,64,128]{2,1,0:T(8,128)(2,1)S(1)} %all-gather.2.recv_hbm, f32[16,8,128]{2,1,0:T(8,128)S(1)} %get-tuple-element.27.map_hbm, bf16[4,2,256,128]{3,2,1,0:T(8,128)(2,1)S(1)} %schur_z.1.refs_0_, bf16[4,2,256,128]{3,2,1,0:T(8,128)(2,1)S(1)} %collective-permute-done.4.refs_1_, ...), custom_call_target="tpu_custom_call" | custom-call | flops 1000000000 | bytes 3145728 | tf_op jit(solution)/shard_map/pallas_call | solution.py:345
  125.8 20.3 %all_to_all.22.recv_hbm = bf16[16,16,256]{2,1,0:T(8,128)(2,1)S(1)} all-to-all(bf16[16,16,256]{2,1,0:T(8,128)(2,1)S(1)} %get-tuple-element.28), channel_id=1, replica_groups={{256,288,320,352,384,416,448,480,0,32,64,96,128,160,192,224},{257,289,3..., dimensions={0} | all-to-all | bytes 262144 | tf_op jit(solution)/shard_map/all_to_all | solution.py:323
  146.1 2.4 %shard_map.126 = (f32[8,16,400]{2,1,0:T(8,128)}, f32[8,16,400]{2,1,0:T(8,128)}) custom-call(bf16[16,16,256]{2,1,0:T(8,128)(2,1)S(1)} %all_to_all.22.recv_hbm, f32[8,16,400]{2,1,0:T(8,128)S(1)} %get-tuple-element.29.prev_hbm, f32[8,16,400]{2,1,0:T(8,128)S(1)} %get-tuple-element.30.volt_hbm, f32[8,16,400]{2,1,0:T(8,128)S(1)} %get-tuple-element.31.curr_hbm, ...), custom_call_target="tpu_custom_call" | custom-call | flops 1000000000 | bytes 2097152 | tf_op jit(solution)/shard_map/pallas_call | solution.py:346
  (26 shorter events, 0.1 us)
Async XLA Ops:
  0.6 12.9 %copy-start.8 = (bf16[256,128]{1,0:T(8,128)(2,1)S(1)}, bf16[256,128]{1,0:T(8,128)(2,1)}, u32[]{:S(2)}) copy-start(bf16[256,128]{1,0:T(8,128)(2,1)} %own_ref.1) | copy-start | bytes 196612
  0.6 12.9 %collective-permute-start = (bf16[256,128]{1,0:T(8,128)(2,1)}, bf16[256,128]{1,0:T(8,128)(2,1)S(1)}, u32[]{:S(2)}, u32[]{:S(2)}) collective-permute-start(bf16[256,128]{1,0:T(8,128)(2,1)} %own_ref.1), channel_id=1, source_target_pairs={{0,4},{1,5},{2,6},{3,7},{4,0},{5,1},{6,2},{7,3},{8,12},{9,13},{10,... | collective-permute-start | bytes 196616 | tf_op jit(solution)/shard_map/schur_z/ppermute | solution.py:315
  13.5 17.3 %collective-permute-start.3 = (bf16[2,256,128]{2,1,0:T(8,128)(2,1)S(1)}, bf16[2,256,128]{2,1,0:T(8,128)(2,1)S(1)}, u32[]{:S(2)}, u32[]{:S(2)}) collective-permute-start(bf16[2,256,128]{2,1,0:T(8,128)(2,1)S(1)} %pad_maximum_fusion), channel_id=1, source_target_pairs={{0,3},{1,2},{2,1},{3,0},{4,7},{5,6},{6,5},{7,4},{8,11},{9,10},{10,... | collective-permute-start | bytes 393224 | tf_op jit(solution)/shard_map/schur_z/ppermute | solution.py:315
  15.5 15.3 %collective-permute-start.2 = (bf16[2,256,128]{2,1,0:T(8,128)(2,1)S(1)}, bf16[2,256,128]{2,1,0:T(8,128)(2,1)S(1)}, u32[]{:S(2)}, u32[]{:S(2)}) collective-permute-start(bf16[2,256,128]{2,1,0:T(8,128)(2,1)S(1)} %pad_maximum_fusion), channel_id=1, source_target_pairs={{0,2},{1,3},{2,0},{3,1},{4,6},{5,7},{6,4},{7,5},{8,10},{9,11},{10,... | collective-permute-start | bytes 393224 | tf_op jit(solution)/shard_map/schur_z/ppermute | solution.py:315
  22.1 8.8 %collective-permute-start.1 = (bf16[2,256,128]{2,1,0:T(8,128)(2,1)S(1)}, bf16[2,256,128]{2,1,0:T(8,128)(2,1)S(1)}, u32[]{:S(2)}, u32[]{:S(2)}) collective-permute-start(bf16[2,256,128]{2,1,0:T(8,128)(2,1)S(1)} %pad_maximum_fusion), channel_id=1, source_target_pairs={{0,1},{1,0},{2,3},{3,2},{4,5},{5,4},{6,7},{7,6},{8,9},{9,8},{10,11... | collective-permute-start | bytes 393224 | tf_op jit(solution)/shard_map/schur_z/ppermute | solution.py:315
  24.0 31.4 %all-to-all-start = ((f32[8,72,128]{2,1,0:T(8,128)}), f32[8,72,128]{2,1,0:T(8,128)}, u32[]{:S(2)}, u32[]{:S(2)}) async-start(f32[8,72,128]{2,1,0:T(8,128)} %get-tuple-element.20), calls=%async_computation | async-start | bytes 589824 | tf_op jit(solution)/shard_map/all_to_all | solution.py:323
  30.9 15.4 %collective-permute-start.5 = (bf16[4,2,256,128]{3,2,1,0:T(8,128)(2,1)S(1)}, bf16[4,2,256,128]{3,2,1,0:T(8,128)(2,1)S(1)}, u32[]{:S(2)}, u32[]{:S(2)}) collective-permute-start(bf16[4,2,256,128]{3,2,1,0:T(8,128)(2,1)S(1)} %schur_z.1.refs_0_), channel_id=1, source_target_pairs={{0,24},{1,25},{2,26},{3,27},{4,28},{5,29},{6,30},{7,31},{8,0},{9,1... | collective-permute-start | bytes 1572872 | tf_op jit(solution)/shard_map/schur_y/ppermute | solution.py:319
  35.8 16.1 %collective-permute-start.4 = (bf16[4,2,256,128]{3,2,1,0:T(8,128)(2,1)S(1)}, bf16[4,2,256,128]{3,2,1,0:T(8,128)(2,1)S(1)}, u32[]{:S(2)}, u32[]{:S(2)}) collective-permute-start(bf16[4,2,256,128]{3,2,1,0:T(8,128)(2,1)S(1)} %schur_z.1.refs_0_), channel_id=1, source_target_pairs={{0,8},{1,9},{2,10},{3,11},{4,12},{5,13},{6,14},{7,15},{8,16},{9,17... | collective-permute-start | bytes 1572872 | tf_op jit(solution)/shard_map/schur_y/ppermute | solution.py:319
  46.3 14.1 %collective-permute-start.7 = (bf16[2,2,256,128]{3,2,1,0:T(8,128)(2,1)S(1)}, bf16[2,2,256,128]{3,2,1,0:T(8,128)(2,1)S(1)}, u32[]{:S(2)}, u32[]{:S(2)}) collective-permute-start(bf16[2,2,256,128]{3,2,1,0:T(8,128)(2,1)S(1)} %slice.9), channel_id=1, source_target_pairs={{0,24},{1,25},{2,26},{3,27},{4,28},{5,29},{6,30},{7,31},{8,0},{9,1... | collective-permute-start | bytes 786440 | tf_op jit(solution)/shard_map/schur_y/ppermute | solution.py:319
  52.0 9.5 %collective-permute-start.6 = (bf16[2,2,256,128]{3,2,1,0:T(8,128)(2,1)S(1)}, bf16[2,2,256,128]{3,2,1,0:T(8,128)(2,1)S(1)}, u32[]{:S(2)}, u32[]{:S(2)}) collective-permute-start(bf16[2,2,256,128]{3,2,1,0:T(8,128)(2,1)S(1)} %slice.8), channel_id=1, source_target_pairs={{0,8},{1,9},{2,10},{3,11},{4,12},{5,13},{6,14},{7,15},{8,16},{9,17... | collective-permute-start | bytes 786440 | tf_op jit(solution)/shard_map/schur_y/ppermute | solution.py:319
  57.8 36.8 %copy-start = (bf16[8,400,400]{2,1,0:T(8,128)(2,1)S(1)}, bf16[8,400,400]{2,1,0:T(8,128)(2,1)}, u32[]{:S(2)}) copy-start(bf16[8,400,400]{2,1,0:T(8,128)(2,1)} %inv_hbm.5) | copy-start | bytes 7680004
  57.8 36.8 %copy-start.1 = (s32[8,16,400]{2,1,0:T(8,128)S(1)}, s32[8,16,400]{2,1,0:T(8,128)}, u32[]{:S(2)}) copy-start(s32[8,16,400]{2,1,0:T(8,128)} %breaker_hbm.5) | copy-start | bytes 614404
  57.8 36.8 %copy-start.2 = (f32[8,16,400]{2,1,0:T(8,128)S(1)}, f32[8,16,400]{2,1,0:T(8,128)}, u32[]{:S(2)}) copy-start(f32[8,16,400]{2,1,0:T(8,128)} %volt_hbm.3) | copy-start | bytes 614404
  57.8 36.8 %copy-start.3 = (f32[8,16,400]{2,1,0:T(8,128)S(1)}, f32[8,16,400]{2,1,0:T(8,128)}, u32[]{:S(2)}) copy-start(f32[8,16,400]{2,1,0:T(8,128)} %curr_hbm.3) | copy-start | bytes 614404
  57.8 36.8 %copy-start.4 = (bf16[256,512]{1,0:T(8,128)(2,1)S(1)}, bf16[256,512]{1,0:T(8,128)(2,1)}, u32[]{:S(2)}) copy-start(bf16[256,512]{1,0:T(8,128)(2,1)} %get-tuple-element.24.right_hbm) | copy-start | bytes 786436
  57.9 36.8 %copy-start.5 = (f32[8,16,400]{2,1,0:T(8,128)S(1)}, f32[8,16,400]{2,1,0:T(8,128)}, u32[]{:S(2)}) copy-start(f32[8,16,400]{2,1,0:T(8,128)} %get-tuple-element.23.prev_hbm) | copy-start | bytes 614404
  57.9 36.8 %copy-start.6 = (f32[8,400]{1,0:T(8,128)S(1)}, f32[8,400]{1,0:T(8,128)}, u32[]{:S(2)}) copy-start(f32[8,400]{1,0:T(8,128)} %gain_hbm.5) | copy-start | bytes 38404
  57.9 36.8 %copy-start.7 = (f32[8,512]{1,0:T(8,128)S(1)}, f32[8,512]{1,0:T(8,128)}, u32[]{:S(2)}) copy-start(f32[8,512]{1,0:T(8,128)} %get-tuple-element.25.rows_hbm) | copy-start | bytes 49156
  57.9 36.8 %copy-start.9 = (f32[8,64]{1,0:T(8,128)S(1)}, f32[8,64]{1,0:T(8,128)}, u32[]{:S(2)}) copy-start(f32[8,64]{1,0:T(8,128)} %tie_hbm.3) | copy-start | bytes 6148
  57.9 36.8 %copy-start.10 = (s32[16]{0:T(128)S(1)}, s32[16]{0:T(128)}, u32[]{:S(2)}) copy-start(s32[16]{0:T(128)} %time_ref.3) | copy-start | bytes 196
  57.9 36.8 %copy-start.11 = (s32[16]{0:T(128)S(1)}, s32[16]{0:T(128)}, u32[]{:S(2)}) copy-start(s32[16]{0:T(128)} %node_ref.3) | copy-start | bytes 196

commit v9 on v8

--- a/solution.py
+++ b/solution.py
@@ -134,22 +134,17 @@
         out_ref[x] = quads[x - 1][...]
 
 
-def schur_copies(parts, schur_ref, sems):
+def schur_product(rhs_ref, parts):
     own, back, ahead, far_low, far_high = parts
-    low, high = schur_ref.at[2, pl.ds(0, 2)], schur_ref.at[2, pl.ds(2, 2)]
-    return fetch([own, back, ahead, far_low, far_high], [schur_ref.at[0], schur_ref.at[1], schur_ref.at[3], low, high], sems)
-
-
-def schur_product(rhs_ref, schur_ref, copies):
     col = lax.axis_index("col")
     own_y, own_z = col // 8, col % 8
-    wait_for(copies)
     left, right = [], []
     for n in range(4):
         for x in range(4):
             for o in range(2):
                 left.append(rhs_ref[8 * ((own_y + 4 - n) % 4) + jnp.bitwise_xor(own_z, x + 4 * o)])
-                right.append(schur_ref[n, x, o])
+                far = far_low if x < 2 else far_high
+                right.append((own, back, far, ahead)[n][x % 2 if n == 2 else x, o])
     return dot(jnp.concatenate(left, axis=1), jnp.concatenate(right, axis=1), NT)
 
 
@@ -159,28 +154,22 @@
             rhs_ref[2 * h + side] = rhs[h, :, side * LANES : (side + 1) * LANES]
 
 
-def rhs_kernel(recv_hbm, rhs_ref, map_out, recv_ref, sems):
-    wait_for(fetch([recv_hbm], [recv_ref], sems))
+def rhs_kernel(recv_ref, rhs_ref, map_out):
     map_out[...] = recv_ref[:, VALUE_ROWS:, :]
     keep(right_hand_side(recv_ref, map_out), rhs_ref)
 
 
-def product_kernel(rhs_hbm, *refs):
-    parts, (send_ref, schur_ref, rhs_ref, sems, rhs_sem) = refs[:5], refs[5:]
-    copies = schur_copies(parts, schur_ref, sems)
-    wait_for(fetch([rhs_hbm], [rhs_ref], rhs_sem))
-    total = schur_product(rhs_ref, schur_ref, copies)
+def product_kernel(rhs_ref, *refs):
+    parts, (send_ref,) = refs[:5], refs[5:]
+    total = schur_product(rhs_ref, parts)
     for r in range(send_ref.shape[0]):
         send_ref[r] = total
 
 
-def interface_kernel(recv_hbm, map_hbm, *refs):
-    parts, (iface_ref, send_ref, schur_ref, rhs_ref, recv_ref, map_ref, sems, recv_sems) = refs[:5], refs[5:]
-    arrived = fetch([map_hbm, recv_hbm], [map_ref, recv_ref], recv_sems)
-    copies = schur_copies(parts, schur_ref, sems)
-    wait_for(arrived)
+def interface_kernel(recv_ref, map_ref, *refs):
+    parts, (iface_ref, send_ref, rhs_ref) = refs[:5], refs[5:]
     keep(right_hand_side(recv_ref, map_ref), rhs_ref)
-    total = schur_product(rhs_ref, schur_ref, copies)
+    total = schur_product(rhs_ref, parts)
     iface_ref[...] = total
     half = total.astype(BF16)
     for r in range(ROWS):
@@ -207,30 +196,18 @@
     return CORES[place // (ROWS // 2)][place % (ROWS // 2)]
 
 
-def middle_kernel(time_ref, node_ref, recv_hbm, prev_hbm, volt_hbm, curr_hbm, breaker_hbm, gain_hbm, tie_hbm, right_hbm, rows_hbm, inv_hbm, volt_out, curr_out, open_ref, send_ref, recv_ref, prev_ref, right_ref, rows_ref, gain_ref, tie_ref, volt_ref, curr_ref, breaker_ref, inv_ref, sems):
-    copies = fetch(
-        [right_hbm, rows_hbm, recv_hbm, prev_hbm, volt_hbm, curr_hbm, breaker_hbm, gain_hbm, tie_hbm] + each(inv_hbm, SUBS),
-        [right_ref, rows_ref, recv_ref, prev_ref, volt_ref, curr_ref, breaker_ref, gain_ref, tie_ref] + each(inv_ref, SUBS),
-        sems,
-    )
-    wait_for(copies[:3])
+def middle_kernel(time_ref, node_ref, recv_ref, prev_ref, volt_ref, curr_ref, breaker_ref, gain_ref, tie_ref, right_ref, rows_ref, inv_ref, volt_out, curr_out, open_ref, send_ref):
     drive = driven(recv_ref, right_ref, rows_ref, paired_sender)
-    wait_for(copies[3:9])
     for k in range(SUBS):
-        copies[9 + k].wait()
         volt_out[k], curr_out[k] = update(k, drive, prev_ref, inv_ref[k, :PORTS, :], volt_ref[k], curr_ref[k], breaker_ref, gain_ref)
     open_circuit(1, volt_out, curr_out, breaker_ref, gain_ref, None, inv_ref, time_ref, node_ref, tie_ref, open_ref, send_ref)
 
 
-def last_kernel(recv_hbm, prev_hbm, volt_hbm, curr_hbm, breaker_hbm, gain_hbm, right_hbm, rows_hbm, inv_hbm, volt_out, curr_out, recv_ref, prev_ref, right_ref, rows_ref, gain_ref, volt_ref, curr_ref, breaker_ref, inv_ref, sems):
-    copies = fetch(
-        [right_hbm, rows_hbm, recv_hbm, prev_hbm, volt_hbm, curr_hbm, breaker_hbm, gain_hbm] + [inv_hbm.at[k, pl.ds(0, PORTS)] for k in range(SUBS)],
-        [right_ref, rows_ref, recv_ref, prev_ref, volt_ref, curr_ref, breaker_ref, gain_ref] + each(inv_ref, SUBS),
-        sems,
-    )
-    wait_for(copies[:3])
+def last_kernel(recv_ref, prev_ref, volt_ref, curr_ref, breaker_ref, gain_ref, right_ref, rows_ref, face_ref, inv_hbm, volt_out, curr_out, face_out, inv_ref, sems):
+    copies = fetch([inv_hbm.at[k, pl.ds(0, PORTS)] for k in range(SUBS)], each(inv_ref, SUBS), sems)
+    face_out[...] = face_ref[...]
     drive = driven(recv_ref, right_ref, rows_ref, TURNED.__getitem__)
-    wait_for(copies[3:])
+    wait_for(copies)
     for k in range(SUBS):
         volt_out[k], curr_out[k] = update(k, drive, prev_ref, inv_ref[k], volt_ref[k], curr_ref[k], breaker_ref, gain_ref)
 
@@ -240,7 +217,6 @@
 HBM = pl.BlockSpec(memory_space=pltpu.HBM)
 
 STATE = ((SUBS, SCEN, NODES), F32)
-SCHUR = ((4, 4, 2, BLOCK, LANES), BF16)
 RHS = ((COLS, SCEN, LANES), BF16)
 MAPS = ((ROWS, MAP_ROWS, LANES), F32)
 FACE = (ROWS, SCEN, BLOCK)
@@ -283,29 +259,15 @@
     ALL_VMEM,
 )
 join = call(join_kernel, [VMEM] * 5, [((4, 2, BLOCK, LANES), BF16)], [], 100_000 * GIGA, 1 << 20, 8 << 20)
-summed = call(rhs_kernel, [HBM], [RHS, MAPS], held(((ROWS, VALUE_ROWS + MAP_ROWS, LANES), F32)) + copies_of(1), GIGA, 1 << 20)
-product = call(product_kernel, [HBM] * 6, [((ROWS // 2, SCEN, BLOCK), F32)], held(SCHUR, RHS) + copies_of(5) + copies_of(1), GIGA, 3 << 20)
-interface = call(
-    interface_kernel,
-    [HBM] * 7,
-    [(FACE[1:], F32), (FACE, BF16)],
-    held(SCHUR, RHS, ((ROWS, VALUE_ROWS, LANES), BF16), MAPS) + copies_of(5) + copies_of(2),
-    GIGA,
-    3 << 20,
-)
-middle = call(
-    middle_kernel,
-    [SMEM] * 2 + [HBM] * 10,
-    [STATE, STATE, STATE, ((ROWS // 2, VALUE_ROWS, LANES), BF16)],
-    held((FACE, F32), STATE, *PICK) + [GAIN, TIE] + held(STATE, STATE) + BREAKER + INVERSE + copies_of(9 + SUBS),
-    GIGA,
-    4 << 20,
-)
+summed = call(rhs_kernel, [VMEM], [RHS, MAPS], [], GIGA, 1 << 20)
+product = call(product_kernel, [VMEM] * 6, [((ROWS // 2, SCEN, BLOCK), F32)], [], GIGA, 3 << 20)
+interface = call(interface_kernel, [VMEM] * 7, [(FACE[1:], F32), (FACE, BF16)], held(RHS), GIGA, 3 << 20)
+middle = call(middle_kernel, [SMEM] * 2 + [VMEM] * 10, [STATE, STATE, STATE, ((ROWS // 2, VALUE_ROWS, LANES), BF16)], [], GIGA, 4 << 20)
 last = call(
     last_kernel,
-    [HBM] * 9,
-    [STATE, STATE],
-    held((FACE, BF16), STATE, *PICK) + [GAIN] + held(STATE, STATE) + BREAKER + held(((SUBS, PORTS, NODES), BF16)) + copies_of(8 + SUBS),
+    [VMEM] * 9 + [HBM],
+    [STATE, STATE, (FACE[1:], F32)],
+    held(((SUBS, PORTS, NODES), BF16)) + copies_of(SUBS),
     GIGA,
     2 << 20,
 )
@@ -342,9 +304,8 @@
     rhs, maps = summed(paired_exchange(send))
     (send,) = product(rhs, *schur_rows)
     volt, curr, opened, send = middle(fault_time, fault_node, paired_exchange(send), opened, volt, curr, breaker, ind_gain, tie, *pick, local_inverse)
-    iface_block, send = interface(paired_exchange(send), maps, *schur_rows)
-    volt, curr = last(exchange(send, [TURNED]), opened, volt, curr, breaker, ind_gain, *pick, local_inverse)
-    return volt, curr, iface_block
+    face, send = interface(paired_exchange(send), maps, *schur_rows)
+    return tuple(last(exchange(send, [TURNED]), opened, volt, curr, breaker, ind_gain, *pick, face, local_inverse))
 
 
 def solution(mesh):

time: 149 us -> 144 us (0.966)
  Pallas kernels: 18.7 us -> 14 us
    pallas_call x1, Pallas kernels: 4.44 us -> 1.6 us  [local(): middle(fault_time, fault_node, paired_exchange(send), opened, volt, curr,...]
where the time goes in v9:
time: 144 us
  blocking collectives  77.5 us (54%)
  starting transfers between devices  37.2 us (26%)
  waiting for transfers between devices  14.1 us (10%)
  Pallas kernels  14 us (10%)
    all_to_all x3, blocking collectives, exchange(): return lax.all_to_all(send, 'row', 0, 0, axis_index_groups=groups)  71.2 us
    ppermute x4, starting transfers between devices, along_z(): return lax.ppermute(block, 'col', [(c, c ^ flip) for c in range(COLS)])  16 us
    ppermute x4, starting transfers between devices, along_y(): lax.ppermute(block, 'col', [(c, (c + 8 * steps) % COLS) for c in range(CO...  14.4 us
    ppermute x4, waiting for transfers between devices, along_y(): lax.ppermute(block, 'col', [(c, (c + 8 * steps) % COLS) for c in range(CO...  9.72 us
    all_to_all x1, starting transfers between devices, exchange(): return lax.all_to_all(send, 'row', 0, 0, axis_index_groups=groups)  6.81 us
    all_gather x3, blocking collectives, paired_exchange(): both = lax.all_gather(exchange(send, CORES), 'row', axis_index_groups=PAIRS)  6.39 us
    pallas_call x1, Pallas kernels, local(): first(fault_time, fault_node, volt, curr, breaker, ind_gain, tie, port_ma...  4.38 us
    pallas_call x1, Pallas kernels, local(): face, send = interface(paired_exchange(send), maps, *schur_rows)  2.94 us
  transfers between devices with their start and end apart: 9, of which 4 were waited for; matrix products, arithmetic and copies ran while one was open for 0% of the time, Pallas kernels for 5%

profile of v9, /device:TPU:448, one launch (start us, length us, event | category | flops | bytes accessed | tf_op | source)
XLA Modules:
  0.0 143.9 jit_solution(2694031182016650317)
XLA Ops:
  0.6 5.6 %collective-permute-start = (bf16[256,128]{1,0:T(8,128)(2,1)}, bf16[256,128]{1,0:T(8,128)(2,1)S(1)}, u32[]{:S(2)}, u32[]{:S(2)}) collective-permute-start(bf16[256,128]{1,0:T(8,128)(2,1)} %own_ref.1), channel_id=1, source_target_pairs={{0,4},{1,5},{2,6},{3,7},{4,0},{5,1},{6,2},{7,3},{8,12},{9,13},{10,... | collective-permute-start | bytes 196616 | tf_op jit(solution)/shard_map/schur_z/ppermute | solution.py:277
  6.2 4.4 %shard_map.121 = (f32[8,16,400]{2,1,0:T(8,128)}, f32[8,72,128]{2,1,0:T(8,128)}, bf16[256,512]{1,0:T(8,128)(2,1)}, f32[8,512]{1,0:T(8,128)}) custom-call(s32[16]{0:T(128)} %time_ref.3, s32[16]{0:T(128)} %node_ref.3, f32[8,16,400]{2,1,0:T(8,128)} %volt_ref.1, f32[8,16,400]{2,1,0:T(8,128)} %curr_ref.1, s32[8,16,400]{2,1,0:T(8,128)} %breaker_ref.3, ...), custom_call_target="tpu_custom_call" | custom-call | flops 1000000000 | bytes 4194304 | tf_op jit(solution)/shard_map/pallas_call | solution.py:296
  10.6 2.9 %collective-permute-done.across_ref = bf16[256,128]{1,0:T(8,128)(2,1)S(1)} collective-permute-done((bf16[256,128]{1,0:T(8,128)(2,1)}, bf16[256,128]{1,0:T(8,128)(2,1)S(1)}, u32[]{:S(2)}, u32[]{:S(2)}) %collective-permute-start) | collective-permute-done | bytes 65568 | tf_op jit(solution)/shard_map/schur_z/ppermute | solution.py:277
  13.5 1.9 %collective-permute-start.3 = (bf16[2,256,128]{2,1,0:T(8,128)(2,1)S(1)}, bf16[2,256,128]{2,1,0:T(8,128)(2,1)S(1)}, u32[]{:S(2)}, u32[]{:S(2)}) collective-permute-start(bf16[2,256,128]{2,1,0:T(8,128)(2,1)S(1)} %pad_maximum_fusion), channel_id=1, source_target_pairs={{0,3},{1,2},{2,1},{3,0},{4,7},{5,6},{6,5},{7,4},{8,11},{9,10},{10,... | collective-permute-start | bytes 393224 | tf_op jit(solution)/shard_map/schur_z/ppermute | solution.py:277
  15.5 6.6 %collective-permute-start.2 = (bf16[2,256,128]{2,1,0:T(8,128)(2,1)S(1)}, bf16[2,256,128]{2,1,0:T(8,128)(2,1)S(1)}, u32[]{:S(2)}, u32[]{:S(2)}) collective-permute-start(bf16[2,256,128]{2,1,0:T(8,128)(2,1)S(1)} %pad_maximum_fusion), channel_id=1, source_target_pairs={{0,2},{1,3},{2,0},{3,1},{4,6},{5,7},{6,4},{7,5},{8,10},{9,11},{10,... | collective-permute-start | bytes 393224 | tf_op jit(solution)/shard_map/schur_z/ppermute | solution.py:277
  22.1 1.9 %collective-permute-start.1 = (bf16[2,256,128]{2,1,0:T(8,128)(2,1)S(1)}, bf16[2,256,128]{2,1,0:T(8,128)(2,1)S(1)}, u32[]{:S(2)}, u32[]{:S(2)}) collective-permute-start(bf16[2,256,128]{2,1,0:T(8,128)(2,1)S(1)} %pad_maximum_fusion), channel_id=1, source_target_pairs={{0,1},{1,0},{2,3},{3,2},{4,5},{5,4},{6,7},{7,6},{8,9},{9,8},{10,11... | collective-permute-start | bytes 393224 | tf_op jit(solution)/shard_map/schur_z/ppermute | solution.py:277
  24.0 6.8 %all-to-all-start = ((f32[8,72,128]{2,1,0:T(8,128)}), f32[8,72,128]{2,1,0:T(8,128)}, u32[]{:S(2)}, u32[]{:S(2)}) async-start(f32[8,72,128]{2,1,0:T(8,128)} %get-tuple-element.18), calls=%async_computation | async-start | bytes 589824 | tf_op jit(solution)/shard_map/all_to_all | solution.py:285
  30.9 4.9 %collective-permute-start.5 = (bf16[4,2,256,128]{3,2,1,0:T(8,128)(2,1)S(1)}, bf16[4,2,256,128]{3,2,1,0:T(8,128)(2,1)S(1)}, u32[]{:S(2)}, u32[]{:S(2)}) collective-permute-start(bf16[4,2,256,128]{3,2,1,0:T(8,128)(2,1)S(1)} %schur_z.1.refs_0_), channel_id=1, source_target_pairs={{0,24},{1,25},{2,26},{3,27},{4,28},{5,29},{6,30},{7,31},{8,0},{9,1... | collective-permute-start | bytes 1572872 | tf_op jit(solution)/shard_map/schur_y/ppermute | solution.py:281
  35.8 1.9 %collective-permute-start.4 = (bf16[4,2,256,128]{3,2,1,0:T(8,128)(2,1)S(1)}, bf16[4,2,256,128]{3,2,1,0:T(8,128)(2,1)S(1)}, u32[]{:S(2)}, u32[]{:S(2)}) collective-permute-start(bf16[4,2,256,128]{3,2,1,0:T(8,128)(2,1)S(1)} %schur_z.1.refs_0_), channel_id=1, source_target_pairs={{0,8},{1,9},{2,10},{3,11},{4,12},{5,13},{6,14},{7,15},{8,16},{9,17... | collective-permute-start | bytes 1572872 | tf_op jit(solution)/shard_map/schur_y/ppermute | solution.py:281
  37.7 8.6 %collective-permute-done.5.refs_2_ = bf16[4,2,256,128]{3,2,1,0:T(8,128)(2,1)S(1)} collective-permute-done((bf16[4,2,256,128]{3,2,1,0:T(8,128)(2,1)S(1)}, bf16[4,2,256,128]{3,2,1,0:T(8,128)(2,1)S(1)}, u32[]{:S(2)}, u32[]{:S(2)}) %collective-permute-start.5) | collective-permute-done | bytes 524320 | tf_op jit(solution)/shard_map/schur_y/ppermute | solution.py:281
  46.3 5.6 %collective-permute-start.7 = (bf16[2,2,256,128]{3,2,1,0:T(8,128)(2,1)S(1)}, bf16[2,2,256,128]{3,2,1,0:T(8,128)(2,1)S(1)}, u32[]{:S(2)}, u32[]{:S(2)}) collective-permute-start(bf16[2,2,256,128]{3,2,1,0:T(8,128)(2,1)S(1)} %slice.9), channel_id=1, source_target_pairs={{0,24},{1,25},{2,26},{3,27},{4,28},{5,29},{6,30},{7,31},{8,0},{9,1... | collective-permute-start | bytes 786440 | tf_op jit(solution)/shard_map/schur_y/ppermute | solution.py:281
  52.0 1.9 %collective-permute-start.6 = (bf16[2,2,256,128]{3,2,1,0:T(8,128)(2,1)S(1)}, bf16[2,2,256,128]{3,2,1,0:T(8,128)(2,1)S(1)}, u32[]{:S(2)}, u32[]{:S(2)}) collective-permute-start(bf16[2,2,256,128]{3,2,1,0:T(8,128)(2,1)S(1)} %slice.8), channel_id=1, source_target_pairs={{0,8},{1,9},{2,10},{3,11},{4,12},{5,13},{6,14},{7,15},{8,16},{9,17... | collective-permute-start | bytes 786440 | tf_op jit(solution)/shard_map/schur_y/ppermute | solution.py:281
  53.9 1.5 %all-to-all-done = f32[8,72,128]{2,1,0:T(8,128)} async-done(((f32[8,72,128]{2,1,0:T(8,128)}), f32[8,72,128]{2,1,0:T(8,128)}, u32[]{:S(2)}, u32[]{:S(2)}) %all-to-all-start) | async-done | bytes 294944 | tf_op jit(solution)/shard_map/all_to_all | solution.py:285
  55.4 2.4 %all-gather.recv_ref = f32[16,72,128]{2,1,0:T(8,128)S(1)} all-gather(f32[8,72,128]{2,1,0:T(8,128)} %all-to-all-done), channel_id=2, replica_groups={{0,32},{64,96},{128,160},{192,224},{256,288},{320,352},{384,416},{448,4..., dimensions={0}, use_global_device_ids=true | all-gather | bytes 884736 | tf_op jit(solution)/shard_map/all_gather | solution.py:289
  57.8 0.0 copy-start.4
  57.9 0.0 copy-start.5
  57.9 0.0 copy-start.6
  57.9 0.0 copy-start.7
  57.9 0.0 copy-start.9
  57.9 0.0 copy-start.10
  57.9 0.0 copy-start.11
  57.9 2.4 %shard_map.122 = (bf16[32,16,128]{2,1,0:T(8,128)(2,1)S(1)}, f32[16,8,128]{2,1,0:T(8,128)S(1)}) custom-call(f32[16,72,128]{2,1,0:T(8,128)S(1)} %all-gather.recv_ref), custom_call_target="tpu_custom_call" | custom-call | flops 1000000000 | bytes 1048576 | tf_op jit(solution)/shard_map/pallas_call | solution.py:304
  60.3 1.1 collective-permute-done.6.refs_3_
  61.5 0.7 shard_map.123
  62.1 30.2 %all_to_all.20 = f32[8,16,256]{2,1,0:T(8,128)S(1)} all-to-all(f32[8,16,256]{2,1,0:T(8,128)S(1)} %shard_map.123), channel_id=1, replica_groups={{256,320,384,448,0,64,128,192},{288,352,416,480,32,96,160,224},{257,321..., dimensions={0} | all-to-all | bytes 262144 | tf_op jit(solution)/shard_map/all_to_all | solution.py:285
  92.3 2.0 %all-gather.1.recv_ref = f32[16,16,256]{2,1,0:T(8,128)S(1)} all-gather(f32[8,16,256]{2,1,0:T(8,128)S(1)} %all_to_all.20), channel_id=3, replica_groups={{0,32},{64,96},{128,160},{192,224},{256,288},{320,352},{384,416},{448,4..., dimensions={0}, use_global_device_ids=true | all-gather | bytes 393216 | tf_op jit(solution)/shard_map/all_gather | solution.py:289
  94.4 1.6 %shard_map.124 = (f32[8,16,400]{2,1,0:T(8,128)S(1)}, f32[8,16,400]{2,1,0:T(8,128)S(1)}, f32[8,16,400]{2,1,0:T(8,128)S(1)}, bf16[8,64,128]{2,1,0:T(8,128)(2,1)S(1)}) custom-call(s32[16]{0:T(128)S(1)} %copy-done.10, s32[16]{0:T(128)S(1)} %copy-done.11, f32[16,16,256]{2,1,0:T(8,128)S(1)} %all-gather.1.recv_ref, f32[8,16,400]{2,1,0:T(8,128)S(1)} %copy-done.5, ...), custom_call_target="tpu_custom_call" | custom-call | flops 1000000000 | bytes 4194304 | tf_op jit(solution)/shard_map/pallas_call | solution.py:306
  96.0 20.7 %all_to_all.21 = bf16[8,64,128]{2,1,0:T(8,128)(2,1)S(1)} all-to-all(bf16[8,64,128]{2,1,0:T(8,128)(2,1)S(1)} %get-tuple-element.24), channel_id=1, replica_groups={{256,320,384,448,0,64,128,192},{288,352,416,480,32,96,160,224},{257,321..., dimensions={0} | all-to-all | bytes 262144 | tf_op jit(solution)/shard_map/all_to_all | solution.py:285
  116.7 2.0 %all-gather.2.recv_ref = bf16[16,64,128]{2,1,0:T(8,128)(2,1)S(1)} all-gather(bf16[8,64,128]{2,1,0:T(8,128)(2,1)S(1)} %all_to_all.21), channel_id=4, replica_groups={{0,32},{64,96},{128,160},{192,224},{256,288},{320,352},{384,416},{448,4..., dimensions={0}, use_global_device_ids=true | all-gather | bytes 393216 | tf_op jit(solution)/shard_map/all_gather | solution.py:289
  118.6 2.9 %shard_map.125 = (f32[16,256]{1,0:T(8,128)S(1)}, bf16[16,16,256]{2,1,0:T(8,128)(2,1)S(1)}) custom-call(bf16[16,64,128]{2,1,0:T(8,128)(2,1)S(1)} %all-gather.2.recv_ref, f32[16,8,128]{2,1,0:T(8,128)S(1)} %get-tuple-element.25.map_ref, bf16[4,2,256,128]{3,2,1,0:T(8,128)(2,1)S(1)} %schur_z.1.refs_0_, ...), custom_call_target="tpu_custom_call" | custom-call | flops 1000000000 | bytes 3145728 | tf_op jit(solution)/shard_map/pallas_call | solution.py:307
  121.6 20.3 %all_to_all.22.recv_ref = bf16[16,16,256]{2,1,0:T(8,128)(2,1)S(1)} all-to-all(bf16[16,16,256]{2,1,0:T(8,128)(2,1)S(1)} %get-tuple-element.26), channel_id=1, replica_groups={{256,288,320,352,384,416,448,480,0,32,64,96,128,160,192,224},{257,289,3..., dimensions={0} | all-to-all | bytes 262144 | tf_op jit(solution)/shard_map/all_to_all | solution.py:285
  141.9 2.0 %shard_map.126 = (f32[8,16,400]{2,1,0:T(8,128)}, f32[8,16,400]{2,1,0:T(8,128)}, f32[16,256]{1,0:T(8,128)}) custom-call(bf16[16,16,256]{2,1,0:T(8,128)(2,1)S(1)} %all_to_all.22.recv_ref, f32[8,16,400]{2,1,0:T(8,128)S(1)} %get-tuple-element.27.prev_ref, f32[8,16,400]{2,1,0:T(8,128)S(1)} %get-tuple-element.28.volt_ref, ...), custom_call_target="tpu_custom_call" | custom-call | flops 1000000000 | bytes 2097152 | tf_op jit(solution)/shard_map/pallas_call | solution.py:308
  (26 shorter events, 0.1 us)
Async XLA Ops:
  0.6 12.9 %copy-start.8 = (bf16[256,128]{1,0:T(8,128)(2,1)S(1)}, bf16[256,128]{1,0:T(8,128)(2,1)}, u32[]{:S(2)}) copy-start(bf16[256,128]{1,0:T(8,128)(2,1)} %own_ref.1) | copy-start | bytes 196612
  0.6 12.9 %collective-permute-start = (bf16[256,128]{1,0:T(8,128)(2,1)}, bf16[256,128]{1,0:T(8,128)(2,1)S(1)}, u32[]{:S(2)}, u32[]{:S(2)}) collective-permute-start(bf16[256,128]{1,0:T(8,128)(2,1)} %own_ref.1), channel_id=1, source_target_pairs={{0,4},{1,5},{2,6},{3,7},{4,0},{5,1},{6,2},{7,3},{8,12},{9,13},{10,... | collective-permute-start | bytes 196616 | tf_op jit(solution)/shard_map/schur_z/ppermute | solution.py:277
  13.5 17.3 %collective-permute-start.3 = (bf16[2,256,128]{2,1,0:T(8,128)(2,1)S(1)}, bf16[2,256,128]{2,1,0:T(8,128)(2,1)S(1)}, u32[]{:S(2)}, u32[]{:S(2)}) collective-permute-start(bf16[2,256,128]{2,1,0:T(8,128)(2,1)S(1)} %pad_maximum_fusion), channel_id=1, source_target_pairs={{0,3},{1,2},{2,1},{3,0},{4,7},{5,6},{6,5},{7,4},{8,11},{9,10},{10,... | collective-permute-start | bytes 393224 | tf_op jit(solution)/shard_map/schur_z/ppermute | solution.py:277
  15.5 15.3 %collective-permute-start.2 = (bf16[2,256,128]{2,1,0:T(8,128)(2,1)S(1)}, bf16[2,256,128]{2,1,0:T(8,128)(2,1)S(1)}, u32[]{:S(2)}, u32[]{:S(2)}) collective-permute-start(bf16[2,256,128]{2,1,0:T(8,128)(2,1)S(1)} %pad_maximum_fusion), channel_id=1, source_target_pairs={{0,2},{1,3},{2,0},{3,1},{4,6},{5,7},{6,4},{7,5},{8,10},{9,11},{10,... | collective-permute-start | bytes 393224 | tf_op jit(solution)/shard_map/schur_z/ppermute | solution.py:277
  22.1 8.8 %collective-permute-start.1 = (bf16[2,256,128]{2,1,0:T(8,128)(2,1)S(1)}, bf16[2,256,128]{2,1,0:T(8,128)(2,1)S(1)}, u32[]{:S(2)}, u32[]{:S(2)}) collective-permute-start(bf16[2,256,128]{2,1,0:T(8,128)(2,1)S(1)} %pad_maximum_fusion), channel_id=1, source_target_pairs={{0,1},{1,0},{2,3},{3,2},{4,5},{5,4},{6,7},{7,6},{8,9},{9,8},{10,11... | collective-permute-start | bytes 393224 | tf_op jit(solution)/shard_map/schur_z/ppermute | solution.py:277
  24.0 31.4 %all-to-all-start = ((f32[8,72,128]{2,1,0:T(8,128)}), f32[8,72,128]{2,1,0:T(8,128)}, u32[]{:S(2)}, u32[]{:S(2)}) async-start(f32[8,72,128]{2,1,0:T(8,128)} %get-tuple-element.18), calls=%async_computation | async-start | bytes 589824 | tf_op jit(solution)/shard_map/all_to_all | solution.py:285
  30.9 15.4 %collective-permute-start.5 = (bf16[4,2,256,128]{3,2,1,0:T(8,128)(2,1)S(1)}, bf16[4,2,256,128]{3,2,1,0:T(8,128)(2,1)S(1)}, u32[]{:S(2)}, u32[]{:S(2)}) collective-permute-start(bf16[4,2,256,128]{3,2,1,0:T(8,128)(2,1)S(1)} %schur_z.1.refs_0_), channel_id=1, source_target_pairs={{0,24},{1,25},{2,26},{3,27},{4,28},{5,29},{6,30},{7,31},{8,0},{9,1... | collective-permute-start | bytes 1572872 | tf_op jit(solution)/shard_map/schur_y/ppermute | solution.py:281
  35.8 16.1 %collective-permute-start.4 = (bf16[4,2,256,128]{3,2,1,0:T(8,128)(2,1)S(1)}, bf16[4,2,256,128]{3,2,1,0:T(8,128)(2,1)S(1)}, u32[]{:S(2)}, u32[]{:S(2)}) collective-permute-start(bf16[4,2,256,128]{3,2,1,0:T(8,128)(2,1)S(1)} %schur_z.1.refs_0_), channel_id=1, source_target_pairs={{0,8},{1,9},{2,10},{3,11},{4,12},{5,13},{6,14},{7,15},{8,16},{9,17... | collective-permute-start | bytes 1572872 | tf_op jit(solution)/shard_map/schur_y/ppermute | solution.py:281
  46.3 14.0 %collective-permute-start.7 = (bf16[2,2,256,128]{3,2,1,0:T(8,128)(2,1)S(1)}, bf16[2,2,256,128]{3,2,1,0:T(8,128)(2,1)S(1)}, u32[]{:S(2)}, u32[]{:S(2)}) collective-permute-start(bf16[2,2,256,128]{3,2,1,0:T(8,128)(2,1)S(1)} %slice.9), channel_id=1, source_target_pairs={{0,24},{1,25},{2,26},{3,27},{4,28},{5,29},{6,30},{7,31},{8,0},{9,1... | collective-permute-start | bytes 786440 | tf_op jit(solution)/shard_map/schur_y/ppermute | solution.py:281
  52.0 9.5 %collective-permute-start.6 = (bf16[2,2,256,128]{3,2,1,0:T(8,128)(2,1)S(1)}, bf16[2,2,256,128]{3,2,1,0:T(8,128)(2,1)S(1)}, u32[]{:S(2)}, u32[]{:S(2)}) collective-permute-start(bf16[2,2,256,128]{3,2,1,0:T(8,128)(2,1)S(1)} %slice.8), channel_id=1, source_target_pairs={{0,8},{1,9},{2,10},{3,11},{4,12},{5,13},{6,14},{7,15},{8,16},{9,17... | collective-permute-start | bytes 786440 | tf_op jit(solution)/shard_map/schur_y/ppermute | solution.py:281
  57.8 36.4 %copy-start = (bf16[8,400,400]{2,1,0:T(8,128)(2,1)S(1)}, bf16[8,400,400]{2,1,0:T(8,128)(2,1)}, u32[]{:S(2)}) copy-start(bf16[8,400,400]{2,1,0:T(8,128)(2,1)} %inv_hbm.3) | copy-start | bytes 7680004
  57.8 36.5 %copy-start.1 = (s32[8,16,400]{2,1,0:T(8,128)S(1)}, s32[8,16,400]{2,1,0:T(8,128)}, u32[]{:S(2)}) copy-start(s32[8,16,400]{2,1,0:T(8,128)} %breaker_ref.3) | copy-start | bytes 614404
  57.8 36.5 %copy-start.2 = (f32[8,16,400]{2,1,0:T(8,128)S(1)}, f32[8,16,400]{2,1,0:T(8,128)}, u32[]{:S(2)}) copy-start(f32[8,16,400]{2,1,0:T(8,128)} %volt_ref.1) | copy-start | bytes 614404
  57.8 36.5 %copy-start.3 = (f32[8,16,400]{2,1,0:T(8,128)S(1)}, f32[8,16,400]{2,1,0:T(8,128)}, u32[]{:S(2)}) copy-start(f32[8,16,400]{2,1,0:T(8,128)} %curr_ref.1) | copy-start | bytes 614404
  57.8 36.5 %copy-start.4 = (bf16[256,512]{1,0:T(8,128)(2,1)S(1)}, bf16[256,512]{1,0:T(8,128)(2,1)}, u32[]{:S(2)}) copy-start(bf16[256,512]{1,0:T(8,128)(2,1)} %get-tuple-element.22.right_ref) | copy-start | bytes 786436
  57.9 36.5 %copy-start.5 = (f32[8,16,400]{2,1,0:T(8,128)S(1)}, f32[8,16,400]{2,1,0:T(8,128)}, u32[]{:S(2)}) copy-start(f32[8,16,400]{2,1,0:T(8,128)} %get-tuple-element.21.prev_ref) | copy-start | bytes 614404
  57.9 36.5 %copy-start.6 = (f32[8,400]{1,0:T(8,128)S(1)}, f32[8,400]{1,0:T(8,128)}, u32[]{:S(2)}) copy-start(f32[8,400]{1,0:T(8,128)} %gain_ref.3) | copy-start | bytes 38404
  57.9 36.5 %copy-start.7 = (f32[8,512]{1,0:T(8,128)S(1)}, f32[8,512]{1,0:T(8,128)}, u32[]{:S(2)}) copy-start(f32[8,512]{1,0:T(8,128)} %get-tuple-element.23.rows_ref) | copy-start | bytes 49156
  57.9 36.4 %copy-start.9 = (f32[8,64]{1,0:T(8,128)S(1)}, f32[8,64]{1,0:T(8,128)}, u32[]{:S(2)}) copy-start(f32[8,64]{1,0:T(8,128)} %tie_ref.1) | copy-start | bytes 6148
  57.9 36.4 %copy-start.10 = (s32[16]{0:T(128)S(1)}, s32[16]{0:T(128)}, u32[]{:S(2)}) copy-start(s32[16]{0:T(128)} %time_ref.3) | copy-start | bytes 196
  57.9 36.4 %copy-start.11 = (s32[16]{0:T(128)S(1)}, s32[16]{0:T(128)}, u32[]{:S(2)}) copy-start(s32[16]{0:T(128)} %node_ref.3) | copy-start | bytes 196

commit v10 on v9

--- a/solution.py
+++ b/solution.py
@@ -172,17 +172,17 @@
     total = schur_product(rhs_ref, parts)
     iface_ref[...] = total
     half = total.astype(BF16)
-    for r in range(ROWS):
+    for r in range(send_ref.shape[0]):
         send_ref[r] = half
 
 
-def driven(recv_ref, right_ref, rows_ref, sender):
+def driven(recv_ref, right_ref, rows_ref):
     hi = rows_ref[0:1, :].astype(jnp.int32)
     volts = recv_ref[...].reshape(ROWS * SCEN, BLOCK)
     found = sum(dot(part, right_ref[...]) for part in (halves(volts) if volts.dtype == F32 else (volts,)))
     picked = jnp.zeros((SCEN, OWN), F32)
     for n in range(ROWS):
-        picked += jnp.where(hi == sender(n), found[n * SCEN : (n + 1) * SCEN, :], 0.0)
+        picked += jnp.where(hi == paired_sender(n), found[n * SCEN : (n + 1) * SCEN, :], 0.0)
     return (rows_ref[1:2, :] * picked).astype(BF16)
 
 
@@ -197,7 +197,7 @@
 
 
 def middle_kernel(time_ref, node_ref, recv_ref, prev_ref, volt_ref, curr_ref, breaker_ref, gain_ref, tie_ref, right_ref, rows_ref, inv_ref, volt_out, curr_out, open_ref, send_ref):
-    drive = driven(recv_ref, right_ref, rows_ref, paired_sender)
+    drive = driven(recv_ref, right_ref, rows_ref)
     for k in range(SUBS):
         volt_out[k], curr_out[k] = update(k, drive, prev_ref, inv_ref[k, :PORTS, :], volt_ref[k], curr_ref[k], breaker_ref, gain_ref)
     open_circuit(1, volt_out, curr_out, breaker_ref, gain_ref, None, inv_ref, time_ref, node_ref, tie_ref, open_ref, send_ref)
@@ -206,7 +206,7 @@
 def last_kernel(recv_ref, prev_ref, volt_ref, curr_ref, breaker_ref, gain_ref, right_ref, rows_ref, face_ref, inv_hbm, volt_out, curr_out, face_out, inv_ref, sems):
     copies = fetch([inv_hbm.at[k, pl.ds(0, PORTS)] for k in range(SUBS)], each(inv_ref, SUBS), sems)
     face_out[...] = face_ref[...]
-    drive = driven(recv_ref, right_ref, rows_ref, TURNED.__getitem__)
+    drive = driven(recv_ref, right_ref, rows_ref)
     wait_for(copies)
     for k in range(SUBS):
         volt_out[k], curr_out[k] = update(k, drive, prev_ref, inv_ref[k], volt_ref[k], curr_ref[k], breaker_ref, gain_ref)
@@ -261,7 +261,7 @@
 join = call(join_kernel, [VMEM] * 5, [((4, 2, BLOCK, LANES), BF16)], [], 100_000 * GIGA, 1 << 20, 8 << 20)
 summed = call(rhs_kernel, [VMEM], [RHS, MAPS], [], GIGA, 1 << 20)
 product = call(product_kernel, [VMEM] * 6, [((ROWS // 2, SCEN, BLOCK), F32)], [], GIGA, 3 << 20)
-interface = call(interface_kernel, [VMEM] * 7, [(FACE[1:], F32), (FACE, BF16)], held(RHS), GIGA, 3 << 20)
+interface = call(interface_kernel, [VMEM] * 7, [(FACE[1:], F32), ((ROWS // 2, SCEN, BLOCK), BF16)], held(RHS), GIGA, 3 << 20)
 middle = call(middle_kernel, [SMEM] * 2 + [VMEM] * 10, [STATE, STATE, STATE, ((ROWS // 2, VALUE_ROWS, LANES), BF16)], [], GIGA, 4 << 20)
 last = call(
     last_kernel,
@@ -305,7 +305,7 @@
     (send,) = product(rhs, *schur_rows)
     volt, curr, opened, send = middle(fault_time, fault_node, paired_exchange(send), opened, volt, curr, breaker, ind_gain, tie, *pick, local_inverse)
     face, send = interface(paired_exchange(send), maps, *schur_rows)
-    return tuple(last(exchange(send, [TURNED]), opened, volt, curr, breaker, ind_gain, *pick, face, local_inverse))
+    return tuple(last(paired_exchange(send), opened, volt, curr, breaker, ind_gain, *pick, face, local_inverse))
 
 
 def solution(mesh):

time: 144 us -> 144 us (level)
  the two profiles are of different devices: /device:TPU:448 before, /device:TPU:449 now
where the time goes in v10:
time: 144 us; the launch traced here: 143 us
  blocking collectives  78.2 us (54%)
  starting transfers between devices  36 us (25%)
  waiting for transfers between devices  14 us (10%)
  Pallas kernels  13.9 us (10%)
    all_to_all x3, blocking collectives, exchange(): return lax.all_to_all(send, 'row', 0, 0, axis_index_groups=groups)  64.2 us
    ppermute x4, starting transfers between devices, along_z(): return lax.ppermute(block, 'col', [(c, c ^ flip) for c in range(COLS)])  15.2 us
    all_gather x4, blocking collectives, paired_exchange(): both = lax.all_gather(exchange(send, CORES), 'row', axis_index_groups=PAIRS)  14 us
    ppermute x4, starting transfers between devices, along_y(): lax.ppermute(block, 'col', [(c, (c + 8 * steps) % COLS) for c in range(CO...  13.8 us
    ppermute x4, waiting for transfers between devices, along_y(): lax.ppermute(block, 'col', [(c, (c + 8 * steps) % COLS) for c in range(CO...  7.94 us
    all_to_all x1, starting transfers between devices, exchange(): return lax.all_to_all(send, 'row', 0, 0, axis_index_groups=groups)  6.99 us
    pallas_call x1, Pallas kernels, local(): first(fault_time, fault_node, volt, curr, breaker, ind_gain, tie, port_ma...  4.38 us
    all_to_all x1, waiting for transfers between devices, exchange(): return lax.all_to_all(send, 'row', 0, 0, axis_index_groups=groups)  3.24 us
  transfers between devices with their start and end apart: 9, of which 3 were waited for; matrix products, arithmetic and copies ran while one was open for 0% of the time, Pallas kernels for 5%

profile of v10, /device:TPU:449, one launch (start us, length us, event | category | flops | bytes accessed | tf_op | source)
XLA Modules:
  0.0 143.2 jit_solution(12207687588996721397)
XLA Ops:
  0.6 5.3 %collective-permute-start = (bf16[256,128]{1,0:T(8,128)(2,1)}, bf16[256,128]{1,0:T(8,128)(2,1)S(1)}, u32[]{:S(2)}, u32[]{:S(2)}) collective-permute-start(bf16[256,128]{1,0:T(8,128)(2,1)} %own_ref.1), channel_id=1, source_target_pairs={{0,4},{1,5},{2,6},{3,7},{4,0},{5,1},{6,2},{7,3},{8,12},{9,13},{10,... | collective-permute-start | bytes 196616 | tf_op jit(solution)/shard_map/schur_z/ppermute | solution.py:277
  6.0 4.4 %shard_map.121 = (f32[8,16,400]{2,1,0:T(8,128)}, f32[8,72,128]{2,1,0:T(8,128)}, bf16[256,512]{1,0:T(8,128)(2,1)}, f32[8,512]{1,0:T(8,128)}) custom-call(s32[16]{0:T(128)} %time_ref.3, s32[16]{0:T(128)} %node_ref.3, f32[8,16,400]{2,1,0:T(8,128)} %volt_ref.1, f32[8,16,400]{2,1,0:T(8,128)} %curr_ref.1, s32[8,16,400]{2,1,0:T(8,128)} %breaker_ref.3, ...), custom_call_target="tpu_custom_call" | custom-call | flops 1000000000 | bytes 4194304 | tf_op jit(solution)/shard_map/pallas_call | solution.py:296
  10.3 2.8 %collective-permute-done.across_ref = bf16[256,128]{1,0:T(8,128)(2,1)S(1)} collective-permute-done((bf16[256,128]{1,0:T(8,128)(2,1)}, bf16[256,128]{1,0:T(8,128)(2,1)S(1)}, u32[]{:S(2)}, u32[]{:S(2)}) %collective-permute-start) | collective-permute-done | bytes 65568 | tf_op jit(solution)/shard_map/schur_z/ppermute | solution.py:277
  13.2 1.9 %collective-permute-start.3 = (bf16[2,256,128]{2,1,0:T(8,128)(2,1)S(1)}, bf16[2,256,128]{2,1,0:T(8,128)(2,1)S(1)}, u32[]{:S(2)}, u32[]{:S(2)}) collective-permute-start(bf16[2,256,128]{2,1,0:T(8,128)(2,1)S(1)} %pad_maximum_fusion), channel_id=1, source_target_pairs={{0,3},{1,2},{2,1},{3,0},{4,7},{5,6},{6,5},{7,4},{8,11},{9,10},{10,... | collective-permute-start | bytes 393224 | tf_op jit(solution)/shard_map/schur_z/ppermute | solution.py:277
  15.1 6.1 %collective-permute-start.2 = (bf16[2,256,128]{2,1,0:T(8,128)(2,1)S(1)}, bf16[2,256,128]{2,1,0:T(8,128)(2,1)S(1)}, u32[]{:S(2)}, u32[]{:S(2)}) collective-permute-start(bf16[2,256,128]{2,1,0:T(8,128)(2,1)S(1)} %pad_maximum_fusion), channel_id=1, source_target_pairs={{0,2},{1,3},{2,0},{3,1},{4,6},{5,7},{6,4},{7,5},{8,10},{9,11},{10,... | collective-permute-start | bytes 393224 | tf_op jit(solution)/shard_map/schur_z/ppermute | solution.py:277
  21.2 1.9 %collective-permute-start.1 = (bf16[2,256,128]{2,1,0:T(8,128)(2,1)S(1)}, bf16[2,256,128]{2,1,0:T(8,128)(2,1)S(1)}, u32[]{:S(2)}, u32[]{:S(2)}) collective-permute-start(bf16[2,256,128]{2,1,0:T(8,128)(2,1)S(1)} %pad_maximum_fusion), channel_id=1, source_target_pairs={{0,1},{1,0},{2,3},{3,2},{4,5},{5,4},{6,7},{7,6},{8,9},{9,8},{10,11... | collective-permute-start | bytes 393224 | tf_op jit(solution)/shard_map/schur_z/ppermute | solution.py:277
  23.2 7.0 %all-to-all-start = ((f32[8,72,128]{2,1,0:T(8,128)}), f32[8,72,128]{2,1,0:T(8,128)}, u32[]{:S(2)}, u32[]{:S(2)}) async-start(f32[8,72,128]{2,1,0:T(8,128)} %get-tuple-element.18), calls=%async_computation | async-start | bytes 589824 | tf_op jit(solution)/shard_map/all_to_all | solution.py:285
  30.2 4.6 %collective-permute-start.5 = (bf16[4,2,256,128]{3,2,1,0:T(8,128)(2,1)S(1)}, bf16[4,2,256,128]{3,2,1,0:T(8,128)(2,1)S(1)}, u32[]{:S(2)}, u32[]{:S(2)}) collective-permute-start(bf16[4,2,256,128]{3,2,1,0:T(8,128)(2,1)S(1)} %schur_z.1.refs_0_), channel_id=1, source_target_pairs={{0,24},{1,25},{2,26},{3,27},{4,28},{5,29},{6,30},{7,31},{8,0},{9,1... | collective-permute-start | bytes 1572872 | tf_op jit(solution)/shard_map/schur_y/ppermute | solution.py:281
  34.9 1.9 %collective-permute-start.4 = (bf16[4,2,256,128]{3,2,1,0:T(8,128)(2,1)S(1)}, bf16[4,2,256,128]{3,2,1,0:T(8,128)(2,1)S(1)}, u32[]{:S(2)}, u32[]{:S(2)}) collective-permute-start(bf16[4,2,256,128]{3,2,1,0:T(8,128)(2,1)S(1)} %schur_z.1.refs_0_), channel_id=1, source_target_pairs={{0,8},{1,9},{2,10},{3,11},{4,12},{5,13},{6,14},{7,15},{8,16},{9,17... | collective-permute-start | bytes 1572872 | tf_op jit(solution)/shard_map/schur_y/ppermute | solution.py:281
  36.8 7.9 %collective-permute-done.5.refs_2_ = bf16[4,2,256,128]{3,2,1,0:T(8,128)(2,1)S(1)} collective-permute-done((bf16[4,2,256,128]{3,2,1,0:T(8,128)(2,1)S(1)}, bf16[4,2,256,128]{3,2,1,0:T(8,128)(2,1)S(1)}, u32[]{:S(2)}, u32[]{:S(2)}) %collective-permute-start.5) | collective-permute-done | bytes 524320 | tf_op jit(solution)/shard_map/schur_y/ppermute | solution.py:281
  44.8 5.3 %collective-permute-start.7 = (bf16[2,2,256,128]{3,2,1,0:T(8,128)(2,1)S(1)}, bf16[2,2,256,128]{3,2,1,0:T(8,128)(2,1)S(1)}, u32[]{:S(2)}, u32[]{:S(2)}) collective-permute-start(bf16[2,2,256,128]{3,2,1,0:T(8,128)(2,1)S(1)} %slice.9), channel_id=1, source_target_pairs={{0,24},{1,25},{2,26},{3,27},{4,28},{5,29},{6,30},{7,31},{8,0},{9,1... | collective-permute-start | bytes 786440 | tf_op jit(solution)/shard_map/schur_y/ppermute | solution.py:281
  50.1 1.9 %collective-permute-start.6 = (bf16[2,2,256,128]{3,2,1,0:T(8,128)(2,1)S(1)}, bf16[2,2,256,128]{3,2,1,0:T(8,128)(2,1)S(1)}, u32[]{:S(2)}, u32[]{:S(2)}) collective-permute-start(bf16[2,2,256,128]{3,2,1,0:T(8,128)(2,1)S(1)} %slice.8), channel_id=1, source_target_pairs={{0,8},{1,9},{2,10},{3,11},{4,12},{5,13},{6,14},{7,15},{8,16},{9,17... | collective-permute-start | bytes 786440 | tf_op jit(solution)/shard_map/schur_y/ppermute | solution.py:281
  52.0 3.2 %all-to-all-done = f32[8,72,128]{2,1,0:T(8,128)} async-done(((f32[8,72,128]{2,1,0:T(8,128)}), f32[8,72,128]{2,1,0:T(8,128)}, u32[]{:S(2)}, u32[]{:S(2)}) %all-to-all-start) | async-done | bytes 294944 | tf_op jit(solution)/shard_map/all_to_all | solution.py:285
  55.3 2.8 %all-gather.recv_ref = f32[16,72,128]{2,1,0:T(8,128)S(1)} all-gather(f32[8,72,128]{2,1,0:T(8,128)} %all-to-all-done), channel_id=2, replica_groups={{0,32},{64,96},{128,160},{192,224},{256,288},{320,352},{384,416},{448,4..., dimensions={0}, use_global_device_ids=true | all-gather | bytes 884736 | tf_op jit(solution)/shard_map/all_gather | solution.py:289
  58.1 0.0 copy-start.4
  58.2 0.0 copy-start.5
  58.2 0.0 copy-start.6
  58.2 0.0 copy-start.7
  58.2 0.0 copy-start.9
  58.2 0.0 copy-start.10
  58.2 0.0 copy-start.11
  58.2 2.4 %shard_map.122 = (bf16[32,16,128]{2,1,0:T(8,128)(2,1)S(1)}, f32[16,8,128]{2,1,0:T(8,128)S(1)}) custom-call(f32[16,72,128]{2,1,0:T(8,128)S(1)} %all-gather.recv_ref), custom_call_target="tpu_custom_call" | custom-call | flops 1000000000 | bytes 1048576 | tf_op jit(solution)/shard_map/pallas_call | solution.py:304
  60.6 0.7 shard_map.123
  61.3 27.3 %all_to_all.20 = f32[8,16,256]{2,1,0:T(8,128)S(1)} all-to-all(f32[8,16,256]{2,1,0:T(8,128)S(1)} %shard_map.123), channel_id=1, replica_groups={{256,320,384,448,0,64,128,192},{288,352,416,480,32,96,160,224},{257,321..., dimensions={0} | all-to-all | bytes 262144 | tf_op jit(solution)/shard_map/all_to_all | solution.py:285
  88.6 6.0 %all-gather.1.recv_ref = f32[16,16,256]{2,1,0:T(8,128)S(1)} all-gather(f32[8,16,256]{2,1,0:T(8,128)S(1)} %all_to_all.20), channel_id=3, replica_groups={{0,32},{64,96},{128,160},{192,224},{256,288},{320,352},{384,416},{448,4..., dimensions={0}, use_global_device_ids=true | all-gather | bytes 393216 | tf_op jit(solution)/shard_map/all_gather | solution.py:289
  94.7 1.6 %shard_map.124 = (f32[8,16,400]{2,1,0:T(8,128)S(1)}, f32[8,16,400]{2,1,0:T(8,128)S(1)}, f32[8,16,400]{2,1,0:T(8,128)S(1)}, bf16[8,64,128]{2,1,0:T(8,128)(2,1)S(1)}) custom-call(s32[16]{0:T(128)S(1)} %copy-done.10, s32[16]{0:T(128)S(1)} %copy-done.11, f32[16,16,256]{2,1,0:T(8,128)S(1)} %all-gather.1.recv_ref, f32[8,16,400]{2,1,0:T(8,128)S(1)} %copy-done.5, ...), custom_call_target="tpu_custom_call" | custom-call | flops 1000000000 | bytes 4194304 | tf_op jit(solution)/shard_map/pallas_call | solution.py:306
  96.3 20.3 %all_to_all.21 = bf16[8,64,128]{2,1,0:T(8,128)(2,1)S(1)} all-to-all(bf16[8,64,128]{2,1,0:T(8,128)(2,1)S(1)} %get-tuple-element.24), channel_id=1, replica_groups={{256,320,384,448,0,64,128,192},{288,352,416,480,32,96,160,224},{257,321..., dimensions={0} | all-to-all | bytes 262144 | tf_op jit(solution)/shard_map/all_to_all | solution.py:285
  116.6 2.3 %all-gather.2.recv_ref = bf16[16,64,128]{2,1,0:T(8,128)(2,1)S(1)} all-gather(bf16[8,64,128]{2,1,0:T(8,128)(2,1)S(1)} %all_to_all.21), channel_id=4, replica_groups={{0,32},{64,96},{128,160},{192,224},{256,288},{320,352},{384,416},{448,4..., dimensions={0}, use_global_device_ids=true | all-gather | bytes 393216 | tf_op jit(solution)/shard_map/all_gather | solution.py:289
  119.0 2.9 %shard_map.125 = (f32[16,256]{1,0:T(8,128)S(1)}, bf16[8,16,256]{2,1,0:T(8,128)(2,1)S(1)}) custom-call(bf16[16,64,128]{2,1,0:T(8,128)(2,1)S(1)} %all-gather.2.recv_ref, f32[16,8,128]{2,1,0:T(8,128)S(1)} %get-tuple-element.25.map_ref, bf16[4,2,256,128]{3,2,1,0:T(8,128)(2,1)S(1)} %schur_z.1.refs_0_, ...), custom_call_target="tpu_custom_call" | custom-call | flops 1000000000 | bytes 3145728 | tf_op jit(solution)/shard_map/pallas_call | solution.py:307
  121.9 16.6 %all_to_all.22 = bf16[8,16,256]{2,1,0:T(8,128)(2,1)S(1)} all-to-all(bf16[8,16,256]{2,1,0:T(8,128)(2,1)S(1)} %get-tuple-element.26), channel_id=1, replica_groups={{256,320,384,448,0,64,128,192},{288,352,416,480,32,96,160,224},{257,321..., dimensions={0} | all-to-all | bytes 131072 | tf_op jit(solution)/shard_map/all_to_all | solution.py:285
  138.4 2.8 %all-gather.3.recv_ref = bf16[16,16,256]{2,1,0:T(8,128)(2,1)S(1)} all-gather(bf16[8,16,256]{2,1,0:T(8,128)(2,1)S(1)} %all_to_all.22), channel_id=5, replica_groups={{0,32},{64,96},{128,160},{192,224},{256,288},{320,352},{384,416},{448,4..., dimensions={0}, use_global_device_ids=true | all-gather | bytes 196608 | tf_op jit(solution)/shard_map/all_gather | solution.py:289
  141.2 2.0 %shard_map.126 = (f32[8,16,400]{2,1,0:T(8,128)}, f32[8,16,400]{2,1,0:T(8,128)}, f32[16,256]{1,0:T(8,128)}) custom-call(bf16[16,16,256]{2,1,0:T(8,128)(2,1)S(1)} %all-gather.3.recv_ref, f32[8,16,400]{2,1,0:T(8,128)S(1)} %get-tuple-element.27.prev_ref, f32[8,16,400]{2,1,0:T(8,128)S(1)} %get-tuple-element.28.volt_ref, ...), custom_call_target="tpu_custom_call" | custom-call | flops 1000000000 | bytes 2097152 | tf_op jit(solution)/shard_map/pallas_call | solution.py:308
  (27 shorter events, 0.1 us)
Async XLA Ops:
  0.6 12.6 %copy-start.8 = (bf16[256,128]{1,0:T(8,128)(2,1)S(1)}, bf16[256,128]{1,0:T(8,128)(2,1)}, u32[]{:S(2)}) copy-start(bf16[256,128]{1,0:T(8,128)(2,1)} %own_ref.1) | copy-start | bytes 196612
  0.6 12.5 %collective-permute-start = (bf16[256,128]{1,0:T(8,128)(2,1)}, bf16[256,128]{1,0:T(8,128)(2,1)S(1)}, u32[]{:S(2)}, u32[]{:S(2)}) collective-permute-start(bf16[256,128]{1,0:T(8,128)(2,1)} %own_ref.1), channel_id=1, source_target_pairs={{0,4},{1,5},{2,6},{3,7},{4,0},{5,1},{6,2},{7,3},{8,12},{9,13},{10,... | collective-permute-start | bytes 196616 | tf_op jit(solution)/shard_map/schur_z/ppermute | solution.py:277
  13.2 16.9 %collective-permute-start.3 = (bf16[2,256,128]{2,1,0:T(8,128)(2,1)S(1)}, bf16[2,256,128]{2,1,0:T(8,128)(2,1)S(1)}, u32[]{:S(2)}, u32[]{:S(2)}) collective-permute-start(bf16[2,256,128]{2,1,0:T(8,128)(2,1)S(1)} %pad_maximum_fusion), channel_id=1, source_target_pairs={{0,3},{1,2},{2,1},{3,0},{4,7},{5,6},{6,5},{7,4},{8,11},{9,10},{10,... | collective-permute-start | bytes 393224 | tf_op jit(solution)/shard_map/schur_z/ppermute | solution.py:277
  15.1 15.0 %collective-permute-start.2 = (bf16[2,256,128]{2,1,0:T(8,128)(2,1)S(1)}, bf16[2,256,128]{2,1,0:T(8,128)(2,1)S(1)}, u32[]{:S(2)}, u32[]{:S(2)}) collective-permute-start(bf16[2,256,128]{2,1,0:T(8,128)(2,1)S(1)} %pad_maximum_fusion), channel_id=1, source_target_pairs={{0,2},{1,3},{2,0},{3,1},{4,6},{5,7},{6,4},{7,5},{8,10},{9,11},{10,... | collective-permute-start | bytes 393224 | tf_op jit(solution)/shard_map/schur_z/ppermute | solution.py:277
  21.2 8.9 %collective-permute-start.1 = (bf16[2,256,128]{2,1,0:T(8,128)(2,1)S(1)}, bf16[2,256,128]{2,1,0:T(8,128)(2,1)S(1)}, u32[]{:S(2)}, u32[]{:S(2)}) collective-permute-start(bf16[2,256,128]{2,1,0:T(8,128)(2,1)S(1)} %pad_maximum_fusion), channel_id=1, source_target_pairs={{0,1},{1,0},{2,3},{3,2},{4,5},{5,4},{6,7},{7,6},{8,9},{9,8},{10,11... | collective-permute-start | bytes 393224 | tf_op jit(solution)/shard_map/schur_z/ppermute | solution.py:277
  23.2 32.1 %all-to-all-start = ((f32[8,72,128]{2,1,0:T(8,128)}), f32[8,72,128]{2,1,0:T(8,128)}, u32[]{:S(2)}, u32[]{:S(2)}) async-start(f32[8,72,128]{2,1,0:T(8,128)} %get-tuple-element.18), calls=%async_computation | async-start | bytes 589824 | tf_op jit(solution)/shard_map/all_to_all | solution.py:285
  30.2 14.5 %collective-permute-start.5 = (bf16[4,2,256,128]{3,2,1,0:T(8,128)(2,1)S(1)}, bf16[4,2,256,128]{3,2,1,0:T(8,128)(2,1)S(1)}, u32[]{:S(2)}, u32[]{:S(2)}) collective-permute-start(bf16[4,2,256,128]{3,2,1,0:T(8,128)(2,1)S(1)} %schur_z.1.refs_0_), channel_id=1, source_target_pairs={{0,24},{1,25},{2,26},{3,27},{4,28},{5,29},{6,30},{7,31},{8,0},{9,1... | collective-permute-start | bytes 1572872 | tf_op jit(solution)/shard_map/schur_y/ppermute | solution.py:281
  34.9 15.2 %collective-permute-start.4 = (bf16[4,2,256,128]{3,2,1,0:T(8,128)(2,1)S(1)}, bf16[4,2,256,128]{3,2,1,0:T(8,128)(2,1)S(1)}, u32[]{:S(2)}, u32[]{:S(2)}) collective-permute-start(bf16[4,2,256,128]{3,2,1,0:T(8,128)(2,1)S(1)} %schur_z.1.refs_0_), channel_id=1, source_target_pairs={{0,8},{1,9},{2,10},{3,11},{4,12},{5,13},{6,14},{7,15},{8,16},{9,17... | collective-permute-start | bytes 1572872 | tf_op jit(solution)/shard_map/schur_y/ppermute | solution.py:281
  44.8 15.9 %collective-permute-start.7 = (bf16[2,2,256,128]{3,2,1,0:T(8,128)(2,1)S(1)}, bf16[2,2,256,128]{3,2,1,0:T(8,128)(2,1)S(1)}, u32[]{:S(2)}, u32[]{:S(2)}) collective-permute-start(bf16[2,2,256,128]{3,2,1,0:T(8,128)(2,1)S(1)} %slice.9), channel_id=1, source_target_pairs={{0,24},{1,25},{2,26},{3,27},{4,28},{5,29},{6,30},{7,31},{8,0},{9,1... | collective-permute-start | bytes 786440 | tf_op jit(solution)/shard_map/schur_y/ppermute | solution.py:281
  50.1 10.5 %collective-permute-start.6 = (bf16[2,2,256,128]{3,2,1,0:T(8,128)(2,1)S(1)}, bf16[2,2,256,128]{3,2,1,0:T(8,128)(2,1)S(1)}, u32[]{:S(2)}, u32[]{:S(2)}) collective-permute-start(bf16[2,2,256,128]{3,2,1,0:T(8,128)(2,1)S(1)} %slice.8), channel_id=1, source_target_pairs={{0,8},{1,9},{2,10},{3,11},{4,12},{5,13},{6,14},{7,15},{8,16},{9,17... | collective-permute-start | bytes 786440 | tf_op jit(solution)/shard_map/schur_y/ppermute | solution.py:281
  58.1 36.5 %copy-start = (bf16[8,400,400]{2,1,0:T(8,128)(2,1)S(1)}, bf16[8,400,400]{2,1,0:T(8,128)(2,1)}, u32[]{:S(2)}) copy-start(bf16[8,400,400]{2,1,0:T(8,128)(2,1)} %inv_hbm.3) | copy-start | bytes 7680004
  58.1 36.5 %copy-start.1 = (s32[8,16,400]{2,1,0:T(8,128)S(1)}, s32[8,16,400]{2,1,0:T(8,128)}, u32[]{:S(2)}) copy-start(s32[8,16,400]{2,1,0:T(8,128)} %breaker_ref.3) | copy-start | bytes 614404
  58.1 36.5 %copy-start.2 = (f32[8,16,400]{2,1,0:T(8,128)S(1)}, f32[8,16,400]{2,1,0:T(8,128)}, u32[]{:S(2)}) copy-start(f32[8,16,400]{2,1,0:T(8,128)} %volt_ref.1) | copy-start | bytes 614404
  58.1 36.5 %copy-start.3 = (f32[8,16,400]{2,1,0:T(8,128)S(1)}, f32[8,16,400]{2,1,0:T(8,128)}, u32[]{:S(2)}) copy-start(f32[8,16,400]{2,1,0:T(8,128)} %curr_ref.1) | copy-start | bytes 614404
  58.1 36.5 %copy-start.4 = (bf16[256,512]{1,0:T(8,128)(2,1)S(1)}, bf16[256,512]{1,0:T(8,128)(2,1)}, u32[]{:S(2)}) copy-start(bf16[256,512]{1,0:T(8,128)(2,1)} %get-tuple-element.22.right_ref) | copy-start | bytes 786436
  58.2 36.5 %copy-start.5 = (f32[8,16,400]{2,1,0:T(8,128)S(1)}, f32[8,16,400]{2,1,0:T(8,128)}, u32[]{:S(2)}) copy-start(f32[8,16,400]{2,1,0:T(8,128)} %get-tuple-element.21.prev_ref) | copy-start | bytes 614404
  58.2 36.5 %copy-start.6 = (f32[8,400]{1,0:T(8,128)S(1)}, f32[8,400]{1,0:T(8,128)}, u32[]{:S(2)}) copy-start(f32[8,400]{1,0:T(8,128)} %gain_ref.3) | copy-start | bytes 38404
  58.2 36.5 %copy-start.7 = (f32[8,512]{1,0:T(8,128)S(1)}, f32[8,512]{1,0:T(8,128)}, u32[]{:S(2)}) copy-start(f32[8,512]{1,0:T(8,128)} %get-tuple-element.23.rows_ref) | copy-start | bytes 49156
  58.2 36.5 %copy-start.9 = (f32[8,64]{1,0:T(8,128)S(1)}, f32[8,64]{1,0:T(8,128)}, u32[]{:S(2)}) copy-start(f32[8,64]{1,0:T(8,128)} %tie_ref.1) | copy-start | bytes 6148
  58.2 36.5 %copy-start.10 = (s32[16]{0:T(128)S(1)}, s32[16]{0:T(128)}, u32[]{:S(2)}) copy-start(s32[16]{0:T(128)} %time_ref.3) | copy-start | bytes 196
  58.2 36.5 %copy-start.11 = (s32[16]{0:T(128)S(1)}, s32[16]{0:T(128)}, u32[]{:S(2)}) copy-start(s32[16]{0:T(128)} %node_ref.3) | copy-start | bytes 196

commit v11 on v10

--- a/solution.py
+++ b/solution.py
@@ -126,16 +126,16 @@
     return rhs.astype(BF16).reshape(ROWS, SCEN, BLOCK)
 
 
-def join_kernel(own_ref, across_ref, *refs):
-    quads, (out_ref,) = refs[:3], refs[3:]
-    out_ref[0, 0] = own_ref[...]
-    out_ref[0, 1] = across_ref[...]
-    for x in (1, 2, 3):
-        out_ref[x] = quads[x - 1][...]
+def join_kernel(own_ref, across_ref, near_ref, mid_ref, far_ref, low_ref, high_ref):
+    low_ref[0, 0] = own_ref[...]
+    low_ref[0, 1] = across_ref[...]
+    low_ref[1] = near_ref[...]
+    high_ref[0] = mid_ref[...]
+    high_ref[1] = far_ref[...]
 
 
 def schur_product(rhs_ref, parts):
-    own, back, ahead, far_low, far_high = parts
+    parts = [parts[2 * y : 2 * y + 2] for y in range(4)]
     col = lax.axis_index("col")
     own_y, own_z = col // 8, col % 8
     left, right = [], []
@@ -143,8 +143,7 @@
         for x in range(4):
             for o in range(2):
                 left.append(rhs_ref[8 * ((own_y + 4 - n) % 4) + jnp.bitwise_xor(own_z, x + 4 * o)])
-                far = far_low if x < 2 else far_high
-                right.append((own, back, far, ahead)[n][x % 2 if n == 2 else x, o])
+                right.append(parts[n][x // 2][x % 2, o])
     return dot(jnp.concatenate(left, axis=1), jnp.concatenate(right, axis=1), NT)
 
 
@@ -160,14 +159,14 @@
 
 
 def product_kernel(rhs_ref, *refs):
-    parts, (send_ref,) = refs[:5], refs[5:]
+    parts, (send_ref,) = refs[:8], refs[8:]
     total = schur_product(rhs_ref, parts)
     for r in range(send_ref.shape[0]):
         send_ref[r] = total
 
 
 def interface_kernel(recv_ref, map_ref, *refs):
-    parts, (iface_ref, send_ref, rhs_ref) = refs[:5], refs[5:]
+    parts, (iface_ref, send_ref, rhs_ref) = refs[:8], refs[8:]
     keep(right_hand_side(recv_ref, map_ref), rhs_ref)
     total = schur_product(rhs_ref, parts)
     iface_ref[...] = total
@@ -258,10 +257,10 @@
     4 << 20,
     ALL_VMEM,
 )
-join = call(join_kernel, [VMEM] * 5, [((4, 2, BLOCK, LANES), BF16)], [], 100_000 * GIGA, 1 << 20, 8 << 20)
+join = call(join_kernel, [VMEM] * 5, [((2, 2, BLOCK, LANES), BF16)] * 2, [], 100_000 * GIGA, 1 << 20, 8 << 20)
 summed = call(rhs_kernel, [VMEM], [RHS, MAPS], [], GIGA, 1 << 20)
-product = call(product_kernel, [VMEM] * 6, [((ROWS // 2, SCEN, BLOCK), F32)], [], GIGA, 3 << 20)
-interface = call(interface_kernel, [VMEM] * 7, [(FACE[1:], F32), ((ROWS // 2, SCEN, BLOCK), BF16)], held(RHS), GIGA, 3 << 20)
+product = call(product_kernel, [VMEM] * 9, [((ROWS // 2, SCEN, BLOCK), F32)], [], GIGA, 3 << 20)
+interface = call(interface_kernel, [VMEM] * 10, [(FACE[1:], F32), ((ROWS // 2, SCEN, BLOCK), BF16)], held(RHS), GIGA, 3 << 20)
 middle = call(middle_kernel, [SMEM] * 2 + [VMEM] * 10, [STATE, STATE, STATE, ((ROWS // 2, VALUE_ROWS, LANES), BF16)], [], GIGA, 4 << 20)
 last = call(
     last_kernel,
@@ -297,10 +296,10 @@
     across, send = lax.optimization_barrier((across, send))
     with jax.named_scope("schur_z"):
         pair = jnp.stack([schur_inverse, across])
-        (own,) = join(schur_inverse, across, *(along_z(pair, x) for x in (1, 2, 3)))
+        low, high = join(schur_inverse, across, *(along_z(pair, x) for x in (1, 2, 3)))
     with jax.named_scope("schur_y"):
-        back, ahead = along_y(own, 1), along_y(own, -1)
-        schur_rows = own, back, ahead, along_y(back[:2], 1), along_y(ahead[2:], -1)
+        back, ahead = along_y(low, 1), along_y(high, -1)
+        schur_rows = low, high, back, along_y(high, 1), along_y(back, 1), along_y(ahead, -1), along_y(low, -1), ahead
     rhs, maps = summed(paired_exchange(send))
     (send,) = product(rhs, *schur_rows)
     volt, curr, opened, send = middle(fault_time, fault_node, paired_exchange(send), opened, volt, curr, breaker, ind_gain, tie, *pick, local_inverse)

time: 144 us -> 140 us (0.972)
  starting transfers between devices: 36 us -> 40.6 us
  waiting for transfers between devices: 14 us -> 9.53 us
  blocking collectives: 78.2 us -> 74 us
    ppermute x4 -> x6, waiting for transfers between devices: 7.94 us -> 0.02 us  [along_y(): lax.ppermute(block, 'col', [(c, (c + 8 * steps) % COLS) for c in range(CO...]
    ppermute x4 -> x6, starting transfers between devices: 13.8 us -> 18.3 us  [along_y(): lax.ppermute(block, 'col', [(c, (c + 8 * steps) % COLS) for c in range(CO...]
    all_to_all x1, waiting for transfers between devices: 3.24 us -> 6.66 us  [exchange(): return lax.all_to_all(send, 'row', 0, 0, axis_index_groups=groups)]
    all_gather x4, blocking collectives: 14 us -> 10.8 us  [paired_exchange(): both = lax.all_gather(exchange(send, CORES), 'row', axis_index_groups=PAIRS)]
  transfers between devices with their start and end apart: 9 -> 11, of which waited for: 3 -> 2; matrix products, arithmetic and copies ran while one was open for 0% -> 0% of each run, Pallas kernels for 5% -> 5%
where the time goes in v11:
time: 140 us; the launch traced here: 139 us
  blocking collectives  74 us (53%)
  starting transfers between devices  40.6 us (29%)
  Pallas kernels  13.9 us (10%)
  waiting for transfers between devices  9.53 us (7%)
    all_to_all x3, blocking collectives, exchange(): return lax.all_to_all(send, 'row', 0, 0, axis_index_groups=groups)  63.2 us
    ppermute x6, starting transfers between devices, along_y(): lax.ppermute(block, 'col', [(c, (c + 8 * steps) % COLS) for c in range(CO...  18.3 us
    ppermute x4, starting transfers between devices, along_z(): return lax.ppermute(block, 'col', [(c, c ^ flip) for c in range(COLS)])  15.2 us
    all_gather x4, blocking collectives, paired_exchange(): both = lax.all_gather(exchange(send, CORES), 'row', axis_index_groups=PAIRS)  10.8 us
    all_to_all x1, starting transfers between devices, exchange(): return lax.all_to_all(send, 'row', 0, 0, axis_index_groups=groups)  6.99 us
    all_to_all x1, waiting for transfers between devices, exchange(): return lax.all_to_all(send, 'row', 0, 0, axis_index_groups=groups)  6.66 us
    pallas_call x1, Pallas kernels, local(): first(fault_time, fault_node, volt, curr, breaker, ind_gain, tie, port_ma...  4.38 us
    pallas_call x1, Pallas kernels, local(): face, send = interface(paired_exchange(send), maps, *schur_rows)  2.91 us
  transfers between devices with their start and end apart: 11, of which 2 were waited for; matrix products, arithmetic and copies ran while one was open for 0% of the time, Pallas kernels for 5%

profile of v11, /device:TPU:449, one launch (start us, length us, event | category | flops | bytes accessed | tf_op | source)
XLA Modules:
  0.0 139.1 jit_solution(7864960949447714829)
XLA Ops:
  0.6 5.3 %collective-permute-start = (bf16[256,128]{1,0:T(8,128)(2,1)}, bf16[256,128]{1,0:T(8,128)(2,1)S(1)}, u32[]{:S(2)}, u32[]{:S(2)}) collective-permute-start(bf16[256,128]{1,0:T(8,128)(2,1)} %own_ref.1), channel_id=1, source_target_pairs={{0,4},{1,5},{2,6},{3,7},{4,0},{5,1},{6,2},{7,3},{8,12},{9,13},{10,... | collective-permute-start | bytes 196616 | tf_op jit(solution)/shard_map/schur_z/ppermute | solution.py:276
  6.0 4.4 %shard_map.121 = (f32[8,16,400]{2,1,0:T(8,128)}, f32[8,72,128]{2,1,0:T(8,128)}, bf16[256,512]{1,0:T(8,128)(2,1)}, f32[8,512]{1,0:T(8,128)}) custom-call(s32[16]{0:T(128)} %time_ref.3, s32[16]{0:T(128)} %node_ref.3, f32[8,16,400]{2,1,0:T(8,128)} %volt_ref.1, f32[8,16,400]{2,1,0:T(8,128)} %curr_ref.1, s32[8,16,400]{2,1,0:T(8,128)} %breaker_ref.3, ...), custom_call_target="tpu_custom_call" | custom-call | flops 1000000000 | bytes 4194304 | tf_op jit(solution)/shard_map/pallas_call | solution.py:295
  10.3 2.8 %collective-permute-done.across_ref = bf16[256,128]{1,0:T(8,128)(2,1)S(1)} collective-permute-done((bf16[256,128]{1,0:T(8,128)(2,1)}, bf16[256,128]{1,0:T(8,128)(2,1)S(1)}, u32[]{:S(2)}, u32[]{:S(2)}) %collective-permute-start) | collective-permute-done | bytes 65568 | tf_op jit(solution)/shard_map/schur_z/ppermute | solution.py:276
  13.2 1.9 %collective-permute-start.3 = (bf16[2,256,128]{2,1,0:T(8,128)(2,1)S(1)}, bf16[2,256,128]{2,1,0:T(8,128)(2,1)S(1)}, u32[]{:S(2)}, u32[]{:S(2)}) collective-permute-start(bf16[2,256,128]{2,1,0:T(8,128)(2,1)S(1)} %pad_maximum_fusion), channel_id=1, source_target_pairs={{0,3},{1,2},{2,1},{3,0},{4,7},{5,6},{6,5},{7,4},{8,11},{9,10},{10,... | collective-permute-start | bytes 393224 | tf_op jit(solution)/shard_map/schur_z/ppermute | solution.py:276
  15.1 6.1 %collective-permute-start.2 = (bf16[2,256,128]{2,1,0:T(8,128)(2,1)S(1)}, bf16[2,256,128]{2,1,0:T(8,128)(2,1)S(1)}, u32[]{:S(2)}, u32[]{:S(2)}) collective-permute-start(bf16[2,256,128]{2,1,0:T(8,128)(2,1)S(1)} %pad_maximum_fusion), channel_id=1, source_target_pairs={{0,2},{1,3},{2,0},{3,1},{4,6},{5,7},{6,4},{7,5},{8,10},{9,11},{10,... | collective-permute-start | bytes 393224 | tf_op jit(solution)/shard_map/schur_z/ppermute | solution.py:276
  21.2 1.9 %collective-permute-start.1 = (bf16[2,256,128]{2,1,0:T(8,128)(2,1)S(1)}, bf16[2,256,128]{2,1,0:T(8,128)(2,1)S(1)}, u32[]{:S(2)}, u32[]{:S(2)}) collective-permute-start(bf16[2,256,128]{2,1,0:T(8,128)(2,1)S(1)} %pad_maximum_fusion), channel_id=1, source_target_pairs={{0,1},{1,0},{2,3},{3,2},{4,5},{5,4},{6,7},{7,6},{8,9},{9,8},{10,11... | collective-permute-start | bytes 393224 | tf_op jit(solution)/shard_map/schur_z/ppermute | solution.py:276
  23.2 7.0 %all-to-all-start = ((f32[8,72,128]{2,1,0:T(8,128)}), f32[8,72,128]{2,1,0:T(8,128)}, u32[]{:S(2)}, u32[]{:S(2)}) async-start(f32[8,72,128]{2,1,0:T(8,128)} %get-tuple-element.20), calls=%async_computation | async-start | bytes 589824 | tf_op jit(solution)/shard_map/all_to_all | solution.py:284
  30.2 3.2 %collective-permute-start.4 = (bf16[2,2,256,128]{3,2,1,0:T(8,128)(2,1)S(1)}, bf16[2,2,256,128]{3,2,1,0:T(8,128)(2,1)S(1)}, u32[]{:S(2)}, u32[]{:S(2)}) collective-permute-start(bf16[2,2,256,128]{3,2,1,0:T(8,128)(2,1)S(1)} %get-tuple-element.23.refs_0_), channel_id=1, source_target_pairs={{0,8},{1,9},{2,10},{3,11},{4,12},{5,13},{6,14},{7,15},{8,16},{9,17... | collective-permute-start | bytes 786440 | tf_op jit(solution)/shard_map/schur_y/ppermute | solution.py:280
  33.4 3.4 %collective-permute-start.7 = (bf16[2,2,256,128]{3,2,1,0:T(8,128)(2,1)S(1)}, bf16[2,2,256,128]{3,2,1,0:T(8,128)(2,1)S(1)}, u32[]{:S(2)}, u32[]{:S(2)}) collective-permute-start(bf16[2,2,256,128]{3,2,1,0:T(8,128)(2,1)S(1)} %get-tuple-element.24.refs_1_), channel_id=1, source_target_pairs={{0,24},{1,25},{2,26},{3,27},{4,28},{5,29},{6,30},{7,31},{8,0},{9,1... | collective-permute-start | bytes 786440 | tf_op jit(solution)/shard_map/schur_y/ppermute | solution.py:280
  36.8 3.4 %collective-permute-start.9 = (bf16[2,2,256,128]{3,2,1,0:T(8,128)(2,1)S(1)}, bf16[2,2,256,128]{3,2,1,0:T(8,128)(2,1)S(1)}, u32[]{:S(2)}, u32[]{:S(2)}) collective-permute-start(bf16[2,2,256,128]{3,2,1,0:T(8,128)(2,1)S(1)} %get-tuple-element.23.refs_0_), channel_id=1, source_target_pairs={{0,24},{1,25},{2,26},{3,27},{4,28},{5,29},{6,30},{7,31},{8,0},{9,1... | collective-permute-start | bytes 786440 | tf_op jit(solution)/shard_map/schur_y/ppermute | solution.py:280
  40.2 1.9 %collective-permute-start.5 = (bf16[2,2,256,128]{3,2,1,0:T(8,128)(2,1)S(1)}, bf16[2,2,256,128]{3,2,1,0:T(8,128)(2,1)S(1)}, u32[]{:S(2)}, u32[]{:S(2)}) collective-permute-start(bf16[2,2,256,128]{3,2,1,0:T(8,128)(2,1)S(1)} %get-tuple-element.24.refs_1_), channel_id=1, source_target_pairs={{0,8},{1,9},{2,10},{3,11},{4,12},{5,13},{6,14},{7,15},{8,16},{9,17... | collective-permute-start | bytes 786440 | tf_op jit(solution)/shard_map/schur_y/ppermute | solution.py:280
  42.1 1.9 %collective-permute-start.6 = (bf16[2,2,256,128]{3,2,1,0:T(8,128)(2,1)S(1)}, bf16[2,2,256,128]{3,2,1,0:T(8,128)(2,1)S(1)}, u32[]{:S(2)}, u32[]{:S(2)}) collective-permute-start(bf16[2,2,256,128]{3,2,1,0:T(8,128)(2,1)S(1)} %collective-permute-done.4.refs_2_), channel_id=1, source_target_pairs={{0,8},{1,9},{2,10},{3,11},{4,12},{5,13},{6,14},{7,15},{8,16},{9,17... | collective-permute-start | bytes 786440 | tf_op jit(solution)/shard_map/schur_y/ppermute | solution.py:280
  44.0 4.6 %collective-permute-start.8 = (bf16[2,2,256,128]{3,2,1,0:T(8,128)(2,1)S(1)}, bf16[2,2,256,128]{3,2,1,0:T(8,128)(2,1)S(1)}, u32[]{:S(2)}, u32[]{:S(2)}) collective-permute-start(bf16[2,2,256,128]{3,2,1,0:T(8,128)(2,1)S(1)} %collective-permute-done.7.refs_7_), channel_id=1, source_target_pairs={{0,24},{1,25},{2,26},{3,27},{4,28},{5,29},{6,30},{7,31},{8,0},{9,1... | collective-permute-start | bytes 786440 | tf_op jit(solution)/shard_map/schur_y/ppermute | solution.py:280
  48.6 6.7 %all-to-all-done = f32[8,72,128]{2,1,0:T(8,128)} async-done(((f32[8,72,128]{2,1,0:T(8,128)}), f32[8,72,128]{2,1,0:T(8,128)}, u32[]{:S(2)}, u32[]{:S(2)}) %all-to-all-start) | async-done | bytes 294944 | tf_op jit(solution)/shard_map/all_to_all | solution.py:284
  55.3 2.8 %all-gather.recv_ref = f32[16,72,128]{2,1,0:T(8,128)S(1)} all-gather(f32[8,72,128]{2,1,0:T(8,128)} %all-to-all-done), channel_id=2, replica_groups={{0,32},{64,96},{128,160},{192,224},{256,288},{320,352},{384,416},{448,4..., dimensions={0}, use_global_device_ids=true | all-gather | bytes 884736 | tf_op jit(solution)/shard_map/all_gather | solution.py:288
  58.1 0.0 copy-start.4
  58.2 0.0 copy-start.5
  58.2 0.0 copy-start.6
  58.2 0.0 copy-start.7
  58.2 0.0 copy-start.9
  58.2 0.0 copy-start.11
  58.2 2.4 %shard_map.122 = (bf16[32,16,128]{2,1,0:T(8,128)(2,1)S(1)}, f32[16,8,128]{2,1,0:T(8,128)S(1)}) custom-call(f32[16,72,128]{2,1,0:T(8,128)S(1)} %all-gather.recv_ref), custom_call_target="tpu_custom_call" | custom-call | flops 1000000000 | bytes 1048576 | tf_op jit(solution)/shard_map/pallas_call | solution.py:303
  60.6 0.7 shard_map.123
  61.3 28.3 %all_to_all.20 = f32[8,16,256]{2,1,0:T(8,128)S(1)} all-to-all(f32[8,16,256]{2,1,0:T(8,128)S(1)} %shard_map.123), channel_id=1, replica_groups={{256,320,384,448,0,64,128,192},{288,352,416,480,32,96,160,224},{257,321..., dimensions={0} | all-to-all | bytes 262144 | tf_op jit(solution)/shard_map/all_to_all | solution.py:284
  89.6 2.3 %all-gather.1.recv_ref = f32[16,16,256]{2,1,0:T(8,128)S(1)} all-gather(f32[8,16,256]{2,1,0:T(8,128)S(1)} %all_to_all.20), channel_id=3, replica_groups={{0,32},{64,96},{128,160},{192,224},{256,288},{320,352},{384,416},{448,4..., dimensions={0}, use_global_device_ids=true | all-gather | bytes 393216 | tf_op jit(solution)/shard_map/all_gather | solution.py:288
  92.1 1.6 %shard_map.124 = (f32[8,16,400]{2,1,0:T(8,128)S(1)}, f32[8,16,400]{2,1,0:T(8,128)S(1)}, f32[8,16,400]{2,1,0:T(8,128)S(1)}, bf16[8,64,128]{2,1,0:T(8,128)(2,1)S(1)}) custom-call(s32[16]{0:T(128)S(1)} %copy-done.10, s32[16]{0:T(128)S(1)} %copy-done.11, f32[16,16,256]{2,1,0:T(8,128)S(1)} %all-gather.1.recv_ref, f32[8,16,400]{2,1,0:T(8,128)S(1)} %copy-done.5, ...), custom_call_target="tpu_custom_call" | custom-call | flops 1000000000 | bytes 4194304 | tf_op jit(solution)/shard_map/pallas_call | solution.py:305
  93.7 18.5 %all_to_all.21 = bf16[8,64,128]{2,1,0:T(8,128)(2,1)S(1)} all-to-all(bf16[8,64,128]{2,1,0:T(8,128)(2,1)S(1)} %get-tuple-element.28), channel_id=1, replica_groups={{256,320,384,448,0,64,128,192},{288,352,416,480,32,96,160,224},{257,321..., dimensions={0} | all-to-all | bytes 262144 | tf_op jit(solution)/shard_map/all_to_all | solution.py:284
  112.2 2.3 %all-gather.2.recv_ref = bf16[16,64,128]{2,1,0:T(8,128)(2,1)S(1)} all-gather(bf16[8,64,128]{2,1,0:T(8,128)(2,1)S(1)} %all_to_all.21), channel_id=4, replica_groups={{0,32},{64,96},{128,160},{192,224},{256,288},{320,352},{384,416},{448,4..., dimensions={0}, use_global_device_ids=true | all-gather | bytes 393216 | tf_op jit(solution)/shard_map/all_gather | solution.py:288
  114.6 2.9 %shard_map.125 = (f32[16,256]{1,0:T(8,128)S(1)}, bf16[8,16,256]{2,1,0:T(8,128)(2,1)S(1)}) custom-call(bf16[16,64,128]{2,1,0:T(8,128)(2,1)S(1)} %all-gather.2.recv_ref, f32[16,8,128]{2,1,0:T(8,128)S(1)} %get-tuple-element.29.map_ref, bf16[2,2,256,128]{3,2,1,0:T(8,128)(2,1)S(1)} %get-tuple-element.23.refs_0_, ...), custom_call_target="tpu_custom_call" | custom-call | flops 1000000000 | bytes 3145728 | tf_op jit(solution)/shard_map/pallas_call | solution.py:306
  117.5 16.3 %all_to_all.22 = bf16[8,16,256]{2,1,0:T(8,128)(2,1)S(1)} all-to-all(bf16[8,16,256]{2,1,0:T(8,128)(2,1)S(1)} %get-tuple-element.30), channel_id=1, replica_groups={{256,320,384,448,0,64,128,192},{288,352,416,480,32,96,160,224},{257,321..., dimensions={0} | all-to-all | bytes 131072 | tf_op jit(solution)/shard_map/all_to_all | solution.py:284
  133.8 3.3 %all-gather.3.recv_ref = bf16[16,16,256]{2,1,0:T(8,128)(2,1)S(1)} all-gather(bf16[8,16,256]{2,1,0:T(8,128)(2,1)S(1)} %all_to_all.22), channel_id=5, replica_groups={{0,32},{64,96},{128,160},{192,224},{256,288},{320,352},{384,416},{448,4..., dimensions={0}, use_global_device_ids=true | all-gather | bytes 196608 | tf_op jit(solution)/shard_map/all_gather | solution.py:288
  137.1 2.0 %shard_map.126 = (f32[8,16,400]{2,1,0:T(8,128)}, f32[8,16,400]{2,1,0:T(8,128)}, f32[16,256]{1,0:T(8,128)}) custom-call(bf16[16,16,256]{2,1,0:T(8,128)(2,1)S(1)} %all-gather.3.recv_ref, f32[8,16,400]{2,1,0:T(8,128)S(1)} %get-tuple-element.31.prev_ref, f32[8,16,400]{2,1,0:T(8,128)S(1)} %get-tuple-element.32.volt_ref, ...), custom_call_target="tpu_custom_call" | custom-call | flops 1000000000 | bytes 2097152 | tf_op jit(solution)/shard_map/pallas_call | solution.py:307
  (29 shorter events, 0.1 us)
Async XLA Ops:
  0.6 12.6 %copy-start.8 = (bf16[256,128]{1,0:T(8,128)(2,1)S(1)}, bf16[256,128]{1,0:T(8,128)(2,1)}, u32[]{:S(2)}) copy-start(bf16[256,128]{1,0:T(8,128)(2,1)} %own_ref.1) | copy-start | bytes 196612
  0.6 12.5 %collective-permute-start = (bf16[256,128]{1,0:T(8,128)(2,1)}, bf16[256,128]{1,0:T(8,128)(2,1)S(1)}, u32[]{:S(2)}, u32[]{:S(2)}) collective-permute-start(bf16[256,128]{1,0:T(8,128)(2,1)} %own_ref.1), channel_id=1, source_target_pairs={{0,4},{1,5},{2,6},{3,7},{4,0},{5,1},{6,2},{7,3},{8,12},{9,13},{10,... | collective-permute-start | bytes 196616 | tf_op jit(solution)/shard_map/schur_z/ppermute | solution.py:276
  13.2 16.9 %collective-permute-start.3 = (bf16[2,256,128]{2,1,0:T(8,128)(2,1)S(1)}, bf16[2,256,128]{2,1,0:T(8,128)(2,1)S(1)}, u32[]{:S(2)}, u32[]{:S(2)}) collective-permute-start(bf16[2,256,128]{2,1,0:T(8,128)(2,1)S(1)} %pad_maximum_fusion), channel_id=1, source_target_pairs={{0,3},{1,2},{2,1},{3,0},{4,7},{5,6},{6,5},{7,4},{8,11},{9,10},{10,... | collective-permute-start | bytes 393224 | tf_op jit(solution)/shard_map/schur_z/ppermute | solution.py:276
  15.1 15.0 %collective-permute-start.2 = (bf16[2,256,128]{2,1,0:T(8,128)(2,1)S(1)}, bf16[2,256,128]{2,1,0:T(8,128)(2,1)S(1)}, u32[]{:S(2)}, u32[]{:S(2)}) collective-permute-start(bf16[2,256,128]{2,1,0:T(8,128)(2,1)S(1)} %pad_maximum_fusion), channel_id=1, source_target_pairs={{0,2},{1,3},{2,0},{3,1},{4,6},{5,7},{6,4},{7,5},{8,10},{9,11},{10,... | collective-permute-start | bytes 393224 | tf_op jit(solution)/shard_map/schur_z/ppermute | solution.py:276
  21.2 8.9 %collective-permute-start.1 = (bf16[2,256,128]{2,1,0:T(8,128)(2,1)S(1)}, bf16[2,256,128]{2,1,0:T(8,128)(2,1)S(1)}, u32[]{:S(2)}, u32[]{:S(2)}) collective-permute-start(bf16[2,256,128]{2,1,0:T(8,128)(2,1)S(1)} %pad_maximum_fusion), channel_id=1, source_target_pairs={{0,1},{1,0},{2,3},{3,2},{4,5},{5,4},{6,7},{7,6},{8,9},{9,8},{10,11... | collective-permute-start | bytes 393224 | tf_op jit(solution)/shard_map/schur_z/ppermute | solution.py:276
  23.2 32.1 %all-to-all-start = ((f32[8,72,128]{2,1,0:T(8,128)}), f32[8,72,128]{2,1,0:T(8,128)}, u32[]{:S(2)}, u32[]{:S(2)}) async-start(f32[8,72,128]{2,1,0:T(8,128)} %get-tuple-element.20), calls=%async_computation | async-start | bytes 589824 | tf_op jit(solution)/shard_map/all_to_all | solution.py:284
  30.2 11.9 %collective-permute-start.4 = (bf16[2,2,256,128]{3,2,1,0:T(8,128)(2,1)S(1)}, bf16[2,2,256,128]{3,2,1,0:T(8,128)(2,1)S(1)}, u32[]{:S(2)}, u32[]{:S(2)}) collective-permute-start(bf16[2,2,256,128]{3,2,1,0:T(8,128)(2,1)S(1)} %get-tuple-element.23.refs_0_), channel_id=1, source_target_pairs={{0,8},{1,9},{2,10},{3,11},{4,12},{5,13},{6,14},{7,15},{8,16},{9,17... | collective-permute-start | bytes 786440 | tf_op jit(solution)/shard_map/schur_y/ppermute | solution.py:280
  33.4 10.6 %collective-permute-start.7 = (bf16[2,2,256,128]{3,2,1,0:T(8,128)(2,1)S(1)}, bf16[2,2,256,128]{3,2,1,0:T(8,128)(2,1)S(1)}, u32[]{:S(2)}, u32[]{:S(2)}) collective-permute-start(bf16[2,2,256,128]{3,2,1,0:T(8,128)(2,1)S(1)} %get-tuple-element.24.refs_1_), channel_id=1, source_target_pairs={{0,24},{1,25},{2,26},{3,27},{4,28},{5,29},{6,30},{7,31},{8,0},{9,1... | collective-permute-start | bytes 786440 | tf_op jit(solution)/shard_map/schur_y/ppermute | solution.py:280
  36.8 23.8 %collective-permute-start.9 = (bf16[2,2,256,128]{3,2,1,0:T(8,128)(2,1)S(1)}, bf16[2,2,256,128]{3,2,1,0:T(8,128)(2,1)S(1)}, u32[]{:S(2)}, u32[]{:S(2)}) collective-permute-start(bf16[2,2,256,128]{3,2,1,0:T(8,128)(2,1)S(1)} %get-tuple-element.23.refs_0_), channel_id=1, source_target_pairs={{0,24},{1,25},{2,26},{3,27},{4,28},{5,29},{6,30},{7,31},{8,0},{9,1... | collective-permute-start | bytes 786440 | tf_op jit(solution)/shard_map/schur_y/ppermute | solution.py:280
  40.2 20.4 %collective-permute-start.5 = (bf16[2,2,256,128]{3,2,1,0:T(8,128)(2,1)S(1)}, bf16[2,2,256,128]{3,2,1,0:T(8,128)(2,1)S(1)}, u32[]{:S(2)}, u32[]{:S(2)}) collective-permute-start(bf16[2,2,256,128]{3,2,1,0:T(8,128)(2,1)S(1)} %get-tuple-element.24.refs_1_), channel_id=1, source_target_pairs={{0,8},{1,9},{2,10},{3,11},{4,12},{5,13},{6,14},{7,15},{8,16},{9,17... | collective-permute-start | bytes 786440 | tf_op jit(solution)/shard_map/schur_y/ppermute | solution.py:280
  42.1 18.5 %collective-permute-start.6 = (bf16[2,2,256,128]{3,2,1,0:T(8,128)(2,1)S(1)}, bf16[2,2,256,128]{3,2,1,0:T(8,128)(2,1)S(1)}, u32[]{:S(2)}, u32[]{:S(2)}) collective-permute-start(bf16[2,2,256,128]{3,2,1,0:T(8,128)(2,1)S(1)} %collective-permute-done.4.refs_2_), channel_id=1, source_target_pairs={{0,8},{1,9},{2,10},{3,11},{4,12},{5,13},{6,14},{7,15},{8,16},{9,17... | collective-permute-start | bytes 786440 | tf_op jit(solution)/shard_map/schur_y/ppermute | solution.py:280
  44.0 16.6 %collective-permute-start.8 = (bf16[2,2,256,128]{3,2,1,0:T(8,128)(2,1)S(1)}, bf16[2,2,256,128]{3,2,1,0:T(8,128)(2,1)S(1)}, u32[]{:S(2)}, u32[]{:S(2)}) collective-permute-start(bf16[2,2,256,128]{3,2,1,0:T(8,128)(2,1)S(1)} %collective-permute-done.7.refs_7_), channel_id=1, source_target_pairs={{0,24},{1,25},{2,26},{3,27},{4,28},{5,29},{6,30},{7,31},{8,0},{9,1... | collective-permute-start | bytes 786440 | tf_op jit(solution)/shard_map/schur_y/ppermute | solution.py:280
  58.1 33.9 %copy-start = (bf16[8,400,400]{2,1,0:T(8,128)(2,1)S(1)}, bf16[8,400,400]{2,1,0:T(8,128)(2,1)}, u32[]{:S(2)}) copy-start(bf16[8,400,400]{2,1,0:T(8,128)(2,1)} %inv_hbm.3) | copy-start | bytes 7680004
  58.1 33.9 %copy-start.1 = (s32[8,16,400]{2,1,0:T(8,128)S(1)}, s32[8,16,400]{2,1,0:T(8,128)}, u32[]{:S(2)}) copy-start(s32[8,16,400]{2,1,0:T(8,128)} %breaker_ref.3) | copy-start | bytes 614404
  58.1 33.9 %copy-start.2 = (f32[8,16,400]{2,1,0:T(8,128)S(1)}, f32[8,16,400]{2,1,0:T(8,128)}, u32[]{:S(2)}) copy-start(f32[8,16,400]{2,1,0:T(8,128)} %volt_ref.1) | copy-start | bytes 614404
  58.1 33.9 %copy-start.3 = (f32[8,16,400]{2,1,0:T(8,128)S(1)}, f32[8,16,400]{2,1,0:T(8,128)}, u32[]{:S(2)}) copy-start(f32[8,16,400]{2,1,0:T(8,128)} %curr_ref.1) | copy-start | bytes 614404
  58.1 33.9 %copy-start.4 = (bf16[256,512]{1,0:T(8,128)(2,1)S(1)}, bf16[256,512]{1,0:T(8,128)(2,1)}, u32[]{:S(2)}) copy-start(bf16[256,512]{1,0:T(8,128)(2,1)} %get-tuple-element.26.right_ref) | copy-start | bytes 786436
  58.2 33.9 %copy-start.5 = (f32[8,16,400]{2,1,0:T(8,128)S(1)}, f32[8,16,400]{2,1,0:T(8,128)}, u32[]{:S(2)}) copy-start(f32[8,16,400]{2,1,0:T(8,128)} %get-tuple-element.25.prev_ref) | copy-start | bytes 614404
  58.2 33.9 %copy-start.6 = (f32[8,400]{1,0:T(8,128)S(1)}, f32[8,400]{1,0:T(8,128)}, u32[]{:S(2)}) copy-start(f32[8,400]{1,0:T(8,128)} %gain_ref.3) | copy-start | bytes 38404
  58.2 33.9 %copy-start.7 = (f32[8,512]{1,0:T(8,128)S(1)}, f32[8,512]{1,0:T(8,128)}, u32[]{:S(2)}) copy-start(f32[8,512]{1,0:T(8,128)} %get-tuple-element.27.rows_ref) | copy-start | bytes 49156
  58.2 33.9 %copy-start.9 = (f32[8,64]{1,0:T(8,128)S(1)}, f32[8,64]{1,0:T(8,128)}, u32[]{:S(2)}) copy-start(f32[8,64]{1,0:T(8,128)} %tie_ref.1) | copy-start | bytes 6148
  58.2 33.9 %copy-start.10 = (s32[16]{0:T(128)S(1)}, s32[16]{0:T(128)}, u32[]{:S(2)}) copy-start(s32[16]{0:T(128)} %time_ref.3) | copy-start | bytes 196
  58.2 33.9 %copy-start.11 = (s32[16]{0:T(128)S(1)}, s32[16]{0:T(128)}, u32[]{:S(2)}) copy-start(s32[16]{0:T(128)} %node_ref.3) | copy-start | bytes 196

commit v12 on v11

--- a/solution.py
+++ b/solution.py
@@ -17,7 +17,7 @@
 TILES = OWN // LANES
 VALUE_ROWS = TILES * SCEN
 MAP_ROWS = 2 * TILES
-TURNED = [(n + ROWS // 2) % ROWS for n in range(ROWS)]
+TURNED = [ROWS - 1 - n for n in range(ROWS)]
 CORES = [[r for r in TURNED if r % 2 == core] for core in range(2)]
 PAIRS = [[2 * n, 2 * n + 1] for n in range(ROWS // 2)]
 VMEM_BYTES = 16 << 20
@@ -202,13 +202,11 @@
     open_circuit(1, volt_out, curr_out, breaker_ref, gain_ref, None, inv_ref, time_ref, node_ref, tie_ref, open_ref, send_ref)
 
 
-def last_kernel(recv_ref, prev_ref, volt_ref, curr_ref, breaker_ref, gain_ref, right_ref, rows_ref, face_ref, inv_hbm, volt_out, curr_out, face_out, inv_ref, sems):
-    copies = fetch([inv_hbm.at[k, pl.ds(0, PORTS)] for k in range(SUBS)], each(inv_ref, SUBS), sems)
+def last_kernel(recv_ref, prev_ref, volt_ref, curr_ref, breaker_ref, gain_ref, right_ref, rows_ref, face_ref, inv_ref, volt_out, curr_out, face_out):
     face_out[...] = face_ref[...]
     drive = driven(recv_ref, right_ref, rows_ref)
-    wait_for(copies)
     for k in range(SUBS):
-        volt_out[k], curr_out[k] = update(k, drive, prev_ref, inv_ref[k], volt_ref[k], curr_ref[k], breaker_ref, gain_ref)
+        volt_out[k], curr_out[k] = update(k, drive, prev_ref, inv_ref[k, :PORTS, :], volt_ref[k], curr_ref[k], breaker_ref, gain_ref)
 
 
 SMEM = pl.BlockSpec(memory_space=pltpu.SMEM)
@@ -264,9 +262,9 @@
 middle = call(middle_kernel, [SMEM] * 2 + [VMEM] * 10, [STATE, STATE, STATE, ((ROWS // 2, VALUE_ROWS, LANES), BF16)], [], GIGA, 4 << 20)
 last = call(
     last_kernel,
-    [VMEM] * 9 + [HBM],
+    [VMEM] * 10,
     [STATE, STATE, (FACE[1:], F32)],
-    held(((SUBS, PORTS, NODES), BF16)) + copies_of(SUBS),
+    [],
     GIGA,
     2 << 20,
 )

time: 140 us -> 138 us (0.986)
    all_to_all x3, blocking collectives: 63.2 us -> 60.2 us  [exchange(): return lax.all_to_all(send, 'row', 0, 0, axis_index_groups=groups)]
    all_gather x4, blocking collectives: 10.8 us -> 13.4 us  [paired_exchange(): both = lax.all_gather(exchange(send, CORES), 'row', axis_index_groups=PAIRS)]
where the time goes in v12:
time: 138 us
  blocking collectives  73.6 us (53%)
  starting transfers between devices  41.4 us (30%)
  Pallas kernels  13.2 us (10%)
  waiting for transfers between devices  8.38 us (6%)
    all_to_all x3, blocking collectives, exchange(): return lax.all_to_all(send, 'row', 0, 0, axis_index_groups=groups)  60.2 us
    ppermute x6, starting transfers between devices, along_y(): lax.ppermute(block, 'col', [(c, (c + 8 * steps) % COLS) for c in range(CO...  18.3 us
    ppermute x4, starting transfers between devices, along_z(): return lax.ppermute(block, 'col', [(c, c ^ flip) for c in range(COLS)])  15.2 us
    all_gather x4, blocking collectives, paired_exchange(): both = lax.all_gather(exchange(send, CORES), 'row', axis_index_groups=PAIRS)  13.4 us
    all_to_all x1, starting transfers between devices, exchange(): return lax.all_to_all(send, 'row', 0, 0, axis_index_groups=groups)  7.85 us
    all_to_all x1, waiting for transfers between devices, exchange(): return lax.all_to_all(send, 'row', 0, 0, axis_index_groups=groups)  5.52 us
    pallas_call x1, Pallas kernels, local(): first(fault_time, fault_node, volt, curr, breaker, ind_gain, tie, port_ma...  4.38 us
    pallas_call x1, Pallas kernels, local(): face, send = interface(paired_exchange(send), maps, *schur_rows)  2.91 us
  transfers between devices with their start and end apart: 11, of which 2 were waited for; matrix products, arithmetic and copies ran while one was open for 0% of the time, Pallas kernels for 5%

profile of v12, /device:TPU:449, one launch (start us, length us, event | category | flops | bytes accessed | tf_op | source)
XLA Modules:
  0.0 137.6 jit_solution(11589775997158147560)
XLA Ops:
  0.6 5.3 %collective-permute-start = (bf16[256,128]{1,0:T(8,128)(2,1)}, bf16[256,128]{1,0:T(8,128)(2,1)S(1)}, u32[]{:S(2)}, u32[]{:S(2)}) collective-permute-start(bf16[256,128]{1,0:T(8,128)(2,1)} %own_ref.1), channel_id=1, source_target_pairs={{0,4},{1,5},{2,6},{3,7},{4,0},{5,1},{6,2},{7,3},{8,12},{9,13},{10,... | collective-permute-start | bytes 196616 | tf_op jit(solution)/shard_map/schur_z/ppermute | solution.py:274
  6.0 4.4 %shard_map.121 = (f32[8,16,400]{2,1,0:T(8,128)}, f32[8,72,128]{2,1,0:T(8,128)}, bf16[256,512]{1,0:T(8,128)(2,1)}, f32[8,512]{1,0:T(8,128)}) custom-call(s32[16]{0:T(128)} %time_ref.3, s32[16]{0:T(128)} %node_ref.3, f32[8,16,400]{2,1,0:T(8,128)} %volt_ref.1, f32[8,16,400]{2,1,0:T(8,128)} %curr_ref.1, s32[8,16,400]{2,1,0:T(8,128)} %breaker_ref.3, ...), custom_call_target="tpu_custom_call" | custom-call | flops 1000000000 | bytes 4194304 | tf_op jit(solution)/shard_map/pallas_call | solution.py:293
  10.3 2.8 %collective-permute-done.across_ref = bf16[256,128]{1,0:T(8,128)(2,1)S(1)} collective-permute-done((bf16[256,128]{1,0:T(8,128)(2,1)}, bf16[256,128]{1,0:T(8,128)(2,1)S(1)}, u32[]{:S(2)}, u32[]{:S(2)}) %collective-permute-start) | collective-permute-done | bytes 65568 | tf_op jit(solution)/shard_map/schur_z/ppermute | solution.py:274
  13.2 1.9 %collective-permute-start.3 = (bf16[2,256,128]{2,1,0:T(8,128)(2,1)S(1)}, bf16[2,256,128]{2,1,0:T(8,128)(2,1)S(1)}, u32[]{:S(2)}, u32[]{:S(2)}) collective-permute-start(bf16[2,256,128]{2,1,0:T(8,128)(2,1)S(1)} %pad_maximum_fusion), channel_id=1, source_target_pairs={{0,3},{1,2},{2,1},{3,0},{4,7},{5,6},{6,5},{7,4},{8,11},{9,10},{10,... | collective-permute-start | bytes 393224 | tf_op jit(solution)/shard_map/schur_z/ppermute | solution.py:274
  15.1 6.1 %collective-permute-start.2 = (bf16[2,256,128]{2,1,0:T(8,128)(2,1)S(1)}, bf16[2,256,128]{2,1,0:T(8,128)(2,1)S(1)}, u32[]{:S(2)}, u32[]{:S(2)}) collective-permute-start(bf16[2,256,128]{2,1,0:T(8,128)(2,1)S(1)} %pad_maximum_fusion), channel_id=1, source_target_pairs={{0,2},{1,3},{2,0},{3,1},{4,6},{5,7},{6,4},{7,5},{8,10},{9,11},{10,... | collective-permute-start | bytes 393224 | tf_op jit(solution)/shard_map/schur_z/ppermute | solution.py:274
  21.2 1.9 %collective-permute-start.1 = (bf16[2,256,128]{2,1,0:T(8,128)(2,1)S(1)}, bf16[2,256,128]{2,1,0:T(8,128)(2,1)S(1)}, u32[]{:S(2)}, u32[]{:S(2)}) collective-permute-start(bf16[2,256,128]{2,1,0:T(8,128)(2,1)S(1)} %pad_maximum_fusion), channel_id=1, source_target_pairs={{0,1},{1,0},{2,3},{3,2},{4,5},{5,4},{6,7},{7,6},{8,9},{9,8},{10,11... | collective-permute-start | bytes 393224 | tf_op jit(solution)/shard_map/schur_z/ppermute | solution.py:274
  23.2 7.8 %all-to-all-start = ((f32[8,72,128]{2,1,0:T(8,128)}), f32[8,72,128]{2,1,0:T(8,128)}, u32[]{:S(2)}, u32[]{:S(2)}) async-start(f32[8,72,128]{2,1,0:T(8,128)} %get-tuple-element.20), calls=%async_computation | async-start | bytes 589824 | tf_op jit(solution)/shard_map/all_to_all | solution.py:282
  31.1 3.2 %collective-permute-start.4 = (bf16[2,2,256,128]{3,2,1,0:T(8,128)(2,1)S(1)}, bf16[2,2,256,128]{3,2,1,0:T(8,128)(2,1)S(1)}, u32[]{:S(2)}, u32[]{:S(2)}) collective-permute-start(bf16[2,2,256,128]{3,2,1,0:T(8,128)(2,1)S(1)} %get-tuple-element.23.refs_0_), channel_id=1, source_target_pairs={{0,8},{1,9},{2,10},{3,11},{4,12},{5,13},{6,14},{7,15},{8,16},{9,17... | collective-permute-start | bytes 786440 | tf_op jit(solution)/shard_map/schur_y/ppermute | solution.py:278
  34.3 3.4 %collective-permute-start.7 = (bf16[2,2,256,128]{3,2,1,0:T(8,128)(2,1)S(1)}, bf16[2,2,256,128]{3,2,1,0:T(8,128)(2,1)S(1)}, u32[]{:S(2)}, u32[]{:S(2)}) collective-permute-start(bf16[2,2,256,128]{3,2,1,0:T(8,128)(2,1)S(1)} %get-tuple-element.24.refs_1_), channel_id=1, source_target_pairs={{0,24},{1,25},{2,26},{3,27},{4,28},{5,29},{6,30},{7,31},{8,0},{9,1... | collective-permute-start | bytes 786440 | tf_op jit(solution)/shard_map/schur_y/ppermute | solution.py:278
  37.6 3.4 %collective-permute-start.9 = (bf16[2,2,256,128]{3,2,1,0:T(8,128)(2,1)S(1)}, bf16[2,2,256,128]{3,2,1,0:T(8,128)(2,1)S(1)}, u32[]{:S(2)}, u32[]{:S(2)}) collective-permute-start(bf16[2,2,256,128]{3,2,1,0:T(8,128)(2,1)S(1)} %get-tuple-element.23.refs_0_), channel_id=1, source_target_pairs={{0,24},{1,25},{2,26},{3,27},{4,28},{5,29},{6,30},{7,31},{8,0},{9,1... | collective-permute-start | bytes 786440 | tf_op jit(solution)/shard_map/schur_y/ppermute | solution.py:278
  41.0 1.9 %collective-permute-start.5 = (bf16[2,2,256,128]{3,2,1,0:T(8,128)(2,1)S(1)}, bf16[2,2,256,128]{3,2,1,0:T(8,128)(2,1)S(1)}, u32[]{:S(2)}, u32[]{:S(2)}) collective-permute-start(bf16[2,2,256,128]{3,2,1,0:T(8,128)(2,1)S(1)} %get-tuple-element.24.refs_1_), channel_id=1, source_target_pairs={{0,8},{1,9},{2,10},{3,11},{4,12},{5,13},{6,14},{7,15},{8,16},{9,17... | collective-permute-start | bytes 786440 | tf_op jit(solution)/shard_map/schur_y/ppermute | solution.py:278
  43.0 1.9 %collective-permute-start.6 = (bf16[2,2,256,128]{3,2,1,0:T(8,128)(2,1)S(1)}, bf16[2,2,256,128]{3,2,1,0:T(8,128)(2,1)S(1)}, u32[]{:S(2)}, u32[]{:S(2)}) collective-permute-start(bf16[2,2,256,128]{3,2,1,0:T(8,128)(2,1)S(1)} %collective-permute-done.4.refs_2_), channel_id=1, source_target_pairs={{0,8},{1,9},{2,10},{3,11},{4,12},{5,13},{6,14},{7,15},{8,16},{9,17... | collective-permute-start | bytes 786440 | tf_op jit(solution)/shard_map/schur_y/ppermute | solution.py:278
  44.9 4.6 %collective-permute-start.8 = (bf16[2,2,256,128]{3,2,1,0:T(8,128)(2,1)S(1)}, bf16[2,2,256,128]{3,2,1,0:T(8,128)(2,1)S(1)}, u32[]{:S(2)}, u32[]{:S(2)}) collective-permute-start(bf16[2,2,256,128]{3,2,1,0:T(8,128)(2,1)S(1)} %collective-permute-done.7.refs_7_), channel_id=1, source_target_pairs={{0,24},{1,25},{2,26},{3,27},{4,28},{5,29},{6,30},{7,31},{8,0},{9,1... | collective-permute-start | bytes 786440 | tf_op jit(solution)/shard_map/schur_y/ppermute | solution.py:278
  49.5 5.5 %all-to-all-done = f32[8,72,128]{2,1,0:T(8,128)} async-done(((f32[8,72,128]{2,1,0:T(8,128)}), f32[8,72,128]{2,1,0:T(8,128)}, u32[]{:S(2)}, u32[]{:S(2)}) %all-to-all-start) | async-done | bytes 294944 | tf_op jit(solution)/shard_map/all_to_all | solution.py:282
  55.0 2.6 %all-gather.recv_ref = f32[16,72,128]{2,1,0:T(8,128)S(1)} all-gather(f32[8,72,128]{2,1,0:T(8,128)} %all-to-all-done), channel_id=2, replica_groups={{0,32},{64,96},{128,160},{192,224},{256,288},{320,352},{384,416},{448,4..., dimensions={0}, use_global_device_ids=true | all-gather | bytes 884736 | tf_op jit(solution)/shard_map/all_gather | solution.py:286
  57.6 0.0 copy-start.4
  57.6 0.0 copy-start.5
  57.6 0.0 copy-start.6
  57.6 0.0 copy-start.7
  57.6 0.0 copy-start.9
  57.6 0.0 copy-start.11
  57.6 2.4 %shard_map.122 = (bf16[32,16,128]{2,1,0:T(8,128)(2,1)S(1)}, f32[16,8,128]{2,1,0:T(8,128)S(1)}) custom-call(f32[16,72,128]{2,1,0:T(8,128)S(1)} %all-gather.recv_ref), custom_call_target="tpu_custom_call" | custom-call | flops 1000000000 | bytes 1048576 | tf_op jit(solution)/shard_map/pallas_call | solution.py:301
  60.1 0.7 shard_map.123
  60.7 23.9 %all_to_all.20 = f32[8,16,256]{2,1,0:T(8,128)S(1)} all-to-all(f32[8,16,256]{2,1,0:T(8,128)S(1)} %shard_map.123), channel_id=1, replica_groups={{448,384,320,256,192,128,64,0},{480,416,352,288,224,160,96,32},{449,385..., dimensions={0} | all-to-all | bytes 262144 | tf_op jit(solution)/shard_map/all_to_all | solution.py:282
  84.6 5.4 %all-gather.1.recv_ref = f32[16,16,256]{2,1,0:T(8,128)S(1)} all-gather(f32[8,16,256]{2,1,0:T(8,128)S(1)} %all_to_all.20), channel_id=3, replica_groups={{0,32},{64,96},{128,160},{192,224},{256,288},{320,352},{384,416},{448,4..., dimensions={0}, use_global_device_ids=true | all-gather | bytes 393216 | tf_op jit(solution)/shard_map/all_gather | solution.py:286
  90.1 1.6 %shard_map.124 = (f32[8,16,400]{2,1,0:T(8,128)S(1)}, f32[8,16,400]{2,1,0:T(8,128)S(1)}, f32[8,16,400]{2,1,0:T(8,128)S(1)}, bf16[8,64,128]{2,1,0:T(8,128)(2,1)S(1)}) custom-call(s32[16]{0:T(128)S(1)} %copy-done.10, s32[16]{0:T(128)S(1)} %copy-done.11, f32[16,16,256]{2,1,0:T(8,128)S(1)} %all-gather.1.recv_ref, f32[8,16,400]{2,1,0:T(8,128)S(1)} %copy-done.5, ...), custom_call_target="tpu_custom_call" | custom-call | flops 1000000000 | bytes 4194304 | tf_op jit(solution)/shard_map/pallas_call | solution.py:303
  91.7 19.8 %all_to_all.21 = bf16[8,64,128]{2,1,0:T(8,128)(2,1)S(1)} all-to-all(bf16[8,64,128]{2,1,0:T(8,128)(2,1)S(1)} %get-tuple-element.28), channel_id=1, replica_groups={{448,384,320,256,192,128,64,0},{480,416,352,288,224,160,96,32},{449,385..., dimensions={0} | all-to-all | bytes 262144 | tf_op jit(solution)/shard_map/all_to_all | solution.py:282
  111.4 2.2 %all-gather.2.recv_ref = bf16[16,64,128]{2,1,0:T(8,128)(2,1)S(1)} all-gather(bf16[8,64,128]{2,1,0:T(8,128)(2,1)S(1)} %all_to_all.21), channel_id=4, replica_groups={{0,32},{64,96},{128,160},{192,224},{256,288},{320,352},{384,416},{448,4..., dimensions={0}, use_global_device_ids=true | all-gather | bytes 393216 | tf_op jit(solution)/shard_map/all_gather | solution.py:286
  113.6 2.9 %shard_map.125 = (f32[16,256]{1,0:T(8,128)S(1)}, bf16[8,16,256]{2,1,0:T(8,128)(2,1)S(1)}) custom-call(bf16[16,64,128]{2,1,0:T(8,128)(2,1)S(1)} %all-gather.2.recv_ref, f32[16,8,128]{2,1,0:T(8,128)S(1)} %get-tuple-element.29.map_ref, bf16[2,2,256,128]{3,2,1,0:T(8,128)(2,1)S(1)} %get-tuple-element.23.refs_0_, ...), custom_call_target="tpu_custom_call" | custom-call | flops 1000000000 | bytes 3145728 | tf_op jit(solution)/shard_map/pallas_call | solution.py:304
  116.5 16.5 %all_to_all.22 = bf16[8,16,256]{2,1,0:T(8,128)(2,1)S(1)} all-to-all(bf16[8,16,256]{2,1,0:T(8,128)(2,1)S(1)} %get-tuple-element.30), channel_id=1, replica_groups={{448,384,320,256,192,128,64,0},{480,416,352,288,224,160,96,32},{449,385..., dimensions={0} | all-to-all | bytes 131072 | tf_op jit(solution)/shard_map/all_to_all | solution.py:282
  133.1 3.3 %all-gather.3.recv_ref = bf16[16,16,256]{2,1,0:T(8,128)(2,1)S(1)} all-gather(bf16[8,16,256]{2,1,0:T(8,128)(2,1)S(1)} %all_to_all.22), channel_id=5, replica_groups={{0,32},{64,96},{128,160},{192,224},{256,288},{320,352},{384,416},{448,4..., dimensions={0}, use_global_device_ids=true | all-gather | bytes 196608 | tf_op jit(solution)/shard_map/all_gather | solution.py:286
  136.3 1.3 shard_map.126
  (29 shorter events, 0.1 us)
Async XLA Ops:
  0.6 12.6 %copy-start.8 = (bf16[256,128]{1,0:T(8,128)(2,1)S(1)}, bf16[256,128]{1,0:T(8,128)(2,1)}, u32[]{:S(2)}) copy-start(bf16[256,128]{1,0:T(8,128)(2,1)} %own_ref.1) | copy-start | bytes 196612
  0.6 12.5 %collective-permute-start = (bf16[256,128]{1,0:T(8,128)(2,1)}, bf16[256,128]{1,0:T(8,128)(2,1)S(1)}, u32[]{:S(2)}, u32[]{:S(2)}) collective-permute-start(bf16[256,128]{1,0:T(8,128)(2,1)} %own_ref.1), channel_id=1, source_target_pairs={{0,4},{1,5},{2,6},{3,7},{4,0},{5,1},{6,2},{7,3},{8,12},{9,13},{10,... | collective-permute-start | bytes 196616 | tf_op jit(solution)/shard_map/schur_z/ppermute | solution.py:274
  13.2 17.8 %collective-permute-start.3 = (bf16[2,256,128]{2,1,0:T(8,128)(2,1)S(1)}, bf16[2,256,128]{2,1,0:T(8,128)(2,1)S(1)}, u32[]{:S(2)}, u32[]{:S(2)}) collective-permute-start(bf16[2,256,128]{2,1,0:T(8,128)(2,1)S(1)} %pad_maximum_fusion), channel_id=1, source_target_pairs={{0,3},{1,2},{2,1},{3,0},{4,7},{5,6},{6,5},{7,4},{8,11},{9,10},{10,... | collective-permute-start | bytes 393224 | tf_op jit(solution)/shard_map/schur_z/ppermute | solution.py:274
  15.1 15.9 %collective-permute-start.2 = (bf16[2,256,128]{2,1,0:T(8,128)(2,1)S(1)}, bf16[2,256,128]{2,1,0:T(8,128)(2,1)S(1)}, u32[]{:S(2)}, u32[]{:S(2)}) collective-permute-start(bf16[2,256,128]{2,1,0:T(8,128)(2,1)S(1)} %pad_maximum_fusion), channel_id=1, source_target_pairs={{0,2},{1,3},{2,0},{3,1},{4,6},{5,7},{6,4},{7,5},{8,10},{9,11},{10,... | collective-permute-start | bytes 393224 | tf_op jit(solution)/shard_map/schur_z/ppermute | solution.py:274
  21.2 9.8 %collective-permute-start.1 = (bf16[2,256,128]{2,1,0:T(8,128)(2,1)S(1)}, bf16[2,256,128]{2,1,0:T(8,128)(2,1)S(1)}, u32[]{:S(2)}, u32[]{:S(2)}) collective-permute-start(bf16[2,256,128]{2,1,0:T(8,128)(2,1)S(1)} %pad_maximum_fusion), channel_id=1, source_target_pairs={{0,1},{1,0},{2,3},{3,2},{4,5},{5,4},{6,7},{7,6},{8,9},{9,8},{10,11... | collective-permute-start | bytes 393224 | tf_op jit(solution)/shard_map/schur_z/ppermute | solution.py:274
  23.2 31.8 %all-to-all-start = ((f32[8,72,128]{2,1,0:T(8,128)}), f32[8,72,128]{2,1,0:T(8,128)}, u32[]{:S(2)}, u32[]{:S(2)}) async-start(f32[8,72,128]{2,1,0:T(8,128)} %get-tuple-element.20), calls=%async_computation | async-start | bytes 589824 | tf_op jit(solution)/shard_map/all_to_all | solution.py:282
  31.1 11.9 %collective-permute-start.4 = (bf16[2,2,256,128]{3,2,1,0:T(8,128)(2,1)S(1)}, bf16[2,2,256,128]{3,2,1,0:T(8,128)(2,1)S(1)}, u32[]{:S(2)}, u32[]{:S(2)}) collective-permute-start(bf16[2,2,256,128]{3,2,1,0:T(8,128)(2,1)S(1)} %get-tuple-element.23.refs_0_), channel_id=1, source_target_pairs={{0,8},{1,9},{2,10},{3,11},{4,12},{5,13},{6,14},{7,15},{8,16},{9,17... | collective-permute-start | bytes 786440 | tf_op jit(solution)/shard_map/schur_y/ppermute | solution.py:278
  34.3 10.6 %collective-permute-start.7 = (bf16[2,2,256,128]{3,2,1,0:T(8,128)(2,1)S(1)}, bf16[2,2,256,128]{3,2,1,0:T(8,128)(2,1)S(1)}, u32[]{:S(2)}, u32[]{:S(2)}) collective-permute-start(bf16[2,2,256,128]{3,2,1,0:T(8,128)(2,1)S(1)} %get-tuple-element.24.refs_1_), channel_id=1, source_target_pairs={{0,24},{1,25},{2,26},{3,27},{4,28},{5,29},{6,30},{7,31},{8,0},{9,1... | collective-permute-start | bytes 786440 | tf_op jit(solution)/shard_map/schur_y/ppermute | solution.py:278
  37.6 22.4 %collective-permute-start.9 = (bf16[2,2,256,128]{3,2,1,0:T(8,128)(2,1)S(1)}, bf16[2,2,256,128]{3,2,1,0:T(8,128)(2,1)S(1)}, u32[]{:S(2)}, u32[]{:S(2)}) collective-permute-start(bf16[2,2,256,128]{3,2,1,0:T(8,128)(2,1)S(1)} %get-tuple-element.23.refs_0_), channel_id=1, source_target_pairs={{0,24},{1,25},{2,26},{3,27},{4,28},{5,29},{6,30},{7,31},{8,0},{9,1... | collective-permute-start | bytes 786440 | tf_op jit(solution)/shard_map/schur_y/ppermute | solution.py:278
  41.0 19.0 %collective-permute-start.5 = (bf16[2,2,256,128]{3,2,1,0:T(8,128)(2,1)S(1)}, bf16[2,2,256,128]{3,2,1,0:T(8,128)(2,1)S(1)}, u32[]{:S(2)}, u32[]{:S(2)}) collective-permute-start(bf16[2,2,256,128]{3,2,1,0:T(8,128)(2,1)S(1)} %get-tuple-element.24.refs_1_), channel_id=1, source_target_pairs={{0,8},{1,9},{2,10},{3,11},{4,12},{5,13},{6,14},{7,15},{8,16},{9,17... | collective-permute-start | bytes 786440 | tf_op jit(solution)/shard_map/schur_y/ppermute | solution.py:278
  43.0 17.1 %collective-permute-start.6 = (bf16[2,2,256,128]{3,2,1,0:T(8,128)(2,1)S(1)}, bf16[2,2,256,128]{3,2,1,0:T(8,128)(2,1)S(1)}, u32[]{:S(2)}, u32[]{:S(2)}) collective-permute-start(bf16[2,2,256,128]{3,2,1,0:T(8,128)(2,1)S(1)} %collective-permute-done.4.refs_2_), channel_id=1, source_target_pairs={{0,8},{1,9},{2,10},{3,11},{4,12},{5,13},{6,14},{7,15},{8,16},{9,17... | collective-permute-start | bytes 786440 | tf_op jit(solution)/shard_map/schur_y/ppermute | solution.py:278
  44.9 15.1 %collective-permute-start.8 = (bf16[2,2,256,128]{3,2,1,0:T(8,128)(2,1)S(1)}, bf16[2,2,256,128]{3,2,1,0:T(8,128)(2,1)S(1)}, u32[]{:S(2)}, u32[]{:S(2)}) collective-permute-start(bf16[2,2,256,128]{3,2,1,0:T(8,128)(2,1)S(1)} %collective-permute-done.7.refs_7_), channel_id=1, source_target_pairs={{0,24},{1,25},{2,26},{3,27},{4,28},{5,29},{6,30},{7,31},{8,0},{9,1... | collective-permute-start | bytes 786440 | tf_op jit(solution)/shard_map/schur_y/ppermute | solution.py:278
  57.5 32.5 %copy-start = (bf16[8,400,400]{2,1,0:T(8,128)(2,1)S(1)}, bf16[8,400,400]{2,1,0:T(8,128)(2,1)}, u32[]{:S(2)}) copy-start(bf16[8,400,400]{2,1,0:T(8,128)(2,1)} %inv_ref.3) | copy-start | bytes 7680004
  57.5 32.5 %copy-start.1 = (s32[8,16,400]{2,1,0:T(8,128)S(1)}, s32[8,16,400]{2,1,0:T(8,128)}, u32[]{:S(2)}) copy-start(s32[8,16,400]{2,1,0:T(8,128)} %breaker_ref.3) | copy-start | bytes 614404
  57.5 32.5 %copy-start.2 = (f32[8,16,400]{2,1,0:T(8,128)S(1)}, f32[8,16,400]{2,1,0:T(8,128)}, u32[]{:S(2)}) copy-start(f32[8,16,400]{2,1,0:T(8,128)} %volt_ref.1) | copy-start | bytes 614404
  57.6 32.5 %copy-start.3 = (f32[8,16,400]{2,1,0:T(8,128)S(1)}, f32[8,16,400]{2,1,0:T(8,128)}, u32[]{:S(2)}) copy-start(f32[8,16,400]{2,1,0:T(8,128)} %curr_ref.1) | copy-start | bytes 614404
  57.6 32.5 %copy-start.4 = (bf16[256,512]{1,0:T(8,128)(2,1)S(1)}, bf16[256,512]{1,0:T(8,128)(2,1)}, u32[]{:S(2)}) copy-start(bf16[256,512]{1,0:T(8,128)(2,1)} %get-tuple-element.26.right_ref) | copy-start | bytes 786436
  57.6 32.5 %copy-start.5 = (f32[8,16,400]{2,1,0:T(8,128)S(1)}, f32[8,16,400]{2,1,0:T(8,128)}, u32[]{:S(2)}) copy-start(f32[8,16,400]{2,1,0:T(8,128)} %get-tuple-element.25.prev_ref) | copy-start | bytes 614404
  57.6 32.5 %copy-start.6 = (f32[8,400]{1,0:T(8,128)S(1)}, f32[8,400]{1,0:T(8,128)}, u32[]{:S(2)}) copy-start(f32[8,400]{1,0:T(8,128)} %gain_ref.3) | copy-start | bytes 38404
  57.6 32.5 %copy-start.7 = (f32[8,512]{1,0:T(8,128)S(1)}, f32[8,512]{1,0:T(8,128)}, u32[]{:S(2)}) copy-start(f32[8,512]{1,0:T(8,128)} %get-tuple-element.27.rows_ref) | copy-start | bytes 49156
  57.6 32.5 %copy-start.9 = (f32[8,64]{1,0:T(8,128)S(1)}, f32[8,64]{1,0:T(8,128)}, u32[]{:S(2)}) copy-start(f32[8,64]{1,0:T(8,128)} %tie_ref.1) | copy-start | bytes 6148
  57.6 32.5 %copy-start.10 = (s32[16]{0:T(128)S(1)}, s32[16]{0:T(128)}, u32[]{:S(2)}) copy-start(s32[16]{0:T(128)} %time_ref.3) | copy-start | bytes 196
  57.6 32.4 %copy-start.11 = (s32[16]{0:T(128)S(1)}, s32[16]{0:T(128)}, u32[]{:S(2)}) copy-start(s32[16]{0:T(128)} %node_ref.3) | copy-start | bytes 196

commit v13 on v12

--- a/solution.py
+++ b/solution.py
@@ -197,9 +197,10 @@
 
 def middle_kernel(time_ref, node_ref, recv_ref, prev_ref, volt_ref, curr_ref, breaker_ref, gain_ref, tie_ref, right_ref, rows_ref, inv_ref, volt_out, curr_out, open_ref, send_ref):
     drive = driven(recv_ref, right_ref, rows_ref)
+    volts, currs = zip(*(update(k, drive, prev_ref, inv_ref[k, :PORTS, :], volt_ref[k], curr_ref[k], breaker_ref, gain_ref) for k in range(SUBS)))
     for k in range(SUBS):
-        volt_out[k], curr_out[k] = update(k, drive, prev_ref, inv_ref[k, :PORTS, :], volt_ref[k], curr_ref[k], breaker_ref, gain_ref)
-    open_circuit(1, volt_out, curr_out, breaker_ref, gain_ref, None, inv_ref, time_ref, node_ref, tie_ref, open_ref, send_ref)
+        volt_out[k], curr_out[k] = volts[k], currs[k]
+    open_circuit(1, volts, currs, breaker_ref, gain_ref, None, inv_ref, time_ref, node_ref, tie_ref, open_ref, send_ref)
 
 
 def last_kernel(recv_ref, prev_ref, volt_ref, curr_ref, breaker_ref, gain_ref, right_ref, rows_ref, face_ref, inv_ref, volt_out, curr_out, face_out):

time: 138 us -> 138 us (level)
  no operation moved by 1% of the time
where the time goes in v13:
time: 138 us
  blocking collectives  73.6 us (53%)
  starting transfers between devices  41.4 us (30%)
  Pallas kernels  13.2 us (10%)
  waiting for transfers between devices  8.38 us (6%)
    all_to_all x3, blocking collectives, exchange(): return lax.all_to_all(send, 'row', 0, 0, axis_index_groups=groups)  60.2 us
    ppermute x6, starting transfers between devices, along_y(): lax.ppermute(block, 'col', [(c, (c + 8 * steps) % COLS) for c in range(CO...  18.3 us
    ppermute x4, starting transfers between devices, along_z(): return lax.ppermute(block, 'col', [(c, c ^ flip) for c in range(COLS)])  15.2 us
    all_gather x4, blocking collectives, paired_exchange(): both = lax.all_gather(exchange(send, CORES), 'row', axis_index_groups=PAIRS)  13.4 us
    all_to_all x1, starting transfers between devices, exchange(): return lax.all_to_all(send, 'row', 0, 0, axis_index_groups=groups)  7.85 us
    all_to_all x1, waiting for transfers between devices, exchange(): return lax.all_to_all(send, 'row', 0, 0, axis_index_groups=groups)  5.52 us
    pallas_call x1, Pallas kernels, local(): first(fault_time, fault_node, volt, curr, breaker, ind_gain, tie, port_ma...  4.38 us
    pallas_call x1, Pallas kernels, local(): face, send = interface(paired_exchange(send), maps, *schur_rows)  2.91 us
  transfers between devices with their start and end apart: 11, of which 2 were waited for; matrix products, arithmetic and copies ran while one was open for 0% of the time, Pallas kernels for 5%

profile of v13, /device:TPU:449, one launch (start us, length us, event | category | flops | bytes accessed | tf_op | source)
XLA Modules:
  0.0 137.6 jit_solution(16509528972542841546)
XLA Ops:
  0.6 5.3 %collective-permute-start = (bf16[256,128]{1,0:T(8,128)(2,1)}, bf16[256,128]{1,0:T(8,128)(2,1)S(1)}, u32[]{:S(2)}, u32[]{:S(2)}) collective-permute-start(bf16[256,128]{1,0:T(8,128)(2,1)} %own_ref.1), channel_id=1, source_target_pairs={{0,4},{1,5},{2,6},{3,7},{4,0},{5,1},{6,2},{7,3},{8,12},{9,13},{10,... | collective-permute-start | bytes 196616 | tf_op jit(solution)/shard_map/schur_z/ppermute | solution.py:275
  6.0 4.4 %shard_map.121 = (f32[8,16,400]{2,1,0:T(8,128)}, f32[8,72,128]{2,1,0:T(8,128)}, bf16[256,512]{1,0:T(8,128)(2,1)}, f32[8,512]{1,0:T(8,128)}) custom-call(s32[16]{0:T(128)} %time_ref.3, s32[16]{0:T(128)} %node_ref.3, f32[8,16,400]{2,1,0:T(8,128)} %volt_ref.1, f32[8,16,400]{2,1,0:T(8,128)} %curr_ref.1, s32[8,16,400]{2,1,0:T(8,128)} %breaker_ref.3, ...), custom_call_target="tpu_custom_call" | custom-call | flops 1000000000 | bytes 4194304 | tf_op jit(solution)/shard_map/pallas_call | solution.py:294
  10.3 2.8 %collective-permute-done.across_ref = bf16[256,128]{1,0:T(8,128)(2,1)S(1)} collective-permute-done((bf16[256,128]{1,0:T(8,128)(2,1)}, bf16[256,128]{1,0:T(8,128)(2,1)S(1)}, u32[]{:S(2)}, u32[]{:S(2)}) %collective-permute-start) | collective-permute-done | bytes 65568 | tf_op jit(solution)/shard_map/schur_z/ppermute | solution.py:275
  13.2 1.9 %collective-permute-start.3 = (bf16[2,256,128]{2,1,0:T(8,128)(2,1)S(1)}, bf16[2,256,128]{2,1,0:T(8,128)(2,1)S(1)}, u32[]{:S(2)}, u32[]{:S(2)}) collective-permute-start(bf16[2,256,128]{2,1,0:T(8,128)(2,1)S(1)} %pad_maximum_fusion), channel_id=1, source_target_pairs={{0,3},{1,2},{2,1},{3,0},{4,7},{5,6},{6,5},{7,4},{8,11},{9,10},{10,... | collective-permute-start | bytes 393224 | tf_op jit(solution)/shard_map/schur_z/ppermute | solution.py:275
  15.1 6.1 %collective-permute-start.2 = (bf16[2,256,128]{2,1,0:T(8,128)(2,1)S(1)}, bf16[2,256,128]{2,1,0:T(8,128)(2,1)S(1)}, u32[]{:S(2)}, u32[]{:S(2)}) collective-permute-start(bf16[2,256,128]{2,1,0:T(8,128)(2,1)S(1)} %pad_maximum_fusion), channel_id=1, source_target_pairs={{0,2},{1,3},{2,0},{3,1},{4,6},{5,7},{6,4},{7,5},{8,10},{9,11},{10,... | collective-permute-start | bytes 393224 | tf_op jit(solution)/shard_map/schur_z/ppermute | solution.py:275
  21.2 1.9 %collective-permute-start.1 = (bf16[2,256,128]{2,1,0:T(8,128)(2,1)S(1)}, bf16[2,256,128]{2,1,0:T(8,128)(2,1)S(1)}, u32[]{:S(2)}, u32[]{:S(2)}) collective-permute-start(bf16[2,256,128]{2,1,0:T(8,128)(2,1)S(1)} %pad_maximum_fusion), channel_id=1, source_target_pairs={{0,1},{1,0},{2,3},{3,2},{4,5},{5,4},{6,7},{7,6},{8,9},{9,8},{10,11... | collective-permute-start | bytes 393224 | tf_op jit(solution)/shard_map/schur_z/ppermute | solution.py:275
  23.2 7.8 %all-to-all-start = ((f32[8,72,128]{2,1,0:T(8,128)}), f32[8,72,128]{2,1,0:T(8,128)}, u32[]{:S(2)}, u32[]{:S(2)}) async-start(f32[8,72,128]{2,1,0:T(8,128)} %get-tuple-element.20), calls=%async_computation | async-start | bytes 589824 | tf_op jit(solution)/shard_map/all_to_all | solution.py:283
  31.1 3.2 %collective-permute-start.4 = (bf16[2,2,256,128]{3,2,1,0:T(8,128)(2,1)S(1)}, bf16[2,2,256,128]{3,2,1,0:T(8,128)(2,1)S(1)}, u32[]{:S(2)}, u32[]{:S(2)}) collective-permute-start(bf16[2,2,256,128]{3,2,1,0:T(8,128)(2,1)S(1)} %get-tuple-element.23.refs_0_), channel_id=1, source_target_pairs={{0,8},{1,9},{2,10},{3,11},{4,12},{5,13},{6,14},{7,15},{8,16},{9,17... | collective-permute-start | bytes 786440 | tf_op jit(solution)/shard_map/schur_y/ppermute | solution.py:279
  34.3 3.4 %collective-permute-start.7 = (bf16[2,2,256,128]{3,2,1,0:T(8,128)(2,1)S(1)}, bf16[2,2,256,128]{3,2,1,0:T(8,128)(2,1)S(1)}, u32[]{:S(2)}, u32[]{:S(2)}) collective-permute-start(bf16[2,2,256,128]{3,2,1,0:T(8,128)(2,1)S(1)} %get-tuple-element.24.refs_1_), channel_id=1, source_target_pairs={{0,24},{1,25},{2,26},{3,27},{4,28},{5,29},{6,30},{7,31},{8,0},{9,1... | collective-permute-start | bytes 786440 | tf_op jit(solution)/shard_map/schur_y/ppermute | solution.py:279
  37.6 3.4 %collective-permute-start.9 = (bf16[2,2,256,128]{3,2,1,0:T(8,128)(2,1)S(1)}, bf16[2,2,256,128]{3,2,1,0:T(8,128)(2,1)S(1)}, u32[]{:S(2)}, u32[]{:S(2)}) collective-permute-start(bf16[2,2,256,128]{3,2,1,0:T(8,128)(2,1)S(1)} %get-tuple-element.23.refs_0_), channel_id=1, source_target_pairs={{0,24},{1,25},{2,26},{3,27},{4,28},{5,29},{6,30},{7,31},{8,0},{9,1... | collective-permute-start | bytes 786440 | tf_op jit(solution)/shard_map/schur_y/ppermute | solution.py:279
  41.0 1.9 %collective-permute-start.5 = (bf16[2,2,256,128]{3,2,1,0:T(8,128)(2,1)S(1)}, bf16[2,2,256,128]{3,2,1,0:T(8,128)(2,1)S(1)}, u32[]{:S(2)}, u32[]{:S(2)}) collective-permute-start(bf16[2,2,256,128]{3,2,1,0:T(8,128)(2,1)S(1)} %get-tuple-element.24.refs_1_), channel_id=1, source_target_pairs={{0,8},{1,9},{2,10},{3,11},{4,12},{5,13},{6,14},{7,15},{8,16},{9,17... | collective-permute-start | bytes 786440 | tf_op jit(solution)/shard_map/schur_y/ppermute | solution.py:279
  43.0 1.9 %collective-permute-start.6 = (bf16[2,2,256,128]{3,2,1,0:T(8,128)(2,1)S(1)}, bf16[2,2,256,128]{3,2,1,0:T(8,128)(2,1)S(1)}, u32[]{:S(2)}, u32[]{:S(2)}) collective-permute-start(bf16[2,2,256,128]{3,2,1,0:T(8,128)(2,1)S(1)} %collective-permute-done.4.refs_2_), channel_id=1, source_target_pairs={{0,8},{1,9},{2,10},{3,11},{4,12},{5,13},{6,14},{7,15},{8,16},{9,17... | collective-permute-start | bytes 786440 | tf_op jit(solution)/shard_map/schur_y/ppermute | solution.py:279
  44.9 4.6 %collective-permute-start.8 = (bf16[2,2,256,128]{3,2,1,0:T(8,128)(2,1)S(1)}, bf16[2,2,256,128]{3,2,1,0:T(8,128)(2,1)S(1)}, u32[]{:S(2)}, u32[]{:S(2)}) collective-permute-start(bf16[2,2,256,128]{3,2,1,0:T(8,128)(2,1)S(1)} %collective-permute-done.7.refs_7_), channel_id=1, source_target_pairs={{0,24},{1,25},{2,26},{3,27},{4,28},{5,29},{6,30},{7,31},{8,0},{9,1... | collective-permute-start | bytes 786440 | tf_op jit(solution)/shard_map/schur_y/ppermute | solution.py:279
  49.5 5.5 %all-to-all-done = f32[8,72,128]{2,1,0:T(8,128)} async-done(((f32[8,72,128]{2,1,0:T(8,128)}), f32[8,72,128]{2,1,0:T(8,128)}, u32[]{:S(2)}, u32[]{:S(2)}) %all-to-all-start) | async-done | bytes 294944 | tf_op jit(solution)/shard_map/all_to_all | solution.py:283
  55.0 2.6 %all-gather.recv_ref = f32[16,72,128]{2,1,0:T(8,128)S(1)} all-gather(f32[8,72,128]{2,1,0:T(8,128)} %all-to-all-done), channel_id=2, replica_groups={{0,32},{64,96},{128,160},{192,224},{256,288},{320,352},{384,416},{448,4..., dimensions={0}, use_global_device_ids=true | all-gather | bytes 884736 | tf_op jit(solution)/shard_map/all_gather | solution.py:287
  57.6 0.0 copy-start.4
  57.6 0.0 copy-start.5
  57.6 0.0 copy-start.6
  57.6 0.0 copy-start.7
  57.6 0.0 copy-start.9
  57.6 0.0 copy-start.11
  57.6 2.4 %shard_map.122 = (bf16[32,16,128]{2,1,0:T(8,128)(2,1)S(1)}, f32[16,8,128]{2,1,0:T(8,128)S(1)}) custom-call(f32[16,72,128]{2,1,0:T(8,128)S(1)} %all-gather.recv_ref), custom_call_target="tpu_custom_call" | custom-call | flops 1000000000 | bytes 1048576 | tf_op jit(solution)/shard_map/pallas_call | solution.py:302
  60.1 0.7 shard_map.123
  60.7 23.9 %all_to_all.20 = f32[8,16,256]{2,1,0:T(8,128)S(1)} all-to-all(f32[8,16,256]{2,1,0:T(8,128)S(1)} %shard_map.123), channel_id=1, replica_groups={{448,384,320,256,192,128,64,0},{480,416,352,288,224,160,96,32},{449,385..., dimensions={0} | all-to-all | bytes 262144 | tf_op jit(solution)/shard_map/all_to_all | solution.py:283
  84.6 5.4 %all-gather.1.recv_ref = f32[16,16,256]{2,1,0:T(8,128)S(1)} all-gather(f32[8,16,256]{2,1,0:T(8,128)S(1)} %all_to_all.20), channel_id=3, replica_groups={{0,32},{64,96},{128,160},{192,224},{256,288},{320,352},{384,416},{448,4..., dimensions={0}, use_global_device_ids=true | all-gather | bytes 393216 | tf_op jit(solution)/shard_map/all_gather | solution.py:287
  90.1 1.6 %shard_map.124 = (f32[8,16,400]{2,1,0:T(8,128)S(1)}, f32[8,16,400]{2,1,0:T(8,128)S(1)}, f32[8,16,400]{2,1,0:T(8,128)S(1)}, bf16[8,64,128]{2,1,0:T(8,128)(2,1)S(1)}) custom-call(s32[16]{0:T(128)S(1)} %copy-done.10, s32[16]{0:T(128)S(1)} %copy-done.11, f32[16,16,256]{2,1,0:T(8,128)S(1)} %all-gather.1.recv_ref, f32[8,16,400]{2,1,0:T(8,128)S(1)} %copy-done.5, ...), custom_call_target="tpu_custom_call" | custom-call | flops 1000000000 | bytes 4194304 | tf_op jit(solution)/shard_map/pallas_call | solution.py:304
  91.7 19.8 %all_to_all.21 = bf16[8,64,128]{2,1,0:T(8,128)(2,1)S(1)} all-to-all(bf16[8,64,128]{2,1,0:T(8,128)(2,1)S(1)} %get-tuple-element.28), channel_id=1, replica_groups={{448,384,320,256,192,128,64,0},{480,416,352,288,224,160,96,32},{449,385..., dimensions={0} | all-to-all | bytes 262144 | tf_op jit(solution)/shard_map/all_to_all | solution.py:283
  111.5 2.2 %all-gather.2.recv_ref = bf16[16,64,128]{2,1,0:T(8,128)(2,1)S(1)} all-gather(bf16[8,64,128]{2,1,0:T(8,128)(2,1)S(1)} %all_to_all.21), channel_id=4, replica_groups={{0,32},{64,96},{128,160},{192,224},{256,288},{320,352},{384,416},{448,4..., dimensions={0}, use_global_device_ids=true | all-gather | bytes 393216 | tf_op jit(solution)/shard_map/all_gather | solution.py:287
  113.6 2.9 %shard_map.125 = (f32[16,256]{1,0:T(8,128)S(1)}, bf16[8,16,256]{2,1,0:T(8,128)(2,1)S(1)}) custom-call(bf16[16,64,128]{2,1,0:T(8,128)(2,1)S(1)} %all-gather.2.recv_ref, f32[16,8,128]{2,1,0:T(8,128)S(1)} %get-tuple-element.29.map_ref, bf16[2,2,256,128]{3,2,1,0:T(8,128)(2,1)S(1)} %get-tuple-element.23.refs_0_, ...), custom_call_target="tpu_custom_call" | custom-call | flops 1000000000 | bytes 3145728 | tf_op jit(solution)/shard_map/pallas_call | solution.py:305
  116.5 16.5 %all_to_all.22 = bf16[8,16,256]{2,1,0:T(8,128)(2,1)S(1)} all-to-all(bf16[8,16,256]{2,1,0:T(8,128)(2,1)S(1)} %get-tuple-element.30), channel_id=1, replica_groups={{448,384,320,256,192,128,64,0},{480,416,352,288,224,160,96,32},{449,385..., dimensions={0} | all-to-all | bytes 131072 | tf_op jit(solution)/shard_map/all_to_all | solution.py:283
  133.1 3.3 %all-gather.3.recv_ref = bf16[16,16,256]{2,1,0:T(8,128)(2,1)S(1)} all-gather(bf16[8,16,256]{2,1,0:T(8,128)(2,1)S(1)} %all_to_all.22), channel_id=5, replica_groups={{0,32},{64,96},{128,160},{192,224},{256,288},{320,352},{384,416},{448,4..., dimensions={0}, use_global_device_ids=true | all-gather | bytes 196608 | tf_op jit(solution)/shard_map/all_gather | solution.py:287
  136.4 1.3 shard_map.126
  (29 shorter events, 0.1 us)
Async XLA Ops:
  0.6 12.6 %copy-start.8 = (bf16[256,128]{1,0:T(8,128)(2,1)S(1)}, bf16[256,128]{1,0:T(8,128)(2,1)}, u32[]{:S(2)}) copy-start(bf16[256,128]{1,0:T(8,128)(2,1)} %own_ref.1) | copy-start | bytes 196612
  0.6 12.5 %collective-permute-start = (bf16[256,128]{1,0:T(8,128)(2,1)}, bf16[256,128]{1,0:T(8,128)(2,1)S(1)}, u32[]{:S(2)}, u32[]{:S(2)}) collective-permute-start(bf16[256,128]{1,0:T(8,128)(2,1)} %own_ref.1), channel_id=1, source_target_pairs={{0,4},{1,5},{2,6},{3,7},{4,0},{5,1},{6,2},{7,3},{8,12},{9,13},{10,... | collective-permute-start | bytes 196616 | tf_op jit(solution)/shard_map/schur_z/ppermute | solution.py:275
  13.2 17.8 %collective-permute-start.3 = (bf16[2,256,128]{2,1,0:T(8,128)(2,1)S(1)}, bf16[2,256,128]{2,1,0:T(8,128)(2,1)S(1)}, u32[]{:S(2)}, u32[]{:S(2)}) collective-permute-start(bf16[2,256,128]{2,1,0:T(8,128)(2,1)S(1)} %pad_maximum_fusion), channel_id=1, source_target_pairs={{0,3},{1,2},{2,1},{3,0},{4,7},{5,6},{6,5},{7,4},{8,11},{9,10},{10,... | collective-permute-start | bytes 393224 | tf_op jit(solution)/shard_map/schur_z/ppermute | solution.py:275
  15.1 15.9 %collective-permute-start.2 = (bf16[2,256,128]{2,1,0:T(8,128)(2,1)S(1)}, bf16[2,256,128]{2,1,0:T(8,128)(2,1)S(1)}, u32[]{:S(2)}, u32[]{:S(2)}) collective-permute-start(bf16[2,256,128]{2,1,0:T(8,128)(2,1)S(1)} %pad_maximum_fusion), channel_id=1, source_target_pairs={{0,2},{1,3},{2,0},{3,1},{4,6},{5,7},{6,4},{7,5},{8,10},{9,11},{10,... | collective-permute-start | bytes 393224 | tf_op jit(solution)/shard_map/schur_z/ppermute | solution.py:275
  21.2 9.8 %collective-permute-start.1 = (bf16[2,256,128]{2,1,0:T(8,128)(2,1)S(1)}, bf16[2,256,128]{2,1,0:T(8,128)(2,1)S(1)}, u32[]{:S(2)}, u32[]{:S(2)}) collective-permute-start(bf16[2,256,128]{2,1,0:T(8,128)(2,1)S(1)} %pad_maximum_fusion), channel_id=1, source_target_pairs={{0,1},{1,0},{2,3},{3,2},{4,5},{5,4},{6,7},{7,6},{8,9},{9,8},{10,11... | collective-permute-start | bytes 393224 | tf_op jit(solution)/shard_map/schur_z/ppermute | solution.py:275
  23.2 31.8 %all-to-all-start = ((f32[8,72,128]{2,1,0:T(8,128)}), f32[8,72,128]{2,1,0:T(8,128)}, u32[]{:S(2)}, u32[]{:S(2)}) async-start(f32[8,72,128]{2,1,0:T(8,128)} %get-tuple-element.20), calls=%async_computation | async-start | bytes 589824 | tf_op jit(solution)/shard_map/all_to_all | solution.py:283
  31.1 11.9 %collective-permute-start.4 = (bf16[2,2,256,128]{3,2,1,0:T(8,128)(2,1)S(1)}, bf16[2,2,256,128]{3,2,1,0:T(8,128)(2,1)S(1)}, u32[]{:S(2)}, u32[]{:S(2)}) collective-permute-start(bf16[2,2,256,128]{3,2,1,0:T(8,128)(2,1)S(1)} %get-tuple-element.23.refs_0_), channel_id=1, source_target_pairs={{0,8},{1,9},{2,10},{3,11},{4,12},{5,13},{6,14},{7,15},{8,16},{9,17... | collective-permute-start | bytes 786440 | tf_op jit(solution)/shard_map/schur_y/ppermute | solution.py:279
  34.3 10.6 %collective-permute-start.7 = (bf16[2,2,256,128]{3,2,1,0:T(8,128)(2,1)S(1)}, bf16[2,2,256,128]{3,2,1,0:T(8,128)(2,1)S(1)}, u32[]{:S(2)}, u32[]{:S(2)}) collective-permute-start(bf16[2,2,256,128]{3,2,1,0:T(8,128)(2,1)S(1)} %get-tuple-element.24.refs_1_), channel_id=1, source_target_pairs={{0,24},{1,25},{2,26},{3,27},{4,28},{5,29},{6,30},{7,31},{8,0},{9,1... | collective-permute-start | bytes 786440 | tf_op jit(solution)/shard_map/schur_y/ppermute | solution.py:279
  37.6 22.4 %collective-permute-start.9 = (bf16[2,2,256,128]{3,2,1,0:T(8,128)(2,1)S(1)}, bf16[2,2,256,128]{3,2,1,0:T(8,128)(2,1)S(1)}, u32[]{:S(2)}, u32[]{:S(2)}) collective-permute-start(bf16[2,2,256,128]{3,2,1,0:T(8,128)(2,1)S(1)} %get-tuple-element.23.refs_0_), channel_id=1, source_target_pairs={{0,24},{1,25},{2,26},{3,27},{4,28},{5,29},{6,30},{7,31},{8,0},{9,1... | collective-permute-start | bytes 786440 | tf_op jit(solution)/shard_map/schur_y/ppermute | solution.py:279
  41.0 19.0 %collective-permute-start.5 = (bf16[2,2,256,128]{3,2,1,0:T(8,128)(2,1)S(1)}, bf16[2,2,256,128]{3,2,1,0:T(8,128)(2,1)S(1)}, u32[]{:S(2)}, u32[]{:S(2)}) collective-permute-start(bf16[2,2,256,128]{3,2,1,0:T(8,128)(2,1)S(1)} %get-tuple-element.24.refs_1_), channel_id=1, source_target_pairs={{0,8},{1,9},{2,10},{3,11},{4,12},{5,13},{6,14},{7,15},{8,16},{9,17... | collective-permute-start | bytes 786440 | tf_op jit(solution)/shard_map/schur_y/ppermute | solution.py:279
  43.0 17.1 %collective-permute-start.6 = (bf16[2,2,256,128]{3,2,1,0:T(8,128)(2,1)S(1)}, bf16[2,2,256,128]{3,2,1,0:T(8,128)(2,1)S(1)}, u32[]{:S(2)}, u32[]{:S(2)}) collective-permute-start(bf16[2,2,256,128]{3,2,1,0:T(8,128)(2,1)S(1)} %collective-permute-done.4.refs_2_), channel_id=1, source_target_pairs={{0,8},{1,9},{2,10},{3,11},{4,12},{5,13},{6,14},{7,15},{8,16},{9,17... | collective-permute-start | bytes 786440 | tf_op jit(solution)/shard_map/schur_y/ppermute | solution.py:279
  44.9 15.1 %collective-permute-start.8 = (bf16[2,2,256,128]{3,2,1,0:T(8,128)(2,1)S(1)}, bf16[2,2,256,128]{3,2,1,0:T(8,128)(2,1)S(1)}, u32[]{:S(2)}, u32[]{:S(2)}) collective-permute-start(bf16[2,2,256,128]{3,2,1,0:T(8,128)(2,1)S(1)} %collective-permute-done.7.refs_7_), channel_id=1, source_target_pairs={{0,24},{1,25},{2,26},{3,27},{4,28},{5,29},{6,30},{7,31},{8,0},{9,1... | collective-permute-start | bytes 786440 | tf_op jit(solution)/shard_map/schur_y/ppermute | solution.py:279
  57.5 32.5 %copy-start = (bf16[8,400,400]{2,1,0:T(8,128)(2,1)S(1)}, bf16[8,400,400]{2,1,0:T(8,128)(2,1)}, u32[]{:S(2)}) copy-start(bf16[8,400,400]{2,1,0:T(8,128)(2,1)} %inv_ref.3) | copy-start | bytes 7680004
  57.5 32.5 %copy-start.1 = (s32[8,16,400]{2,1,0:T(8,128)S(1)}, s32[8,16,400]{2,1,0:T(8,128)}, u32[]{:S(2)}) copy-start(s32[8,16,400]{2,1,0:T(8,128)} %breaker_ref.3) | copy-start | bytes 614404
  57.5 32.5 %copy-start.2 = (f32[8,16,400]{2,1,0:T(8,128)S(1)}, f32[8,16,400]{2,1,0:T(8,128)}, u32[]{:S(2)}) copy-start(f32[8,16,400]{2,1,0:T(8,128)} %volt_ref.1) | copy-start | bytes 614404
  57.6 32.5 %copy-start.3 = (f32[8,16,400]{2,1,0:T(8,128)S(1)}, f32[8,16,400]{2,1,0:T(8,128)}, u32[]{:S(2)}) copy-start(f32[8,16,400]{2,1,0:T(8,128)} %curr_ref.1) | copy-start | bytes 614404
  57.6 32.5 %copy-start.4 = (bf16[256,512]{1,0:T(8,128)(2,1)S(1)}, bf16[256,512]{1,0:T(8,128)(2,1)}, u32[]{:S(2)}) copy-start(bf16[256,512]{1,0:T(8,128)(2,1)} %get-tuple-element.26.right_ref) | copy-start | bytes 786436
  57.6 32.5 %copy-start.5 = (f32[8,16,400]{2,1,0:T(8,128)S(1)}, f32[8,16,400]{2,1,0:T(8,128)}, u32[]{:S(2)}) copy-start(f32[8,16,400]{2,1,0:T(8,128)} %get-tuple-element.25.prev_ref) | copy-start | bytes 614404
  57.6 32.5 %copy-start.6 = (f32[8,400]{1,0:T(8,128)S(1)}, f32[8,400]{1,0:T(8,128)}, u32[]{:S(2)}) copy-start(f32[8,400]{1,0:T(8,128)} %gain_ref.3) | copy-start | bytes 38404
  57.6 32.5 %copy-start.7 = (f32[8,512]{1,0:T(8,128)S(1)}, f32[8,512]{1,0:T(8,128)}, u32[]{:S(2)}) copy-start(f32[8,512]{1,0:T(8,128)} %get-tuple-element.27.rows_ref) | copy-start | bytes 49156
  57.6 32.5 %copy-start.9 = (f32[8,64]{1,0:T(8,128)S(1)}, f32[8,64]{1,0:T(8,128)}, u32[]{:S(2)}) copy-start(f32[8,64]{1,0:T(8,128)} %tie_ref.1) | copy-start | bytes 6148
  57.6 32.5 %copy-start.10 = (s32[16]{0:T(128)S(1)}, s32[16]{0:T(128)}, u32[]{:S(2)}) copy-start(s32[16]{0:T(128)} %time_ref.3) | copy-start | bytes 196
  57.6 32.4 %copy-start.11 = (s32[16]{0:T(128)S(1)}, s32[16]{0:T(128)}, u32[]{:S(2)}) copy-start(s32[16]{0:T(128)} %node_ref.3) | copy-start | bytes 196
